TPU v7x, 512 devices: a whole 4x8x8 slice. The times are simulated.
512 devices in a mesh: dp: 32 (over z, x_hi, core), expert: 16 (over x_lo, y).
Axes of the slice: x: 4 (x_hi: 2, x_lo: 2; x = x_hi * 2 + x_lo), y: 8, z: 8, core: 2. Of those that a mesh axis runs over, the one named last changes fastest.
Arguments:
- tokens: bfloat16 [4096, 2048], P('dp'), may hold values from -6 to 6
- out_grad: bfloat16 [4096, 2048], P('dp', 'expert'), may hold values from -6 to 6
- modality: int32 [4096], P('dp'), may hold values 0 or 1
- within_route: int32 [4096], P('dp'), may hold values from 0 to 3
- gate_values: float32 [4096], P('dp'), may hold values from 0.2 to 1
- w_gate: bfloat16 [16, 5504, 2048], P('expert', 'dp'), may hold values from -0.125 to 0.125
- w_up: bfloat16 [16, 5504, 2048], P('expert', 'dp'), may hold values from -0.125 to 0.125
- w_down: bfloat16 [16, 5504, 2048], P('expert', 'dp'), may hold values from -0.0546875 to 0.0546875
Outputs:
- grad_gate: bfloat16 [16, 5504, 2048], P('expert', 'dp')
- grad_up: bfloat16 [16, 5504, 2048], P('expert', 'dp')
- grad_down: bfloat16 [16, 5504, 2048], P('expert', 'dp')
- grad_tokens: bfloat16 [4096, 2048], P('dp', 'expert')
All inputs are finite; a program needn't handle non-finite values. No bound on the sum of `modality` on one device may be relied on, other than what follows from the above.
Results may differ from a plain program's by a relative error of at most 0.0058.
Values may be sent and summed in bfloat16 or wider, within the bound.
No kernel may reach another device: no remote copies, remote signals or barrier semaphores. Data moves between devices by JAX's collectives and lax.ppermute only.
A program may use at most 64 MiB of HBM per device.

v0:
```python
import jax
import jax.numpy as jnp
from jax import lax
from jax.sharding import PartitionSpec as P


def sum_sources(received):
    return jnp.sum(received, axis=0)


def local(tokens, out_grad, modality, within_route, gate_values, w_gate, w_up, w_down):
    tok_count = tokens.shape[0]
    width = tokens.shape[1]
    experts_all = lax.axis_size("expert") // 2
    per_modality = experts_all // 2
    capacity = tok_count * 3 // (2 * experts_all)
    position = lax.axis_index("expert")
    own_expert = position // 2
    expert_id = per_modality * modality + within_route
    one_hot = (expert_id[:, None] == jnp.arange(experts_all, dtype=jnp.int32)[None, :]).astype(
        jnp.int32
    )
    before = jnp.cumsum(one_hot, axis=0) - one_hot
    slot_rank = jnp.sum(before * one_hot, axis=1)
    picked = (expert_id == own_expert)[None, :] & (
        slot_rank[None, :] == jnp.arange(capacity, dtype=jnp.int32)[:, None]
    )
    select = picked.astype(jnp.bfloat16)
    full_grad = lax.all_gather(out_grad, "expert", axis=1, tiled=True)
    scaled = (gate_values[:, None] * full_grad.astype(jnp.float32)).astype(jnp.bfloat16)
    x_local = jnp.dot(select, tokens, preferred_element_type=jnp.float32).astype(jnp.bfloat16)
    dy_local = jnp.dot(select, scaled, preferred_element_type=jnp.float32).astype(jnp.bfloat16)
    x_rows, dy_rows = (
        lax.all_gather(x_local, "dp", axis=0, tiled=True),
        lax.all_gather(dy_local, "dp", axis=0, tiled=True),
    )
    wg = w_gate[0]
    wu = w_up[0]
    wd = w_down[0]
    feat_dims = (((1,), (1,)), ((), ()))
    gate_pre = lax.dot_general(x_rows, wg, feat_dims, preferred_element_type=jnp.float32)
    up_pre = lax.dot_general(x_rows, wu, feat_dims, preferred_element_type=jnp.float32)
    sig_gate = jax.nn.sigmoid(gate_pre)
    silu_gate = gate_pre * sig_gate
    hidden = (silu_gate * up_pre).astype(jnp.bfloat16)
    d_hidden = lax.dot_general(dy_rows, wd, feat_dims, preferred_element_type=jnp.float32)
    d_gate = (d_hidden * up_pre * sig_gate * (1.0 + gate_pre * (1.0 - sig_gate))).astype(
        jnp.bfloat16
    )
    d_up = (d_hidden * silu_gate).astype(jnp.bfloat16)
    rows_dims = (((0,), (0,)), ((), ()))
    grad_g = lax.dot_general(d_gate, x_rows, rows_dims, preferred_element_type=jnp.float32).astype(
        jnp.bfloat16
    )
    grad_u = lax.dot_general(d_up, x_rows, rows_dims, preferred_element_type=jnp.float32).astype(
        jnp.bfloat16
    )
    grad_d = lax.dot_general(hidden, dy_rows, rows_dims, preferred_element_type=jnp.float32).astype(
        jnp.bfloat16
    )
    terms = jnp.dot(d_gate, wg, preferred_element_type=jnp.float32)
    terms = terms + jnp.dot(d_up, wu, preferred_element_type=jnp.float32)
    terms = terms.reshape(-1, capacity, width)
    group_terms = sum_sources(lax.all_to_all(terms, "dp", split_axis=0, concat_axis=0, tiled=True))
    token_terms = jnp.dot(
        picked.astype(jnp.float32).T, group_terms, precision=lax.Precision.HIGHEST
    )
    grad_tokens = lax.psum_scatter(token_terms, "expert", scatter_dimension=1, tiled=True).astype(
        jnp.bfloat16
    )
    return (grad_g[None], grad_u[None], grad_d[None], grad_tokens)


def solution(mesh):
    placed = (
        P("dp", None),
        P("dp", "expert"),
        P("dp"),
        P("dp"),
        P("dp"),
        P("expert", "dp", None),
        P("expert", "dp", None),
        P("expert", "dp", None),
    )
    return jax.shard_map(
        local,
        mesh=mesh,
        in_specs=placed,
        out_specs=(
            P("expert", "dp", None),
            P("expert", "dp", None),
            P("expert", "dp", None),
            P("dp", "expert"),
        ),
        check_vma=False,
    )
```

profile of v0, /device:TPU:4, one launch (start us, length us, event | category | flops | bytes accessed | tf_op | source)
XLA Modules:
  0.0 430.1 jit_solution(12573858632057254544)
XLA Ops:
  7.2 0.0 copy-start
  7.2 0.0 all-gather.5.cloned.1.call-start
  7.2 0.7 broadcast_compare_fusion
  8.0 0.1 fusion.15
  8.1 0.2 reduce_window_sum.11
  8.2 0.2 select_reduce_fusion
  8.4 1.9 convolution_convert_fusion.3
  10.3 0.0 all-gather.5.cloned.1.call-update
  10.3 0.0 all-gather.3.cloned.1.call-start
  10.4 36.7 %all_gather.9 = bf16[128,2048]{1,0:T(8,128)(2,1)S(1)} all-gather(bf16[128,128]{1,0:T(8,128)(2,1)} %param.9), channel_id=1, replica_groups=mesh['dp'=32,'expert'=16] {'expert'}, dimensions={1}, use_global_device_ids=true | all-gather | bytes 557056 | tf_op jit(solution)/shard_map/all_gather | solution.py:29
  47.0 1.6 convolution_convert_fusion.4
  48.6 0.0 copy-start.3
  48.6 0.0 all-gather.3.cloned.1.call-update
  48.6 0.0 reduce-scatter.2.cloned.1.call-start
  48.7 55.1 %all-gather.5.cloned.1.call-done = bf16[768,2048]{1,0:T(8,128)(2,1)} async-done(((bf16[24,2048]{1,0:T(8,128)(2,1)}), bf16[768,2048]{1,0:T(8,128)(2,1)}) %all-gather.5.cloned.1.call-update) | async-done | bytes 3145744 | tf_op jit(solution)/shard_map/all_gather | solution.py:34
  103.8 0.0 copy-done
  103.8 0.0 copy-start.1
  103.8 3.2 fusion.5
  107.1 0.0 copy-done.3
  107.1 0.0 copy-done.1
  107.1 0.0 copy-start.5
  107.1 2.0 fusion.8
  109.1 84.5 %all-gather.3.cloned.1.call-done = bf16[768,2048]{1,0:T(8,128)(2,1)} async-done(((bf16[24,2048]{1,0:T(8,128)(2,1)}), bf16[768,2048]{1,0:T(8,128)(2,1)}) %all-gather.3.cloned.1.call-update) | async-done | bytes 3145744 | tf_op jit(solution)/shard_map/all_gather | solution.py:35
  193.6 0.0 copy-done.5
  193.6 3.3 multiply_convert_fusion.2
  196.9 1.0 fusion.3
  197.9 1.1 convolution_add_fusion
  198.9 148.3 %all_to_all.5 = f32[32,24,2048]{2,1,0:T(8,128)} all-to-all(f32[32,24,2048]{2,1,0:T(8,128)S(1)} %bitcast.34), channel_id=1, replica_groups=mesh['dp'=32,'expert'=16] {'dp'}, dimensions={0} | all-to-all | bytes 12582912 | tf_op jit(solution)/shard_map/all_to_all | solution.py:64
  347.3 3.1 reduce_sum.19
  350.4 1.6 fusion.17
  352.0 0.0 reduce-scatter.2.cloned.1.call-update
  352.0 0.0 copy-start.2
  352.0 0.0 copy-start.4
  352.0 0.0 copy-start.6
  352.0 3.6 fusion.1
  355.6 0.0 copy-done.2
  355.6 1.6 fusion
  357.3 0.0 copy-done.4
  357.3 0.0 copy-done.6
  357.3 1.7 fusion.2
  358.9 63.2 %reduce-scatter.2.cloned.1.call-done = f32[128,128]{1,0:T(8,128)} async-done(((f32[128,2048]{1,0:T(8,128)}), f32[128,128]{1,0:T(8,128)}) %reduce-scatter.2.cloned.1.call-update) | async-done | bytes 65552 | tf_op jit(solution)/shard_map/reduce_scatter | solution.py:68
  422.1 1.5 convert_element_type.49
Async XLA Ops:
  7.2 96.7 %copy-start = (bf16[1,172,2048]{2,1,0:T(8,128)(2,1)S(1)}, bf16[1,172,2048]{2,1,0:T(8,128)(2,1)}, u32[]{:S(2)}) copy-start(bf16[1,172,2048]{2,1,0:T(8,128)(2,1)} %param.13) | copy-start | bytes 2113540
  7.2 96.7 %all-gather.5.cloned.1.call-start = ((), (), s32[]{:S(2)}) async-start(), calls=%async_computation.3 | async-start | bytes 3244032 | tf_op jit(solution)/shard_map/all_gather | solution.py:34
  10.3 183.3 %all-gather.3.cloned.1.call-start = ((), (), s32[]{:S(2)}) async-start(), calls=%async_computation.2 | async-start | bytes 3244032 | tf_op jit(solution)/shard_map/all_gather | solution.py:35
  48.6 58.5 %copy-start.3 = (bf16[1,172,2048]{2,1,0:T(8,128)(2,1)S(1)}, bf16[1,172,2048]{2,1,0:T(8,128)(2,1)}, u32[]{:S(2)}) copy-start(bf16[1,172,2048]{2,1,0:T(8,128)(2,1)} %param.14) | copy-start | bytes 2113540
  48.6 373.5 %reduce-scatter.2.cloned.1.call-start = ((), (), s32[]{:S(2)}) async-start(), calls=%async_computation.4 | async-start | bytes 1114112 | tf_op jit(solution)/shard_map/reduce_scatter | solution.py:68
  103.8 3.2 copy-start.1
  107.1 86.5 %copy-start.5 = (bf16[1,172,2048]{2,1,0:T(8,128)(2,1)S(1)}, bf16[1,172,2048]{2,1,0:T(8,128)(2,1)}, u32[]{:S(2)}) copy-start(bf16[1,172,2048]{2,1,0:T(8,128)(2,1)} %param.15) | copy-start | bytes 2113540
  352.0 3.7 copy-start.2
  352.0 5.3 %copy-start.4 = (bf16[768,2048]{1,0:T(8,128)(2,1)S(1)}, bf16[768,2048]{1,0:T(8,128)(2,1)}, u32[]{:S(2)}) copy-start(bf16[768,2048]{1,0:T(8,128)(2,1)} %all-gather.3.cloned.1.call-done) | copy-start | bytes 9437188
  352.0 5.3 %copy-start.6 = (f32[768,172]{0,1:T(8,128)S(1)}, f32[768,172]{0,1:T(8,128)}, u32[]{:S(2)}) copy-start(f32[768,172]{0,1:T(8,128)} %fusion.8) | copy-start | bytes 1585156
Sparse Core Ops, SparseCore 0:
  11.9 91.8 all-gather.4
  107.8 85.7 all-gather.2
  352.1 69.9 reduce-scatter.1
where the time goes:
time: 430 us
  waiting for transfers between devices  203 us (47%)
  blocking collectives  185 us (43%)
  matrix products  22.5 us (5%)
  between operations  13.9 us (3%)
  other arithmetic  5.73 us (1%)
    all_to_all x1, blocking collectives, local(): lax.all_to_all(terms, 'dp', split_axis=0, concat_axis=0, tiled=True)  148 us
    all_gather x1, waiting for transfers between devices, local(): lax.all_gather(dy_local, 'dp', axis=0, tiled=True)  84.5 us
    reduce_scatter x1, waiting for transfers between devices, local(): lax.psum_scatter(token_terms, 'expert', scatter_dimension=1, tiled=True)  63.2 us
    all_gather x1, waiting for transfers between devices, local(): lax.all_gather(x_local, 'dp', axis=0, tiled=True)  55.1 us
    all_gather x1, blocking collectives, local(): full_grad = lax.all_gather(out_grad, 'expert', axis=1, tiled=True)  36.7 us
  transfers between devices with their start and end apart: 3, of which 3 were waited for; matrix products, arithmetic and copies ran while one was open for 3% of the time, Pallas kernels for 0%

commit v1 on v0

v1 whole, which is shorter than its diff:
```python
import jax
import jax.numpy as jnp
from jax import lax
from jax.sharding import Mesh
from jax.sharding import PartitionSpec as P

BF = jnp.bfloat16
F32 = jnp.float32
Z, XH, CORE, XL, Y = 8, 2, 2, 2, 8
AXES = ("z", "xh", "core", "xl", "y")
EXPERT = ("xl", "y")
SWAP = [(0, 1), (1, 0)]
CROSS = [(0, 3), (1, 2), (2, 1), (3, 0)]
ONWARD = [(2 * z + c, 2 * ((z + 1 - 2 * c) % Z) + c) for z in range(Z) for c in range(2)]
HOMEWARD = [(b, a) for a, b in ONWARD]
PAD = 176


def dot(a, b, dims=((1,), (0,))):
    return lax.dot_general(a, b, (dims, ((), ())), preferred_element_type=F32)


def onward(a):
    return lax.ppermute(a, ("z", "core"), ONWARD)


def homeward(a):
    return lax.ppermute(a, ("z", "core"), HOMEWARD)


def plane_rows(a):
    return jnp.concatenate(
        [
            a,
            lax.ppermute(a, "xh", SWAP),
            lax.ppermute(a, "core", SWAP),
            lax.ppermute(a, ("xh", "core"), CROSS),
        ],
        axis=0,
    )


def ring_rows(rows):
    half = rows.shape[0] // 2
    one = onward(rows)
    two = onward(one)
    three = onward(two)
    four = onward(three[:half])
    return [rows[:half], one, two, three, four]


def local(tokens, out_grad, modality, within_route, gate_values, w_gate, w_up, w_down):
    tok_count, width = tokens.shape
    experts_all = XL * Y // 2
    per_modality = experts_all // 2
    capacity = tok_count * 3 // (2 * experts_all)
    hidden_own = w_gate.shape[1]
    position = lax.axis_index(EXPERT)
    own_expert = position // 2
    expert_id = per_modality * modality + within_route
    one_hot = (expert_id[:, None] == jnp.arange(experts_all, dtype=jnp.int32)[None, :]).astype(
        jnp.int32
    )
    before = jnp.cumsum(one_hot, axis=0) - one_hot
    slot_rank = jnp.sum(before * one_hot, axis=1)
    kept = slot_rank < capacity
    slot = jnp.where(kept, expert_id * capacity + slot_rank, -1)
    slots = jnp.arange(experts_all * capacity, dtype=jnp.int32)
    select = (slot[None, :] == slots[:, None]).astype(BF)
    own_slots = own_expert * capacity + jnp.arange(capacity, dtype=jnp.int32)
    select_own = (slot[None, :] == own_slots[:, None]).astype(BF)

    pad = ((0, PAD - hidden_own), (0, 0))
    own_w = jnp.stack([jnp.pad(w_gate[0], pad), jnp.pad(w_up[0], pad), jnp.pad(w_down[0], pad)])
    other_w = lax.ppermute(own_w, "core", SWAP)
    wg = jnp.concatenate([own_w[0], other_w[0]], axis=0)
    wu = jnp.concatenate([own_w[1], other_w[1]], axis=0)
    wd = jnp.concatenate([own_w[2], other_w[2]], axis=0)

    x_own = dot(select_own, tokens).astype(BF)
    x_plane, wg, wu, wd = lax.optimization_barrier((plane_rows(x_own), wg, wu, wd))
    x_parts = ring_rows(x_plane)
    scaled = (gate_values[:, None] * out_grad.astype(F32)).astype(BF)
    dy_slices = dot(select, scaled).astype(BF).reshape(experts_all, 1, capacity, -1)
    dy_slices = jnp.broadcast_to(dy_slices, (experts_all, 2) + dy_slices.shape[2:])
    dy_slices = dy_slices.reshape((2 * experts_all,) + dy_slices.shape[2:])
    dy_slices = lax.all_to_all(dy_slices, EXPERT, 0, 0, tiled=True)
    dy_own = jnp.transpose(dy_slices, (1, 0, 2)).reshape(capacity, width)
    dy_parts = ring_rows(plane_rows(dy_own))

    cols = ((1,), (1,))
    terms, hiddens, d_gates, d_ups = [], [], [], []
    for x_rows, dy_rows in zip(x_parts, dy_parts):
        gate_pre = dot(x_rows, wg, cols)
        up_pre = dot(x_rows, wu, cols)
        sig_gate = jax.nn.sigmoid(gate_pre)
        silu_gate = gate_pre * sig_gate
        hiddens.append((silu_gate * up_pre).astype(BF))
        d_hidden = dot(dy_rows, wd, cols)
        d_gate = (d_hidden * up_pre * sig_gate * (1.0 + gate_pre * (1.0 - sig_gate))).astype(BF)
        d_up = (d_hidden * silu_gate).astype(BF)
        d_gates.append(d_gate)
        d_ups.append(d_up)
        terms.append(dot(d_gate, wg) + dot(d_up, wu))

    half = terms[0].shape[0]
    travelling = homeward(terms[4].astype(BF)).astype(F32)
    travelling = jnp.concatenate([terms[3][:half] + travelling, terms[3][half:]], axis=0)
    travelling = homeward(travelling.astype(BF)).astype(F32)
    travelling = homeward((terms[2] + travelling).astype(BF)).astype(F32)
    travelling = homeward((terms[1] + travelling).astype(BF)).astype(F32)
    across = lax.ppermute(travelling[half:].astype(BF), "core", SWAP).astype(F32)
    travelling = terms[0] + travelling[:half] + across
    across = lax.ppermute(travelling[capacity:].astype(BF), "xh", SWAP).astype(F32)
    summed = (travelling[:capacity] + across).reshape(capacity, 2 * experts_all, -1)
    summed = jnp.transpose(summed, (1, 0, 2)).astype(BF)
    summed = lax.all_to_all(summed, EXPERT, 0, 0, tiled=True)

    from_slots = jnp.arange(2 * experts_all * capacity, dtype=jnp.int32)
    from_slots = from_slots // (2 * capacity) * capacity + from_slots % capacity
    place = (slot[:, None] == from_slots[None, :]).astype(BF)
    grad_tokens = dot(place, summed.reshape(2 * experts_all * capacity, -1)).astype(BF)

    x_all = jnp.concatenate(x_parts, axis=0)
    dy_all = jnp.concatenate(dy_parts, axis=0)
    rows = ((0,), (0,))
    grads = [
        dot(jnp.concatenate(d_gates, axis=0), x_all, rows),
        dot(jnp.concatenate(d_ups, axis=0), x_all, rows),
        dot(jnp.concatenate(hiddens, axis=0), dy_all, rows),
    ]
    outs = []
    for grad in grads:
        received = lax.ppermute(grad[PAD:].astype(BF), "core", SWAP).astype(F32)
        outs.append((grad[:PAD] + received)[:hidden_own].astype(BF)[None])
    return (*outs, grad_tokens)


def solution(mesh):
    fine = Mesh(mesh.devices.reshape(Z, XH, CORE, XL, Y), AXES)
    dp = ("z", "xh", "core")
    placed = (
        P(dp, None),
        P(dp, EXPERT),
        P(dp),
        P(dp),
        P(dp),
        P(EXPERT, dp, None),
        P(EXPERT, dp, None),
        P(EXPERT, dp, None),
    )
    return jax.shard_map(
        local,
        mesh=fine,
        in_specs=placed,
        out_specs=(
            P(EXPERT, dp, None),
            P(EXPERT, dp, None),
            P(EXPERT, dp, None),
            P(dp, EXPERT),
        ),
        check_vma=False,
    )
```

time: 430 us -> 208 us (0.48)
  the two profiles are of different devices: /device:TPU:4 before, /device:TPU:1 now
where the time goes in v1:
time: 208 us; the launch traced here: 206 us
  starting transfers between devices  118 us (57%)
  waiting for transfers between devices  54 us (26%)
  matrix products  17.6 us (8%)
  local copies, waits for them, and re-layouts  7.67 us (4%)
  other arithmetic  7.2 us (3%)
    ppermute x8, starting transfers between devices, onward(): return lax.ppermute(a, ('z', 'core'), ONWARD)  40.4 us
    ppermute x3, starting transfers between devices, local(): received = lax.ppermute(grad[PAD:].astype(BF), 'core', SWAP).astype(F32)  24.7 us
    ppermute x8, waiting for transfers between devices, onward(): return lax.ppermute(a, ('z', 'core'), ONWARD)  22.6 us
    dot_general x31, matrix products, dot(): return lax.dot_general(a, b, (dims, ((), ())), preferred_element_type=F32)  17.6 us
    ppermute x4, waiting for transfers between devices, homeward(): return lax.ppermute(a, ('z', 'core'), HOMEWARD)  14.8 us
    all_to_all x1, starting transfers between devices, local(): dy_slices = lax.all_to_all(dy_slices, EXPERT, 0, 0, tiled=True)  8.68 us
    ppermute x2, starting transfers between devices, plane_rows(): lax.ppermute(a, ('xh', 'core'), CROSS)  8.27 us
    ppermute x4, starting transfers between devices, homeward(): return lax.ppermute(a, ('z', 'core'), HOMEWARD)  7.86 us
  transfers between devices with their start and end apart: 26, of which 13 were waited for; matrix products, arithmetic and copies ran while one was open for 10% of the time, Pallas kernels for 0%

profile of v1, /device:TPU:1, one launch (start us, length us, event | category | flops | bytes accessed | tf_op | source)
XLA Modules:
  0.0 205.8 jit_solution(11328239656133988504)
XLA Ops:
  0.7 0.8 multiply_add_fusion
  1.9 1.0 convolution_convert_fusion.1
  2.9 0.7 broadcast_in_dim.16
  3.5 8.7 %all-to-all-start = ((bf16[16,24,128]{2,1,0:T(8,128)(2,1)}), bf16[16,24,128]{2,1,0:T(8,128)(2,1)S(1)}, u32[]{:S(2)}, u32[]{:S(2)}) async-start(bf16[16,24,128]{2,1,0:T(8,128)(2,1)} %bitcast.1), calls=%async_computation | async-start | bytes 196608 | tf_op jit(solution)/shard_map/all_to_all | solution.py:87
  12.2 1.3 fusion.48
  13.8 1.6 pad_maximum_fusion
  15.4 3.6 %collective-permute-start.4 = (bf16[3,176,2048]{2,1,0:T(8,128)(2,1)}, bf16[3,176,2048]{2,1,0:T(8,128)(2,1)}, u32[]{:S(2)}, u32[]{:S(2)}) collective-permute-start(bf16[3,176,2048]{2,1,0:T(8,128)(2,1)} %pad_maximum_fusion), channel_id=1, source_target_pairs={{0,16},{16,0},{1,17},{17,1},{2,18},{18,2},{3,19},{19,3},{4,20},{20... | collective-permute-start | bytes 6488072 | tf_op jit(solution)/shard_map/ppermute | solution.py:75
  19.0 0.6 all-to-all-done
  19.6 6.3 %collective-permute-start.6 = (bf16[24,2048]{1,0:T(8,128)(2,1)S(1)}, bf16[24,2048]{1,0:T(8,128)(2,1)S(1)}, u32[]{:S(2)}, u32[]{:S(2)}) collective-permute-start(bf16[24,2048]{1,0:T(8,128)(2,1)S(1)} %copy_bitcast_fusion), channel_id=1, source_target_pairs={{0,48},{16,32},{32,16},{48,0},{1,49},{17,33},{33,17},{49,1},{2,50}... | collective-permute-start | bytes 294920 | tf_op jit(solution)/shard_map/ppermute | solution.py:37
  26.0 1.9 collective-permute-start.5
  27.9 3.1 %collective-permute-start = (bf16[24,2048]{1,0:T(8,128)(2,1)S(1)}, bf16[24,2048]{1,0:T(8,128)(2,1)S(1)}, u32[]{:S(2)}, u32[]{:S(2)}) collective-permute-start(bf16[24,2048]{1,0:T(8,128)(2,1)S(1)} %copy_bitcast_fusion), channel_id=1, source_target_pairs={{0,32},{32,0},{1,33},{33,1},{2,34},{34,2},{3,35},{35,3},{4,36},{36... | collective-permute-start | bytes 294920 | tf_op jit(solution)/shard_map/ppermute | solution.py:35
  31.1 4.1 %collective-permute-done = bf16[24,2048]{1,0:T(8,128)(2,1)S(1)} collective-permute-done((bf16[24,2048]{1,0:T(8,128)(2,1)S(1)}, bf16[24,2048]{1,0:T(8,128)(2,1)S(1)}, u32[]{:S(2)}, u32[]{:S(2)}) %collective-permute-start) | collective-permute-done | bytes 98336 | tf_op jit(solution)/shard_map/ppermute | solution.py:35
  35.2 10.7 %collective-permute-start.7 = (bf16[96,2048]{1,0:T(8,128)(2,1)S(1)}, bf16[96,2048]{1,0:T(8,128)(2,1)S(1)}, u32[]{:S(2)}, u32[]{:S(2)}) collective-permute-start(bf16[96,2048]{1,0:T(8,128)(2,1)S(1)} %pad_maximum_fusion.5), channel_id=1, source_target_pairs={{0,64},{16,464},{64,128},{80,16},{128,192},{144,80},{192,256},{208... | collective-permute-start | bytes 1179656 | tf_op jit(solution)/shard_map/ppermute | solution.py:24
  46.1 1.9 collective-permute-start.3
  48.0 2.8 %collective-permute-start.2 = (bf16[24,2048]{1,0:T(8,128)(2,1)S(1)}, bf16[24,2048]{1,0:T(8,128)(2,1)S(1)}, u32[]{:S(2)}, u32[]{:S(2)}) collective-permute-start(bf16[24,2048]{1,0:T(8,128)(2,1)S(1)} %convolution_convert_fusion), channel_id=1, source_target_pairs={{0,16},{16,0},{1,17},{17,1},{2,18},{18,2},{3,19},{19,3},{4,20},{20... | collective-permute-start | bytes 294920 | tf_op jit(solution)/shard_map/ppermute | solution.py:36
  50.9 4.4 %collective-permute-start.1 = (bf16[24,2048]{1,0:T(8,128)(2,1)S(1)}, bf16[24,2048]{1,0:T(8,128)(2,1)S(1)}, u32[]{:S(2)}, u32[]{:S(2)}) collective-permute-start(bf16[24,2048]{1,0:T(8,128)(2,1)S(1)} %convolution_convert_fusion), channel_id=1, source_target_pairs={{0,32},{32,0},{1,33},{33,1},{2,34},{34,2},{3,35},{35,3},{4,36},{36... | collective-permute-start | bytes 294920 | tf_op jit(solution)/shard_map/ppermute | solution.py:35
  55.3 3.4 %collective-permute-done.1 = bf16[24,2048]{1,0:T(8,128)(2,1)S(1)} collective-permute-done((bf16[24,2048]{1,0:T(8,128)(2,1)S(1)}, bf16[24,2048]{1,0:T(8,128)(2,1)S(1)}, u32[]{:S(2)}, u32[]{:S(2)}) %collective-permute-start.1) | collective-permute-done | bytes 98336 | tf_op jit(solution)/shard_map/ppermute | solution.py:35
  58.7 2.2 %collective-permute-start.9 = (bf16[96,2048]{1,0:T(8,128)(2,1)S(1)}, bf16[96,2048]{1,0:T(8,128)(2,1)S(1)}, u32[]{:S(2)}, u32[]{:S(2)}) collective-permute-start(bf16[96,2048]{1,0:T(8,128)(2,1)S(1)} %collective-permute-done.7), channel_id=1, source_target_pairs={{0,64},{16,464},{64,128},{80,16},{128,192},{144,80},{192,256},{208... | collective-permute-start | bytes 1179656 | tf_op jit(solution)/shard_map/ppermute | solution.py:24
  61.0 6.6 %collective-permute-done.9 = bf16[96,2048]{1,0:T(8,128)(2,1)S(1)} collective-permute-done((bf16[96,2048]{1,0:T(8,128)(2,1)S(1)}, bf16[96,2048]{1,0:T(8,128)(2,1)S(1)}, u32[]{:S(2)}, u32[]{:S(2)}) %collective-permute-start.9) | collective-permute-done | bytes 393248 | tf_op jit(solution)/shard_map/ppermute | solution.py:24
  67.5 3.1 %collective-permute-start.11 = (bf16[96,2048]{1,0:T(8,128)(2,1)S(1)}, bf16[96,2048]{1,0:T(8,128)(2,1)S(1)}, u32[]{:S(2)}, u32[]{:S(2)}) collective-permute-start(bf16[96,2048]{1,0:T(8,128)(2,1)S(1)} %collective-permute-done.9), channel_id=1, source_target_pairs={{0,64},{16,464},{64,128},{80,16},{128,192},{144,80},{192,256},{208... | collective-permute-start | bytes 1179656 | tf_op jit(solution)/shard_map/ppermute | solution.py:24
  70.7 5.3 %collective-permute-done.11 = bf16[96,2048]{1,0:T(8,128)(2,1)S(1)} collective-permute-done((bf16[96,2048]{1,0:T(8,128)(2,1)S(1)}, bf16[96,2048]{1,0:T(8,128)(2,1)S(1)}, u32[]{:S(2)}, u32[]{:S(2)}) %collective-permute-start.11) | collective-permute-done | bytes 393248 | tf_op jit(solution)/shard_map/ppermute | solution.py:24
  76.1 4.3 %collective-permute-start.13 = (bf16[48,2048]{1,0:T(8,128)(2,1)S(1)}, bf16[48,2048]{1,0:T(8,128)(2,1)S(1)}, u32[]{:S(2)}, u32[]{:S(2)}) collective-permute-start(bf16[48,2048]{1,0:T(8,128)(2,1)S(1)} %slice.102), channel_id=1, source_target_pairs={{0,64},{16,464},{64,128},{80,16},{128,192},{144,80},{192,256},{208... | collective-permute-start | bytes 589832 | tf_op jit(solution)/shard_map/ppermute | solution.py:24
  80.5 2.6 %collective-permute-done.13 = bf16[48,2048]{1,0:T(8,128)(2,1)S(1)} collective-permute-done((bf16[48,2048]{1,0:T(8,128)(2,1)S(1)}, bf16[48,2048]{1,0:T(8,128)(2,1)S(1)}, u32[]{:S(2)}, u32[]{:S(2)}) %collective-permute-start.13) | collective-permute-done | bytes 196640 | tf_op jit(solution)/shard_map/ppermute | solution.py:24
  83.0 1.7 slice_bitcast_fusion
  85.1 5.0 %collective-permute-start.8 = (bf16[96,2048]{1,0:T(8,128)(2,1)S(1)}, bf16[96,2048]{1,0:T(8,128)(2,1)S(1)}, u32[]{:S(2)}, u32[]{:S(2)}) collective-permute-start(bf16[96,2048]{1,0:T(8,128)(2,1)S(1)} %pad_maximum_fusion.4), channel_id=1, source_target_pairs={{0,64},{16,464},{64,128},{80,16},{128,192},{144,80},{192,256},{208... | collective-permute-start | bytes 1179656 | tf_op jit(solution)/shard_map/ppermute | solution.py:24
  91.3 0.6 constant_dynamic-update-slice_fusion.4
  92.6 0.6 fusion.53
  93.2 0.6 fusion.51
  95.5 4.9 %collective-permute-start.10 = (bf16[96,2048]{1,0:T(8,128)(2,1)S(1)}, bf16[96,2048]{1,0:T(8,128)(2,1)S(1)}, u32[]{:S(2)}, u32[]{:S(2)}) collective-permute-start(bf16[96,2048]{1,0:T(8,128)(2,1)S(1)} %collective-permute-done.8), channel_id=1, source_target_pairs={{0,64},{16,464},{64,128},{80,16},{128,192},{144,80},{192,256},{208... | collective-permute-start | bytes 1179656 | tf_op jit(solution)/shard_map/ppermute | solution.py:24
  100.5 0.6 constant_dynamic-update-slice_fusion.3
  101.6 3.6 %collective-permute-done.10 = bf16[96,2048]{1,0:T(8,128)(2,1)S(1)} collective-permute-done((bf16[96,2048]{1,0:T(8,128)(2,1)S(1)}, bf16[96,2048]{1,0:T(8,128)(2,1)S(1)}, u32[]{:S(2)}, u32[]{:S(2)}) %collective-permute-start.10) | collective-permute-done | bytes 393248 | tf_op jit(solution)/shard_map/ppermute | solution.py:24
  105.8 5.0 %collective-permute-start.12 = (bf16[96,2048]{1,0:T(8,128)(2,1)S(1)}, bf16[96,2048]{1,0:T(8,128)(2,1)S(1)}, u32[]{:S(2)}, u32[]{:S(2)}) collective-permute-start(bf16[96,2048]{1,0:T(8,128)(2,1)S(1)} %collective-permute-done.10), channel_id=1, source_target_pairs={{0,64},{16,464},{64,128},{80,16},{128,192},{144,80},{192,256},{208... | collective-permute-start | bytes 1179656 | tf_op jit(solution)/shard_map/ppermute | solution.py:24
  110.8 0.6 constant_dynamic-update-slice_fusion.2
  111.9 3.6 %collective-permute-done.12 = bf16[96,2048]{1,0:T(8,128)(2,1)S(1)} collective-permute-done((bf16[96,2048]{1,0:T(8,128)(2,1)S(1)}, bf16[96,2048]{1,0:T(8,128)(2,1)S(1)}, u32[]{:S(2)}, u32[]{:S(2)}) %collective-permute-start.12) | collective-permute-done | bytes 393248 | tf_op jit(solution)/shard_map/ppermute | solution.py:24
  115.5 5.0 %collective-permute-start.14 = (bf16[48,2048]{1,0:T(8,128)(2,1)S(1)}, bf16[48,2048]{1,0:T(8,128)(2,1)S(1)}, u32[]{:S(2)}, u32[]{:S(2)}) collective-permute-start(bf16[48,2048]{1,0:T(8,128)(2,1)S(1)} %slice.103), channel_id=1, source_target_pairs={{0,64},{16,464},{64,128},{80,16},{128,192},{144,80},{192,256},{208... | collective-permute-start | bytes 589832 | tf_op jit(solution)/shard_map/ppermute | solution.py:24
  120.5 0.6 fusion.54
  121.1 0.6 constant_dynamic-update-slice_fusion.1
  122.2 1.0 collective-permute-done.14
  123.7 0.6 constant_dynamic-update-slice_fusion
  125.0 1.9 collective-permute-start.18
  127.4 7.1 %collective-permute-done.18 = bf16[48,2048]{1,0:T(8,128)(2,1)S(1)} collective-permute-done((bf16[48,2048]{1,0:T(8,128)(2,1)S(1)}, bf16[48,2048]{1,0:T(8,128)(2,1)S(1)}, u32[]{:S(2)}, u32[]{:S(2)}) %collective-permute-start.18) | collective-permute-done | bytes 196640 | tf_op jit(solution)/shard_map/ppermute | solution.py:28
  134.6 1.9 collective-permute-start.19
  136.6 7.7 %collective-permute-done.19 = bf16[96,2048]{1,0:T(8,128)(2,1)S(1)} collective-permute-done((bf16[96,2048]{1,0:T(8,128)(2,1)S(1)}, bf16[96,2048]{1,0:T(8,128)(2,1)S(1)}, u32[]{:S(2)}, u32[]{:S(2)}) %collective-permute-start.19) | collective-permute-done | bytes 393248 | tf_op jit(solution)/shard_map/ppermute | solution.py:28
  144.8 2.1 %collective-permute-start.20 = (bf16[96,2048]{1,0:T(8,128)(2,1)S(1)}, bf16[96,2048]{1,0:T(8,128)(2,1)S(1)}, u32[]{:S(2)}, u32[]{:S(2)}) collective-permute-start(bf16[96,2048]{1,0:T(8,128)(2,1)S(1)} %add_convert_fusion.1), channel_id=1, source_target_pairs={{64,0},{464,16},{128,64},{16,80},{192,128},{80,144},{256,192},{144... | collective-permute-start | bytes 1179656 | tf_op jit(solution)/shard_map/ppermute | solution.py:28
  146.9 0.9 fusion.59
  148.0 15.1 %collective-permute-start.17 = (bf16[176,2048]{1,0:T(8,128)(2,1)S(1)}, bf16[176,2048]{1,0:T(8,128)(2,1)S(1)}, u32[]{:S(2)}, u32[]{:S(2)}) collective-permute-start(bf16[176,2048]{1,0:T(8,128)(2,1)S(1)} %slice.163), channel_id=1, source_target_pairs={{0,16},{16,0},{1,17},{17,1},{2,18},{18,2},{3,19},{19,3},{4,20},{20... | collective-permute-start | bytes 2162696 | tf_op jit(solution)/shard_map/ppermute | solution.py:134
  163.6 1.9 collective-permute-start.21
  165.5 0.9 fusion.58
  166.6 1.5 copy-done.2
  168.0 0.9 fusion.57
  169.0 1.0 slice.165
  170.0 0.7 copy-done.3
  170.8 7.7 %collective-permute-start.16 = (bf16[176,2048]{1,0:T(8,128)(2,1)S(1)}, bf16[176,2048]{1,0:T(8,128)(2,1)S(1)}, u32[]{:S(2)}, u32[]{:S(2)}) collective-permute-start(bf16[176,2048]{1,0:T(8,128)(2,1)S(1)} %slice.164), channel_id=1, source_target_pairs={{0,16},{16,0},{1,17},{17,1},{2,18},{18,2},{3,19},{19,3},{4,20},{20... | collective-permute-start | bytes 2162696 | tf_op jit(solution)/shard_map/ppermute | solution.py:134
  178.5 1.9 collective-permute-start.15
  180.4 2.5 %collective-permute-start.22 = (bf16[48,2048]{1,0:T(8,128)(2,1)S(1)}, bf16[48,2048]{1,0:T(8,128)(2,1)S(1)}, u32[]{:S(2)}, u32[]{:S(2)}) collective-permute-start(bf16[48,2048]{1,0:T(8,128)(2,1)S(1)} %slice.119), channel_id=1, source_target_pairs={{0,16},{16,0},{1,17},{17,1},{2,18},{18,2},{3,19},{19,3},{4,20},{20... | collective-permute-start | bytes 589832 | tf_op jit(solution)/shard_map/ppermute | solution.py:112
  183.0 1.1 fusion.6
  184.1 4.5 %collective-permute-start.23 = (bf16[24,2048]{1,0:T(8,128)(2,1)S(1)}, bf16[24,2048]{1,0:T(8,128)(2,1)S(1)}, u32[]{:S(2)}, u32[]{:S(2)}) collective-permute-start(bf16[24,2048]{1,0:T(8,128)(2,1)S(1)} %slice.167), channel_id=1, source_target_pairs={{0,32},{32,0},{1,33},{33,1},{2,34},{34,2},{3,35},{35,3},{4,36},{36... | collective-permute-start | bytes 294920 | tf_op jit(solution)/shard_map/ppermute | solution.py:114
  188.7 1.1 fusion.5
  189.7 2.0 collective-permute-done.23
  191.7 0.7 bitcast_bitcast_fusion
  192.4 5.1 %all-to-all-start.1 = ((bf16[16,24,128]{2,1,0:T(8,128)(2,1)}), bf16[16,24,128]{2,1,0:T(8,128)(2,1)S(1)}, u32[]{:S(2)}, u32[]{:S(2)}) async-start(bf16[16,24,128]{2,1,0:T(8,128)(2,1)} %bitcast_bitcast_fusion), calls=%async_computation.1 | async-start | bytes 196608 | tf_op jit(solution)/shard_map/all_to_all | solution.py:117
  197.5 1.0 fusion.4
  198.6 6.4 %all-to-all-done.1 = bf16[16,24,128]{2,1,0:T(8,128)(2,1)S(1)} async-done(((bf16[16,24,128]{2,1,0:T(8,128)(2,1)}), bf16[16,24,128]{2,1,0:T(8,128)(2,1)S(1)}, u32[]{:S(2)}, u32[]{:S(2)}) %all-to-all-start.1) | async-done | bytes 98336 | tf_op jit(solution)/shard_map/all_to_all | solution.py:117
  204.9 0.8 convolution_convert_fusion.2
  (81 shorter events, 10.1 us)
Async XLA Ops:
  0.6 45.2 %copy-start = (bf16[128,2048]{1,0:T(8,128)(2,1)S(1)}, bf16[128,2048]{1,0:T(8,128)(2,1)}, u32[]{:S(2)}) copy-start(bf16[128,2048]{1,0:T(8,128)(2,1)} %param.8) | copy-start | bytes 1572868
  0.6 12.9 %copy-start.4 = (bf16[1,172,2048]{2,1,0:T(8,128)(2,1)S(1)}, bf16[1,172,2048]{2,1,0:T(8,128)(2,1)}, u32[]{:S(2)}) copy-start(bf16[1,172,2048]{2,1,0:T(8,128)(2,1)} %param.15) | copy-start | bytes 2113540
  3.5 16.1 %all-to-all-start = ((bf16[16,24,128]{2,1,0:T(8,128)(2,1)}), bf16[16,24,128]{2,1,0:T(8,128)(2,1)S(1)}, u32[]{:S(2)}, u32[]{:S(2)}) async-start(bf16[16,24,128]{2,1,0:T(8,128)(2,1)} %bitcast.1), calls=%async_computation | async-start | bytes 196608 | tf_op jit(solution)/shard_map/all_to_all | solution.py:87
  12.2 1.3 copy-start.5
  15.4 67.7 %collective-permute-start.4 = (bf16[3,176,2048]{2,1,0:T(8,128)(2,1)}, bf16[3,176,2048]{2,1,0:T(8,128)(2,1)}, u32[]{:S(2)}, u32[]{:S(2)}) collective-permute-start(bf16[3,176,2048]{2,1,0:T(8,128)(2,1)} %pad_maximum_fusion), channel_id=1, source_target_pairs={{0,16},{16,0},{1,17},{17,1},{2,18},{18,2},{3,19},{19,3},{4,20},{20... | collective-permute-start | bytes 6488072 | tf_op jit(solution)/shard_map/ppermute | solution.py:75
  19.6 11.4 %collective-permute-start.6 = (bf16[24,2048]{1,0:T(8,128)(2,1)S(1)}, bf16[24,2048]{1,0:T(8,128)(2,1)S(1)}, u32[]{:S(2)}, u32[]{:S(2)}) collective-permute-start(bf16[24,2048]{1,0:T(8,128)(2,1)S(1)} %copy_bitcast_fusion), channel_id=1, source_target_pairs={{0,48},{16,32},{32,16},{48,0},{1,49},{17,33},{33,17},{49,1},{2,50}... | collective-permute-start | bytes 294920 | tf_op jit(solution)/shard_map/ppermute | solution.py:37
  26.0 5.1 %collective-permute-start.5 = (bf16[24,2048]{1,0:T(8,128)(2,1)S(1)}, bf16[24,2048]{1,0:T(8,128)(2,1)S(1)}, u32[]{:S(2)}, u32[]{:S(2)}) collective-permute-start(bf16[24,2048]{1,0:T(8,128)(2,1)S(1)} %copy_bitcast_fusion), channel_id=1, source_target_pairs={{0,16},{16,0},{1,17},{17,1},{2,18},{18,2},{3,19},{19,3},{4,20},{20... | collective-permute-start | bytes 294920 | tf_op jit(solution)/shard_map/ppermute | solution.py:36
  27.9 7.3 %collective-permute-start = (bf16[24,2048]{1,0:T(8,128)(2,1)S(1)}, bf16[24,2048]{1,0:T(8,128)(2,1)S(1)}, u32[]{:S(2)}, u32[]{:S(2)}) collective-permute-start(bf16[24,2048]{1,0:T(8,128)(2,1)S(1)} %copy_bitcast_fusion), channel_id=1, source_target_pairs={{0,32},{32,0},{1,33},{33,1},{2,34},{34,2},{3,35},{35,3},{4,36},{36... | collective-permute-start | bytes 294920 | tf_op jit(solution)/shard_map/ppermute | solution.py:35
  35.2 23.5 %collective-permute-start.7 = (bf16[96,2048]{1,0:T(8,128)(2,1)S(1)}, bf16[96,2048]{1,0:T(8,128)(2,1)S(1)}, u32[]{:S(2)}, u32[]{:S(2)}) collective-permute-start(bf16[96,2048]{1,0:T(8,128)(2,1)S(1)} %pad_maximum_fusion.5), channel_id=1, source_target_pairs={{0,64},{16,464},{64,128},{80,16},{128,192},{144,80},{192,256},{208... | collective-permute-start | bytes 1179656 | tf_op jit(solution)/shard_map/ppermute | solution.py:24
  46.1 9.1 %collective-permute-start.3 = (bf16[24,2048]{1,0:T(8,128)(2,1)S(1)}, bf16[24,2048]{1,0:T(8,128)(2,1)S(1)}, u32[]{:S(2)}, u32[]{:S(2)}) collective-permute-start(bf16[24,2048]{1,0:T(8,128)(2,1)S(1)} %convolution_convert_fusion), channel_id=1, source_target_pairs={{0,48},{16,32},{32,16},{48,0},{1,49},{17,33},{33,17},{49,1},{2,50}... | collective-permute-start | bytes 294920 | tf_op jit(solution)/shard_map/ppermute | solution.py:37
  48.0 7.2 %collective-permute-start.2 = (bf16[24,2048]{1,0:T(8,128)(2,1)S(1)}, bf16[24,2048]{1,0:T(8,128)(2,1)S(1)}, u32[]{:S(2)}, u32[]{:S(2)}) collective-permute-start(bf16[24,2048]{1,0:T(8,128)(2,1)S(1)} %convolution_convert_fusion), channel_id=1, source_target_pairs={{0,16},{16,0},{1,17},{17,1},{2,18},{18,2},{3,19},{19,3},{4,20},{20... | collective-permute-start | bytes 294920 | tf_op jit(solution)/shard_map/ppermute | solution.py:36
  50.9 7.8 %collective-permute-start.1 = (bf16[24,2048]{1,0:T(8,128)(2,1)S(1)}, bf16[24,2048]{1,0:T(8,128)(2,1)S(1)}, u32[]{:S(2)}, u32[]{:S(2)}) collective-permute-start(bf16[24,2048]{1,0:T(8,128)(2,1)S(1)} %convolution_convert_fusion), channel_id=1, source_target_pairs={{0,32},{32,0},{1,33},{33,1},{2,34},{34,2},{3,35},{35,3},{4,36},{36... | collective-permute-start | bytes 294920 | tf_op jit(solution)/shard_map/ppermute | solution.py:35
  58.7 8.8 %collective-permute-start.9 = (bf16[96,2048]{1,0:T(8,128)(2,1)S(1)}, bf16[96,2048]{1,0:T(8,128)(2,1)S(1)}, u32[]{:S(2)}, u32[]{:S(2)}) collective-permute-start(bf16[96,2048]{1,0:T(8,128)(2,1)S(1)} %collective-permute-done.7), channel_id=1, source_target_pairs={{0,64},{16,464},{64,128},{80,16},{128,192},{144,80},{192,256},{208... | collective-permute-start | bytes 1179656 | tf_op jit(solution)/shard_map/ppermute | solution.py:24
  67.5 8.5 %collective-permute-start.11 = (bf16[96,2048]{1,0:T(8,128)(2,1)S(1)}, bf16[96,2048]{1,0:T(8,128)(2,1)S(1)}, u32[]{:S(2)}, u32[]{:S(2)}) collective-permute-start(bf16[96,2048]{1,0:T(8,128)(2,1)S(1)} %collective-permute-done.9), channel_id=1, source_target_pairs={{0,64},{16,464},{64,128},{80,16},{128,192},{144,80},{192,256},{208... | collective-permute-start | bytes 1179656 | tf_op jit(solution)/shard_map/ppermute | solution.py:24
  76.1 6.9 %collective-permute-start.13 = (bf16[48,2048]{1,0:T(8,128)(2,1)S(1)}, bf16[48,2048]{1,0:T(8,128)(2,1)S(1)}, u32[]{:S(2)}, u32[]{:S(2)}) collective-permute-start(bf16[48,2048]{1,0:T(8,128)(2,1)S(1)} %slice.102), channel_id=1, source_target_pairs={{0,64},{16,464},{64,128},{80,16},{128,192},{144,80},{192,256},{208... | collective-permute-start | bytes 589832 | tf_op jit(solution)/shard_map/ppermute | solution.py:24
  85.1 9.8 %collective-permute-start.8 = (bf16[96,2048]{1,0:T(8,128)(2,1)S(1)}, bf16[96,2048]{1,0:T(8,128)(2,1)S(1)}, u32[]{:S(2)}, u32[]{:S(2)}) collective-permute-start(bf16[96,2048]{1,0:T(8,128)(2,1)S(1)} %pad_maximum_fusion.4), channel_id=1, source_target_pairs={{0,64},{16,464},{64,128},{80,16},{128,192},{144,80},{192,256},{208... | collective-permute-start | bytes 1179656 | tf_op jit(solution)/shard_map/ppermute | solution.py:24
  95.5 9.6 %collective-permute-start.10 = (bf16[96,2048]{1,0:T(8,128)(2,1)S(1)}, bf16[96,2048]{1,0:T(8,128)(2,1)S(1)}, u32[]{:S(2)}, u32[]{:S(2)}) collective-permute-start(bf16[96,2048]{1,0:T(8,128)(2,1)S(1)} %collective-permute-done.8), channel_id=1, source_target_pairs={{0,64},{16,464},{64,128},{80,16},{128,192},{144,80},{192,256},{208... | collective-permute-start | bytes 1179656 | tf_op jit(solution)/shard_map/ppermute | solution.py:24
  105.8 9.7 %collective-permute-start.12 = (bf16[96,2048]{1,0:T(8,128)(2,1)S(1)}, bf16[96,2048]{1,0:T(8,128)(2,1)S(1)}, u32[]{:S(2)}, u32[]{:S(2)}) collective-permute-start(bf16[96,2048]{1,0:T(8,128)(2,1)S(1)} %collective-permute-done.10), channel_id=1, source_target_pairs={{0,64},{16,464},{64,128},{80,16},{128,192},{144,80},{192,256},{208... | collective-permute-start | bytes 1179656 | tf_op jit(solution)/shard_map/ppermute | solution.py:24
  115.5 7.6 %collective-permute-start.14 = (bf16[48,2048]{1,0:T(8,128)(2,1)S(1)}, bf16[48,2048]{1,0:T(8,128)(2,1)S(1)}, u32[]{:S(2)}, u32[]{:S(2)}) collective-permute-start(bf16[48,2048]{1,0:T(8,128)(2,1)S(1)} %slice.103), channel_id=1, source_target_pairs={{0,64},{16,464},{64,128},{80,16},{128,192},{144,80},{192,256},{208... | collective-permute-start | bytes 589832 | tf_op jit(solution)/shard_map/ppermute | solution.py:24
  125.0 9.5 %collective-permute-start.18 = (bf16[48,2048]{1,0:T(8,128)(2,1)S(1)}, bf16[48,2048]{1,0:T(8,128)(2,1)S(1)}, u32[]{:S(2)}, u32[]{:S(2)}) collective-permute-start(bf16[48,2048]{1,0:T(8,128)(2,1)S(1)} %fusion), channel_id=1, source_target_pairs={{64,0},{464,16},{128,64},{16,80},{192,128},{80,144},{256,192},{144... | collective-permute-start | bytes 589832 | tf_op jit(solution)/shard_map/ppermute | solution.py:28
  134.6 9.7 %collective-permute-start.19 = (bf16[96,2048]{1,0:T(8,128)(2,1)S(1)}, bf16[96,2048]{1,0:T(8,128)(2,1)S(1)}, u32[]{:S(2)}, u32[]{:S(2)}) collective-permute-start(bf16[96,2048]{1,0:T(8,128)(2,1)S(1)} %pad_maximum_fusion.6), channel_id=1, source_target_pairs={{64,0},{464,16},{128,64},{16,80},{192,128},{80,144},{256,192},{144... | collective-permute-start | bytes 1179656 | tf_op jit(solution)/shard_map/ppermute | solution.py:28
  144.8 18.3 %collective-permute-start.20 = (bf16[96,2048]{1,0:T(8,128)(2,1)S(1)}, bf16[96,2048]{1,0:T(8,128)(2,1)S(1)}, u32[]{:S(2)}, u32[]{:S(2)}) collective-permute-start(bf16[96,2048]{1,0:T(8,128)(2,1)S(1)} %add_convert_fusion.1), channel_id=1, source_target_pairs={{64,0},{464,16},{128,64},{16,80},{192,128},{80,144},{256,192},{144... | collective-permute-start | bytes 1179656 | tf_op jit(solution)/shard_map/ppermute | solution.py:28
  147.9 18.6 %copy-start.1 = (f32[352,2048]{1,0:T(8,128)}, f32[352,2048]{1,0:T(8,128)S(1)}, u32[]{:S(2)}) copy-start(f32[352,2048]{1,0:T(8,128)S(1)} %fusion.59) | copy-start | bytes 8650756
  148.0 35.0 %collective-permute-start.17 = (bf16[176,2048]{1,0:T(8,128)(2,1)S(1)}, bf16[176,2048]{1,0:T(8,128)(2,1)S(1)}, u32[]{:S(2)}, u32[]{:S(2)}) collective-permute-start(bf16[176,2048]{1,0:T(8,128)(2,1)S(1)} %slice.163), channel_id=1, source_target_pairs={{0,16},{16,0},{1,17},{17,1},{2,18},{18,2},{3,19},{19,3},{4,20},{20... | collective-permute-start | bytes 2162696 | tf_op jit(solution)/shard_map/ppermute | solution.py:134
  163.6 16.8 %collective-permute-start.21 = (bf16[96,2048]{1,0:T(8,128)(2,1)S(1)}, bf16[96,2048]{1,0:T(8,128)(2,1)S(1)}, u32[]{:S(2)}, u32[]{:S(2)}) collective-permute-start(bf16[96,2048]{1,0:T(8,128)(2,1)S(1)} %add_convert_fusion), channel_id=1, source_target_pairs={{64,0},{464,16},{128,64},{16,80},{192,128},{80,144},{256,192},{144... | collective-permute-start | bytes 1179656 | tf_op jit(solution)/shard_map/ppermute | solution.py:28
  166.4 1.6 copy-start.2
  169.0 1.8 copy-start.3
  170.0 13.0 %slice-start = ((f32[352,2048]{1,0:T(8,128)}), f32[176,2048]{1,0:T(8,128)S(1)}, s32[]{:S(2)}) async-start(f32[352,2048]{1,0:T(8,128)} %copy-done.1), calls=%async_computation.2 | async-start | bytes 2883584 | tf_op jit(solution)/shard_map/slice | solution.py:135
  170.8 17.9 %collective-permute-start.16 = (bf16[176,2048]{1,0:T(8,128)(2,1)S(1)}, bf16[176,2048]{1,0:T(8,128)(2,1)S(1)}, u32[]{:S(2)}, u32[]{:S(2)}) collective-permute-start(bf16[176,2048]{1,0:T(8,128)(2,1)S(1)} %slice.164), channel_id=1, source_target_pairs={{0,16},{16,0},{1,17},{17,1},{2,18},{18,2},{3,19},{19,3},{4,20},{20... | collective-permute-start | bytes 2162696 | tf_op jit(solution)/shard_map/ppermute | solution.py:134
  178.5 19.1 %collective-permute-start.15 = (bf16[176,2048]{1,0:T(8,128)(2,1)}, bf16[176,2048]{1,0:T(8,128)(2,1)S(1)}, u32[]{:S(2)}, u32[]{:S(2)}) collective-permute-start(bf16[176,2048]{1,0:T(8,128)(2,1)} %slice.165), channel_id=1, source_target_pairs={{0,16},{16,0},{1,17},{17,1},{2,18},{18,2},{3,19},{19,3},{4,20},{20... | collective-permute-start | bytes 2162696 | tf_op jit(solution)/shard_map/ppermute | solution.py:134
  180.4 8.2 %slice-start.1 = ((f32[352,2048]{1,0:T(8,128)}), f32[176,2048]{1,0:T(8,128)S(1)}, s32[]{:S(2)}) async-start(f32[352,2048]{1,0:T(8,128)} %copy-done.2), calls=%async_computation.3 | async-start | bytes 2883584 | tf_op jit(solution)/shard_map/slice | solution.py:135
  180.4 3.6 %collective-permute-start.22 = (bf16[48,2048]{1,0:T(8,128)(2,1)S(1)}, bf16[48,2048]{1,0:T(8,128)(2,1)S(1)}, u32[]{:S(2)}, u32[]{:S(2)}) collective-permute-start(bf16[48,2048]{1,0:T(8,128)(2,1)S(1)} %slice.119), channel_id=1, source_target_pairs={{0,16},{16,0},{1,17},{17,1},{2,18},{18,2},{3,19},{19,3},{4,20},{20... | collective-permute-start | bytes 589832 | tf_op jit(solution)/shard_map/ppermute | solution.py:112
  184.1 13.4 %slice-start.2 = ((f32[352,2048]{1,0:T(8,128)}), f32[176,2048]{1,0:T(8,128)S(1)}, s32[]{:S(2)}) async-start(f32[352,2048]{1,0:T(8,128)} %copy-done.3), calls=%async_computation.4 | async-start | bytes 2883584 | tf_op jit(solution)/shard_map/slice | solution.py:135
  184.1 7.6 %collective-permute-start.23 = (bf16[24,2048]{1,0:T(8,128)(2,1)S(1)}, bf16[24,2048]{1,0:T(8,128)(2,1)S(1)}, u32[]{:S(2)}, u32[]{:S(2)}) collective-permute-start(bf16[24,2048]{1,0:T(8,128)(2,1)S(1)} %slice.167), channel_id=1, source_target_pairs={{0,32},{32,0},{1,33},{33,1},{2,34},{34,2},{3,35},{35,3},{4,36},{36... | collective-permute-start | bytes 294920 | tf_op jit(solution)/shard_map/ppermute | solution.py:114
  192.4 12.5 %all-to-all-start.1 = ((bf16[16,24,128]{2,1,0:T(8,128)(2,1)}), bf16[16,24,128]{2,1,0:T(8,128)(2,1)S(1)}, u32[]{:S(2)}, u32[]{:S(2)}) async-start(bf16[16,24,128]{2,1,0:T(8,128)(2,1)} %bitcast_bitcast_fusion), calls=%async_computation.1 | async-start | bytes 196608 | tf_op jit(solution)/shard_map/all_to_all | solution.py:117

commit v2 on v1

v2 whole, which is shorter than its diff:
```python
import jax
import jax.numpy as jnp
from jax import lax
from jax.sharding import Mesh
from jax.sharding import PartitionSpec as P

BF = jnp.bfloat16
F32 = jnp.float32
Z, XH, CORE, XL, Y = 8, 2, 2, 2, 8
AXES = ("z", "xh", "core", "xl", "y")
EXPERT = ("xl", "y")
PLANE = ("z", "xh", "core")
PAD = 176


def hops(step, across=False, other=False):
    pairs = []
    for z in range(Z):
        for x in range(XH):
            for c in range(CORE):
                there = ((z + step * (1 - 2 * c)) % Z, x ^ across, c ^ other)
                pairs.append(((z * XH + x) * CORE + c, (there[0] * XH + there[1]) * CORE + there[2]))
    return pairs


def send(a, step, across=False, other=False):
    return lax.ppermute(a, PLANE, hops(step, across, other))


def dot(a, b, dims=((1,), (0,))):
    return lax.dot_general(a, b, (dims, ((), ())), preferred_element_type=F32)


def local(tokens, out_grad, modality, within_route, gate_values, w_gate, w_up, w_down):
    tok_count, width = tokens.shape
    experts_all = XL * Y // 2
    per_modality = experts_all // 2
    capacity = tok_count * 3 // (2 * experts_all)
    hidden_own = w_gate.shape[1]
    position = lax.axis_index(EXPERT)
    own_expert = position // 2
    expert_id = per_modality * modality + within_route
    one_hot = (expert_id[:, None] == jnp.arange(experts_all, dtype=jnp.int32)[None, :]).astype(
        jnp.int32
    )
    before = jnp.cumsum(one_hot, axis=0) - one_hot
    slot_rank = jnp.sum(before * one_hot, axis=1)
    kept = slot_rank < capacity
    slot = jnp.where(kept, expert_id * capacity + slot_rank, -1)
    slots = jnp.arange(experts_all * capacity, dtype=jnp.int32)
    select = (slot[None, :] == slots[:, None]).astype(BF)
    own_slots = own_expert * capacity + jnp.arange(capacity, dtype=jnp.int32)
    select_own = (slot[None, :] == own_slots[:, None]).astype(BF)

    pad = ((0, PAD - hidden_own), (0, 0))
    own_w = jnp.stack([jnp.pad(w_gate[0], pad), jnp.pad(w_up[0], pad), jnp.pad(w_down[0], pad)])
    other_w = send(own_w, 0, other=True)
    wg = jnp.concatenate([own_w[0], other_w[0]], axis=0)
    wu = jnp.concatenate([own_w[1], other_w[1]], axis=0)
    wd = jnp.concatenate([own_w[2], other_w[2]], axis=0)

    scaled = (gate_values[:, None] * out_grad.astype(F32)).astype(BF)
    dy_slices = dot(select, scaled).astype(BF).reshape(experts_all, 1, capacity, -1)
    dy_slices = jnp.broadcast_to(dy_slices, (experts_all, 2) + dy_slices.shape[2:])
    dy_slices = dy_slices.reshape((2 * experts_all,) + dy_slices.shape[2:])
    dy_slices = lax.all_to_all(dy_slices, EXPERT, 0, 0, tiled=True)
    x_own = dot(select_own, tokens).astype(BF)
    dy_own = jnp.transpose(dy_slices, (1, 0, 2)).reshape(capacity, width)
    own = jnp.concatenate([x_own, dy_own], axis=0)
    across = send(own, 0, across=True)

    near = 2 * capacity
    packet = jnp.concatenate(
        [own[:capacity], across[:capacity], own[capacity:], across[capacity:]], axis=0
    )
    packet = packet + other_w[2, hidden_own, 0]
    chain_a = [send(packet, 1)]
    chain_b = [send(packet, -1, other=True)]
    for step in (1, 2):
        chain_a.append(send(chain_a[-1], 1))
        chain_b.append(send(chain_b[-1], 1))
    chain_a.append(send(chain_a[-1], 1))
    chunks = [(packet[:near], packet[near:])]
    for a, b in zip(chain_a[:3], chain_b):
        chunks.append(
            (
                jnp.concatenate([a[:near], b[:near]], axis=0),
                jnp.concatenate([a[near:], b[near:]], axis=0),
            )
        )
    chunks.append((chain_a[3][:near], chain_a[3][near:]))

    cols = ((1,), (1,))
    terms, hiddens, d_gates, d_ups = [], [], [], []
    for x_rows, dy_rows in chunks:
        gate_pre = dot(x_rows, wg, cols)
        up_pre = dot(x_rows, wu, cols)
        sig_gate = jax.nn.sigmoid(gate_pre)
        silu_gate = gate_pre * sig_gate
        hiddens.append((silu_gate * up_pre).astype(BF))
        d_hidden = dot(dy_rows, wd, cols)
        d_gate = (d_hidden * up_pre * sig_gate * (1.0 + gate_pre * (1.0 - sig_gate))).astype(BF)
        d_up = (d_hidden * silu_gate).astype(BF)
        d_gates.append(d_gate)
        d_ups.append(d_up)
        terms.append(dot(d_gate, wg) + dot(d_up, wu))

    x_all = jnp.concatenate([x for x, _ in chunks], axis=0)
    dy_all = jnp.concatenate([dy for _, dy in chunks], axis=0)
    rows = ((0,), (0,))
    grads = [
        dot(jnp.concatenate(d_gates, axis=0), x_all, rows),
        dot(jnp.concatenate(d_ups, axis=0), x_all, rows),
        dot(jnp.concatenate(hiddens, axis=0), dy_all, rows),
    ]
    received = send(jnp.stack([grad[PAD:].astype(BF) for grad in grads]), 0, other=True)

    home_b = terms[3][near:]
    home_b = terms[2][near:] + send(home_b.astype(BF), -1).astype(F32)
    home_b = (terms[1][near:] + send(home_b.astype(BF), -1).astype(F32)).astype(BF)
    home_a = terms[4]
    home_a = terms[3][:near] + send(home_a.astype(BF), -1).astype(F32)
    home_a = terms[2][:near] + send(home_a.astype(BF), -1).astype(F32)
    home_a = (terms[1][:near] + send(home_a.astype(BF), -1).astype(F32)).astype(BF)
    summed = terms[0][:capacity]
    summed = summed + send(terms[0][capacity:].astype(BF), 0, across=True).astype(F32)
    summed = summed + send(home_b[:capacity], -1, other=True).astype(F32)
    summed = summed + send(home_b[capacity:], -1, across=True, other=True).astype(F32)
    summed = summed + send(home_a[:capacity], -1).astype(F32)
    summed = summed + send(home_a[capacity:], -1, across=True).astype(F32)
    summed = summed + received[2, hidden_own, 0].astype(F32)
    summed = summed.reshape(capacity, 2 * experts_all, -1)
    summed = jnp.transpose(summed, (1, 0, 2)).astype(BF)
    summed = lax.all_to_all(summed, EXPERT, 0, 0, tiled=True)

    from_slots = jnp.arange(2 * experts_all * capacity, dtype=jnp.int32)
    from_slots = from_slots // (2 * capacity) * capacity + from_slots % capacity
    place = (slot[:, None] == from_slots[None, :]).astype(BF)
    grad_tokens = dot(place, summed.reshape(2 * experts_all * capacity, -1)).astype(BF)

    outs = [
        (grad[:PAD] + extra.astype(F32))[:hidden_own].astype(BF)[None]
        for grad, extra in zip(grads, received)
    ]
    return (*outs, grad_tokens)


def solution(mesh):
    fine = Mesh(mesh.devices.reshape(Z, XH, CORE, XL, Y), AXES)
    dp = ("z", "xh", "core")
    placed = (
        P(dp, None),
        P(dp, EXPERT),
        P(dp),
        P(dp),
        P(dp),
        P(EXPERT, dp, None),
        P(EXPERT, dp, None),
        P(EXPERT, dp, None),
    )
    return jax.shard_map(
        local,
        mesh=fine,
        in_specs=placed,
        out_specs=(
            P(EXPERT, dp, None),
            P(EXPERT, dp, None),
            P(EXPERT, dp, None),
            P(dp, EXPERT),
        ),
        check_vma=False,
    )
```

time: 208 us -> 172 us (0.83)
  starting transfers between devices: 118 us -> 89.8 us
  waiting for transfers between devices: 54 us -> 41.1 us
  local copies, waits for them, and re-layouts: 7.67 us -> 10.8 us
    ppermute x24 -> x20, starting transfers between devices: 104 us -> 82 us  [send(): return lax.ppermute(a, PLANE, hops(step, across, other))]
    ppermute x24 -> x20, waiting for transfers between devices: 47 us -> 32.1 us  [send(): return lax.ppermute(a, PLANE, hops(step, across, other))]
    all_to_all x1, waiting for transfers between devices: 0.62 us -> 7.14 us  [local(): dy_slices = lax.all_to_all(dy_slices, EXPERT, 0, 0, tiled=True)]
    all_to_all x1, starting transfers between devices: 8.68 us -> 4.15 us  [local(): dy_slices = lax.all_to_all(dy_slices, EXPERT, 0, 0, tiled=True)]
    all_to_all x1, waiting for transfers between devices: 6.36 us -> 1.88 us  [local(): summed = lax.all_to_all(summed, EXPERT, 0, 0, tiled=True)]
  transfers between devices with their start and end apart: 26 -> 22, of which waited for: 13 -> 10; matrix products, arithmetic and copies ran while one was open for 10% -> 16% of each run, Pallas kernels for 0% -> 0%
where the time goes in v2:
time: 172 us; the launch traced here: 170 us
  starting transfers between devices  89.8 us (52%)
  waiting for transfers between devices  41.1 us (24%)
  matrix products  17.6 us (10%)
  local copies, waits for them, and re-layouts  10.8 us (6%)
  other arithmetic  8.16 us (5%)
  between operations  2.16 us (1%)
    ppermute x20, starting transfers between devices, send(): return lax.ppermute(a, PLANE, hops(step, across, other))  82 us
    ppermute x20, waiting for transfers between devices, send(): return lax.ppermute(a, PLANE, hops(step, across, other))  32.1 us
    dot_general x31, matrix products, dot(): return lax.dot_general(a, b, (dims, ((), ())), preferred_element_type=F32)  17.6 us
    all_to_all x1, waiting for transfers between devices, local(): dy_slices = lax.all_to_all(dy_slices, EXPERT, 0, 0, tiled=True)  7.14 us
    all_to_all x1, starting transfers between devices, local(): dy_slices = lax.all_to_all(dy_slices, EXPERT, 0, 0, tiled=True)  4.15 us
    all_to_all x1, starting transfers between devices, local(): summed = lax.all_to_all(summed, EXPERT, 0, 0, tiled=True)  3.62 us
  transfers between devices with their start and end apart: 22, of which 10 were waited for; matrix products, arithmetic and copies ran while one was open for 16% of the time, Pallas kernels for 0%

profile of v2, /device:TPU:1, one launch (start us, length us, event | category | flops | bytes accessed | tf_op | source)
XLA Modules:
  0.0 169.6 jit_solution(49212623031028247)
XLA Ops:
  0.7 1.3 fusion.95
  2.2 1.3 fusion.93
  3.6 1.6 pad_maximum_fusion
  5.1 8.8 %collective-permute-start.1 = (bf16[3,176,2048]{2,1,0:T(8,128)(2,1)}, bf16[3,176,2048]{2,1,0:T(8,128)(2,1)S(1)}, u32[]{:S(2)}, u32[]{:S(2)}) collective-permute-start(bf16[3,176,2048]{2,1,0:T(8,128)(2,1)} %pad_maximum_fusion), channel_id=1, source_target_pairs={{0,16},{16,0},{32,48},{48,32},{64,80},{80,64},{96,112},{112,96},{1... | collective-permute-start | bytes 6488072 | tf_op jit(solution)/shard_map/ppermute | solution.py:27
  14.4 1.0 convolution_convert_fusion.1
  15.4 0.7 broadcast_in_dim.16
  16.1 4.2 %all-to-all-start = ((bf16[16,24,128]{2,1,0:T(8,128)(2,1)}), bf16[16,24,128]{2,1,0:T(8,128)(2,1)}, u32[]{:S(2)}, u32[]{:S(2)}) async-start(bf16[16,24,128]{2,1,0:T(8,128)(2,1)} %bitcast.1), calls=%async_computation | async-start | bytes 196608 | tf_op jit(solution)/shard_map/all_to_all | solution.py:66
  20.5 7.1 %all-to-all-done = bf16[16,24,128]{2,1,0:T(8,128)(2,1)} async-done(((bf16[16,24,128]{2,1,0:T(8,128)(2,1)}), bf16[16,24,128]{2,1,0:T(8,128)(2,1)}, u32[]{:S(2)}, u32[]{:S(2)}) %all-to-all-start) | async-done | bytes 98336 | tf_op jit(solution)/shard_map/all_to_all | solution.py:66
  27.6 0.9 copy_bitcast_fusion
  28.5 2.9 %collective-permute-start = (bf16[48,2048]{1,0:T(8,128)(2,1)S(1)}, bf16[48,2048]{1,0:T(8,128)(2,1)S(1)}, u32[]{:S(2)}, u32[]{:S(2)}) collective-permute-start(bf16[48,2048]{1,0:T(8,128)(2,1)S(1)} %pad_maximum_fusion.14), channel_id=1, source_target_pairs={{0,32},{16,48},{32,0},{48,16},{64,96},{80,112},{96,64},{112,80},{1... | collective-permute-start | bytes 589832 | tf_op jit(solution)/shard_map/ppermute | solution.py:27
  31.4 5.6 %collective-permute-done = bf16[48,2048]{1,0:T(8,128)(2,1)S(1)} collective-permute-done((bf16[48,2048]{1,0:T(8,128)(2,1)S(1)}, bf16[48,2048]{1,0:T(8,128)(2,1)S(1)}, u32[]{:S(2)}, u32[]{:S(2)}) %collective-permute-start) | collective-permute-done | bytes 196640 | tf_op jit(solution)/shard_map/ppermute | solution.py:27
  37.5 0.7 maximum_add_fusion
  38.3 4.8 %collective-permute-start.3 = (bf16[96,2048]{1,0:T(8,128)(2,1)S(1)}, bf16[96,2048]{1,0:T(8,128)(2,1)S(1)}, u32[]{:S(2)}, u32[]{:S(2)}) collective-permute-start(bf16[96,2048]{1,0:T(8,128)(2,1)S(1)} %maximum_add_fusion), channel_id=1, source_target_pairs={{0,464},{16,64},{32,496},{48,96},{64,16},{80,128},{96,48},{112,160... | collective-permute-start | bytes 1179656 | tf_op jit(solution)/shard_map/ppermute | solution.py:27
  43.1 6.3 %collective-permute-start.2 = (bf16[96,2048]{1,0:T(8,128)(2,1)S(1)}, bf16[96,2048]{1,0:T(8,128)(2,1)S(1)}, u32[]{:S(2)}, u32[]{:S(2)}) collective-permute-start(bf16[96,2048]{1,0:T(8,128)(2,1)S(1)} %maximum_add_fusion), channel_id=1, source_target_pairs={{0,64},{16,464},{32,96},{48,496},{64,128},{80,16},{96,160},{112,48... | collective-permute-start | bytes 1179656 | tf_op jit(solution)/shard_map/ppermute | solution.py:27
  49.7 0.6 fusion.50
  50.2 0.6 fusion.48
  51.4 0.6 constant_dynamic-update-slice_fusion.15
  52.7 4.4 %collective-permute-start.10 = (bf16[24,2048]{1,0:T(8,128)(2,1)S(1)}, bf16[24,2048]{1,0:T(8,128)(2,1)}, u32[]{:S(2)}, u32[]{:S(2)}) collective-permute-start(bf16[24,2048]{1,0:T(8,128)(2,1)S(1)} %slice.322), channel_id=1, source_target_pairs={{0,32},{16,48},{32,0},{48,16},{64,96},{80,112},{96,64},{112,80},{1... | collective-permute-start | bytes 294920 | tf_op jit(solution)/shard_map/ppermute | solution.py:27
  57.3 0.6 fusion.31
  57.9 0.6 fusion.32
  58.5 5.6 %collective-permute-start.5 = (bf16[96,2048]{1,0:T(8,128)(2,1)S(1)}, bf16[96,2048]{1,0:T(8,128)(2,1)S(1)}, u32[]{:S(2)}, u32[]{:S(2)}) collective-permute-start(bf16[96,2048]{1,0:T(8,128)(2,1)S(1)} %collective-permute-done.3), channel_id=1, source_target_pairs={{0,64},{16,464},{32,96},{48,496},{64,128},{80,16},{96,160},{112,48... | collective-permute-start | bytes 1179656 | tf_op jit(solution)/shard_map/ppermute | solution.py:27
  64.1 2.2 %collective-permute-start.4 = (bf16[96,2048]{1,0:T(8,128)(2,1)S(1)}, bf16[96,2048]{1,0:T(8,128)(2,1)S(1)}, u32[]{:S(2)}, u32[]{:S(2)}) collective-permute-start(bf16[96,2048]{1,0:T(8,128)(2,1)S(1)} %collective-permute-done.2), channel_id=1, source_target_pairs={{0,64},{16,464},{32,96},{48,496},{64,128},{80,16},{96,160},{112,48... | collective-permute-start | bytes 1179656 | tf_op jit(solution)/shard_map/ppermute | solution.py:27
  66.3 0.6 constant_dynamic-update-slice_fusion.14
  67.3 5.6 %collective-permute-done.4 = bf16[96,2048]{1,0:T(8,128)(2,1)S(1)} collective-permute-done((bf16[96,2048]{1,0:T(8,128)(2,1)S(1)}, bf16[96,2048]{1,0:T(8,128)(2,1)S(1)}, u32[]{:S(2)}, u32[]{:S(2)}) %collective-permute-start.4) | collective-permute-done | bytes 393248 | tf_op jit(solution)/shard_map/ppermute | solution.py:27
  73.2 0.6 fusion.29
  73.7 0.6 fusion.30
  74.3 5.0 %collective-permute-start.7 = (bf16[96,2048]{1,0:T(8,128)(2,1)S(1)}, bf16[96,2048]{1,0:T(8,128)(2,1)S(1)}, u32[]{:S(2)}, u32[]{:S(2)}) collective-permute-start(bf16[96,2048]{1,0:T(8,128)(2,1)S(1)} %collective-permute-done.5), channel_id=1, source_target_pairs={{0,64},{16,464},{32,96},{48,496},{64,128},{80,16},{96,160},{112,48... | collective-permute-start | bytes 1179656 | tf_op jit(solution)/shard_map/ppermute | solution.py:27
  79.4 1.9 %collective-permute-start.6 = (bf16[96,2048]{1,0:T(8,128)(2,1)S(1)}, bf16[96,2048]{1,0:T(8,128)(2,1)S(1)}, u32[]{:S(2)}, u32[]{:S(2)}) collective-permute-start(bf16[96,2048]{1,0:T(8,128)(2,1)S(1)} %collective-permute-done.4), channel_id=1, source_target_pairs={{0,64},{16,464},{32,96},{48,496},{64,128},{80,16},{96,160},{112,48... | collective-permute-start | bytes 1179656 | tf_op jit(solution)/shard_map/ppermute | solution.py:27
  81.3 0.6 constant_dynamic-update-slice_fusion.13
  82.3 5.9 %collective-permute-done.6 = bf16[96,2048]{1,0:T(8,128)(2,1)S(1)} collective-permute-done((bf16[96,2048]{1,0:T(8,128)(2,1)S(1)}, bf16[96,2048]{1,0:T(8,128)(2,1)S(1)}, u32[]{:S(2)}, u32[]{:S(2)}) %collective-permute-start.6) | collective-permute-done | bytes 393248 | tf_op jit(solution)/shard_map/ppermute | solution.py:27
  88.4 0.6 fusion.27
  89.0 0.6 fusion.28
  89.6 0.6 constant_dynamic-update-slice_fusion.12
  90.2 5.0 %collective-permute-start.8 = (bf16[96,2048]{1,0:T(8,128)(2,1)S(1)}, bf16[96,2048]{1,0:T(8,128)(2,1)S(1)}, u32[]{:S(2)}, u32[]{:S(2)}) collective-permute-start(bf16[96,2048]{1,0:T(8,128)(2,1)S(1)} %collective-permute-done.6), channel_id=1, source_target_pairs={{0,64},{16,464},{32,96},{48,496},{64,128},{80,16},{96,160},{112,48... | collective-permute-start | bytes 1179656 | tf_op jit(solution)/shard_map/ppermute | solution.py:27
  96.1 1.9 %collective-permute-start.11 = (bf16[48,2048]{1,0:T(8,128)(2,1)S(1)}, bf16[48,2048]{1,0:T(8,128)(2,1)S(1)}, u32[]{:S(2)}, u32[]{:S(2)}) collective-permute-start(bf16[48,2048]{1,0:T(8,128)(2,1)S(1)} %slice.321), channel_id=1, source_target_pairs={{0,448},{16,80},{32,480},{48,112},{64,0},{80,144},{96,32},{112,176... | collective-permute-start | bytes 589832 | tf_op jit(solution)/shard_map/ppermute | solution.py:27
  98.1 1.9 %collective-permute-done.8 = bf16[96,2048]{1,0:T(8,128)(2,1)S(1)} collective-permute-done((bf16[96,2048]{1,0:T(8,128)(2,1)S(1)}, bf16[96,2048]{1,0:T(8,128)(2,1)S(1)}, u32[]{:S(2)}, u32[]{:S(2)}) %collective-permute-start.8) | collective-permute-done | bytes 393248 | tf_op jit(solution)/shard_map/ppermute | solution.py:27
  99.9 0.6 fusion.44
  101.1 0.6 constant_dynamic-update-slice_fusion.11
  102.4 2.1 %collective-permute-start.15 = (bf16[48,2048]{1,0:T(8,128)(2,1)S(1)}, bf16[48,2048]{1,0:T(8,128)(2,1)S(1)}, u32[]{:S(2)}, u32[]{:S(2)}) collective-permute-start(bf16[48,2048]{1,0:T(8,128)(2,1)S(1)} %fusion), channel_id=1, source_target_pairs={{0,448},{16,80},{32,480},{48,112},{64,0},{80,144},{96,32},{112,176... | collective-permute-start | bytes 589832 | tf_op jit(solution)/shard_map/ppermute | solution.py:27
  104.6 0.9 fusion.101
  105.6 0.9 fusion.100
  106.7 0.9 fusion.99
  108.0 8.6 %collective-permute-start.9 = (bf16[3,176,2048]{2,1,0:T(8,128)(2,1)S(1)}, bf16[3,176,2048]{2,1,0:T(8,128)(2,1)S(1)}, u32[]{:S(2)}, u32[]{:S(2)}) collective-permute-start(bf16[3,176,2048]{2,1,0:T(8,128)(2,1)S(1)} %pad_maximum_fusion.1), channel_id=1, source_target_pairs={{0,16},{16,0},{32,48},{48,32},{64,80},{80,64},{96,112},{112,96},{1... | collective-permute-start | bytes 6488072 | tf_op jit(solution)/shard_map/ppermute | solution.py:27
  116.6 3.6 %collective-permute-start.16 = (bf16[48,2048]{1,0:T(8,128)(2,1)S(1)}, bf16[48,2048]{1,0:T(8,128)(2,1)S(1)}, u32[]{:S(2)}, u32[]{:S(2)}) collective-permute-start(bf16[48,2048]{1,0:T(8,128)(2,1)S(1)} %fusion.10), channel_id=1, source_target_pairs={{0,448},{16,80},{32,480},{48,112},{64,0},{80,144},{96,32},{112,176... | collective-permute-start | bytes 589832 | tf_op jit(solution)/shard_map/ppermute | solution.py:27
  120.7 3.5 %collective-permute-done.16 = bf16[48,2048]{1,0:T(8,128)(2,1)S(1)} collective-permute-done((bf16[48,2048]{1,0:T(8,128)(2,1)S(1)}, bf16[48,2048]{1,0:T(8,128)(2,1)S(1)}, u32[]{:S(2)}, u32[]{:S(2)}) %collective-permute-start.16) | collective-permute-done | bytes 196640 | tf_op jit(solution)/shard_map/ppermute | solution.py:27
  124.4 2.7 %collective-permute-start.12 = (bf16[48,2048]{1,0:T(8,128)(2,1)S(1)}, bf16[48,2048]{1,0:T(8,128)(2,1)S(1)}, u32[]{:S(2)}, u32[]{:S(2)}) collective-permute-start(bf16[48,2048]{1,0:T(8,128)(2,1)S(1)} %get-tuple-element.32), channel_id=1, source_target_pairs={{0,448},{16,80},{32,480},{48,112},{64,0},{80,144},{96,32},{112,176... | collective-permute-start | bytes 589832 | tf_op jit(solution)/shard_map/ppermute | solution.py:27
  127.1 1.9 %collective-permute-start.17 = (bf16[48,2048]{1,0:T(8,128)(2,1)S(1)}, bf16[48,2048]{1,0:T(8,128)(2,1)S(1)}, u32[]{:S(2)}, u32[]{:S(2)}) collective-permute-start(bf16[48,2048]{1,0:T(8,128)(2,1)S(1)} %get-tuple-element.33), channel_id=1, source_target_pairs={{0,448},{16,80},{32,480},{48,112},{64,0},{80,144},{96,32},{112,176... | collective-permute-start | bytes 589832 | tf_op jit(solution)/shard_map/ppermute | solution.py:27
  129.5 2.5 %collective-permute-done.12 = bf16[48,2048]{1,0:T(8,128)(2,1)S(1)} collective-permute-done((bf16[48,2048]{1,0:T(8,128)(2,1)S(1)}, bf16[48,2048]{1,0:T(8,128)(2,1)S(1)}, u32[]{:S(2)}, u32[]{:S(2)}) %collective-permute-start.12) | collective-permute-done | bytes 196640 | tf_op jit(solution)/shard_map/ppermute | solution.py:27
  132.0 2.7 %collective-permute-done.17 = bf16[48,2048]{1,0:T(8,128)(2,1)S(1)} collective-permute-done((bf16[48,2048]{1,0:T(8,128)(2,1)S(1)}, bf16[48,2048]{1,0:T(8,128)(2,1)S(1)}, u32[]{:S(2)}, u32[]{:S(2)}) %collective-permute-start.17) | collective-permute-done | bytes 196640 | tf_op jit(solution)/shard_map/ppermute | solution.py:27
  134.8 0.7 fusion.96
  135.5 2.8 %collective-permute-start.13 = (bf16[24,2048]{1,0:T(8,128)(2,1)}, bf16[24,2048]{1,0:T(8,128)(2,1)}, u32[]{:S(2)}, u32[]{:S(2)}) collective-permute-start(bf16[24,2048]{1,0:T(8,128)(2,1)} %get-tuple-element.77), channel_id=1, source_target_pairs={{0,464},{16,64},{32,496},{48,96},{64,16},{80,128},{96,48},{112,160... | collective-permute-start | bytes 294920 | tf_op jit(solution)/shard_map/ppermute | solution.py:27
  138.3 5.0 %collective-permute-start.14 = (bf16[24,2048]{1,0:T(8,128)(2,1)}, bf16[24,2048]{1,0:T(8,128)(2,1)}, u32[]{:S(2)}, u32[]{:S(2)}) collective-permute-start(bf16[24,2048]{1,0:T(8,128)(2,1)} %get-tuple-element.78), channel_id=1, source_target_pairs={{0,496},{16,96},{32,464},{48,64},{64,48},{80,160},{96,16},{112,128... | collective-permute-start | bytes 294920 | tf_op jit(solution)/shard_map/ppermute | solution.py:27
  143.3 0.7 fusion.97
  144.0 2.6 %collective-permute-start.18 = (bf16[24,2048]{1,0:T(8,128)(2,1)}, bf16[24,2048]{1,0:T(8,128)(2,1)}, u32[]{:S(2)}, u32[]{:S(2)}) collective-permute-start(bf16[24,2048]{1,0:T(8,128)(2,1)} %get-tuple-element.79), channel_id=1, source_target_pairs={{0,448},{16,80},{32,480},{48,112},{64,0},{80,144},{96,32},{112,176... | collective-permute-start | bytes 294920 | tf_op jit(solution)/shard_map/ppermute | solution.py:27
  146.6 3.7 %collective-permute-start.19 = (bf16[24,2048]{1,0:T(8,128)(2,1)}, bf16[24,2048]{1,0:T(8,128)(2,1)}, u32[]{:S(2)}, u32[]{:S(2)}) collective-permute-start(bf16[24,2048]{1,0:T(8,128)(2,1)} %get-tuple-element.80), channel_id=1, source_target_pairs={{0,480},{16,112},{32,448},{48,80},{64,32},{80,176},{96,0},{112,144... | collective-permute-start | bytes 294920 | tf_op jit(solution)/shard_map/ppermute | solution.py:27
  151.7 4.3 %collective-permute-done.19 = bf16[24,2048]{1,0:T(8,128)(2,1)} collective-permute-done((bf16[24,2048]{1,0:T(8,128)(2,1)}, bf16[24,2048]{1,0:T(8,128)(2,1)}, u32[]{:S(2)}, u32[]{:S(2)}) %collective-permute-start.19) | collective-permute-done | bytes 98336 | tf_op jit(solution)/shard_map/ppermute | solution.py:27
  155.9 1.8 %bitcast_bitcast_fusion = bf16[16,24,128]{2,1,0:T(8,128)(2,1)} fusion(bf16[24,2048]{1,0:T(8,128)(2,1)} %collective-permute-done.19, bf16[24,2048]{1,0:T(8,128)(2,1)} %collective-permute-done.18, bf16[24,2048]{1,0:T(8,128)(2,1)} %collective-permute-done.14, bf16[24,2048]{1,0:T(8,128)(2,1)} %collective-permute-done.13, ...), kind=kLoop, calls=%fused_computation.111 | loop fusion | flops 589824 | bytes 786436 | tf_op jit(solution)/shard_map/convert_element_type | solution.py:133
  157.7 3.6 %all-to-all-start.1 = ((bf16[16,24,128]{2,1,0:T(8,128)(2,1)}), bf16[16,24,128]{2,1,0:T(8,128)(2,1)S(1)}, u32[]{:S(2)}, u32[]{:S(2)}) async-start(bf16[16,24,128]{2,1,0:T(8,128)(2,1)} %bitcast_bitcast_fusion), calls=%async_computation.1 | async-start | bytes 196608 | tf_op jit(solution)/shard_map/all_to_all | solution.py:134
  161.4 1.8 %slice_bitcast_fusion = (bf16[176,2048]{1,0:T(8,128)(2,1)S(1)}, bf16[176,2048]{1,0:T(8,128)(2,1)S(1)}, bf16[176,2048]{1,0:T(8,128)(2,1)S(1)}) fusion(bf16[3,176,2048]{2,1,0:T(8,128)(2,1)} %copy-done.6), kind=kLoop, calls=%fused_computation.29 | loop fusion | bytes 4325376
  163.4 1.0 fusion.7
  164.7 1.1 fusion.9
  165.8 1.1 fusion.8
  166.9 1.9 %all-to-all-done.1 = bf16[16,24,128]{2,1,0:T(8,128)(2,1)S(1)} async-done(((bf16[16,24,128]{2,1,0:T(8,128)(2,1)}), bf16[16,24,128]{2,1,0:T(8,128)(2,1)S(1)}, u32[]{:S(2)}, u32[]{:S(2)}) %all-to-all-start.1) | async-done | bytes 98336 | tf_op jit(solution)/shard_map/all_to_all | solution.py:134
  168.8 0.8 convolution_convert_fusion.2
  (91 shorter events, 9.3 us)
Async XLA Ops:
  0.6 19.6 %copy-start = (bf16[128,2048]{1,0:T(8,128)(2,1)S(1)}, bf16[128,2048]{1,0:T(8,128)(2,1)}, u32[]{:S(2)}) copy-start(bf16[128,2048]{1,0:T(8,128)(2,1)} %param.8) | copy-start | bytes 1572868
  0.6 1.4 copy-start.8
  0.7 1.6 copy-start.7
  2.0 100.0 %copy-start.4 = (bf16[176,2048]{1,0:T(8,128)(2,1)}, bf16[176,2048]{1,0:T(8,128)(2,1)S(1)}, u32[]{:S(2)}) copy-start(bf16[176,2048]{1,0:T(8,128)(2,1)S(1)} %get-tuple-element.38) | copy-start | bytes 2162692
  3.5 10.4 %copy-start.14 = (s32[128]{0:T(128)S(1)}, s32[128]{0:T(128)}, u32[]{:S(2)}) copy-start(s32[128]{0:T(128)} %param.11) | copy-start | bytes 1540
  3.6 10.4 %copy-start.15 = (s32[128]{0:T(128)S(1)}, s32[128]{0:T(128)}, u32[]{:S(2)}) copy-start(s32[128]{0:T(128)} %param.10) | copy-start | bytes 1540
  3.6 10.9 %copy-start.13 = (f32[128]{0:T(128)S(1)}, f32[128]{0:T(128)}, u32[]{:S(2)}) copy-start(f32[128]{0:T(128)} %param.12) | copy-start | bytes 1540
  5.1 31.9 %collective-permute-start.1 = (bf16[3,176,2048]{2,1,0:T(8,128)(2,1)}, bf16[3,176,2048]{2,1,0:T(8,128)(2,1)S(1)}, u32[]{:S(2)}, u32[]{:S(2)}) collective-permute-start(bf16[3,176,2048]{2,1,0:T(8,128)(2,1)} %pad_maximum_fusion), channel_id=1, source_target_pairs={{0,16},{16,0},{32,48},{48,32},{64,80},{80,64},{96,112},{112,96},{1... | collective-permute-start | bytes 6488072 | tf_op jit(solution)/shard_map/ppermute | solution.py:27
  16.1 11.6 %all-to-all-start = ((bf16[16,24,128]{2,1,0:T(8,128)(2,1)}), bf16[16,24,128]{2,1,0:T(8,128)(2,1)}, u32[]{:S(2)}, u32[]{:S(2)}) async-start(bf16[16,24,128]{2,1,0:T(8,128)(2,1)} %bitcast.1), calls=%async_computation | async-start | bytes 196608 | tf_op jit(solution)/shard_map/all_to_all | solution.py:66
  28.5 8.5 %collective-permute-start = (bf16[48,2048]{1,0:T(8,128)(2,1)S(1)}, bf16[48,2048]{1,0:T(8,128)(2,1)S(1)}, u32[]{:S(2)}, u32[]{:S(2)}) collective-permute-start(bf16[48,2048]{1,0:T(8,128)(2,1)S(1)} %pad_maximum_fusion.14), channel_id=1, source_target_pairs={{0,32},{16,48},{32,0},{48,16},{64,96},{80,112},{96,64},{112,80},{1... | collective-permute-start | bytes 589832 | tf_op jit(solution)/shard_map/ppermute | solution.py:27
  38.3 11.4 %copy-start.9 = (bf16[176,2048]{1,0:T(8,128)(2,1)S(1)}, bf16[176,2048]{1,0:T(8,128)(2,1)}, u32[]{:S(2)}) copy-start(bf16[176,2048]{1,0:T(8,128)(2,1)} %get-tuple-element.34) | copy-start | bytes 2162692
  38.3 18.9 %collective-permute-start.3 = (bf16[96,2048]{1,0:T(8,128)(2,1)S(1)}, bf16[96,2048]{1,0:T(8,128)(2,1)S(1)}, u32[]{:S(2)}, u32[]{:S(2)}) collective-permute-start(bf16[96,2048]{1,0:T(8,128)(2,1)S(1)} %maximum_add_fusion), channel_id=1, source_target_pairs={{0,464},{16,64},{32,496},{48,96},{64,16},{80,128},{96,48},{112,160... | collective-permute-start | bytes 1179656 | tf_op jit(solution)/shard_map/ppermute | solution.py:27
  43.1 14.0 %collective-permute-start.2 = (bf16[96,2048]{1,0:T(8,128)(2,1)S(1)}, bf16[96,2048]{1,0:T(8,128)(2,1)S(1)}, u32[]{:S(2)}, u32[]{:S(2)}) collective-permute-start(bf16[96,2048]{1,0:T(8,128)(2,1)S(1)} %maximum_add_fusion), channel_id=1, source_target_pairs={{0,64},{16,464},{32,96},{48,496},{64,128},{80,16},{96,160},{112,48... | collective-permute-start | bytes 1179656 | tf_op jit(solution)/shard_map/ppermute | solution.py:27
  50.2 1.1 copy-start.10
  52.7 4.6 %copy-start.11 = (f32[48,2048]{1,0:T(8,128)}, f32[48,2048]{1,0:T(8,128)S(1)}, u32[]{:S(2)}) copy-start(f32[48,2048]{1,0:T(8,128)S(1)} %convolution_add_fusion.4) | copy-start | bytes 1179652
  52.7 98.9 %collective-permute-start.10 = (bf16[24,2048]{1,0:T(8,128)(2,1)S(1)}, bf16[24,2048]{1,0:T(8,128)(2,1)}, u32[]{:S(2)}, u32[]{:S(2)}) collective-permute-start(bf16[24,2048]{1,0:T(8,128)(2,1)S(1)} %slice.322), channel_id=1, source_target_pairs={{0,32},{16,48},{32,0},{48,16},{64,96},{80,112},{96,64},{112,80},{1... | collective-permute-start | bytes 294920 | tf_op jit(solution)/shard_map/ppermute | solution.py:27
  58.5 14.6 %collective-permute-start.5 = (bf16[96,2048]{1,0:T(8,128)(2,1)S(1)}, bf16[96,2048]{1,0:T(8,128)(2,1)S(1)}, u32[]{:S(2)}, u32[]{:S(2)}) collective-permute-start(bf16[96,2048]{1,0:T(8,128)(2,1)S(1)} %collective-permute-done.3), channel_id=1, source_target_pairs={{0,64},{16,464},{32,96},{48,496},{64,128},{80,16},{96,160},{112,48... | collective-permute-start | bytes 1179656 | tf_op jit(solution)/shard_map/ppermute | solution.py:27
  64.1 8.9 %collective-permute-start.4 = (bf16[96,2048]{1,0:T(8,128)(2,1)S(1)}, bf16[96,2048]{1,0:T(8,128)(2,1)S(1)}, u32[]{:S(2)}, u32[]{:S(2)}) collective-permute-start(bf16[96,2048]{1,0:T(8,128)(2,1)S(1)} %collective-permute-done.2), channel_id=1, source_target_pairs={{0,64},{16,464},{32,96},{48,496},{64,128},{80,16},{96,160},{112,48... | collective-permute-start | bytes 1179656 | tf_op jit(solution)/shard_map/ppermute | solution.py:27
  74.3 14.0 %collective-permute-start.7 = (bf16[96,2048]{1,0:T(8,128)(2,1)S(1)}, bf16[96,2048]{1,0:T(8,128)(2,1)S(1)}, u32[]{:S(2)}, u32[]{:S(2)}) collective-permute-start(bf16[96,2048]{1,0:T(8,128)(2,1)S(1)} %collective-permute-done.5), channel_id=1, source_target_pairs={{0,64},{16,464},{32,96},{48,496},{64,128},{80,16},{96,160},{112,48... | collective-permute-start | bytes 1179656 | tf_op jit(solution)/shard_map/ppermute | solution.py:27
  79.4 8.9 %collective-permute-start.6 = (bf16[96,2048]{1,0:T(8,128)(2,1)S(1)}, bf16[96,2048]{1,0:T(8,128)(2,1)S(1)}, u32[]{:S(2)}, u32[]{:S(2)}) collective-permute-start(bf16[96,2048]{1,0:T(8,128)(2,1)S(1)} %collective-permute-done.4), channel_id=1, source_target_pairs={{0,64},{16,464},{32,96},{48,496},{64,128},{80,16},{96,160},{112,48... | collective-permute-start | bytes 1179656 | tf_op jit(solution)/shard_map/ppermute | solution.py:27
  90.2 9.7 %collective-permute-start.8 = (bf16[96,2048]{1,0:T(8,128)(2,1)S(1)}, bf16[96,2048]{1,0:T(8,128)(2,1)S(1)}, u32[]{:S(2)}, u32[]{:S(2)}) collective-permute-start(bf16[96,2048]{1,0:T(8,128)(2,1)S(1)} %collective-permute-done.6), channel_id=1, source_target_pairs={{0,64},{16,464},{32,96},{48,496},{64,128},{80,16},{96,160},{112,48... | collective-permute-start | bytes 1179656 | tf_op jit(solution)/shard_map/ppermute | solution.py:27
  96.1 24.6 %collective-permute-start.11 = (bf16[48,2048]{1,0:T(8,128)(2,1)S(1)}, bf16[48,2048]{1,0:T(8,128)(2,1)S(1)}, u32[]{:S(2)}, u32[]{:S(2)}) collective-permute-start(bf16[48,2048]{1,0:T(8,128)(2,1)S(1)} %slice.321), channel_id=1, source_target_pairs={{0,448},{16,80},{32,480},{48,112},{64,0},{80,144},{96,32},{112,176... | collective-permute-start | bytes 589832 | tf_op jit(solution)/shard_map/ppermute | solution.py:27
  102.4 14.2 %collective-permute-start.15 = (bf16[48,2048]{1,0:T(8,128)(2,1)S(1)}, bf16[48,2048]{1,0:T(8,128)(2,1)S(1)}, u32[]{:S(2)}, u32[]{:S(2)}) collective-permute-start(bf16[48,2048]{1,0:T(8,128)(2,1)S(1)} %fusion), channel_id=1, source_target_pairs={{0,448},{16,80},{32,480},{48,112},{64,0},{80,144},{96,32},{112,176... | collective-permute-start | bytes 589832 | tf_op jit(solution)/shard_map/ppermute | solution.py:27
  105.5 44.9 %copy-start.1 = (f32[352,2048]{1,0:T(8,128)}, f32[352,2048]{1,0:T(8,128)S(1)}, u32[]{:S(2)}) copy-start(f32[352,2048]{1,0:T(8,128)S(1)} %fusion.101) | copy-start | bytes 8650756
  106.5 43.9 %copy-start.2 = (f32[352,2048]{1,0:T(8,128)}, f32[352,2048]{1,0:T(8,128)S(1)}, u32[]{:S(2)}) copy-start(f32[352,2048]{1,0:T(8,128)S(1)} %fusion.100) | copy-start | bytes 8650756
  107.6 42.8 %copy-start.3 = (f32[352,2048]{1,0:T(8,128)}, f32[352,2048]{1,0:T(8,128)S(1)}, u32[]{:S(2)}) copy-start(f32[352,2048]{1,0:T(8,128)S(1)} %fusion.99) | copy-start | bytes 8650756
  107.7 12.6 %copy-start.5 = (bf16[176,2048]{1,0:T(8,128)(2,1)S(1)}, bf16[176,2048]{1,0:T(8,128)(2,1)}, u32[]{:S(2)}) copy-start(bf16[176,2048]{1,0:T(8,128)(2,1)} %copy-done.4) | copy-start | bytes 2162692
  108.0 38.6 %collective-permute-start.9 = (bf16[3,176,2048]{2,1,0:T(8,128)(2,1)S(1)}, bf16[3,176,2048]{2,1,0:T(8,128)(2,1)S(1)}, u32[]{:S(2)}, u32[]{:S(2)}) collective-permute-start(bf16[3,176,2048]{2,1,0:T(8,128)(2,1)S(1)} %pad_maximum_fusion.1), channel_id=1, source_target_pairs={{0,16},{16,0},{32,48},{48,32},{64,80},{80,64},{96,112},{112,96},{1... | collective-permute-start | bytes 6488072 | tf_op jit(solution)/shard_map/ppermute | solution.py:27
  116.6 7.6 %collective-permute-start.16 = (bf16[48,2048]{1,0:T(8,128)(2,1)S(1)}, bf16[48,2048]{1,0:T(8,128)(2,1)S(1)}, u32[]{:S(2)}, u32[]{:S(2)}) collective-permute-start(bf16[48,2048]{1,0:T(8,128)(2,1)S(1)} %fusion.10), channel_id=1, source_target_pairs={{0,448},{16,80},{32,480},{48,112},{64,0},{80,144},{96,32},{112,176... | collective-permute-start | bytes 589832 | tf_op jit(solution)/shard_map/ppermute | solution.py:27
  124.4 7.6 %collective-permute-start.12 = (bf16[48,2048]{1,0:T(8,128)(2,1)S(1)}, bf16[48,2048]{1,0:T(8,128)(2,1)S(1)}, u32[]{:S(2)}, u32[]{:S(2)}) collective-permute-start(bf16[48,2048]{1,0:T(8,128)(2,1)S(1)} %get-tuple-element.32), channel_id=1, source_target_pairs={{0,448},{16,80},{32,480},{48,112},{64,0},{80,144},{96,32},{112,176... | collective-permute-start | bytes 589832 | tf_op jit(solution)/shard_map/ppermute | solution.py:27
  127.1 7.6 %collective-permute-start.17 = (bf16[48,2048]{1,0:T(8,128)(2,1)S(1)}, bf16[48,2048]{1,0:T(8,128)(2,1)S(1)}, u32[]{:S(2)}, u32[]{:S(2)}) collective-permute-start(bf16[48,2048]{1,0:T(8,128)(2,1)S(1)} %get-tuple-element.33), channel_id=1, source_target_pairs={{0,448},{16,80},{32,480},{48,112},{64,0},{80,144},{96,32},{112,176... | collective-permute-start | bytes 589832 | tf_op jit(solution)/shard_map/ppermute | solution.py:27
  135.5 16.1 %collective-permute-start.13 = (bf16[24,2048]{1,0:T(8,128)(2,1)}, bf16[24,2048]{1,0:T(8,128)(2,1)}, u32[]{:S(2)}, u32[]{:S(2)}) collective-permute-start(bf16[24,2048]{1,0:T(8,128)(2,1)} %get-tuple-element.77), channel_id=1, source_target_pairs={{0,464},{16,64},{32,496},{48,96},{64,16},{80,128},{96,48},{112,160... | collective-permute-start | bytes 294920 | tf_op jit(solution)/shard_map/ppermute | solution.py:27
  138.3 13.3 %collective-permute-start.14 = (bf16[24,2048]{1,0:T(8,128)(2,1)}, bf16[24,2048]{1,0:T(8,128)(2,1)}, u32[]{:S(2)}, u32[]{:S(2)}) collective-permute-start(bf16[24,2048]{1,0:T(8,128)(2,1)} %get-tuple-element.78), channel_id=1, source_target_pairs={{0,496},{16,96},{32,464},{48,64},{64,48},{80,160},{96,16},{112,128... | collective-permute-start | bytes 294920 | tf_op jit(solution)/shard_map/ppermute | solution.py:27
  144.0 7.7 %collective-permute-start.18 = (bf16[24,2048]{1,0:T(8,128)(2,1)}, bf16[24,2048]{1,0:T(8,128)(2,1)}, u32[]{:S(2)}, u32[]{:S(2)}) collective-permute-start(bf16[24,2048]{1,0:T(8,128)(2,1)} %get-tuple-element.79), channel_id=1, source_target_pairs={{0,448},{16,80},{32,480},{48,112},{64,0},{80,144},{96,32},{112,176... | collective-permute-start | bytes 294920 | tf_op jit(solution)/shard_map/ppermute | solution.py:27
  146.6 3.8 %copy-start.6 = (bf16[3,176,2048]{2,1,0:T(8,128)(2,1)}, bf16[3,176,2048]{2,1,0:T(8,128)(2,1)S(1)}, u32[]{:S(2)}) copy-start(bf16[3,176,2048]{2,1,0:T(8,128)(2,1)S(1)} %collective-permute-done.9) | copy-start | bytes 6488068
  146.6 9.3 %collective-permute-start.19 = (bf16[24,2048]{1,0:T(8,128)(2,1)}, bf16[24,2048]{1,0:T(8,128)(2,1)}, u32[]{:S(2)}, u32[]{:S(2)}) collective-permute-start(bf16[24,2048]{1,0:T(8,128)(2,1)} %get-tuple-element.80), channel_id=1, source_target_pairs={{0,480},{16,112},{32,448},{48,80},{64,32},{80,176},{96,0},{112,144... | collective-permute-start | bytes 294920 | tf_op jit(solution)/shard_map/ppermute | solution.py:27
  150.4 5.5 %copy-start.12 = (f32[48,2048]{1,0:T(8,128)S(1)}, f32[48,2048]{1,0:T(8,128)}, u32[]{:S(2)}) copy-start(f32[48,2048]{1,0:T(8,128)} %copy-done.11) | copy-start | bytes 1179652
  157.7 11.0 %all-to-all-start.1 = ((bf16[16,24,128]{2,1,0:T(8,128)(2,1)}), bf16[16,24,128]{2,1,0:T(8,128)(2,1)S(1)}, u32[]{:S(2)}, u32[]{:S(2)}) async-start(bf16[16,24,128]{2,1,0:T(8,128)(2,1)} %bitcast_bitcast_fusion), calls=%async_computation.1 | async-start | bytes 196608 | tf_op jit(solution)/shard_map/all_to_all | solution.py:134
  161.4 2.0 %slice-start.2 = ((f32[352,2048]{1,0:T(8,128)}), f32[176,2048]{1,0:T(8,128)S(1)}, s32[]{:S(2)}) async-start(f32[352,2048]{1,0:T(8,128)} %copy-done.3), calls=%async_computation.4 | async-start | bytes 2883584 | tf_op jit(solution)/shard_map/slice | solution.py:142
  163.2 1.5 slice-start
  164.4 1.4 slice-start.1

commit v3 on v2

--- a/solution.py
+++ b/solution.py
@@ -31,6 +31,12 @@
     return lax.dot_general(a, b, (dims, ((), ())), preferred_element_type=F32)
 
 
+def after(a, *earlier):
+    for b in earlier:
+        a = a + (b[:1] * 0).astype(a.dtype)
+    return a
+
+
 def local(tokens, out_grad, modality, within_route, gate_values, w_gate, w_up, w_down):
     tok_count, width = tokens.shape
     experts_all = XL * Y // 2
@@ -59,36 +65,30 @@
     wu = jnp.concatenate([own_w[1], other_w[1]], axis=0)
     wd = jnp.concatenate([own_w[2], other_w[2]], axis=0)
 
+    near = 2 * capacity
+    x_own = dot(select_own, tokens).astype(BF)
+    x_across = send(x_own, 0, across=True)
+    x0 = jnp.concatenate([x_own, x_across], axis=0)
+    x1_a, x1_b = send(x0, 1), send(x0, -1, other=True)
+    x1 = jnp.concatenate([x1_a, x1_b], axis=0)
+    x2 = send(x1, 1)
+    x3 = send(x2, 1)
+    x4 = send(x3[:near], 1)
+
     scaled = (gate_values[:, None] * out_grad.astype(F32)).astype(BF)
     dy_slices = dot(select, scaled).astype(BF).reshape(experts_all, 1, capacity, -1)
     dy_slices = jnp.broadcast_to(dy_slices, (experts_all, 2) + dy_slices.shape[2:])
     dy_slices = dy_slices.reshape((2 * experts_all,) + dy_slices.shape[2:])
     dy_slices = lax.all_to_all(dy_slices, EXPERT, 0, 0, tiled=True)
-    x_own = dot(select_own, tokens).astype(BF)
-    dy_own = jnp.transpose(dy_slices, (1, 0, 2)).reshape(capacity, width)
-    own = jnp.concatenate([x_own, dy_own], axis=0)
-    across = send(own, 0, across=True)
-
-    near = 2 * capacity
-    packet = jnp.concatenate(
-        [own[:capacity], across[:capacity], own[capacity:], across[capacity:]], axis=0
-    )
-    packet = packet + other_w[2, hidden_own, 0]
-    chain_a = [send(packet, 1)]
-    chain_b = [send(packet, -1, other=True)]
-    for step in (1, 2):
-        chain_a.append(send(chain_a[-1], 1))
-        chain_b.append(send(chain_b[-1], 1))
-    chain_a.append(send(chain_a[-1], 1))
-    chunks = [(packet[:near], packet[near:])]
-    for a, b in zip(chain_a[:3], chain_b):
-        chunks.append(
-            (
-                jnp.concatenate([a[:near], b[:near]], axis=0),
-                jnp.concatenate([a[near:], b[near:]], axis=0),
-            )
-        )
-    chunks.append((chain_a[3][:near], chain_a[3][near:]))
+    dy_own = after(jnp.transpose(dy_slices, (1, 0, 2)).reshape(capacity, width), x_across)
+    dy0 = jnp.concatenate([dy_own, send(dy_own, 0, across=True)], axis=0)
+    dy0 = after(dy0, x1_a, x1_b)
+    dy1 = jnp.concatenate([send(dy0, 1), send(dy0, -1, other=True)], axis=0)
+    dy1 = after(dy1, x2, other_w[2])
+    dy2 = after(send(dy1, 1), x3)
+    dy3 = send(dy2, 1)
+    dy4 = send(after(dy3[:near], x4), 1)
+    chunks = [(x0, dy0), (x1, dy1), (x2, dy2), (x3, dy3), (x4, dy4)]
 
     cols = ((1,), (1,))
     terms, hiddens, d_gates, d_ups = [], [], [], []
@@ -115,19 +115,25 @@
     ]
     received = send(jnp.stack([grad[PAD:].astype(BF) for grad in grads]), 0, other=True)
 
-    home_b = terms[3][near:]
-    home_b = terms[2][near:] + send(home_b.astype(BF), -1).astype(F32)
-    home_b = (terms[1][near:] + send(home_b.astype(BF), -1).astype(F32)).astype(BF)
-    home_a = terms[4]
-    home_a = terms[3][:near] + send(home_a.astype(BF), -1).astype(F32)
-    home_a = terms[2][:near] + send(home_a.astype(BF), -1).astype(F32)
-    home_a = (terms[1][:near] + send(home_a.astype(BF), -1).astype(F32)).astype(BF)
+    came_b = send(terms[3][near:].astype(BF), -1)
+    came_a = send(terms[4].astype(BF), -1)
+    home_b = terms[2][near:] + came_b.astype(F32)
+    home_a = after(terms[3][:near] + came_a.astype(F32), came_b)
+    came_b = send(home_b.astype(BF), -1)
+    came_a = send(home_a.astype(BF), -1)
+    home_b = (terms[1][near:] + came_b.astype(F32)).astype(BF)
+    home_a = after(terms[2][:near] + came_a.astype(F32), came_b)
+    last_b = [
+        send(home_b[:capacity], -1, other=True),
+        send(home_b[capacity:], -1, across=True, other=True),
+    ]
+    came_a = send(home_a.astype(BF), -1)
+    home_a = after((terms[1][:near] + came_a.astype(F32)).astype(BF), *last_b)
+    last_a = [send(home_a[:capacity], -1), send(home_a[capacity:], -1, across=True)]
+    last_0 = send(terms[0][capacity:].astype(BF), 0, across=True)
     summed = terms[0][:capacity]
-    summed = summed + send(terms[0][capacity:].astype(BF), 0, across=True).astype(F32)
-    summed = summed + send(home_b[:capacity], -1, other=True).astype(F32)
-    summed = summed + send(home_b[capacity:], -1, across=True, other=True).astype(F32)
-    summed = summed + send(home_a[:capacity], -1).astype(F32)
-    summed = summed + send(home_a[capacity:], -1, across=True).astype(F32)
+    for came in (last_0, *last_b, *last_a):
+        summed = summed + came.astype(F32)
     summed = summed + received[2, hidden_own, 0].astype(F32)
     summed = summed.reshape(capacity, 2 * experts_all, -1)
     summed = jnp.transpose(summed, (1, 0, 2)).astype(BF)

time: 172 us -> 185 us (1.076)
  starting transfers between devices: 89.8 us -> 104 us
  waiting for transfers between devices: 41.1 us -> 28 us
  other arithmetic: 8.16 us -> 12.8 us
  matrix products: 17.6 us -> 21.7 us
  local copies, waits for them, and re-layouts: 10.8 us -> 13.8 us
    all_to_all x1, waiting for transfers between devices: 7.14 us -> 0.01 us  [local(): dy_slices = lax.all_to_all(dy_slices, EXPERT, 0, 0, tiled=True)]
    ppermute x20 -> x24, starting transfers between devices: 82 us -> 88 us  [send(): return lax.ppermute(a, PLANE, hops(step, across, other))]
    ppermute x20 -> x24, waiting for transfers between devices: 32.1 us -> 26.1 us  [send(): return lax.ppermute(a, PLANE, hops(step, across, other))]
    all_to_all x1, starting transfers between devices: 4.15 us -> 8.73 us  [local(): dy_slices = lax.all_to_all(dy_slices, EXPERT, 0, 0, tiled=True)]
    dot_general x31, matrix products: 17.6 us -> 21.7 us  [dot(): return lax.dot_general(a, b, (dims, ((), ())), preferred_element_type=F32)]
    all_to_all x1, starting transfers between devices: 3.62 us -> 7.17 us  [local(): summed = lax.all_to_all(summed, EXPERT, 0, 0, tiled=True)]
    mul x0 -> x9, other arithmetic: none -> 3.37 us  [after(): a = a + (b[:1] * 0).astype(a.dtype)]
    unnamed x40 -> x45, local copies, waits for them, and re-layouts: 3.08 us -> 6.13 us
  transfers between devices with their start and end apart: 22 -> 26, of which waited for: 10 -> 10; matrix products, arithmetic and copies ran while one was open for 16% -> 22% of each run, Pallas kernels for 0% -> 0%
where the time goes in v3:
time: 185 us; the launch traced here: 182 us
  starting transfers between devices  104 us (56%)
  waiting for transfers between devices  28 us (15%)
  matrix products  21.7 us (12%)
  local copies, waits for them, and re-layouts  13.8 us (7%)
  other arithmetic  12.8 us (7%)
  between operations  2.27 us (1%)
    ppermute x24, starting transfers between devices, send(): return lax.ppermute(a, PLANE, hops(step, across, other))  88 us
    ppermute x24, waiting for transfers between devices, send(): return lax.ppermute(a, PLANE, hops(step, across, other))  26.1 us
    dot_general x31, matrix products, dot(): return lax.dot_general(a, b, (dims, ((), ())), preferred_element_type=F32)  21.7 us
    all_to_all x1, starting transfers between devices, local(): dy_slices = lax.all_to_all(dy_slices, EXPERT, 0, 0, tiled=True)  8.73 us
    all_to_all x1, starting transfers between devices, local(): summed = lax.all_to_all(summed, EXPERT, 0, 0, tiled=True)  7.17 us
    unnamed x45, local copies, waits for them, and re-layouts  6.13 us
  transfers between devices with their start and end apart: 26, of which 10 were waited for; matrix products, arithmetic and copies ran while one was open for 22% of the time, Pallas kernels for 0%

profile of v3, /device:TPU:1, one launch (start us, length us, event | category | flops | bytes accessed | tf_op | source)
XLA Modules:
  0.0 182.3 jit_solution(7827383194061208513)
XLA Ops:
  0.7 0.8 multiply_add_fusion
  1.9 1.0 convolution_convert_fusion.1
  2.9 0.7 broadcast_in_dim.16
  3.5 8.7 %all-to-all-start = ((bf16[16,24,128]{2,1,0:T(8,128)(2,1)}), bf16[16,24,128]{2,1,0:T(8,128)(2,1)}, u32[]{:S(2)}, u32[]{:S(2)}) async-start(bf16[16,24,128]{2,1,0:T(8,128)(2,1)} %bitcast.1), calls=%async_computation | async-start | bytes 196608 | tf_op jit(solution)/shard_map/all_to_all | solution.py:82
  12.5 4.4 %collective-permute-start = (bf16[24,2048]{1,0:T(8,128)(2,1)S(1)}, bf16[24,2048]{1,0:T(8,128)(2,1)S(1)}, u32[]{:S(2)}, u32[]{:S(2)}) collective-permute-start(bf16[24,2048]{1,0:T(8,128)(2,1)S(1)} %get-tuple-element.66), channel_id=1, source_target_pairs={{0,32},{16,48},{32,0},{48,16},{64,96},{80,112},{96,64},{112,80},{1... | collective-permute-start | bytes 294920 | tf_op jit(solution)/shard_map/ppermute | solution.py:27
  17.0 2.4 %fusion.88 = (bf16[176,2048]{1,0:T(8,128)(2,1)}, bf16[1,176,2048]{2,1,0:T(8,128)(2,1)S(1)}, bf16[1,176,2048]{2,1,0:T(8,128)(2,1)S(1)}, bf16[176,2048]{1,0:T(8,128)(2,1)S(1)}) fusion(bf16[172,2048]{1,0:T(8,128)(2,1)} %bitcast.88, bf16[172,2048]{1,0:T(8,128)(2,1)} %bitcast.89), kind=kLoop, calls=%fused_computation.198 | loop fusion | bytes 4292608 | tf_op jit(solution)/shard_map/jit(_pad)/pad | solution.py:62
  19.4 1.6 pad_maximum_fusion
  21.0 3.1 %collective-permute-start.4 = (bf16[3,176,2048]{2,1,0:T(8,128)(2,1)}, bf16[3,176,2048]{2,1,0:T(8,128)(2,1)}, u32[]{:S(2)}, u32[]{:S(2)}) collective-permute-start(bf16[3,176,2048]{2,1,0:T(8,128)(2,1)} %pad_maximum_fusion), channel_id=1, source_target_pairs={{0,16},{16,0},{32,48},{48,32},{64,80},{80,64},{96,112},{112,96},{1... | collective-permute-start | bytes 6488072 | tf_op jit(solution)/shard_map/ppermute | solution.py:27
  24.2 3.9 %collective-permute-start.3 = (bf16[48,2048]{1,0:T(8,128)(2,1)S(1)}, bf16[48,2048]{1,0:T(8,128)(2,1)S(1)}, u32[]{:S(2)}, u32[]{:S(2)}) collective-permute-start(bf16[48,2048]{1,0:T(8,128)(2,1)S(1)} %pad_maximum_fusion.5), channel_id=1, source_target_pairs={{0,464},{16,64},{32,496},{48,96},{64,16},{80,128},{96,48},{112,160... | collective-permute-start | bytes 589832 | tf_op jit(solution)/shard_map/ppermute | solution.py:27
  28.1 8.7 %collective-permute-start.2 = (bf16[48,2048]{1,0:T(8,128)(2,1)S(1)}, bf16[48,2048]{1,0:T(8,128)(2,1)S(1)}, u32[]{:S(2)}, u32[]{:S(2)}) collective-permute-start(bf16[48,2048]{1,0:T(8,128)(2,1)S(1)} %pad_maximum_fusion.5), channel_id=1, source_target_pairs={{0,64},{16,464},{32,96},{48,496},{64,128},{80,16},{96,160},{112,48... | collective-permute-start | bytes 589832 | tf_op jit(solution)/shard_map/ppermute | solution.py:27
  36.9 3.3 %collective-permute-done.2 = bf16[48,2048]{1,0:T(8,128)(2,1)S(1)} collective-permute-done((bf16[48,2048]{1,0:T(8,128)(2,1)S(1)}, bf16[48,2048]{1,0:T(8,128)(2,1)S(1)}, u32[]{:S(2)}, u32[]{:S(2)}) %collective-permute-start.2) | collective-permute-done | bytes 196640 | tf_op jit(solution)/shard_map/ppermute | solution.py:27
  40.2 0.7 constant_dynamic-update-slice_fusion.11
  40.9 0.7 constant_dynamic-update-slice_fusion.10
  41.6 5.0 %collective-permute-start.7 = (bf16[96,2048]{1,0:T(8,128)(2,1)}, bf16[96,2048]{1,0:T(8,128)(2,1)}, u32[]{:S(2)}, u32[]{:S(2)}) collective-permute-start(bf16[96,2048]{1,0:T(8,128)(2,1)} %get-tuple-element.56), channel_id=1, source_target_pairs={{0,64},{16,464},{32,96},{48,496},{64,128},{80,16},{96,160},{112,48... | collective-permute-start | bytes 1179656 | tf_op jit(solution)/shard_map/ppermute | solution.py:27
  46.7 0.9 bitcast_add_fusion
  47.6 2.4 %collective-permute-start.1 = (bf16[24,2048]{1,0:T(8,128)(2,1)S(1)}, bf16[24,2048]{1,0:T(8,128)(2,1)S(1)}, u32[]{:S(2)}, u32[]{:S(2)}) collective-permute-start(bf16[24,2048]{1,0:T(8,128)(2,1)S(1)} %bitcast_add_fusion), channel_id=1, source_target_pairs={{0,32},{16,48},{32,0},{48,16},{64,96},{80,112},{96,64},{112,80},{1... | collective-permute-start | bytes 294920 | tf_op jit(solution)/shard_map/ppermute | solution.py:27
  50.0 0.8 fusion.47
  50.8 0.8 fusion.46
  51.7 5.0 %collective-permute-start.9 = (bf16[96,2048]{1,0:T(8,128)(2,1)}, bf16[96,2048]{1,0:T(8,128)(2,1)S(1)}, u32[]{:S(2)}, u32[]{:S(2)}) collective-permute-start(bf16[96,2048]{1,0:T(8,128)(2,1)} %collective-permute-done.7), channel_id=1, source_target_pairs={{0,64},{16,464},{32,96},{48,496},{64,128},{80,16},{96,160},{112,48... | collective-permute-start | bytes 1179656 | tf_op jit(solution)/shard_map/ppermute | solution.py:27
  56.8 2.3 %collective-permute-start.6 = (bf16[48,2048]{1,0:T(8,128)(2,1)S(1)}, bf16[48,2048]{1,0:T(8,128)(2,1)S(1)}, u32[]{:S(2)}, u32[]{:S(2)}) collective-permute-start(bf16[48,2048]{1,0:T(8,128)(2,1)S(1)} %get-tuple-element.19), channel_id=1, source_target_pairs={{0,464},{16,64},{32,496},{48,96},{64,16},{80,128},{96,48},{112,160... | collective-permute-start | bytes 589832 | tf_op jit(solution)/shard_map/ppermute | solution.py:27
  59.1 6.1 %collective-permute-start.5 = (bf16[48,2048]{1,0:T(8,128)(2,1)S(1)}, bf16[48,2048]{1,0:T(8,128)(2,1)S(1)}, u32[]{:S(2)}, u32[]{:S(2)}) collective-permute-start(bf16[48,2048]{1,0:T(8,128)(2,1)S(1)} %get-tuple-element.19), channel_id=1, source_target_pairs={{0,64},{16,464},{32,96},{48,496},{64,128},{80,16},{96,160},{112,48... | collective-permute-start | bytes 589832 | tf_op jit(solution)/shard_map/ppermute | solution.py:27
  65.1 0.8 fusion.48
  65.9 1.0 constant_dynamic-update-slice_fusion.9
  67.0 3.6 %collective-permute-start.11 = (bf16[48,2048]{1,0:T(8,128)(2,1)S(1)}, bf16[48,2048]{1,0:T(8,128)(2,1)S(1)}, u32[]{:S(2)}, u32[]{:S(2)}) collective-permute-start(bf16[48,2048]{1,0:T(8,128)(2,1)S(1)} %slice.173), channel_id=1, source_target_pairs={{0,64},{16,464},{32,96},{48,496},{64,128},{80,16},{96,160},{112,48... | collective-permute-start | bytes 589832 | tf_op jit(solution)/shard_map/ppermute | solution.py:27
  70.7 2.7 %collective-permute-done.11 = bf16[48,2048]{1,0:T(8,128)(2,1)S(1)} collective-permute-done((bf16[48,2048]{1,0:T(8,128)(2,1)S(1)}, bf16[48,2048]{1,0:T(8,128)(2,1)S(1)}, u32[]{:S(2)}, u32[]{:S(2)}) %collective-permute-start.11) | collective-permute-done | bytes 196640 | tf_op jit(solution)/shard_map/ppermute | solution.py:27
  73.5 0.8 fusion.49
  74.4 5.0 %collective-permute-start.8 = (bf16[96,2048]{1,0:T(8,128)(2,1)S(1)}, bf16[96,2048]{1,0:T(8,128)(2,1)S(1)}, u32[]{:S(2)}, u32[]{:S(2)}) collective-permute-start(bf16[96,2048]{1,0:T(8,128)(2,1)S(1)} %get-tuple-element.17), channel_id=1, source_target_pairs={{0,64},{16,464},{32,96},{48,496},{64,128},{80,16},{96,160},{112,48... | collective-permute-start | bytes 1179656 | tf_op jit(solution)/shard_map/ppermute | solution.py:27
  79.4 1.7 slice_bitcast_fusion.4
  81.2 1.6 fusion.85
  82.7 1.6 fusion.76
  86.9 0.7 slice.309
  87.6 2.4 %collective-permute-start.14 = (bf16[24,2048]{1,0:T(8,128)(2,1)}, bf16[24,2048]{1,0:T(8,128)(2,1)}, u32[]{:S(2)}, u32[]{:S(2)}) collective-permute-start(bf16[24,2048]{1,0:T(8,128)(2,1)} %slice.309), channel_id=1, source_target_pairs={{0,32},{16,48},{32,0},{48,16},{64,96},{80,112},{96,64},{112,80},{1... | collective-permute-start | bytes 294920 | tf_op jit(solution)/shard_map/ppermute | solution.py:27
  91.6 1.6 fusion.84
  93.2 1.6 fusion.75
  96.5 1.9 %collective-permute-start.10 = (bf16[96,2048]{1,0:T(8,128)(2,1)S(1)}, bf16[96,2048]{1,0:T(8,128)(2,1)S(1)}, u32[]{:S(2)}, u32[]{:S(2)}) collective-permute-start(bf16[96,2048]{1,0:T(8,128)(2,1)S(1)} %get-tuple-element.15), channel_id=1, source_target_pairs={{0,64},{16,464},{32,96},{48,496},{64,128},{80,16},{96,160},{112,48... | collective-permute-start | bytes 1179656 | tf_op jit(solution)/shard_map/ppermute | solution.py:27
  99.9 5.1 %collective-permute-done.10 = bf16[96,2048]{1,0:T(8,128)(2,1)S(1)} collective-permute-done((bf16[96,2048]{1,0:T(8,128)(2,1)S(1)}, bf16[96,2048]{1,0:T(8,128)(2,1)S(1)}, u32[]{:S(2)}, u32[]{:S(2)}) %collective-permute-start.10) | collective-permute-done | bytes 393248 | tf_op jit(solution)/shard_map/ppermute | solution.py:27
  105.0 3.1 %collective-permute-start.12 = (bf16[48,2048]{1,0:T(8,128)(2,1)S(1)}, bf16[48,2048]{1,0:T(8,128)(2,1)S(1)}, u32[]{:S(2)}, u32[]{:S(2)}) collective-permute-start(bf16[48,2048]{1,0:T(8,128)(2,1)S(1)} %slice_add_fusion.9), channel_id=1, source_target_pairs={{0,64},{16,464},{32,96},{48,496},{64,128},{80,16},{96,160},{112,48... | collective-permute-start | bytes 589832 | tf_op jit(solution)/shard_map/ppermute | solution.py:27
  108.7 0.6 constant_dynamic-update-slice_fusion.15
  110.3 2.1 %collective-permute-start.15 = (bf16[48,2048]{1,0:T(8,128)(2,1)S(1)}, bf16[48,2048]{1,0:T(8,128)(2,1)S(1)}, u32[]{:S(2)}, u32[]{:S(2)}) collective-permute-start(bf16[48,2048]{1,0:T(8,128)(2,1)S(1)} %slice.308), channel_id=1, source_target_pairs={{0,448},{16,80},{32,480},{48,112},{64,0},{80,144},{96,32},{112,176... | collective-permute-start | bytes 589832 | tf_op jit(solution)/shard_map/ppermute | solution.py:27
  113.8 1.9 %collective-permute-start.19 = (bf16[48,2048]{1,0:T(8,128)(2,1)S(1)}, bf16[48,2048]{1,0:T(8,128)(2,1)S(1)}, u32[]{:S(2)}, u32[]{:S(2)}) collective-permute-start(bf16[48,2048]{1,0:T(8,128)(2,1)S(1)} %fusion), channel_id=1, source_target_pairs={{0,448},{16,80},{32,480},{48,112},{64,0},{80,144},{96,32},{112,176... | collective-permute-start | bytes 589832 | tf_op jit(solution)/shard_map/ppermute | solution.py:27
  115.7 4.3 %collective-permute-done.15 = bf16[48,2048]{1,0:T(8,128)(2,1)S(1)} collective-permute-done((bf16[48,2048]{1,0:T(8,128)(2,1)S(1)}, bf16[48,2048]{1,0:T(8,128)(2,1)S(1)}, u32[]{:S(2)}, u32[]{:S(2)}) %collective-permute-start.15) | collective-permute-done | bytes 196640 | tf_op jit(solution)/shard_map/ppermute | solution.py:27
  120.1 2.1 %collective-permute-start.16 = (bf16[48,2048]{1,0:T(8,128)(2,1)S(1)}, bf16[48,2048]{1,0:T(8,128)(2,1)S(1)}, u32[]{:S(2)}, u32[]{:S(2)}) collective-permute-start(bf16[48,2048]{1,0:T(8,128)(2,1)S(1)} %fusion.15), channel_id=1, source_target_pairs={{0,448},{16,80},{32,480},{48,112},{64,0},{80,144},{96,32},{112,176... | collective-permute-start | bytes 589832 | tf_op jit(solution)/shard_map/ppermute | solution.py:27
  122.2 0.9 fusion.95
  123.6 0.9 fusion.94
  124.7 0.9 fusion.93
  126.0 7.9 %collective-permute-start.13 = (bf16[3,176,2048]{2,1,0:T(8,128)(2,1)S(1)}, bf16[3,176,2048]{2,1,0:T(8,128)(2,1)S(1)}, u32[]{:S(2)}, u32[]{:S(2)}) collective-permute-start(bf16[3,176,2048]{2,1,0:T(8,128)(2,1)S(1)} %pad_maximum_fusion.1), channel_id=1, source_target_pairs={{0,16},{16,0},{32,48},{48,32},{64,80},{80,64},{96,112},{112,96},{1... | collective-permute-start | bytes 6488072 | tf_op jit(solution)/shard_map/ppermute | solution.py:27
  134.0 1.9 %collective-permute-start.20 = (bf16[48,2048]{1,0:T(8,128)(2,1)S(1)}, bf16[48,2048]{1,0:T(8,128)(2,1)S(1)}, u32[]{:S(2)}, u32[]{:S(2)}) collective-permute-start(bf16[48,2048]{1,0:T(8,128)(2,1)S(1)} %fusion.11), channel_id=1, source_target_pairs={{0,448},{16,80},{32,480},{48,112},{64,0},{80,144},{96,32},{112,176... | collective-permute-start | bytes 589832 | tf_op jit(solution)/shard_map/ppermute | solution.py:27
  136.0 3.5 %collective-permute-start.17 = (bf16[24,2048]{1,0:T(8,128)(2,1)S(1)}, bf16[24,2048]{1,0:T(8,128)(2,1)S(1)}, u32[]{:S(2)}, u32[]{:S(2)}) collective-permute-start(bf16[24,2048]{1,0:T(8,128)(2,1)S(1)} %get-tuple-element.53), channel_id=1, source_target_pairs={{0,464},{16,64},{32,496},{48,96},{64,16},{80,128},{96,48},{112,160... | collective-permute-start | bytes 294920 | tf_op jit(solution)/shard_map/ppermute | solution.py:27
  139.6 4.2 %collective-permute-start.18 = (bf16[24,2048]{1,0:T(8,128)(2,1)S(1)}, bf16[24,2048]{1,0:T(8,128)(2,1)S(1)}, u32[]{:S(2)}, u32[]{:S(2)}) collective-permute-start(bf16[24,2048]{1,0:T(8,128)(2,1)S(1)} %get-tuple-element.54), channel_id=1, source_target_pairs={{0,496},{16,96},{32,464},{48,64},{64,48},{80,160},{96,16},{112,128... | collective-permute-start | bytes 294920 | tf_op jit(solution)/shard_map/ppermute | solution.py:27
  143.9 3.5 %collective-permute-start.21 = (bf16[48,2048]{1,0:T(8,128)(2,1)S(1)}, bf16[48,2048]{1,0:T(8,128)(2,1)S(1)}, u32[]{:S(2)}, u32[]{:S(2)}) collective-permute-start(bf16[48,2048]{1,0:T(8,128)(2,1)S(1)} %fusion.13), channel_id=1, source_target_pairs={{0,448},{16,80},{32,480},{48,112},{64,0},{80,144},{96,32},{112,176... | collective-permute-start | bytes 589832 | tf_op jit(solution)/shard_map/ppermute | solution.py:27
  148.0 4.7 %collective-permute-done.21 = bf16[48,2048]{1,0:T(8,128)(2,1)S(1)} collective-permute-done((bf16[48,2048]{1,0:T(8,128)(2,1)S(1)}, bf16[48,2048]{1,0:T(8,128)(2,1)S(1)}, u32[]{:S(2)}, u32[]{:S(2)}) %collective-permute-start.21) | collective-permute-done | bytes 196640 | tf_op jit(solution)/shard_map/ppermute | solution.py:27
  152.8 0.7 fusion.91
  153.5 1.9 %collective-permute-start.22 = (bf16[24,2048]{1,0:T(8,128)(2,1)}, bf16[24,2048]{1,0:T(8,128)(2,1)}, u32[]{:S(2)}, u32[]{:S(2)}) collective-permute-start(bf16[24,2048]{1,0:T(8,128)(2,1)} %get-tuple-element.51), channel_id=1, source_target_pairs={{0,448},{16,80},{32,480},{48,112},{64,0},{80,144},{96,32},{112,176... | collective-permute-start | bytes 294920 | tf_op jit(solution)/shard_map/ppermute | solution.py:27
  155.4 1.9 %collective-permute-start.23 = (bf16[24,2048]{1,0:T(8,128)(2,1)}, bf16[24,2048]{1,0:T(8,128)(2,1)}, u32[]{:S(2)}, u32[]{:S(2)}) collective-permute-start(bf16[24,2048]{1,0:T(8,128)(2,1)} %get-tuple-element.52), channel_id=1, source_target_pairs={{0,480},{16,112},{32,448},{48,80},{64,32},{80,176},{96,0},{112,144... | collective-permute-start | bytes 294920 | tf_op jit(solution)/shard_map/ppermute | solution.py:27
  157.4 1.3 copy-done.6
  160.3 4.9 %collective-permute-done.23 = bf16[24,2048]{1,0:T(8,128)(2,1)} collective-permute-done((bf16[24,2048]{1,0:T(8,128)(2,1)}, bf16[24,2048]{1,0:T(8,128)(2,1)}, u32[]{:S(2)}, u32[]{:S(2)}) %collective-permute-start.23) | collective-permute-done | bytes 98336 | tf_op jit(solution)/shard_map/ppermute | solution.py:27
  165.2 1.7 bitcast_bitcast_fusion
  166.9 7.2 %all-to-all-start.1 = ((bf16[16,24,128]{2,1,0:T(8,128)(2,1)}), bf16[16,24,128]{2,1,0:T(8,128)(2,1)S(1)}, u32[]{:S(2)}, u32[]{:S(2)}) async-start(bf16[16,24,128]{2,1,0:T(8,128)(2,1)} %bitcast_bitcast_fusion), calls=%async_computation.1 | async-start | bytes 196608 | tf_op jit(solution)/shard_map/all_to_all | solution.py:140
  174.1 1.8 slice_bitcast_fusion
  176.1 1.0 fusion.7
  177.4 1.1 fusion.9
  178.6 1.1 fusion.8
  179.6 1.9 %all-to-all-done.1 = bf16[16,24,128]{2,1,0:T(8,128)(2,1)S(1)} async-done(((bf16[16,24,128]{2,1,0:T(8,128)(2,1)}), bf16[16,24,128]{2,1,0:T(8,128)(2,1)S(1)}, u32[]{:S(2)}, u32[]{:S(2)}) %all-to-all-start.1) | async-done | bytes 98336 | tf_op jit(solution)/shard_map/all_to_all | solution.py:140
  181.5 0.8 convolution_convert_fusion.2
  (120 shorter events, 14.6 us)
Async XLA Ops:
  0.6 11.7 %copy-start = (bf16[128,2048]{1,0:T(8,128)(2,1)S(1)}, bf16[128,2048]{1,0:T(8,128)(2,1)}, u32[]{:S(2)}) copy-start(bf16[128,2048]{1,0:T(8,128)(2,1)} %param.8) | copy-start | bytes 1572868
  0.6 16.3 %copy-start.7 = (bf16[1,172,2048]{2,1,0:T(8,128)(2,1)S(1)}, bf16[1,172,2048]{2,1,0:T(8,128)(2,1)}, u32[]{:S(2)}) copy-start(bf16[1,172,2048]{2,1,0:T(8,128)(2,1)} %param.15) | copy-start | bytes 2113540
  3.5 43.2 %all-to-all-start = ((bf16[16,24,128]{2,1,0:T(8,128)(2,1)}), bf16[16,24,128]{2,1,0:T(8,128)(2,1)}, u32[]{:S(2)}, u32[]{:S(2)}) async-start(bf16[16,24,128]{2,1,0:T(8,128)(2,1)} %bitcast.1), calls=%async_computation | async-start | bytes 196608 | tf_op jit(solution)/shard_map/all_to_all | solution.py:82
  12.5 11.6 %copy-start.11 = (bf16[24,2048]{1,0:T(8,128)(2,1)}, bf16[24,2048]{1,0:T(8,128)(2,1)S(1)}, u32[]{:S(2)}) copy-start(bf16[24,2048]{1,0:T(8,128)(2,1)S(1)} %get-tuple-element.66) | copy-start | bytes 294916
  12.5 11.6 %collective-permute-start = (bf16[24,2048]{1,0:T(8,128)(2,1)S(1)}, bf16[24,2048]{1,0:T(8,128)(2,1)S(1)}, u32[]{:S(2)}, u32[]{:S(2)}) collective-permute-start(bf16[24,2048]{1,0:T(8,128)(2,1)S(1)} %get-tuple-element.66), channel_id=1, source_target_pairs={{0,32},{16,48},{32,0},{48,16},{64,96},{80,112},{96,64},{112,80},{1... | collective-permute-start | bytes 294920 | tf_op jit(solution)/shard_map/ppermute | solution.py:27
  21.0 52.4 %collective-permute-start.4 = (bf16[3,176,2048]{2,1,0:T(8,128)(2,1)}, bf16[3,176,2048]{2,1,0:T(8,128)(2,1)}, u32[]{:S(2)}, u32[]{:S(2)}) collective-permute-start(bf16[3,176,2048]{2,1,0:T(8,128)(2,1)} %pad_maximum_fusion), channel_id=1, source_target_pairs={{0,16},{16,0},{32,48},{48,32},{64,80},{80,64},{96,112},{112,96},{1... | collective-permute-start | bytes 6488072 | tf_op jit(solution)/shard_map/ppermute | solution.py:27
  24.2 17.5 %copy-start.9 = (bf16[24,2048]{1,0:T(8,128)(2,1)}, bf16[24,2048]{1,0:T(8,128)(2,1)S(1)}, u32[]{:S(2)}) copy-start(bf16[24,2048]{1,0:T(8,128)(2,1)S(1)} %collective-permute-done) | copy-start | bytes 294916
  24.2 16.7 %collective-permute-start.3 = (bf16[48,2048]{1,0:T(8,128)(2,1)S(1)}, bf16[48,2048]{1,0:T(8,128)(2,1)S(1)}, u32[]{:S(2)}, u32[]{:S(2)}) collective-permute-start(bf16[48,2048]{1,0:T(8,128)(2,1)S(1)} %pad_maximum_fusion.5), channel_id=1, source_target_pairs={{0,464},{16,64},{32,496},{48,96},{64,16},{80,128},{96,48},{112,160... | collective-permute-start | bytes 589832 | tf_op jit(solution)/shard_map/ppermute | solution.py:27
  28.1 12.0 %collective-permute-start.2 = (bf16[48,2048]{1,0:T(8,128)(2,1)S(1)}, bf16[48,2048]{1,0:T(8,128)(2,1)S(1)}, u32[]{:S(2)}, u32[]{:S(2)}) collective-permute-start(bf16[48,2048]{1,0:T(8,128)(2,1)S(1)} %pad_maximum_fusion.5), channel_id=1, source_target_pairs={{0,64},{16,464},{32,96},{48,496},{64,128},{80,16},{96,160},{112,48... | collective-permute-start | bytes 589832 | tf_op jit(solution)/shard_map/ppermute | solution.py:27
  40.2 1.5 copy-start.16
  40.9 0.7 copy-start.15
  41.6 10.0 %collective-permute-start.7 = (bf16[96,2048]{1,0:T(8,128)(2,1)}, bf16[96,2048]{1,0:T(8,128)(2,1)}, u32[]{:S(2)}, u32[]{:S(2)}) collective-permute-start(bf16[96,2048]{1,0:T(8,128)(2,1)} %get-tuple-element.56), channel_id=1, source_target_pairs={{0,64},{16,464},{32,96},{48,496},{64,128},{80,16},{96,160},{112,48... | collective-permute-start | bytes 1179656 | tf_op jit(solution)/shard_map/ppermute | solution.py:27
  47.6 9.1 %collective-permute-start.1 = (bf16[24,2048]{1,0:T(8,128)(2,1)S(1)}, bf16[24,2048]{1,0:T(8,128)(2,1)S(1)}, u32[]{:S(2)}, u32[]{:S(2)}) collective-permute-start(bf16[24,2048]{1,0:T(8,128)(2,1)S(1)} %bitcast_add_fusion), channel_id=1, source_target_pairs={{0,32},{16,48},{32,0},{48,16},{64,96},{80,112},{96,64},{112,80},{1... | collective-permute-start | bytes 294920 | tf_op jit(solution)/shard_map/ppermute | solution.py:27
  51.7 15.2 %collective-permute-start.9 = (bf16[96,2048]{1,0:T(8,128)(2,1)}, bf16[96,2048]{1,0:T(8,128)(2,1)S(1)}, u32[]{:S(2)}, u32[]{:S(2)}) collective-permute-start(bf16[96,2048]{1,0:T(8,128)(2,1)} %collective-permute-done.7), channel_id=1, source_target_pairs={{0,64},{16,464},{32,96},{48,496},{64,128},{80,16},{96,160},{112,48... | collective-permute-start | bytes 1179656 | tf_op jit(solution)/shard_map/ppermute | solution.py:27
  56.8 17.5 %collective-permute-start.6 = (bf16[48,2048]{1,0:T(8,128)(2,1)S(1)}, bf16[48,2048]{1,0:T(8,128)(2,1)S(1)}, u32[]{:S(2)}, u32[]{:S(2)}) collective-permute-start(bf16[48,2048]{1,0:T(8,128)(2,1)S(1)} %get-tuple-element.19), channel_id=1, source_target_pairs={{0,464},{16,64},{32,496},{48,96},{64,16},{80,128},{96,48},{112,160... | collective-permute-start | bytes 589832 | tf_op jit(solution)/shard_map/ppermute | solution.py:27
  59.1 15.2 %collective-permute-start.5 = (bf16[48,2048]{1,0:T(8,128)(2,1)S(1)}, bf16[48,2048]{1,0:T(8,128)(2,1)S(1)}, u32[]{:S(2)}, u32[]{:S(2)}) collective-permute-start(bf16[48,2048]{1,0:T(8,128)(2,1)S(1)} %get-tuple-element.19), channel_id=1, source_target_pairs={{0,64},{16,464},{32,96},{48,496},{64,128},{80,16},{96,160},{112,48... | collective-permute-start | bytes 589832 | tf_op jit(solution)/shard_map/ppermute | solution.py:27
  67.0 6.4 %collective-permute-start.11 = (bf16[48,2048]{1,0:T(8,128)(2,1)S(1)}, bf16[48,2048]{1,0:T(8,128)(2,1)S(1)}, u32[]{:S(2)}, u32[]{:S(2)}) collective-permute-start(bf16[48,2048]{1,0:T(8,128)(2,1)S(1)} %slice.173), channel_id=1, source_target_pairs={{0,64},{16,464},{32,96},{48,496},{64,128},{80,16},{96,160},{112,48... | collective-permute-start | bytes 589832 | tf_op jit(solution)/shard_map/ppermute | solution.py:27
  73.4 7.7 %copy-start.4 = (bf16[384,2048]{1,0:T(8,128)(2,1)}, bf16[384,2048]{1,0:T(8,128)(2,1)S(1)}, u32[]{:S(2)}) copy-start(bf16[384,2048]{1,0:T(8,128)(2,1)S(1)} %constant_dynamic-update-slice_fusion.7) | copy-start | bytes 4718596
  74.4 6.7 %copy-start.8 = (bf16[176,2048]{1,0:T(8,128)(2,1)S(1)}, bf16[176,2048]{1,0:T(8,128)(2,1)}, u32[]{:S(2)}) copy-start(bf16[176,2048]{1,0:T(8,128)(2,1)} %get-tuple-element.36) | copy-start | bytes 2162692
  74.4 21.9 %collective-permute-start.8 = (bf16[96,2048]{1,0:T(8,128)(2,1)S(1)}, bf16[96,2048]{1,0:T(8,128)(2,1)S(1)}, u32[]{:S(2)}, u32[]{:S(2)}) collective-permute-start(bf16[96,2048]{1,0:T(8,128)(2,1)S(1)} %get-tuple-element.17), channel_id=1, source_target_pairs={{0,64},{16,464},{32,96},{48,496},{64,128},{80,16},{96,160},{112,48... | collective-permute-start | bytes 1179656 | tf_op jit(solution)/shard_map/ppermute | solution.py:27
  82.7 1.6 copy-start.10
  82.7 1.6 copy-start.12
  86.9 3.7 %copy-start.13 = (f32[48,2048]{1,0:T(8,128)}, f32[48,2048]{1,0:T(8,128)S(1)}, u32[]{:S(2)}) copy-start(f32[48,2048]{1,0:T(8,128)S(1)} %convolution_add_fusion.4) | copy-start | bytes 1179652
  87.6 72.4 %collective-permute-start.14 = (bf16[24,2048]{1,0:T(8,128)(2,1)}, bf16[24,2048]{1,0:T(8,128)(2,1)}, u32[]{:S(2)}, u32[]{:S(2)}) collective-permute-start(bf16[24,2048]{1,0:T(8,128)(2,1)} %slice.309), channel_id=1, source_target_pairs={{0,32},{16,48},{32,0},{48,16},{64,96},{80,112},{96,64},{112,80},{1... | collective-permute-start | bytes 294920 | tf_op jit(solution)/shard_map/ppermute | solution.py:27
  96.5 8.5 %collective-permute-start.10 = (bf16[96,2048]{1,0:T(8,128)(2,1)S(1)}, bf16[96,2048]{1,0:T(8,128)(2,1)S(1)}, u32[]{:S(2)}, u32[]{:S(2)}) collective-permute-start(bf16[96,2048]{1,0:T(8,128)(2,1)S(1)} %get-tuple-element.15), channel_id=1, source_target_pairs={{0,64},{16,464},{32,96},{48,496},{64,128},{80,16},{96,160},{112,48... | collective-permute-start | bytes 1179656 | tf_op jit(solution)/shard_map/ppermute | solution.py:27
  105.0 7.5 %collective-permute-start.12 = (bf16[48,2048]{1,0:T(8,128)(2,1)S(1)}, bf16[48,2048]{1,0:T(8,128)(2,1)S(1)}, u32[]{:S(2)}, u32[]{:S(2)}) collective-permute-start(bf16[48,2048]{1,0:T(8,128)(2,1)S(1)} %slice_add_fusion.9), channel_id=1, source_target_pairs={{0,64},{16,464},{32,96},{48,496},{64,128},{80,16},{96,160},{112,48... | collective-permute-start | bytes 589832 | tf_op jit(solution)/shard_map/ppermute | solution.py:27
  110.3 9.8 %collective-permute-start.15 = (bf16[48,2048]{1,0:T(8,128)(2,1)S(1)}, bf16[48,2048]{1,0:T(8,128)(2,1)S(1)}, u32[]{:S(2)}, u32[]{:S(2)}) collective-permute-start(bf16[48,2048]{1,0:T(8,128)(2,1)S(1)} %slice.308), channel_id=1, source_target_pairs={{0,448},{16,80},{32,480},{48,112},{64,0},{80,144},{96,32},{112,176... | collective-permute-start | bytes 589832 | tf_op jit(solution)/shard_map/ppermute | solution.py:27
  113.8 20.1 %collective-permute-start.19 = (bf16[48,2048]{1,0:T(8,128)(2,1)S(1)}, bf16[48,2048]{1,0:T(8,128)(2,1)S(1)}, u32[]{:S(2)}, u32[]{:S(2)}) collective-permute-start(bf16[48,2048]{1,0:T(8,128)(2,1)S(1)} %fusion), channel_id=1, source_target_pairs={{0,448},{16,80},{32,480},{48,112},{64,0},{80,144},{96,32},{112,176... | collective-permute-start | bytes 589832 | tf_op jit(solution)/shard_map/ppermute | solution.py:27
  120.1 15.9 %collective-permute-start.16 = (bf16[48,2048]{1,0:T(8,128)(2,1)S(1)}, bf16[48,2048]{1,0:T(8,128)(2,1)S(1)}, u32[]{:S(2)}, u32[]{:S(2)}) collective-permute-start(bf16[48,2048]{1,0:T(8,128)(2,1)S(1)} %fusion.15), channel_id=1, source_target_pairs={{0,448},{16,80},{32,480},{48,112},{64,0},{80,144},{96,32},{112,176... | collective-permute-start | bytes 589832 | tf_op jit(solution)/shard_map/ppermute | solution.py:27
  122.2 1.4 copy-start.5
  123.2 34.2 %copy-start.1 = (f32[352,2048]{1,0:T(8,128)}, f32[352,2048]{1,0:T(8,128)S(1)}, u32[]{:S(2)}) copy-start(f32[352,2048]{1,0:T(8,128)S(1)} %fusion.95) | copy-start | bytes 8650756
  124.6 32.8 %copy-start.2 = (f32[352,2048]{1,0:T(8,128)}, f32[352,2048]{1,0:T(8,128)S(1)}, u32[]{:S(2)}) copy-start(f32[352,2048]{1,0:T(8,128)S(1)} %fusion.94) | copy-start | bytes 8650756
  125.6 31.7 %copy-start.3 = (f32[352,2048]{1,0:T(8,128)}, f32[352,2048]{1,0:T(8,128)S(1)}, u32[]{:S(2)}) copy-start(f32[352,2048]{1,0:T(8,128)S(1)} %fusion.93) | copy-start | bytes 8650756
  126.0 31.4 %collective-permute-start.13 = (bf16[3,176,2048]{2,1,0:T(8,128)(2,1)S(1)}, bf16[3,176,2048]{2,1,0:T(8,128)(2,1)S(1)}, u32[]{:S(2)}, u32[]{:S(2)}) collective-permute-start(bf16[3,176,2048]{2,1,0:T(8,128)(2,1)S(1)} %pad_maximum_fusion.1), channel_id=1, source_target_pairs={{0,16},{16,0},{32,48},{48,32},{64,80},{80,64},{96,112},{112,96},{1... | collective-permute-start | bytes 6488072 | tf_op jit(solution)/shard_map/ppermute | solution.py:27
  134.0 9.8 %collective-permute-start.20 = (bf16[48,2048]{1,0:T(8,128)(2,1)S(1)}, bf16[48,2048]{1,0:T(8,128)(2,1)S(1)}, u32[]{:S(2)}, u32[]{:S(2)}) collective-permute-start(bf16[48,2048]{1,0:T(8,128)(2,1)S(1)} %fusion.11), channel_id=1, source_target_pairs={{0,448},{16,80},{32,480},{48,112},{64,0},{80,144},{96,32},{112,176... | collective-permute-start | bytes 589832 | tf_op jit(solution)/shard_map/ppermute | solution.py:27
  136.0 11.3 %collective-permute-start.17 = (bf16[24,2048]{1,0:T(8,128)(2,1)S(1)}, bf16[24,2048]{1,0:T(8,128)(2,1)S(1)}, u32[]{:S(2)}, u32[]{:S(2)}) collective-permute-start(bf16[24,2048]{1,0:T(8,128)(2,1)S(1)} %get-tuple-element.53), channel_id=1, source_target_pairs={{0,464},{16,64},{32,496},{48,96},{64,16},{80,128},{96,48},{112,160... | collective-permute-start | bytes 294920 | tf_op jit(solution)/shard_map/ppermute | solution.py:27
  139.6 8.3 %collective-permute-start.18 = (bf16[24,2048]{1,0:T(8,128)(2,1)S(1)}, bf16[24,2048]{1,0:T(8,128)(2,1)S(1)}, u32[]{:S(2)}, u32[]{:S(2)}) collective-permute-start(bf16[24,2048]{1,0:T(8,128)(2,1)S(1)} %get-tuple-element.54), channel_id=1, source_target_pairs={{0,496},{16,96},{32,464},{48,64},{64,48},{80,160},{96,16},{112,128... | collective-permute-start | bytes 294920 | tf_op jit(solution)/shard_map/ppermute | solution.py:27
  143.9 8.8 %collective-permute-start.21 = (bf16[48,2048]{1,0:T(8,128)(2,1)S(1)}, bf16[48,2048]{1,0:T(8,128)(2,1)S(1)}, u32[]{:S(2)}, u32[]{:S(2)}) collective-permute-start(bf16[48,2048]{1,0:T(8,128)(2,1)S(1)} %fusion.13), channel_id=1, source_target_pairs={{0,448},{16,80},{32,480},{48,112},{64,0},{80,144},{96,32},{112,176... | collective-permute-start | bytes 589832 | tf_op jit(solution)/shard_map/ppermute | solution.py:27
  147.9 9.4 %copy-start.17 = (bf16[24,2048]{1,0:T(8,128)(2,1)}, bf16[24,2048]{1,0:T(8,128)(2,1)S(1)}, u32[]{:S(2)}) copy-start(bf16[24,2048]{1,0:T(8,128)(2,1)S(1)} %collective-permute-done.18) | copy-start | bytes 294916
  153.5 6.9 %collective-permute-start.22 = (bf16[24,2048]{1,0:T(8,128)(2,1)}, bf16[24,2048]{1,0:T(8,128)(2,1)}, u32[]{:S(2)}, u32[]{:S(2)}) collective-permute-start(bf16[24,2048]{1,0:T(8,128)(2,1)} %get-tuple-element.51), channel_id=1, source_target_pairs={{0,448},{16,80},{32,480},{48,112},{64,0},{80,144},{96,32},{112,176... | collective-permute-start | bytes 294920 | tf_op jit(solution)/shard_map/ppermute | solution.py:27
  155.4 9.8 %collective-permute-start.23 = (bf16[24,2048]{1,0:T(8,128)(2,1)}, bf16[24,2048]{1,0:T(8,128)(2,1)}, u32[]{:S(2)}, u32[]{:S(2)}) collective-permute-start(bf16[24,2048]{1,0:T(8,128)(2,1)} %get-tuple-element.52), channel_id=1, source_target_pairs={{0,480},{16,112},{32,448},{48,80},{64,32},{80,176},{96,0},{112,144... | collective-permute-start | bytes 294920 | tf_op jit(solution)/shard_map/ppermute | solution.py:27
  157.4 7.8 %copy-start.14 = (f32[48,2048]{1,0:T(8,128)S(1)}, f32[48,2048]{1,0:T(8,128)}, u32[]{:S(2)}) copy-start(f32[48,2048]{1,0:T(8,128)} %copy-done.13) | copy-start | bytes 1179652
  157.4 7.8 %copy-start.18 = (bf16[24,2048]{1,0:T(8,128)(2,1)S(1)}, bf16[24,2048]{1,0:T(8,128)(2,1)}, u32[]{:S(2)}) copy-start(bf16[24,2048]{1,0:T(8,128)(2,1)} %copy-done.17) | copy-start | bytes 294916
  157.4 1.3 copy-start.6
  166.9 14.6 %all-to-all-start.1 = ((bf16[16,24,128]{2,1,0:T(8,128)(2,1)}), bf16[16,24,128]{2,1,0:T(8,128)(2,1)S(1)}, u32[]{:S(2)}, u32[]{:S(2)}) async-start(bf16[16,24,128]{2,1,0:T(8,128)(2,1)} %bitcast_bitcast_fusion), calls=%async_computation.1 | async-start | bytes 196608 | tf_op jit(solution)/shard_map/all_to_all | solution.py:140
  174.1 2.0 %slice-start.2 = ((f32[352,2048]{1,0:T(8,128)}), f32[176,2048]{1,0:T(8,128)S(1)}, s32[]{:S(2)}) async-start(f32[352,2048]{1,0:T(8,128)} %copy-done.3), calls=%async_computation.4 | async-start | bytes 2883584 | tf_op jit(solution)/shard_map/slice | solution.py:148
  175.9 1.5 slice-start
  177.1 1.4 slice-start.1

commit v4 on v1

v4 whole, which is shorter than its diff:
```python
import jax
import jax.numpy as jnp
from jax import lax
from jax.sharding import Mesh
from jax.sharding import PartitionSpec as P

BF = jnp.bfloat16
F32 = jnp.float32
Z, XH, CORE, XL, Y = 8, 2, 2, 2, 8
AXES = ("z", "xh", "core", "xl", "y")
EXPERT = ("xl", "y")
PAD = 176
SWAP = [(0, 1), (1, 0)]


def dot(a, b, dims=((1,), (0,))):
    return lax.dot_general(a, b, (dims, ((), ())), preferred_element_type=F32)


def local(tokens, out_grad, modality, within_route, gate_values, w_gate, w_up, w_down):
    tok_count, width = tokens.shape
    experts_all = XL * Y // 2
    per_modality = experts_all // 2
    capacity = tok_count * 3 // (2 * experts_all)
    hidden_own = w_gate.shape[1]
    position = lax.axis_index(EXPERT)
    own_expert = position // 2
    expert_id = per_modality * modality + within_route
    one_hot = (expert_id[:, None] == jnp.arange(experts_all, dtype=jnp.int32)[None, :]).astype(
        jnp.int32
    )
    before = jnp.cumsum(one_hot, axis=0) - one_hot
    slot_rank = jnp.sum(before * one_hot, axis=1)
    kept = slot_rank < capacity
    slot = jnp.where(kept, expert_id * capacity + slot_rank, -1)
    slots = jnp.arange(experts_all * capacity, dtype=jnp.int32)
    select = (slot[None, :] == slots[:, None]).astype(BF)
    own_slots = own_expert * capacity + jnp.arange(capacity, dtype=jnp.int32)
    select_own = (slot[None, :] == own_slots[:, None]).astype(BF)

    pad = ((0, PAD - hidden_own), (0, 0))
    own_w = jnp.stack([jnp.pad(w_gate[0], pad), jnp.pad(w_up[0], pad), jnp.pad(w_down[0], pad)])
    other_w = lax.ppermute(own_w, "core", SWAP)
    wg = jnp.concatenate([own_w[0], other_w[0]], axis=0)
    wu = jnp.concatenate([own_w[1], other_w[1]], axis=0)
    wd = jnp.concatenate([own_w[2], other_w[2]], axis=0)

    x_own = dot(select_own, tokens).astype(BF)
    x_across = lax.ppermute(x_own, "xh", SWAP)
    scaled = (gate_values[:, None] * out_grad.astype(F32)).astype(BF)
    dy_slices = dot(select, scaled).astype(BF).reshape(1, experts_all, 1, capacity, -1)
    dy_slices = jnp.broadcast_to(dy_slices, (XH, experts_all, 2) + dy_slices.shape[3:])
    dy_slices = dy_slices.reshape((XH * XL * Y,) + dy_slices.shape[3:])
    dy_slices = lax.all_to_all(dy_slices, ("xh",) + EXPERT, 0, 0, tiled=True)
    dy_slices = dy_slices.reshape((XH, XL * Y) + dy_slices.shape[1:])
    dy_near = jnp.transpose(dy_slices, (0, 2, 1, 3)).reshape(2 * capacity, width)
    side = lax.axis_index("xh")
    x_near = jnp.concatenate(
        [jnp.where(side == 0, x_own, x_across), jnp.where(side == 0, x_across, x_own)], axis=0
    )
    packet = jnp.concatenate([x_near, dy_near], axis=1)

    packets = lax.all_gather(packet, "z", axis=0, tiled=True)
    x_rows, dy_rows = packets[:, :width], packets[:, width:]
    cols = ((1,), (1,))
    gate_pre = dot(x_rows, wg, cols)
    up_pre = dot(x_rows, wu, cols)
    sig_gate = jax.nn.sigmoid(gate_pre)
    silu_gate = gate_pre * sig_gate
    hidden = (silu_gate * up_pre).astype(BF)
    d_hidden = dot(dy_rows, wd, cols)
    d_gate = (d_hidden * up_pre * sig_gate * (1.0 + gate_pre * (1.0 - sig_gate))).astype(BF)
    d_up = (d_hidden * silu_gate).astype(BF)
    terms = (dot(d_gate, wg) + dot(d_up, wu)).reshape(Z, 2, capacity, width)

    other_terms = lax.dynamic_index_in_dim(terms, 1 - side, axis=1, keepdims=False)
    own_terms = lax.dynamic_index_in_dim(terms, side, axis=1, keepdims=False)
    came = lax.ppermute(other_terms.astype(BF), "xh", SWAP)
    terms = (own_terms + came.astype(F32)).astype(BF)
    terms = lax.all_to_all(terms, "z", 0, 0, tiled=True)
    summed = jnp.sum(terms.astype(F32), axis=0).reshape(capacity, XL * Y, -1)
    summed = jnp.transpose(summed, (1, 0, 2)).astype(BF)
    summed = lax.all_to_all(summed, EXPERT, 0, 0, tiled=True)

    from_slots = jnp.arange(2 * experts_all * capacity, dtype=jnp.int32)
    from_slots = from_slots // (2 * capacity) * capacity + from_slots % capacity
    place = (slot[:, None] == from_slots[None, :]).astype(BF)
    grad_tokens = dot(place, summed.reshape(2 * experts_all * capacity, -1)).astype(BF)

    rows = ((0,), (0,))
    grads = [dot(d_gate, x_rows, rows), dot(d_up, x_rows, rows), dot(hidden, dy_rows, rows)]
    received = lax.ppermute(jnp.stack([grad[PAD:].astype(BF) for grad in grads]), "core", SWAP)
    outs = [
        (grad[:PAD] + extra.astype(F32))[:hidden_own].astype(BF)[None]
        for grad, extra in zip(grads, received)
    ]
    return (*outs, grad_tokens)


def solution(mesh):
    fine = Mesh(mesh.devices.reshape(Z, XH, CORE, XL, Y), AXES)
    dp = ("z", "xh", "core")
    placed = (
        P(dp, None),
        P(dp, EXPERT),
        P(dp),
        P(dp),
        P(dp),
        P(EXPERT, dp, None),
        P(EXPERT, dp, None),
        P(EXPERT, dp, None),
    )
    return jax.shard_map(
        local,
        mesh=fine,
        in_specs=placed,
        out_specs=(
            P(EXPERT, dp, None),
            P(EXPERT, dp, None),
            P(EXPERT, dp, None),
            P(dp, EXPERT),
        ),
        check_vma=False,
    )
```

time: 208 us -> 170 us (0.82)
  starting transfers between devices: 118 us -> 37.2 us
  waiting for transfers between devices: 54 us -> 80.7 us
  between operations: 1.45 us -> 14.4 us
  matrix products: 17.6 us -> 11.3 us
  local copies, waits for them, and re-layouts: 7.67 us -> 13 us
  other arithmetic: 7.2 us -> 12.4 us
    ppermute x23 -> x3, starting transfers between devices: 100 us -> 12.9 us  [the longest x1 5.48 us: local(): x_across = lax.ppermute(x_own, 'xh', SWAP)]
    ppermute x23 -> x3, waiting for transfers between devices: 47 us -> 7.86 us  [the longest x1 7.85 us: local(): came = lax.ppermute(other_terms.astype(BF), 'xh', SWAP)]
    all_gather x0 -> x1, waiting for transfers between devices: none -> 33.9 us  [local(): packets = lax.all_gather(packet, 'z', axis=0, tiled=True)]
    all_to_all x1 -> x2, waiting for transfers between devices: 0.62 us -> 32.8 us  [the longest x1 23.5 us: local(): terms = lax.all_to_all(terms, 'z', 0, 0, tiled=True)]
    dot_general x31 -> x11, matrix products: 17.6 us -> 11.3 us  [dot(): return lax.dot_general(a, b, (dims, ((), ())), preferred_element_type=F32)]
    all_to_all x1, waiting for transfers between devices: 6.36 us -> 1.89 us  [local(): summed = lax.all_to_all(summed, EXPERT, 0, 0, tiled=True)]
    ppermute x1, waiting for transfers between devices: 0.01 us -> 4.2 us  [local(): other_w = lax.ppermute(own_w, 'core', SWAP)]
    all_to_all x1 -> x2, starting transfers between devices: 8.68 us -> 12 us  [the longest x1 7.79 us: local(): dy_slices = lax.all_to_all(dy_slices, ('xh',) + EXPERT, 0, 0, tiled=True)]
  transfers between devices with their start and end apart: 26 -> 8, of which waited for: 13 -> 6; matrix products, arithmetic and copies ran while one was open for 10% -> 13% of each run, Pallas kernels for 0% -> 0%
where the time goes in v4:
time: 170 us; the launch traced here: 169 us
  waiting for transfers between devices  80.7 us (47%)
  starting transfers between devices  37.2 us (22%)
  between operations  14.4 us (8%)
  local copies, waits for them, and re-layouts  13 us (8%)
  other arithmetic  12.4 us (7%)
  matrix products  11.3 us (7%)
    all_gather x1, waiting for transfers between devices, local(): packets = lax.all_gather(packet, 'z', axis=0, tiled=True)  33.9 us
    all_to_all x1, waiting for transfers between devices, local(): terms = lax.all_to_all(terms, 'z', 0, 0, tiled=True)  23.5 us
    dot_general x11, matrix products, dot(): return lax.dot_general(a, b, (dims, ((), ())), preferred_element_type=F32)  11.3 us
    all_to_all x1, waiting for transfers between devices, local(): dy_slices = lax.all_to_all(dy_slices, ('xh',) + EXPERT, 0, 0, tiled=True)  9.3 us
    ppermute x1, waiting for transfers between devices, local(): came = lax.ppermute(other_terms.astype(BF), 'xh', SWAP)  7.85 us
    all_to_all x1, starting transfers between devices, local(): dy_slices = lax.all_to_all(dy_slices, ('xh',) + EXPERT, 0, 0, tiled=True)  7.79 us
    all_to_all x1, starting transfers between devices, local(): summed = lax.all_to_all(summed, EXPERT, 0, 0, tiled=True)  7.47 us
    ppermute x1, starting transfers between devices, local(): x_across = lax.ppermute(x_own, 'xh', SWAP)  5.48 us
  transfers between devices with their start and end apart: 8, of which 6 were waited for; matrix products, arithmetic and copies ran while one was open for 13% of the time, Pallas kernels for 0%

profile of v4, /device:TPU:1, one launch (start us, length us, event | category | flops | bytes accessed | tf_op | source)
XLA Modules:
  0.0 168.9 jit_solution(12896829392447294650)
XLA Ops:
  7.2 0.0 copy-start
  7.2 0.8 multiply_add_fusion
  8.0 0.1 fusion.32
  8.1 0.2 reduce_window_sum.11
  8.2 0.2 select_reduce_fusion
  8.4 0.2 convolution_convert_fusion
  8.7 5.5 %collective-permute-start = (bf16[24,2048]{1,0:T(8,128)(2,1)S(1)}, bf16[24,2048]{1,0:T(8,128)(2,1)S(1)}, u32[]{:S(2)}, u32[]{:S(2)}) collective-permute-start(bf16[24,2048]{1,0:T(8,128)(2,1)S(1)} %convolution_convert_fusion), channel_id=1, source_target_pairs={{0,32},{32,0},{1,33},{33,1},{2,34},{34,2},{3,35},{35,3},{4,36},{36... | collective-permute-start | bytes 294920 | tf_op jit(solution)/shard_map/ppermute | solution.py:49
  14.2 1.0 convolution_convert_fusion.1
  15.2 0.7 broadcast_in_dim.16
  15.9 7.8 %all-to-all-start = ((bf16[32,24,128]{2,1,0:T(8,128)(2,1)}), bf16[32,24,128]{2,1,0:T(8,128)(2,1)S(1)}, u32[]{:S(2)}, u32[]{:S(2)}) async-start(bf16[32,24,128]{2,1,0:T(8,128)(2,1)} %bitcast.1), calls=%async_computation | async-start | bytes 393216 | tf_op jit(solution)/shard_map/all_to_all | solution.py:54
  23.7 0.0 all-gather.2.cloned.1.call-start
  23.7 0.0 collective-permute-done
  23.7 9.3 %all-to-all-done = bf16[32,24,128]{2,1,0:T(8,128)(2,1)S(1)} async-done(((bf16[32,24,128]{2,1,0:T(8,128)(2,1)}), bf16[32,24,128]{2,1,0:T(8,128)(2,1)S(1)}, u32[]{:S(2)}, u32[]{:S(2)}) %all-to-all-start) | async-done | bytes 196640 | tf_op jit(solution)/shard_map/all_to_all | solution.py:54
  33.1 0.1 copy.20
  33.1 0.8 pad_maximum_fusion.8
  33.9 0.0 all-gather.2.cloned.1.call-update
  33.9 0.0 copy-done.6
  33.9 0.2 fusion.56
  34.1 2.4 %fusion.54 = (bf16[176,2048]{1,0:T(8,128)(2,1)S(1)}, bf16[1,176,2048]{2,1,0:T(8,128)(2,1)S(1)}, bf16[1,176,2048]{2,1,0:T(8,128)(2,1)S(1)}, bf16[176,2048]{1,0:T(8,128)(2,1)}) fusion(bf16[172,2048]{1,0:T(8,128)(2,1)} %bitcast.70, bf16[172,2048]{1,0:T(8,128)(2,1)} %bitcast.71), kind=kLoop, calls=%fused_computation.98 | loop fusion | bytes 4292608 | tf_op jit(solution)/shard_map/jit(_pad)/pad | solution.py:42
  36.5 1.6 pad_maximum_fusion
  38.1 4.8 %collective-permute-start.1 = (bf16[3,176,2048]{2,1,0:T(8,128)(2,1)}, bf16[3,176,2048]{2,1,0:T(8,128)(2,1)}, u32[]{:S(2)}, u32[]{:S(2)}) collective-permute-start(bf16[3,176,2048]{2,1,0:T(8,128)(2,1)} %pad_maximum_fusion), channel_id=1, source_target_pairs={{0,16},{16,0},{1,17},{17,1},{2,18},{18,2},{3,19},{19,3},{4,20},{20... | collective-permute-start | bytes 6488072 | tf_op jit(solution)/shard_map/ppermute | solution.py:43
  42.9 4.2 %collective-permute-done.1 = bf16[3,176,2048]{2,1,0:T(8,128)(2,1)} collective-permute-done((bf16[3,176,2048]{2,1,0:T(8,128)(2,1)}, bf16[3,176,2048]{2,1,0:T(8,128)(2,1)}, u32[]{:S(2)}, u32[]{:S(2)}) %collective-permute-start.1) | collective-permute-done | bytes 2162720 | tf_op jit(solution)/shard_map/ppermute | solution.py:43
  47.1 2.6 %slice_bitcast_fusion.4 = (bf16[176,2048]{1,0:T(8,128)(2,1)S(1)}, bf16[176,2048]{1,0:T(8,128)(2,1)S(1)}, bf16[176,2048]{1,0:T(8,128)(2,1)}) fusion(bf16[3,176,2048]{2,1,0:T(8,128)(2,1)} %collective-permute-done.1), kind=kLoop, calls=%fused_computation.47 | loop fusion | bytes 4325376 | tf_op jit(solution)/shard_map/squeeze | solution.py:45
  49.7 33.9 %all-gather.2.cloned.1.call-done = bf16[384,4096]{1,0:T(8,128)(2,1)} async-done(((bf16[48,4096]{1,0:T(8,128)(2,1)}), bf16[384,4096]{1,0:T(8,128)(2,1)}) %all-gather.2.cloned.1.call-update) | async-done | bytes 3145744 | tf_op jit(solution)/shard_map/all_gather | solution.py:63
  83.6 2.5 %fusion.17 = f32[384,352]{0,1:T(8,128)S(1)} fusion(bf16[384,4096]{1,0:T(8,128)(2,1)} %all-gather.2.cloned.1.call-done, bf16[176,2048]{1,0:T(8,128)(2,1)S(1)} %get-tuple-element.7, bf16[176,2048]{1,0:T(8,128)(2,1)S(1)} %get-tuple-element.12), kind=kOutput, calls=%fused_computation.33 | convolution fusion | flops 556531712 | bytes 3555328 | tf_op jit(solution)/shard_map/dot_general | solution.py:17
  86.1 0.0 copy-start.7
  86.1 0.0 copy-start.8
  86.1 0.9 fusion.15
  87.0 0.2 copy-done.7
  87.2 0.2 copy-done.8
  87.4 1.0 multiply_convert_fusion.1
  88.5 1.0 fusion.19
  89.5 1.0 convolution_add_fusion
  90.5 1.2 fusion.20
  91.7 4.6 %collective-permute-start.3 = (bf16[8,24,2048]{2,1,0:T(8,128)(2,1)}, bf16[8,24,2048]{2,1,0:T(8,128)(2,1)}, u32[]{:S(2)}, u32[]{:S(2)}) collective-permute-start(bf16[8,24,2048]{2,1,0:T(8,128)(2,1)} %fusion.20), channel_id=1, source_target_pairs={{0,32},{32,0},{1,33},{33,1},{2,34},{34,2},{3,35},{35,3},{4,36},{36... | collective-permute-start | bytes 2359304 | tf_op jit(solution)/shard_map/ppermute | solution.py:78
  96.3 0.9 fusion.8
  97.2 0.1 fusion.23
  97.3 0.9 fusion.11
  98.3 0.1 fusion.22
  98.4 0.9 fusion.13
  99.3 0.6 copy-done.2
  99.8 1.5 copy-done.3
  101.4 0.1 fusion.21
  101.5 1.6 pad_maximum_fusion.1
  103.1 2.9 %collective-permute-start.2 = (bf16[3,176,2048]{2,1,0:T(8,128)(2,1)}, bf16[3,176,2048]{2,1,0:T(8,128)(2,1)}, u32[]{:S(2)}, u32[]{:S(2)}) collective-permute-start(bf16[3,176,2048]{2,1,0:T(8,128)(2,1)} %pad_maximum_fusion.1), channel_id=1, source_target_pairs={{0,16},{16,0},{1,17},{17,1},{2,18},{18,2},{3,19},{19,3},{4,20},{20... | collective-permute-start | bytes 6488072 | tf_op jit(solution)/shard_map/ppermute | solution.py:92
  106.0 7.9 %collective-permute-done.3 = bf16[8,24,2048]{2,1,0:T(8,128)(2,1)} collective-permute-done((bf16[8,24,2048]{2,1,0:T(8,128)(2,1)}, bf16[8,24,2048]{2,1,0:T(8,128)(2,1)}, u32[]{:S(2)}, u32[]{:S(2)}) %collective-permute-start.3) | collective-permute-done | bytes 786464 | tf_op jit(solution)/shard_map/ppermute | solution.py:78
  113.8 2.7 %fusion = bf16[8,24,2048]{2,1,0:T(8,128)(2,1)} fusion(bf16[8,24,2048]{2,1,0:T(8,128)(2,1)} %collective-permute-done.3, f32[8,2,24,2048]{3,2,1,0:T(8,128)} %bitcast.65, s32[]{:T(128)S(6)} %select_n.54), kind=kLoop, calls=%fused_computation.5 | loop fusion | flops 1179648 | bytes 3145732 | tf_op jit(solution)/shard_map/convert_element_type | solution.py:79
  116.6 4.2 %all-to-all-start.1 = ((bf16[8,24,2048]{2,1,0:T(8,128)(2,1)}), bf16[8,24,2048]{2,1,0:T(8,128)(2,1)}, u32[]{:S(2)}, u32[]{:S(2)}) async-start(bf16[8,24,2048]{2,1,0:T(8,128)(2,1)} %fusion), calls=%async_computation.1 | async-start | bytes 1572864 | tf_op jit(solution)/shard_map/all_to_all | solution.py:80
  120.8 23.5 %all-to-all-done.1 = bf16[8,24,2048]{2,1,0:T(8,128)(2,1)} async-done(((bf16[8,24,2048]{2,1,0:T(8,128)(2,1)}), bf16[8,24,2048]{2,1,0:T(8,128)(2,1)}, u32[]{:S(2)}, u32[]{:S(2)}) %all-to-all-start.1) | async-done | bytes 786464 | tf_op jit(solution)/shard_map/all_to_all | solution.py:80
  144.3 1.2 reduce_sum.22
  145.6 0.7 copy.16
  146.3 7.5 %all-to-all-start.2 = ((bf16[16,24,128]{2,1,0:T(8,128)(2,1)}), bf16[16,24,128]{2,1,0:T(8,128)(2,1)S(1)}, u32[]{:S(2)}, u32[]{:S(2)}) async-start(bf16[16,24,128]{2,1,0:T(8,128)(2,1)} %copy.16), calls=%async_computation.2 | async-start | bytes 196608 | tf_op jit(solution)/shard_map/all_to_all | solution.py:83
  153.8 0.0 slice-start.2
  153.8 0.0 collective-permute-done.2
  153.8 1.8 %slice_bitcast_fusion = (bf16[176,2048]{1,0:T(8,128)(2,1)S(1)}, bf16[176,2048]{1,0:T(8,128)(2,1)S(1)}, bf16[176,2048]{1,0:T(8,128)(2,1)S(1)}) fusion(bf16[3,176,2048]{2,1,0:T(8,128)(2,1)} %collective-permute-done.2), kind=kLoop, calls=%fused_computation.43 | loop fusion | bytes 4325376
  155.6 0.0 slice-start
  155.6 0.2 slice-done.2
  155.8 1.0 fusion.24
  156.8 0.3 slice-done
  157.1 1.1 fusion.26
  158.2 0.1 slice-done.1
  158.2 1.1 fusion.25
  159.3 1.9 %all-to-all-done.2 = bf16[16,24,128]{2,1,0:T(8,128)(2,1)S(1)} async-done(((bf16[16,24,128]{2,1,0:T(8,128)(2,1)}), bf16[16,24,128]{2,1,0:T(8,128)(2,1)S(1)}, u32[]{:S(2)}, u32[]{:S(2)}) %all-to-all-start.2) | async-done | bytes 98336 | tf_op jit(solution)/shard_map/all_to_all | solution.py:83
  161.2 0.8 convolution_convert_fusion.2
  (17 shorter events, 0.1 us)
Async XLA Ops:
  7.2 1.3 copy-start
  7.2 26.8 %copy-start.6 = (bf16[1,172,2048]{2,1,0:T(8,128)(2,1)S(1)}, bf16[1,172,2048]{2,1,0:T(8,128)(2,1)}, u32[]{:S(2)}) copy-start(bf16[1,172,2048]{2,1,0:T(8,128)(2,1)} %param.13) | copy-start | bytes 2113540
  8.7 15.0 %collective-permute-start = (bf16[24,2048]{1,0:T(8,128)(2,1)S(1)}, bf16[24,2048]{1,0:T(8,128)(2,1)S(1)}, u32[]{:S(2)}, u32[]{:S(2)}) collective-permute-start(bf16[24,2048]{1,0:T(8,128)(2,1)S(1)} %convolution_convert_fusion), channel_id=1, source_target_pairs={{0,32},{32,0},{1,33},{33,1},{2,34},{34,2},{3,35},{35,3},{4,36},{36... | collective-permute-start | bytes 294920 | tf_op jit(solution)/shard_map/ppermute | solution.py:49
  15.9 17.2 %all-to-all-start = ((bf16[32,24,128]{2,1,0:T(8,128)(2,1)}), bf16[32,24,128]{2,1,0:T(8,128)(2,1)S(1)}, u32[]{:S(2)}, u32[]{:S(2)}) async-start(bf16[32,24,128]{2,1,0:T(8,128)(2,1)} %bitcast.1), calls=%async_computation | async-start | bytes 393216 | tf_op jit(solution)/shard_map/all_to_all | solution.py:54
  23.7 59.9 %all-gather.2.cloned.1.call-start = ((), (), s32[]{:S(2)}) async-start(), calls=%async_computation.3 | async-start | bytes 3538944 | tf_op jit(solution)/shard_map/all_gather | solution.py:63
  38.1 9.0 %collective-permute-start.1 = (bf16[3,176,2048]{2,1,0:T(8,128)(2,1)}, bf16[3,176,2048]{2,1,0:T(8,128)(2,1)}, u32[]{:S(2)}, u32[]{:S(2)}) collective-permute-start(bf16[3,176,2048]{2,1,0:T(8,128)(2,1)} %pad_maximum_fusion), channel_id=1, source_target_pairs={{0,16},{16,0},{1,17},{17,1},{2,18},{18,2},{3,19},{19,3},{4,20},{20... | collective-permute-start | bytes 6488072 | tf_op jit(solution)/shard_map/ppermute | solution.py:43
  83.6 2.5 %copy-start.5 = (bf16[384,4096]{1,0:T(8,128)(2,1)S(1)}, bf16[384,4096]{1,0:T(8,128)(2,1)}, u32[]{:S(2)}) copy-start(bf16[384,4096]{1,0:T(8,128)(2,1)} %all-gather.2.cloned.1.call-done) | copy-start | bytes 9437188
  86.1 1.1 copy-start.7
  86.1 1.3 copy-start.8
  90.5 6.7 %copy-start.4 = (f32[384,2048]{1,0:T(8,128)}, f32[384,2048]{1,0:T(8,128)S(1)}, u32[]{:S(2)}) copy-start(f32[384,2048]{1,0:T(8,128)S(1)} %convolution_add_fusion) | copy-start | bytes 9437188
  91.7 22.1 %collective-permute-start.3 = (bf16[8,24,2048]{2,1,0:T(8,128)(2,1)}, bf16[8,24,2048]{2,1,0:T(8,128)(2,1)}, u32[]{:S(2)}, u32[]{:S(2)}) collective-permute-start(bf16[8,24,2048]{2,1,0:T(8,128)(2,1)} %fusion.20), channel_id=1, source_target_pairs={{0,32},{32,0},{1,33},{33,1},{2,34},{34,2},{3,35},{35,3},{4,36},{36... | collective-permute-start | bytes 2359304 | tf_op jit(solution)/shard_map/ppermute | solution.py:78
  97.2 23.6 %copy-start.1 = (f32[352,2048]{1,0:T(8,128)}, f32[352,2048]{1,0:T(8,128)S(1)}, u32[]{:S(2)}) copy-start(f32[352,2048]{1,0:T(8,128)S(1)} %fusion.8) | copy-start | bytes 8650756
  98.2 1.6 copy-start.2
  99.8 1.5 copy-start.3
  103.1 50.7 %collective-permute-start.2 = (bf16[3,176,2048]{2,1,0:T(8,128)(2,1)}, bf16[3,176,2048]{2,1,0:T(8,128)(2,1)}, u32[]{:S(2)}, u32[]{:S(2)}) collective-permute-start(bf16[3,176,2048]{2,1,0:T(8,128)(2,1)} %pad_maximum_fusion.1), channel_id=1, source_target_pairs={{0,16},{16,0},{1,17},{17,1},{2,18},{18,2},{3,19},{19,3},{4,20},{20... | collective-permute-start | bytes 6488072 | tf_op jit(solution)/shard_map/ppermute | solution.py:92
  116.6 27.8 %all-to-all-start.1 = ((bf16[8,24,2048]{2,1,0:T(8,128)(2,1)}), bf16[8,24,2048]{2,1,0:T(8,128)(2,1)}, u32[]{:S(2)}, u32[]{:S(2)}) async-start(bf16[8,24,2048]{2,1,0:T(8,128)(2,1)} %fusion), calls=%async_computation.1 | async-start | bytes 1572864 | tf_op jit(solution)/shard_map/all_to_all | solution.py:80
  146.3 14.9 %all-to-all-start.2 = ((bf16[16,24,128]{2,1,0:T(8,128)(2,1)}), bf16[16,24,128]{2,1,0:T(8,128)(2,1)S(1)}, u32[]{:S(2)}, u32[]{:S(2)}) async-start(bf16[16,24,128]{2,1,0:T(8,128)(2,1)} %copy.16), calls=%async_computation.2 | async-start | bytes 196608 | tf_op jit(solution)/shard_map/all_to_all | solution.py:83
  153.8 2.0 %slice-start.2 = ((f32[352,2048]{1,0:T(8,128)}), f32[176,2048]{1,0:T(8,128)S(1)}, s32[]{:S(2)}) async-start(f32[352,2048]{1,0:T(8,128)} %copy-done.3), calls=%async_computation.6 | async-start | bytes 2883584 | tf_op jit(solution)/shard_map/slice | solution.py:94
  155.6 1.6 slice-start
  156.8 1.4 slice-start.1
Sparse Core Ops, SparseCore 0:
  34.1 49.4 all-gather.1

commit v5 on v4

--- a/solution.py
+++ b/solution.py
@@ -11,6 +11,15 @@
 EXPERT = ("xl", "y")
 PAD = 176
 SWAP = [(0, 1), (1, 0)]
+
+
+def ring(a, step, cross=False):
+    pairs = []
+    for z in range(Z):
+        for c in range(CORE):
+            up = step * (1 - 2 * c) * (-1 if cross and step == 1 else 1)
+            pairs.append((z * CORE + c, (z + up) % Z * CORE + (c ^ cross)))
+    return lax.ppermute(a, ("z", "core"), pairs)
 
 
 def dot(a, b, dims=((1,), (0,))):
@@ -58,37 +67,61 @@
     x_near = jnp.concatenate(
         [jnp.where(side == 0, x_own, x_across), jnp.where(side == 0, x_across, x_own)], axis=0
     )
-    packet = jnp.concatenate([x_near, dy_near], axis=1)
+    near = 2 * capacity
+    packet = jnp.concatenate([x_near, dy_near], axis=0)
+    one = [ring(packet, 1), ring(packet, 1, cross=True)]
+    one = jnp.concatenate([one[0][:near], one[1][:near], one[0][near:], one[1][near:]], axis=0)
+    one = one + other_w[2, PAD - 1 :]
+    two = ring(one, 1)
+    three = ring(two, 1)
+    four = jnp.concatenate([three[:near], three[2 * near : 3 * near]], axis=0)
+    four = ring(four, 1)
+    chunks = []
+    for rows in (packet, one, two, three, four):
+        half = rows.shape[0] // 2
+        chunks.append((rows[:half], rows[half:]))
 
-    packets = lax.all_gather(packet, "z", axis=0, tiled=True)
-    x_rows, dy_rows = packets[:, :width], packets[:, width:]
     cols = ((1,), (1,))
-    gate_pre = dot(x_rows, wg, cols)
-    up_pre = dot(x_rows, wu, cols)
-    sig_gate = jax.nn.sigmoid(gate_pre)
-    silu_gate = gate_pre * sig_gate
-    hidden = (silu_gate * up_pre).astype(BF)
-    d_hidden = dot(dy_rows, wd, cols)
-    d_gate = (d_hidden * up_pre * sig_gate * (1.0 + gate_pre * (1.0 - sig_gate))).astype(BF)
-    d_up = (d_hidden * silu_gate).astype(BF)
-    terms = (dot(d_gate, wg) + dot(d_up, wu)).reshape(Z, 2, capacity, width)
+    terms, hiddens, d_gates, d_ups = [], [], [], []
+    for x_rows, dy_rows in chunks:
+        gate_pre = dot(x_rows, wg, cols)
+        up_pre = dot(x_rows, wu, cols)
+        sig_gate = jax.nn.sigmoid(gate_pre)
+        silu_gate = gate_pre * sig_gate
+        hiddens.append((silu_gate * up_pre).astype(BF))
+        d_hidden = dot(dy_rows, wd, cols)
+        d_gate = (d_hidden * up_pre * sig_gate * (1.0 + gate_pre * (1.0 - sig_gate))).astype(BF)
+        d_up = (d_hidden * silu_gate).astype(BF)
+        d_gates.append(d_gate)
+        d_ups.append(d_up)
+        terms.append(dot(d_gate, wg) + dot(d_up, wu))
 
-    other_terms = lax.dynamic_index_in_dim(terms, 1 - side, axis=1, keepdims=False)
-    own_terms = lax.dynamic_index_in_dim(terms, side, axis=1, keepdims=False)
-    came = lax.ppermute(other_terms.astype(BF), "xh", SWAP)
-    terms = (own_terms + came.astype(F32)).astype(BF)
-    terms = lax.all_to_all(terms, "z", 0, 0, tiled=True)
-    summed = jnp.sum(terms.astype(F32), axis=0).reshape(capacity, XL * Y, -1)
-    summed = jnp.transpose(summed, (1, 0, 2)).astype(BF)
-    summed = lax.all_to_all(summed, EXPERT, 0, 0, tiled=True)
+    home = jnp.concatenate([terms[4].astype(BF), terms[3][near:].astype(BF)], axis=0)
+    home = ring(home, -1)
+    home_a = (terms[3][:near] + home[:near].astype(F32)).astype(BF)
+    home_b = (terms[2][near:] + home[near:].astype(F32)).astype(BF)
+    home = ring(jnp.concatenate([home_a, home_b], axis=0), -1)
+    last_a = ring((terms[2][:near] + home[:near].astype(F32)).astype(BF), -1)
+    last_b = ring((terms[1][near:] + home[near:].astype(F32)).astype(BF), -1, cross=True)
+    last_a = ring((terms[1][:near] + last_a.astype(F32)).astype(BF), -1)
+    summed = terms[0] + last_a.astype(F32) + last_b.astype(F32)
+    summed = summed.reshape(XH, capacity, XL * Y, -1)
+    summed = jnp.transpose(summed, (0, 2, 1, 3)).astype(BF).reshape(XH * XL * Y, capacity, -1)
+    summed = lax.all_to_all(summed, ("xh",) + EXPERT, 0, 0, tiled=True)
 
-    from_slots = jnp.arange(2 * experts_all * capacity, dtype=jnp.int32)
-    from_slots = from_slots // (2 * capacity) * capacity + from_slots % capacity
+    from_slots = jnp.arange(XH * 2 * experts_all * capacity, dtype=jnp.int32)
+    from_slots = from_slots // (2 * capacity) % experts_all * capacity + from_slots % capacity
     place = (slot[:, None] == from_slots[None, :]).astype(BF)
-    grad_tokens = dot(place, summed.reshape(2 * experts_all * capacity, -1)).astype(BF)
+    grad_tokens = dot(place, summed.reshape(from_slots.shape[0], -1)).astype(BF)
 
+    x_all = jnp.concatenate([x for x, _ in chunks], axis=0)
+    dy_all = jnp.concatenate([dy for _, dy in chunks], axis=0)
     rows = ((0,), (0,))
-    grads = [dot(d_gate, x_rows, rows), dot(d_up, x_rows, rows), dot(hidden, dy_rows, rows)]
+    grads = [
+        dot(jnp.concatenate(d_gates, axis=0), x_all, rows),
+        dot(jnp.concatenate(d_ups, axis=0), x_all, rows),
+        dot(jnp.concatenate(hiddens, axis=0), dy_all, rows),
+    ]
     received = lax.ppermute(jnp.stack([grad[PAD:].astype(BF) for grad in grads]), "core", SWAP)
     outs = [
         (grad[:PAD] + extra.astype(F32))[:hidden_own].astype(BF)[None]

time: 170 us -> 160 us (0.941)
  the two profiles are of different devices: /device:TPU:1 before, /device:TPU:8 now
where the time goes in v5:
time: 160 us; the launch traced here: 159 us
  waiting for transfers between devices  60.7 us (38%)
  starting transfers between devices  56.1 us (35%)
  matrix products  19.9 us (12%)
  local copies, waits for them, and re-layouts  12.4 us (8%)
  other arithmetic  8.09 us (5%)
    ppermute x10, waiting for transfers between devices, ring(): return lax.ppermute(a, ('z', 'core'), pairs)  45.2 us
    ppermute x10, starting transfers between devices, ring(): return lax.ppermute(a, ('z', 'core'), pairs)  33.7 us
    dot_general x31, matrix products, dot(): return lax.dot_general(a, b, (dims, ((), ())), preferred_element_type=F32)  19.9 us
    all_to_all x1, waiting for transfers between devices, local(): summed = lax.all_to_all(summed, ('xh',) + EXPERT, 0, 0, tiled=True)  10.5 us
    all_to_all x1, starting transfers between devices, local(): dy_slices = lax.all_to_all(dy_slices, ('xh',) + EXPERT, 0, 0, tiled=True)  8.28 us
    unnamed x33, local copies, waits for them, and re-layouts  5.36 us
    all_to_all x1, starting transfers between devices, local(): summed = lax.all_to_all(summed, ('xh',) + EXPERT, 0, 0, tiled=True)  5.25 us
    ppermute x1, starting transfers between devices, local(): x_across = lax.ppermute(x_own, 'xh', SWAP)  5.06 us
  transfers between devices with their start and end apart: 15, of which 11 were waited for; matrix products, arithmetic and copies ran while one was open for 17% of the time, Pallas kernels for 0%

profile of v5, /device:TPU:8, one launch (start us, length us, event | category | flops | bytes accessed | tf_op | source)
XLA Modules:
  0.0 158.6 jit_solution(11847304993126051461)
XLA Ops:
  0.7 0.8 multiply_add_fusion
  2.2 5.1 %collective-permute-start.1 = (bf16[24,2048]{1,0:T(8,128)(2,1)S(1)}, bf16[24,2048]{1,0:T(8,128)(2,1)S(1)}, u32[]{:S(2)}, u32[]{:S(2)}) collective-permute-start(bf16[24,2048]{1,0:T(8,128)(2,1)S(1)} %convolution_convert_fusion), channel_id=1, source_target_pairs={{0,32},{32,0},{1,33},{33,1},{2,34},{34,2},{3,35},{35,3},{4,36},{36... | collective-permute-start | bytes 294920 | tf_op jit(solution)/shard_map/ppermute | solution.py:58
  7.2 1.0 convolution_convert_fusion.1
  8.2 0.7 broadcast_in_dim.16
  8.9 8.3 %all-to-all-start = ((bf16[32,24,128]{2,1,0:T(8,128)(2,1)}), bf16[32,24,128]{2,1,0:T(8,128)(2,1)S(1)}, u32[]{:S(2)}, u32[]{:S(2)}) async-start(bf16[32,24,128]{2,1,0:T(8,128)(2,1)} %bitcast.1), calls=%async_computation | async-start | bytes 393216 | tf_op jit(solution)/shard_map/all_to_all | solution.py:63
  17.2 1.0 fusion.83
  18.2 1.1 fusion.82
  19.3 1.6 %pad_maximum_fusion = bf16[3,176,2048]{2,1,0:T(8,128)(2,1)} fusion(bf16[1,176,2048]{2,1,0:T(8,128)(2,1)S(1)} %get-tuple-element.47, bf16[1,176,2048]{2,1,0:T(8,128)(2,1)S(1)} %get-tuple-element.45, bf16[1,176,2048]{2,1,0:T(8,128)(2,1)S(1)} %get-tuple-element.73), kind=kLoop, calls=%fused_computation.10 | loop fusion | flops 2162688 | bytes 4325376 | tf_op jit(solution)/shard_map/stack | solution.py:51
  20.9 1.9 %collective-permute-start = (bf16[3,176,2048]{2,1,0:T(8,128)(2,1)}, bf16[3,176,2048]{2,1,0:T(8,128)(2,1)}, u32[]{:S(2)}, u32[]{:S(2)}) collective-permute-start(bf16[3,176,2048]{2,1,0:T(8,128)(2,1)} %pad_maximum_fusion), channel_id=1, source_target_pairs={{0,16},{16,0},{1,17},{17,1},{2,18},{18,2},{3,19},{19,3},{4,20},{20... | collective-permute-start | bytes 6488072 | tf_op jit(solution)/shard_map/ppermute | solution.py:52
  22.9 5.0 %all-to-all-done = bf16[32,24,128]{2,1,0:T(8,128)(2,1)S(1)} async-done(((bf16[32,24,128]{2,1,0:T(8,128)(2,1)}), bf16[32,24,128]{2,1,0:T(8,128)(2,1)S(1)}, u32[]{:S(2)}, u32[]{:S(2)}) %all-to-all-start) | async-done | bytes 196640 | tf_op jit(solution)/shard_map/all_to_all | solution.py:63
  28.1 4.3 %collective-permute-start.2 = (bf16[96,2048]{1,0:T(8,128)(2,1)S(1)}, bf16[96,2048]{1,0:T(8,128)(2,1)S(1)}, u32[]{:S(2)}, u32[]{:S(2)}) collective-permute-start(bf16[96,2048]{1,0:T(8,128)(2,1)S(1)} %pad_maximum_fusion.5), channel_id=1, source_target_pairs={{0,64},{16,464},{64,128},{80,16},{128,192},{144,80},{192,256},{208... | collective-permute-start | bytes 1179656 | tf_op jit(solution)/shard_map/ppermute | solution.py:22
  32.4 6.5 %collective-permute-start.3 = (bf16[96,2048]{1,0:T(8,128)(2,1)S(1)}, bf16[96,2048]{1,0:T(8,128)(2,1)S(1)}, u32[]{:S(2)}, u32[]{:S(2)}) collective-permute-start(bf16[96,2048]{1,0:T(8,128)(2,1)S(1)} %pad_maximum_fusion.5), channel_id=1, source_target_pairs={{0,464},{16,64},{64,16},{80,128},{128,80},{144,192},{192,144},{208... | collective-permute-start | bytes 1179656 | tf_op jit(solution)/shard_map/ppermute | solution.py:22
  38.9 9.6 %collective-permute-done.2 = bf16[96,2048]{1,0:T(8,128)(2,1)S(1)} collective-permute-done((bf16[96,2048]{1,0:T(8,128)(2,1)S(1)}, bf16[96,2048]{1,0:T(8,128)(2,1)S(1)}, u32[]{:S(2)}, u32[]{:S(2)}) %collective-permute-start.2) | collective-permute-done | bytes 393248 | tf_op jit(solution)/shard_map/ppermute | solution.py:22
  48.6 0.8 slice_reduce_fusion
  49.6 2.1 %collective-permute-start.4 = (bf16[192,2048]{1,0:T(8,128)(2,1)S(1)}, bf16[192,2048]{1,0:T(8,128)(2,1)S(1)}, u32[]{:S(2)}, u32[]{:S(2)}) collective-permute-start(bf16[192,2048]{1,0:T(8,128)(2,1)S(1)} %maximum_add_fusion), channel_id=1, source_target_pairs={{0,64},{16,464},{64,128},{80,16},{128,192},{144,80},{192,256},{208... | collective-permute-start | bytes 2359304 | tf_op jit(solution)/shard_map/ppermute | solution.py:22
  51.7 1.7 %slice_bitcast_fusion.4 = (bf16[176,2048]{1,0:T(8,128)(2,1)S(1)}, bf16[176,2048]{1,0:T(8,128)(2,1)S(1)}, bf16[176,2048]{1,0:T(8,128)(2,1)S(1)}) fusion(bf16[3,176,2048]{2,1,0:T(8,128)(2,1)} %collective-permute-done), kind=kLoop, calls=%fused_computation.38 | loop fusion | bytes 4325376 | tf_op jit(solution)/shard_map/squeeze | solution.py:54
  53.4 0.6 fusion.36
  54.0 0.6 fusion.50
  54.6 0.6 fusion.34
  55.2 0.6 fusion.49
  55.7 0.5 copy-done.9
  56.3 0.6 constant_dynamic-update-slice_fusion.11
  56.8 0.6 constant_dynamic-update-slice_fusion.10
  57.4 0.4 fusion.79
  57.9 6.9 %collective-permute-done.4 = bf16[192,2048]{1,0:T(8,128)(2,1)S(1)} collective-permute-done((bf16[192,2048]{1,0:T(8,128)(2,1)S(1)}, bf16[192,2048]{1,0:T(8,128)(2,1)S(1)}, u32[]{:S(2)}, u32[]{:S(2)}) %collective-permute-start.4) | collective-permute-done | bytes 786464 | tf_op jit(solution)/shard_map/ppermute | solution.py:22
  64.9 1.9 %collective-permute-start.5 = (bf16[192,2048]{1,0:T(8,128)(2,1)S(1)}, bf16[192,2048]{1,0:T(8,128)(2,1)S(1)}, u32[]{:S(2)}, u32[]{:S(2)}) collective-permute-start(bf16[192,2048]{1,0:T(8,128)(2,1)S(1)} %collective-permute-done.4), channel_id=1, source_target_pairs={{0,64},{16,464},{64,128},{80,16},{128,192},{144,80},{192,256},{208... | collective-permute-start | bytes 2359304 | tf_op jit(solution)/shard_map/ppermute | solution.py:22
  66.8 0.6 fusion.32
  67.4 0.6 fusion.30
  68.0 0.6 constant_dynamic-update-slice_fusion.9
  69.5 10.5 %collective-permute-done.5 = bf16[192,2048]{1,0:T(8,128)(2,1)S(1)} collective-permute-done((bf16[192,2048]{1,0:T(8,128)(2,1)S(1)}, bf16[192,2048]{1,0:T(8,128)(2,1)S(1)}, u32[]{:S(2)}, u32[]{:S(2)}) %collective-permute-start.5) | collective-permute-done | bytes 786464 | tf_op jit(solution)/shard_map/ppermute | solution.py:22
  80.0 1.9 %collective-permute-start.6 = (bf16[96,2048]{1,0:T(8,128)(2,1)S(1)}, bf16[96,2048]{1,0:T(8,128)(2,1)S(1)}, u32[]{:S(2)}, u32[]{:S(2)}) collective-permute-start(bf16[96,2048]{1,0:T(8,128)(2,1)S(1)} %pad_maximum_fusion.6), channel_id=1, source_target_pairs={{0,64},{16,464},{64,128},{80,16},{128,192},{144,80},{192,256},{208... | collective-permute-start | bytes 1179656 | tf_op jit(solution)/shard_map/ppermute | solution.py:22
  81.9 0.6 fusion.28
  82.5 0.6 fusion.26
  83.1 0.6 constant_dynamic-update-slice_fusion.8
  84.1 0.4 convolution_add_fusion
  84.7 6.2 %collective-permute-done.6 = bf16[96,2048]{1,0:T(8,128)(2,1)S(1)} collective-permute-done((bf16[96,2048]{1,0:T(8,128)(2,1)S(1)}, bf16[96,2048]{1,0:T(8,128)(2,1)S(1)}, u32[]{:S(2)}, u32[]{:S(2)}) %collective-permute-start.6) | collective-permute-done | bytes 393248 | tf_op jit(solution)/shard_map/ppermute | solution.py:22
  90.9 0.6 fusion.44
  91.5 0.6 fusion.42
  92.0 0.6 constant_dynamic-update-slice_fusion.7
  93.4 2.1 %collective-permute-start.8 = (bf16[96,2048]{1,0:T(8,128)(2,1)S(1)}, bf16[96,2048]{1,0:T(8,128)(2,1)S(1)}, u32[]{:S(2)}, u32[]{:S(2)}) collective-permute-start(bf16[96,2048]{1,0:T(8,128)(2,1)S(1)} %pad_maximum_fusion.7), channel_id=1, source_target_pairs={{0,448},{16,80},{64,0},{80,144},{128,64},{144,208},{192,128},{208,... | collective-permute-start | bytes 1179656 | tf_op jit(solution)/shard_map/ppermute | solution.py:22
  95.5 1.2 copy-done.6
  96.7 2.3 %fusion.88 = f32[352,2048]{1,0:T(8,128)S(1)} fusion(bf16[384,352]{1,0:T(8,128)(2,1)S(1)} %get-tuple-element.4, bf16[384,2048]{1,0:T(8,128)(2,1)} %copy-done.6), kind=kOutput, calls=%fused_computation.190 | convolution fusion | flops 553648128 | bytes 4726784 | tf_op jit(solution)/shard_map/dot_general | solution.py:26
  99.2 0.9 fusion.89
  100.2 1.5 copy-done.7
  101.7 0.9 fusion.87
  103.2 3.1 %collective-permute-start.9 = (bf16[96,2048]{1,0:T(8,128)(2,1)S(1)}, bf16[96,2048]{1,0:T(8,128)(2,1)S(1)}, u32[]{:S(2)}, u32[]{:S(2)}) collective-permute-start(bf16[96,2048]{1,0:T(8,128)(2,1)S(1)} %pad_maximum_fusion.8), channel_id=1, source_target_pairs={{0,448},{16,80},{64,0},{80,144},{128,64},{144,208},{192,128},{208,... | collective-permute-start | bytes 1179656 | tf_op jit(solution)/shard_map/ppermute | solution.py:22
  106.5 1.6 pad_maximum_fusion.1
  108.0 1.9 %collective-permute-start.7 = (bf16[3,176,2048]{2,1,0:T(8,128)(2,1)}, bf16[3,176,2048]{2,1,0:T(8,128)(2,1)}, u32[]{:S(2)}, u32[]{:S(2)}) collective-permute-start(bf16[3,176,2048]{2,1,0:T(8,128)(2,1)} %pad_maximum_fusion.1), channel_id=1, source_target_pairs={{0,16},{16,0},{1,17},{17,1},{2,18},{18,2},{3,19},{19,3},{4,20},{20... | collective-permute-start | bytes 6488072 | tf_op jit(solution)/shard_map/ppermute | solution.py:125
  109.9 2.9 %collective-permute-done.9 = bf16[96,2048]{1,0:T(8,128)(2,1)S(1)} collective-permute-done((bf16[96,2048]{1,0:T(8,128)(2,1)S(1)}, bf16[96,2048]{1,0:T(8,128)(2,1)S(1)}, u32[]{:S(2)}, u32[]{:S(2)}) %collective-permute-start.9) | collective-permute-done | bytes 393248 | tf_op jit(solution)/shard_map/ppermute | solution.py:22
  112.9 4.3 %collective-permute-start.10 = (bf16[48,2048]{1,0:T(8,128)(2,1)S(1)}, bf16[48,2048]{1,0:T(8,128)(2,1)S(1)}, u32[]{:S(2)}, u32[]{:S(2)}) collective-permute-start(bf16[48,2048]{1,0:T(8,128)(2,1)S(1)} %fusion.17), channel_id=1, source_target_pairs={{0,448},{16,80},{64,0},{80,144},{128,64},{144,208},{192,128},{208,... | collective-permute-start | bytes 589832 | tf_op jit(solution)/shard_map/ppermute | solution.py:22
  117.3 0.4 convolution_add_fusion.2
  117.7 2.8 %collective-permute-done.10 = bf16[48,2048]{1,0:T(8,128)(2,1)S(1)} collective-permute-done((bf16[48,2048]{1,0:T(8,128)(2,1)S(1)}, bf16[48,2048]{1,0:T(8,128)(2,1)S(1)}, u32[]{:S(2)}, u32[]{:S(2)}) %collective-permute-start.10) | collective-permute-done | bytes 196640 | tf_op jit(solution)/shard_map/ppermute | solution.py:22
  120.6 5.6 %collective-permute-start.11 = (bf16[48,2048]{1,0:T(8,128)(2,1)S(1)}, bf16[48,2048]{1,0:T(8,128)(2,1)S(1)}, u32[]{:S(2)}, u32[]{:S(2)}) collective-permute-start(bf16[48,2048]{1,0:T(8,128)(2,1)S(1)} %get-tuple-element.34), channel_id=1, source_target_pairs={{0,448},{16,80},{64,0},{80,144},{128,64},{144,208},{192,128},{208,... | collective-permute-start | bytes 589832 | tf_op jit(solution)/shard_map/ppermute | solution.py:22
  126.1 1.9 %collective-permute-start.12 = (bf16[48,2048]{1,0:T(8,128)(2,1)S(1)}, bf16[48,2048]{1,0:T(8,128)(2,1)S(1)}, u32[]{:S(2)}, u32[]{:S(2)}) collective-permute-start(bf16[48,2048]{1,0:T(8,128)(2,1)S(1)} %get-tuple-element.35), channel_id=1, source_target_pairs={{0,464},{16,64},{64,16},{80,128},{128,80},{144,192},{192,144},{208... | collective-permute-start | bytes 589832 | tf_op jit(solution)/shard_map/ppermute | solution.py:22
  128.4 0.9 collective-permute-done.11
  129.3 5.0 %collective-permute-done.12 = bf16[48,2048]{1,0:T(8,128)(2,1)S(1)} collective-permute-done((bf16[48,2048]{1,0:T(8,128)(2,1)S(1)}, bf16[48,2048]{1,0:T(8,128)(2,1)S(1)}, u32[]{:S(2)}, u32[]{:S(2)}) %collective-permute-start.12) | collective-permute-done | bytes 196640 | tf_op jit(solution)/shard_map/ppermute | solution.py:22
  134.8 0.7 copy.14
  135.5 5.2 %all-to-all-start.1 = ((bf16[32,24,128]{2,1,0:T(8,128)(2,1)}), bf16[32,24,128]{2,1,0:T(8,128)(2,1)}, u32[]{:S(2)}, u32[]{:S(2)}) async-start(bf16[32,24,128]{2,1,0:T(8,128)(2,1)} %bitcast.81), calls=%async_computation.1 | async-start | bytes 393216 | tf_op jit(solution)/shard_map/all_to_all | solution.py:110
  140.8 10.5 %all-to-all-done.1 = bf16[32,24,128]{2,1,0:T(8,128)(2,1)} async-done(((bf16[32,24,128]{2,1,0:T(8,128)(2,1)}), bf16[32,24,128]{2,1,0:T(8,128)(2,1)}, u32[]{:S(2)}, u32[]{:S(2)}) %all-to-all-start.1) | async-done | bytes 196640 | tf_op jit(solution)/shard_map/all_to_all | solution.py:110
  151.3 1.8 %convolution_convert_fusion.2 = bf16[128,128]{1,0:T(8,128)(2,1)} fusion(bf16[768,128]{1,0:T(8,128)(2,1)} %bitcast.24, s32[768]{0:T(1024)S(1)} %fusion.68, s32[128]{0:T(128)S(1)} %compare_select_fusion), kind=kOutput, calls=%fused_computation.26 | convolution fusion | flops 25280512 | bytes 232960 | tf_op jit(solution)/shard_map/dot_general | solution.py:26
  153.1 1.8 %slice_bitcast_fusion = (bf16[176,2048]{1,0:T(8,128)(2,1)S(1)}, bf16[176,2048]{1,0:T(8,128)(2,1)S(1)}, bf16[176,2048]{1,0:T(8,128)(2,1)S(1)}) fusion(bf16[3,176,2048]{2,1,0:T(8,128)(2,1)} %collective-permute-done.7), kind=kLoop, calls=%fused_computation.34 | loop fusion | bytes 4325376
  155.1 1.0 fusion.13
  156.4 1.1 fusion.12
  157.6 1.1 fusion.11
  (73 shorter events, 5.8 us)
Async XLA Ops:
  0.6 1.3 copy-start
  0.6 16.6 %copy-start.8 = (bf16[1,172,2048]{2,1,0:T(8,128)(2,1)S(1)}, bf16[1,172,2048]{2,1,0:T(8,128)(2,1)}, u32[]{:S(2)}) copy-start(bf16[1,172,2048]{2,1,0:T(8,128)(2,1)} %param.15) | copy-start | bytes 2113540
  2.1 16.1 %copy-start.10 = (bf16[1,172,2048]{2,1,0:T(8,128)(2,1)S(1)}, bf16[1,172,2048]{2,1,0:T(8,128)(2,1)}, u32[]{:S(2)}) copy-start(bf16[1,172,2048]{2,1,0:T(8,128)(2,1)} %param.14) | copy-start | bytes 2113540
  2.2 16.0 %copy-start.11 = (bf16[1,172,2048]{2,1,0:T(8,128)(2,1)S(1)}, bf16[1,172,2048]{2,1,0:T(8,128)(2,1)}, u32[]{:S(2)}) copy-start(bf16[1,172,2048]{2,1,0:T(8,128)(2,1)} %param.13) | copy-start | bytes 2113540
  2.2 20.7 %collective-permute-start.1 = (bf16[24,2048]{1,0:T(8,128)(2,1)S(1)}, bf16[24,2048]{1,0:T(8,128)(2,1)S(1)}, u32[]{:S(2)}, u32[]{:S(2)}) collective-permute-start(bf16[24,2048]{1,0:T(8,128)(2,1)S(1)} %convolution_convert_fusion), channel_id=1, source_target_pairs={{0,32},{32,0},{1,33},{33,1},{2,34},{34,2},{3,35},{35,3},{4,36},{36... | collective-permute-start | bytes 294920 | tf_op jit(solution)/shard_map/ppermute | solution.py:58
  8.9 19.0 %all-to-all-start = ((bf16[32,24,128]{2,1,0:T(8,128)(2,1)}), bf16[32,24,128]{2,1,0:T(8,128)(2,1)S(1)}, u32[]{:S(2)}, u32[]{:S(2)}) async-start(bf16[32,24,128]{2,1,0:T(8,128)(2,1)} %bitcast.1), calls=%async_computation | async-start | bytes 393216 | tf_op jit(solution)/shard_map/all_to_all | solution.py:63
  19.3 73.6 %copy-start.4 = (bf16[176,2048]{1,0:T(8,128)(2,1)}, bf16[176,2048]{1,0:T(8,128)(2,1)S(1)}, u32[]{:S(2)}) copy-start(bf16[176,2048]{1,0:T(8,128)(2,1)S(1)} %get-tuple-element.74) | copy-start | bytes 2162692
  20.9 27.7 %collective-permute-start = (bf16[3,176,2048]{2,1,0:T(8,128)(2,1)}, bf16[3,176,2048]{2,1,0:T(8,128)(2,1)}, u32[]{:S(2)}, u32[]{:S(2)}) collective-permute-start(bf16[3,176,2048]{2,1,0:T(8,128)(2,1)} %pad_maximum_fusion), channel_id=1, source_target_pairs={{0,16},{16,0},{1,17},{17,1},{2,18},{18,2},{3,19},{19,3},{4,20},{20... | collective-permute-start | bytes 6488072 | tf_op jit(solution)/shard_map/ppermute | solution.py:52
  28.1 20.5 %collective-permute-start.2 = (bf16[96,2048]{1,0:T(8,128)(2,1)S(1)}, bf16[96,2048]{1,0:T(8,128)(2,1)S(1)}, u32[]{:S(2)}, u32[]{:S(2)}) collective-permute-start(bf16[96,2048]{1,0:T(8,128)(2,1)S(1)} %pad_maximum_fusion.5), channel_id=1, source_target_pairs={{0,64},{16,464},{64,128},{80,16},{128,192},{144,80},{192,256},{208... | collective-permute-start | bytes 1179656 | tf_op jit(solution)/shard_map/ppermute | solution.py:22
  32.4 16.2 %collective-permute-start.3 = (bf16[96,2048]{1,0:T(8,128)(2,1)S(1)}, bf16[96,2048]{1,0:T(8,128)(2,1)S(1)}, u32[]{:S(2)}, u32[]{:S(2)}) collective-permute-start(bf16[96,2048]{1,0:T(8,128)(2,1)S(1)} %pad_maximum_fusion.5), channel_id=1, source_target_pairs={{0,464},{16,64},{64,16},{80,128},{128,80},{144,192},{192,144},{208... | collective-permute-start | bytes 1179656 | tf_op jit(solution)/shard_map/ppermute | solution.py:22
  49.6 3.8 %copy-start.12 = (bf16[176,2048]{1,0:T(8,128)(2,1)S(1)}, bf16[176,2048]{1,0:T(8,128)(2,1)}, u32[]{:S(2)}) copy-start(bf16[176,2048]{1,0:T(8,128)(2,1)} %get-tuple-element.44) | copy-start | bytes 2162692
  49.6 15.2 %collective-permute-start.4 = (bf16[192,2048]{1,0:T(8,128)(2,1)S(1)}, bf16[192,2048]{1,0:T(8,128)(2,1)S(1)}, u32[]{:S(2)}, u32[]{:S(2)}) collective-permute-start(bf16[192,2048]{1,0:T(8,128)(2,1)S(1)} %maximum_add_fusion), channel_id=1, source_target_pairs={{0,64},{16,464},{64,128},{80,16},{128,192},{144,80},{192,256},{208... | collective-permute-start | bytes 2359304 | tf_op jit(solution)/shard_map/ppermute | solution.py:22
  55.1 1.1 copy-start.9
  64.9 15.1 %collective-permute-start.5 = (bf16[192,2048]{1,0:T(8,128)(2,1)S(1)}, bf16[192,2048]{1,0:T(8,128)(2,1)S(1)}, u32[]{:S(2)}, u32[]{:S(2)}) collective-permute-start(bf16[192,2048]{1,0:T(8,128)(2,1)S(1)} %collective-permute-done.4), channel_id=1, source_target_pairs={{0,64},{16,464},{64,128},{80,16},{128,192},{144,80},{192,256},{208... | collective-permute-start | bytes 2359304 | tf_op jit(solution)/shard_map/ppermute | solution.py:22
  80.0 10.9 %collective-permute-start.6 = (bf16[96,2048]{1,0:T(8,128)(2,1)S(1)}, bf16[96,2048]{1,0:T(8,128)(2,1)S(1)}, u32[]{:S(2)}, u32[]{:S(2)}) collective-permute-start(bf16[96,2048]{1,0:T(8,128)(2,1)S(1)} %pad_maximum_fusion.6), channel_id=1, source_target_pairs={{0,64},{16,464},{64,128},{80,16},{128,192},{144,80},{192,256},{208... | collective-permute-start | bytes 1179656 | tf_op jit(solution)/shard_map/ppermute | solution.py:22
  93.4 9.7 %collective-permute-start.8 = (bf16[96,2048]{1,0:T(8,128)(2,1)S(1)}, bf16[96,2048]{1,0:T(8,128)(2,1)S(1)}, u32[]{:S(2)}, u32[]{:S(2)}) collective-permute-start(bf16[96,2048]{1,0:T(8,128)(2,1)S(1)} %pad_maximum_fusion.7), channel_id=1, source_target_pairs={{0,448},{16,80},{64,0},{80,144},{128,64},{144,208},{192,128},{208,... | collective-permute-start | bytes 1179656 | tf_op jit(solution)/shard_map/ppermute | solution.py:22
  95.5 1.2 copy-start.6
  99.1 41.7 %copy-start.1 = (f32[352,2048]{1,0:T(8,128)}, f32[352,2048]{1,0:T(8,128)S(1)}, u32[]{:S(2)}) copy-start(f32[352,2048]{1,0:T(8,128)S(1)} %fusion.88) | copy-start | bytes 8650756
  99.2 2.6 %copy-start.7 = (bf16[384,2048]{1,0:T(8,128)(2,1)S(1)}, bf16[384,2048]{1,0:T(8,128)(2,1)}, u32[]{:S(2)}) copy-start(bf16[384,2048]{1,0:T(8,128)(2,1)} %copy-done.6) | copy-start | bytes 4718596
  100.1 2.6 %copy-start.2 = (f32[352,2048]{1,0:T(8,128)}, f32[352,2048]{1,0:T(8,128)S(1)}, u32[]{:S(2)}) copy-start(f32[352,2048]{1,0:T(8,128)S(1)} %fusion.89) | copy-start | bytes 8650756
  102.7 3.6 %copy-start.3 = (f32[352,2048]{1,0:T(8,128)}, f32[352,2048]{1,0:T(8,128)S(1)}, u32[]{:S(2)}) copy-start(f32[352,2048]{1,0:T(8,128)S(1)} %fusion.87) | copy-start | bytes 8650756
  103.2 9.7 %collective-permute-start.9 = (bf16[96,2048]{1,0:T(8,128)(2,1)S(1)}, bf16[96,2048]{1,0:T(8,128)(2,1)S(1)}, u32[]{:S(2)}, u32[]{:S(2)}) collective-permute-start(bf16[96,2048]{1,0:T(8,128)(2,1)S(1)} %pad_maximum_fusion.8), channel_id=1, source_target_pairs={{0,448},{16,80},{64,0},{80,144},{128,64},{144,208},{192,128},{208,... | collective-permute-start | bytes 1179656 | tf_op jit(solution)/shard_map/ppermute | solution.py:22
  106.4 10.8 %copy-start.5 = (bf16[176,2048]{1,0:T(8,128)(2,1)S(1)}, bf16[176,2048]{1,0:T(8,128)(2,1)}, u32[]{:S(2)}) copy-start(bf16[176,2048]{1,0:T(8,128)(2,1)} %copy-done.4) | copy-start | bytes 2162692
  108.0 45.1 %collective-permute-start.7 = (bf16[3,176,2048]{2,1,0:T(8,128)(2,1)}, bf16[3,176,2048]{2,1,0:T(8,128)(2,1)}, u32[]{:S(2)}, u32[]{:S(2)}) collective-permute-start(bf16[3,176,2048]{2,1,0:T(8,128)(2,1)} %pad_maximum_fusion.1), channel_id=1, source_target_pairs={{0,16},{16,0},{1,17},{17,1},{2,18},{18,2},{3,19},{19,3},{4,20},{20... | collective-permute-start | bytes 6488072 | tf_op jit(solution)/shard_map/ppermute | solution.py:125
  112.9 7.6 %collective-permute-start.10 = (bf16[48,2048]{1,0:T(8,128)(2,1)S(1)}, bf16[48,2048]{1,0:T(8,128)(2,1)S(1)}, u32[]{:S(2)}, u32[]{:S(2)}) collective-permute-start(bf16[48,2048]{1,0:T(8,128)(2,1)S(1)} %fusion.17), channel_id=1, source_target_pairs={{0,448},{16,80},{64,0},{80,144},{128,64},{144,208},{192,128},{208,... | collective-permute-start | bytes 589832 | tf_op jit(solution)/shard_map/ppermute | solution.py:22
  120.6 8.7 %collective-permute-start.11 = (bf16[48,2048]{1,0:T(8,128)(2,1)S(1)}, bf16[48,2048]{1,0:T(8,128)(2,1)S(1)}, u32[]{:S(2)}, u32[]{:S(2)}) collective-permute-start(bf16[48,2048]{1,0:T(8,128)(2,1)S(1)} %get-tuple-element.34), channel_id=1, source_target_pairs={{0,448},{16,80},{64,0},{80,144},{128,64},{144,208},{192,128},{208,... | collective-permute-start | bytes 589832 | tf_op jit(solution)/shard_map/ppermute | solution.py:22
  126.1 8.2 %collective-permute-start.12 = (bf16[48,2048]{1,0:T(8,128)(2,1)S(1)}, bf16[48,2048]{1,0:T(8,128)(2,1)S(1)}, u32[]{:S(2)}, u32[]{:S(2)}) collective-permute-start(bf16[48,2048]{1,0:T(8,128)(2,1)S(1)} %get-tuple-element.35), channel_id=1, source_target_pairs={{0,464},{16,64},{64,16},{80,128},{128,80},{144,192},{192,144},{208... | collective-permute-start | bytes 589832 | tf_op jit(solution)/shard_map/ppermute | solution.py:22
  135.5 15.8 %all-to-all-start.1 = ((bf16[32,24,128]{2,1,0:T(8,128)(2,1)}), bf16[32,24,128]{2,1,0:T(8,128)(2,1)}, u32[]{:S(2)}, u32[]{:S(2)}) async-start(bf16[32,24,128]{2,1,0:T(8,128)(2,1)} %bitcast.81), calls=%async_computation.1 | async-start | bytes 393216 | tf_op jit(solution)/shard_map/all_to_all | solution.py:110
  153.1 2.0 %slice-start.1 = ((f32[352,2048]{1,0:T(8,128)}), f32[176,2048]{1,0:T(8,128)S(1)}, s32[]{:S(2)}) async-start(f32[352,2048]{1,0:T(8,128)} %copy-done.2), calls=%async_computation.3 | async-start | bytes 2883584 | tf_op jit(solution)/shard_map/slice | solution.py:127
  154.9 1.5 slice-start
  156.1 1.4 slice-start.2

commit v6 on v5

--- a/solution.py
+++ b/solution.py
@@ -13,12 +13,12 @@
 SWAP = [(0, 1), (1, 0)]
 
 
-def ring(a, step, cross=False):
+def ring(a, hops, cross=False):
     pairs = []
     for z in range(Z):
         for c in range(CORE):
-            up = step * (1 - 2 * c) * (-1 if cross and step == 1 else 1)
-            pairs.append((z * CORE + c, (z + up) % Z * CORE + (c ^ cross)))
+            there = c ^ cross
+            pairs.append((z * CORE + c, (z + hops * (1 - 2 * there)) % Z * CORE + there))
     return lax.ppermute(a, ("z", "core"), pairs)
 
 
@@ -96,24 +96,21 @@
         d_ups.append(d_up)
         terms.append(dot(d_gate, wg) + dot(d_up, wu))
 
-    home = jnp.concatenate([terms[4].astype(BF), terms[3][near:].astype(BF)], axis=0)
-    home = ring(home, -1)
-    home_a = (terms[3][:near] + home[:near].astype(F32)).astype(BF)
-    home_b = (terms[2][near:] + home[near:].astype(F32)).astype(BF)
-    home = ring(jnp.concatenate([home_a, home_b], axis=0), -1)
-    last_a = ring((terms[2][:near] + home[:near].astype(F32)).astype(BF), -1)
-    last_b = ring((terms[1][near:] + home[near:].astype(F32)).astype(BF), -1, cross=True)
-    last_a = ring((terms[1][:near] + last_a.astype(F32)).astype(BF), -1)
-    summed = terms[0] + last_a.astype(F32) + last_b.astype(F32)
+    near_terms = ring(terms[2].astype(BF), -1)
+    near_terms = ring((terms[1] + near_terms.astype(F32)).astype(BF), -1)
+    far_b = ring(terms[3][near:].astype(BF), -3)
+    farthest = ring((terms[4] + near_terms[:1].astype(F32) * 0).astype(BF), -1)
+    far_a = terms[3][:near] + farthest.astype(F32) + far_b[:1].astype(F32) * 0
+    far_a = ring(far_a.astype(BF), -3)
+    crossing = (near_terms[near:].astype(F32) + far_b.astype(F32)).astype(BF)
+    crossing = lax.ppermute(crossing, "core", SWAP)
+    summed = terms[0] + near_terms[:near].astype(F32) + crossing.astype(F32) + far_a.astype(F32)
     summed = summed.reshape(XH, capacity, XL * Y, -1)
     summed = jnp.transpose(summed, (0, 2, 1, 3)).astype(BF).reshape(XH * XL * Y, capacity, -1)
     summed = lax.all_to_all(summed, ("xh",) + EXPERT, 0, 0, tiled=True)
 
     from_slots = jnp.arange(XH * 2 * experts_all * capacity, dtype=jnp.int32)
     from_slots = from_slots // (2 * capacity) % experts_all * capacity + from_slots % capacity
-    place = (slot[:, None] == from_slots[None, :]).astype(BF)
-    grad_tokens = dot(place, summed.reshape(from_slots.shape[0], -1)).astype(BF)
-
     x_all = jnp.concatenate([x for x, _ in chunks], axis=0)
     dy_all = jnp.concatenate([dy for _, dy in chunks], axis=0)
     rows = ((0,), (0,))
@@ -122,11 +119,16 @@
         dot(jnp.concatenate(d_ups, axis=0), x_all, rows),
         dot(jnp.concatenate(hiddens, axis=0), dy_all, rows),
     ]
-    received = lax.ppermute(jnp.stack([grad[PAD:].astype(BF) for grad in grads]), "core", SWAP)
+    given = jnp.stack([grad[PAD:].astype(BF) for grad in grads]) + farthest[:1] * 0
+    received = lax.ppermute(given, "core", SWAP)
     outs = [
         (grad[:PAD] + extra.astype(F32))[:hidden_own].astype(BF)[None]
         for grad, extra in zip(grads, received)
     ]
+
+    place = (slot[:, None] == from_slots[None, :]).astype(BF)
+    place = place + received[2, PAD - 1, 0]
+    grad_tokens = dot(place, summed.reshape(from_slots.shape[0], -1)).astype(BF)
     return (*outs, grad_tokens)
 
 

time: 160 us -> 164 us (1.025)
  the two profiles are of different devices: /device:TPU:8 before, /device:TPU:1 now
where the time goes in v6:
time: 164 us; the launch traced here: 163 us
  starting transfers between devices  77.4 us (47%)
  waiting for transfers between devices  47.4 us (29%)
  matrix products  18.3 us (11%)
  local copies, waits for them, and re-layouts  11 us (7%)
  other arithmetic  8.05 us (5%)
    ppermute x10, starting transfers between devices, ring(): return lax.ppermute(a, ('z', 'core'), pairs)  41.3 us
    ppermute x10, waiting for transfers between devices, ring(): return lax.ppermute(a, ('z', 'core'), pairs)  41 us
    dot_general x31, matrix products, dot(): return lax.dot_general(a, b, (dims, ((), ())), preferred_element_type=F32)  18.3 us
    all_to_all x1, starting transfers between devices, local(): summed = lax.all_to_all(summed, ('xh',) + EXPERT, 0, 0, tiled=True)  9.84 us
    all_to_all x1, starting transfers between devices, local(): dy_slices = lax.all_to_all(dy_slices, ('xh',) + EXPERT, 0, 0, tiled=True)  7.79 us
    ppermute x1, starting transfers between devices, local(): x_across = lax.ppermute(x_own, 'xh', SWAP)  5.61 us
    ppermute x1, starting transfers between devices, local(): received = lax.ppermute(given, 'core', SWAP)  5.44 us
    ppermute x1, starting transfers between devices, local(): crossing = lax.ppermute(crossing, 'core', SWAP)  4.24 us
  transfers between devices with their start and end apart: 16, of which 11 were waited for; matrix products, arithmetic and copies ran while one was open for 16% of the time, Pallas kernels for 0%

profile of v6, /device:TPU:1, one launch (start us, length us, event | category | flops | bytes accessed | tf_op | source)
XLA Modules:
  0.0 163.5 jit_solution(3835971380313109651)
XLA Ops:
  0.7 0.8 multiply_add_fusion
  2.2 5.6 %collective-permute-start.1 = (bf16[24,2048]{1,0:T(8,128)(2,1)S(1)}, bf16[24,2048]{1,0:T(8,128)(2,1)S(1)}, u32[]{:S(2)}, u32[]{:S(2)}) collective-permute-start(bf16[24,2048]{1,0:T(8,128)(2,1)S(1)} %convolution_convert_fusion), channel_id=1, source_target_pairs={{0,32},{32,0},{1,33},{33,1},{2,34},{34,2},{3,35},{35,3},{4,36},{36... | collective-permute-start | bytes 294920 | tf_op jit(solution)/shard_map/ppermute | solution.py:58
  7.8 1.0 convolution_convert_fusion.1
  8.8 0.7 broadcast_in_dim.16
  9.5 7.8 %all-to-all-start = ((bf16[32,24,128]{2,1,0:T(8,128)(2,1)}), bf16[32,24,128]{2,1,0:T(8,128)(2,1)S(1)}, u32[]{:S(2)}, u32[]{:S(2)}) async-start(bf16[32,24,128]{2,1,0:T(8,128)(2,1)} %bitcast.1), calls=%async_computation | async-start | bytes 393216 | tf_op jit(solution)/shard_map/all_to_all | solution.py:63
  17.3 1.0 fusion.89
  18.3 1.0 fusion.90
  19.6 1.6 pad_maximum_fusion
  21.2 3.1 %collective-permute-start = (bf16[3,176,2048]{2,1,0:T(8,128)(2,1)}, bf16[3,176,2048]{2,1,0:T(8,128)(2,1)}, u32[]{:S(2)}, u32[]{:S(2)}) collective-permute-start(bf16[3,176,2048]{2,1,0:T(8,128)(2,1)} %pad_maximum_fusion), channel_id=1, source_target_pairs={{0,16},{16,0},{1,17},{17,1},{2,18},{18,2},{3,19},{19,3},{4,20},{20... | collective-permute-start | bytes 6488072 | tf_op jit(solution)/shard_map/ppermute | solution.py:52
  24.4 2.2 %all-to-all-done = bf16[32,24,128]{2,1,0:T(8,128)(2,1)S(1)} async-done(((bf16[32,24,128]{2,1,0:T(8,128)(2,1)}), bf16[32,24,128]{2,1,0:T(8,128)(2,1)S(1)}, u32[]{:S(2)}, u32[]{:S(2)}) %all-to-all-start) | async-done | bytes 196640 | tf_op jit(solution)/shard_map/all_to_all | solution.py:63
  26.8 10.7 %collective-permute-start.2 = (bf16[96,2048]{1,0:T(8,128)(2,1)S(1)}, bf16[96,2048]{1,0:T(8,128)(2,1)S(1)}, u32[]{:S(2)}, u32[]{:S(2)}) collective-permute-start(bf16[96,2048]{1,0:T(8,128)(2,1)S(1)} %pad_maximum_fusion.4), channel_id=1, source_target_pairs={{0,64},{16,464},{64,128},{80,16},{128,192},{144,80},{192,256},{208... | collective-permute-start | bytes 1179656 | tf_op jit(solution)/shard_map/ppermute | solution.py:22
  37.5 1.9 %collective-permute-start.3 = (bf16[96,2048]{1,0:T(8,128)(2,1)S(1)}, bf16[96,2048]{1,0:T(8,128)(2,1)S(1)}, u32[]{:S(2)}, u32[]{:S(2)}) collective-permute-start(bf16[96,2048]{1,0:T(8,128)(2,1)S(1)} %pad_maximum_fusion.4), channel_id=1, source_target_pairs={{0,464},{16,64},{64,16},{80,128},{128,80},{144,192},{192,144},{208... | collective-permute-start | bytes 1179656 | tf_op jit(solution)/shard_map/ppermute | solution.py:22
  39.4 4.1 %collective-permute-done.2 = bf16[96,2048]{1,0:T(8,128)(2,1)S(1)} collective-permute-done((bf16[96,2048]{1,0:T(8,128)(2,1)S(1)}, bf16[96,2048]{1,0:T(8,128)(2,1)S(1)}, u32[]{:S(2)}, u32[]{:S(2)}) %collective-permute-start.2) | collective-permute-done | bytes 393248 | tf_op jit(solution)/shard_map/ppermute | solution.py:22
  43.6 3.3 %collective-permute-done.3 = bf16[96,2048]{1,0:T(8,128)(2,1)S(1)} collective-permute-done((bf16[96,2048]{1,0:T(8,128)(2,1)S(1)}, bf16[96,2048]{1,0:T(8,128)(2,1)S(1)}, u32[]{:S(2)}, u32[]{:S(2)}) %collective-permute-start.3) | collective-permute-done | bytes 393248 | tf_op jit(solution)/shard_map/ppermute | solution.py:22
  46.9 0.8 slice_reduce_fusion
  47.9 4.7 %collective-permute-start.4 = (bf16[192,2048]{1,0:T(8,128)(2,1)S(1)}, bf16[192,2048]{1,0:T(8,128)(2,1)S(1)}, u32[]{:S(2)}, u32[]{:S(2)}) collective-permute-start(bf16[192,2048]{1,0:T(8,128)(2,1)S(1)} %maximum_add_fusion.1), channel_id=1, source_target_pairs={{0,64},{16,464},{64,128},{80,16},{128,192},{144,80},{192,256},{208... | collective-permute-start | bytes 2359304 | tf_op jit(solution)/shard_map/ppermute | solution.py:22
  52.5 1.7 %slice_bitcast_fusion.4 = (bf16[176,2048]{1,0:T(8,128)(2,1)S(1)}, bf16[176,2048]{1,0:T(8,128)(2,1)S(1)}, bf16[176,2048]{1,0:T(8,128)(2,1)S(1)}) fusion(bf16[3,176,2048]{2,1,0:T(8,128)(2,1)} %collective-permute-done), kind=kLoop, calls=%fused_computation.43 | loop fusion | bytes 4325376 | tf_op jit(solution)/shard_map/squeeze | solution.py:54
  54.3 0.6 fusion.37
  54.8 0.6 fusion.53
  55.4 0.6 fusion.35
  56.0 0.6 fusion.52
  56.6 0.5 copy-done.10
  57.1 0.6 constant_dynamic-update-slice_fusion.11
  57.7 0.6 constant_dynamic-update-slice_fusion.10
  58.8 2.7 %collective-permute-done.4 = bf16[192,2048]{1,0:T(8,128)(2,1)S(1)} collective-permute-done((bf16[192,2048]{1,0:T(8,128)(2,1)S(1)}, bf16[192,2048]{1,0:T(8,128)(2,1)S(1)}, u32[]{:S(2)}, u32[]{:S(2)}) %collective-permute-start.4) | collective-permute-done | bytes 786464 | tf_op jit(solution)/shard_map/ppermute | solution.py:22
  61.5 0.6 fusion.33
  62.1 0.6 fusion.31
  62.6 0.6 constant_dynamic-update-slice_fusion.9
  63.7 5.0 %collective-permute-start.5 = (bf16[192,2048]{1,0:T(8,128)(2,1)S(1)}, bf16[192,2048]{1,0:T(8,128)(2,1)S(1)}, u32[]{:S(2)}, u32[]{:S(2)}) collective-permute-start(bf16[192,2048]{1,0:T(8,128)(2,1)S(1)} %collective-permute-done.4), channel_id=1, source_target_pairs={{0,64},{16,464},{64,128},{80,16},{128,192},{144,80},{192,256},{208... | collective-permute-start | bytes 2359304 | tf_op jit(solution)/shard_map/ppermute | solution.py:22
  68.7 0.4 fusion.2
  69.2 1.9 %collective-permute-start.7 = (bf16[96,2048]{1,0:T(8,128)(2,1)S(1)}, bf16[96,2048]{1,0:T(8,128)(2,1)S(1)}, u32[]{:S(2)}, u32[]{:S(2)}) collective-permute-start(bf16[96,2048]{1,0:T(8,128)(2,1)S(1)} %fusion.2), channel_id=1, source_target_pairs={{0,448},{16,80},{64,0},{80,144},{128,64},{144,208},{192,128},{208,... | collective-permute-start | bytes 1179656 | tf_op jit(solution)/shard_map/ppermute | solution.py:22
  71.2 12.2 %collective-permute-done.7 = bf16[96,2048]{1,0:T(8,128)(2,1)S(1)} collective-permute-done((bf16[96,2048]{1,0:T(8,128)(2,1)S(1)}, bf16[96,2048]{1,0:T(8,128)(2,1)S(1)}, u32[]{:S(2)}, u32[]{:S(2)}) %collective-permute-start.7) | collective-permute-done | bytes 393248 | tf_op jit(solution)/shard_map/ppermute | solution.py:22
  83.3 0.5 fusion.1
  83.8 1.9 %collective-permute-start.8 = (bf16[96,2048]{1,0:T(8,128)(2,1)S(1)}, bf16[96,2048]{1,0:T(8,128)(2,1)S(1)}, u32[]{:S(2)}, u32[]{:S(2)}) collective-permute-start(bf16[96,2048]{1,0:T(8,128)(2,1)S(1)} %fusion.1), channel_id=1, source_target_pairs={{0,448},{16,80},{64,0},{80,144},{128,64},{144,208},{192,128},{208,... | collective-permute-start | bytes 1179656 | tf_op jit(solution)/shard_map/ppermute | solution.py:22
  85.7 0.6 fusion.29
  86.3 0.6 fusion.27
  86.9 0.6 constant_dynamic-update-slice_fusion.8
  88.0 4.6 %collective-permute-start.6 = (bf16[96,2048]{1,0:T(8,128)(2,1)S(1)}, bf16[96,2048]{1,0:T(8,128)(2,1)S(1)}, u32[]{:S(2)}, u32[]{:S(2)}) collective-permute-start(bf16[96,2048]{1,0:T(8,128)(2,1)S(1)} %pad_maximum_fusion.5), channel_id=1, source_target_pairs={{0,64},{16,464},{64,128},{80,16},{128,192},{144,80},{192,256},{208... | collective-permute-start | bytes 1179656 | tf_op jit(solution)/shard_map/ppermute | solution.py:22
  92.6 0.9 collective-permute-done.8
  93.5 3.9 %collective-permute-done.6 = bf16[96,2048]{1,0:T(8,128)(2,1)S(1)} collective-permute-done((bf16[96,2048]{1,0:T(8,128)(2,1)S(1)}, bf16[96,2048]{1,0:T(8,128)(2,1)S(1)}, u32[]{:S(2)}, u32[]{:S(2)}) %collective-permute-start.6) | collective-permute-done | bytes 393248 | tf_op jit(solution)/shard_map/ppermute | solution.py:22
  97.4 0.6 fusion.47
  98.0 0.6 fusion.45
  98.5 0.6 constant_dynamic-update-slice_fusion.7
  99.9 2.1 %collective-permute-start.9 = (bf16[48,2048]{1,0:T(8,128)(2,1)S(1)}, bf16[48,2048]{1,0:T(8,128)(2,1)S(1)}, u32[]{:S(2)}, u32[]{:S(2)}) collective-permute-start(bf16[48,2048]{1,0:T(8,128)(2,1)S(1)} %fusion.7), channel_id=1, source_target_pairs={{0,448},{16,80},{64,0},{80,144},{128,64},{144,208},{192,128},{208,... | collective-permute-start | bytes 589832 | tf_op jit(solution)/shard_map/ppermute | solution.py:22
  102.0 0.9 fusion.95
  103.0 0.9 fusion.94
  104.1 0.9 fusion.96
  105.2 2.8 %collective-permute-done.9 = bf16[48,2048]{1,0:T(8,128)(2,1)S(1)} collective-permute-done((bf16[48,2048]{1,0:T(8,128)(2,1)S(1)}, bf16[48,2048]{1,0:T(8,128)(2,1)S(1)}, u32[]{:S(2)}, u32[]{:S(2)}) %collective-permute-start.9) | collective-permute-done | bytes 196640 | tf_op jit(solution)/shard_map/ppermute | solution.py:22
  108.0 1.7 %maximum_add_fusion = bf16[3,176,2048]{2,1,0:T(8,128)(2,1)} fusion(bf16[1,176,2048]{2,1,0:T(8,128)(2,1)S(1)} %fusion.15, bf16[1,176,2048]{2,1,0:T(8,128)(2,1)S(1)} %get-tuple-element.70, bf16[1,176,2048]{2,1,0:T(8,128)(2,1)S(1)} %get-tuple-element.69, bf16[2048]{0:T(1024)(128)(2,1)S(1)} %fusion.70), kind=kLoop, calls=%fused_computation.16 | loop fusion | flops 3244032 | bytes 4329472 | tf_op jit(solution)/shard_map/add | solution.py:122
  109.7 5.4 %collective-permute-start.10 = (bf16[3,176,2048]{2,1,0:T(8,128)(2,1)}, bf16[3,176,2048]{2,1,0:T(8,128)(2,1)}, u32[]{:S(2)}, u32[]{:S(2)}) collective-permute-start(bf16[3,176,2048]{2,1,0:T(8,128)(2,1)} %maximum_add_fusion), channel_id=1, source_target_pairs={{0,16},{16,0},{1,17},{17,1},{2,18},{18,2},{3,19},{19,3},{4,20},{20... | collective-permute-start | bytes 6488072 | tf_op jit(solution)/shard_map/ppermute | solution.py:123
  115.6 3.3 %collective-permute-start.11 = (bf16[48,2048]{1,0:T(8,128)(2,1)S(1)}, bf16[48,2048]{1,0:T(8,128)(2,1)S(1)}, u32[]{:S(2)}, u32[]{:S(2)}) collective-permute-start(bf16[48,2048]{1,0:T(8,128)(2,1)S(1)} %slice.265), channel_id=1, source_target_pairs={{0,320},{16,208},{64,384},{80,272},{128,448},{144,336},{192,0},{20... | collective-permute-start | bytes 589832 | tf_op jit(solution)/shard_map/ppermute | solution.py:22
  118.9 7.2 %collective-permute-done.11 = bf16[48,2048]{1,0:T(8,128)(2,1)S(1)} collective-permute-done((bf16[48,2048]{1,0:T(8,128)(2,1)S(1)}, bf16[48,2048]{1,0:T(8,128)(2,1)S(1)}, u32[]{:S(2)}, u32[]{:S(2)}) %collective-permute-start.11) | collective-permute-done | bytes 196640 | tf_op jit(solution)/shard_map/ppermute | solution.py:22
  126.2 4.2 %collective-permute-start.12 = (bf16[48,2048]{1,0:T(8,128)(2,1)S(1)}, bf16[48,2048]{1,0:T(8,128)(2,1)S(1)}, u32[]{:S(2)}, u32[]{:S(2)}) collective-permute-start(bf16[48,2048]{1,0:T(8,128)(2,1)S(1)} %add_convert_fusion), channel_id=1, source_target_pairs={{0,16},{16,0},{1,17},{17,1},{2,18},{18,2},{3,19},{19,3},{4,20},{20... | collective-permute-start | bytes 589832 | tf_op jit(solution)/shard_map/ppermute | solution.py:106
  130.5 5.2 %collective-permute-start.13 = (bf16[48,2048]{1,0:T(8,128)(2,1)S(1)}, bf16[48,2048]{1,0:T(8,128)(2,1)S(1)}, u32[]{:S(2)}, u32[]{:S(2)}) collective-permute-start(bf16[48,2048]{1,0:T(8,128)(2,1)S(1)} %fusion.20), channel_id=1, source_target_pairs={{0,320},{16,208},{64,384},{80,272},{128,448},{144,336},{192,0},{20... | collective-permute-start | bytes 589832 | tf_op jit(solution)/shard_map/ppermute | solution.py:22
  136.1 4.1 %collective-permute-done.13 = bf16[48,2048]{1,0:T(8,128)(2,1)S(1)} collective-permute-done((bf16[48,2048]{1,0:T(8,128)(2,1)S(1)}, bf16[48,2048]{1,0:T(8,128)(2,1)S(1)}, u32[]{:S(2)}, u32[]{:S(2)}) %collective-permute-start.13) | collective-permute-done | bytes 196640 | tf_op jit(solution)/shard_map/ppermute | solution.py:22
  140.6 0.7 copy.14
  141.4 9.8 %all-to-all-start.1 = ((bf16[32,24,128]{2,1,0:T(8,128)(2,1)}), bf16[32,24,128]{2,1,0:T(8,128)(2,1)S(1)}, u32[]{:S(2)}, u32[]{:S(2)}) async-start(bf16[32,24,128]{2,1,0:T(8,128)(2,1)} %bitcast.26), calls=%async_computation.1 | async-start | bytes 393216 | tf_op jit(solution)/shard_map/all_to_all | solution.py:110
  151.2 1.8 %slice_bitcast_fusion = (bf16[176,2048]{1,0:T(8,128)(2,1)S(1)}, bf16[176,2048]{1,0:T(8,128)(2,1)S(1)}, bf16[176,2048]{1,0:T(8,128)(2,1)S(1)}) fusion(bf16[3,176,2048]{2,1,0:T(8,128)(2,1)} %collective-permute-done.10), kind=kLoop, calls=%fused_computation.39 | loop fusion | bytes 4325376
  153.2 1.0 fusion.18
  154.6 1.1 fusion.17
  155.7 1.2 slice.179
  156.8 1.1 fusion.16
  157.9 4.1 %all-to-all-done.1 = bf16[32,24,128]{2,1,0:T(8,128)(2,1)S(1)} async-done(((bf16[32,24,128]{2,1,0:T(8,128)(2,1)}), bf16[32,24,128]{2,1,0:T(8,128)(2,1)S(1)}, u32[]{:S(2)}, u32[]{:S(2)}) %all-to-all-start.1) | async-done | bytes 196640 | tf_op jit(solution)/shard_map/all_to_all | solution.py:110
  162.0 1.5 convolution_convert_fusion.2
  (72 shorter events, 5.9 us)
Async XLA Ops:
  0.6 1.3 copy-start
  0.6 16.6 %copy-start.6 = (bf16[1,172,2048]{2,1,0:T(8,128)(2,1)S(1)}, bf16[1,172,2048]{2,1,0:T(8,128)(2,1)}, u32[]{:S(2)}) copy-start(bf16[1,172,2048]{2,1,0:T(8,128)(2,1)} %param.14) | copy-start | bytes 2113540
  2.1 16.2 %copy-start.7 = (bf16[1,172,2048]{2,1,0:T(8,128)(2,1)S(1)}, bf16[1,172,2048]{2,1,0:T(8,128)(2,1)}, u32[]{:S(2)}) copy-start(bf16[1,172,2048]{2,1,0:T(8,128)(2,1)} %param.15) | copy-start | bytes 2113540
  2.2 22.2 %collective-permute-start.1 = (bf16[24,2048]{1,0:T(8,128)(2,1)S(1)}, bf16[24,2048]{1,0:T(8,128)(2,1)S(1)}, u32[]{:S(2)}, u32[]{:S(2)}) collective-permute-start(bf16[24,2048]{1,0:T(8,128)(2,1)S(1)} %convolution_convert_fusion), channel_id=1, source_target_pairs={{0,32},{32,0},{1,33},{33,1},{2,34},{34,2},{3,35},{35,3},{4,36},{36... | collective-permute-start | bytes 294920 | tf_op jit(solution)/shard_map/ppermute | solution.py:58
  9.5 17.2 %all-to-all-start = ((bf16[32,24,128]{2,1,0:T(8,128)(2,1)}), bf16[32,24,128]{2,1,0:T(8,128)(2,1)S(1)}, u32[]{:S(2)}, u32[]{:S(2)}) async-start(bf16[32,24,128]{2,1,0:T(8,128)(2,1)} %bitcast.1), calls=%async_computation | async-start | bytes 393216 | tf_op jit(solution)/shard_map/all_to_all | solution.py:63
  18.3 1.2 copy-start.8
  19.6 79.9 %copy-start.4 = (bf16[176,2048]{1,0:T(8,128)(2,1)}, bf16[176,2048]{1,0:T(8,128)(2,1)S(1)}, u32[]{:S(2)}) copy-start(bf16[176,2048]{1,0:T(8,128)(2,1)S(1)} %get-tuple-element.46) | copy-start | bytes 2162692
  21.2 25.7 %collective-permute-start = (bf16[3,176,2048]{2,1,0:T(8,128)(2,1)}, bf16[3,176,2048]{2,1,0:T(8,128)(2,1)}, u32[]{:S(2)}, u32[]{:S(2)}) collective-permute-start(bf16[3,176,2048]{2,1,0:T(8,128)(2,1)} %pad_maximum_fusion), channel_id=1, source_target_pairs={{0,16},{16,0},{1,17},{17,1},{2,18},{18,2},{3,19},{19,3},{4,20},{20... | collective-permute-start | bytes 6488072 | tf_op jit(solution)/shard_map/ppermute | solution.py:52
  26.8 16.8 %collective-permute-start.2 = (bf16[96,2048]{1,0:T(8,128)(2,1)S(1)}, bf16[96,2048]{1,0:T(8,128)(2,1)S(1)}, u32[]{:S(2)}, u32[]{:S(2)}) collective-permute-start(bf16[96,2048]{1,0:T(8,128)(2,1)S(1)} %pad_maximum_fusion.4), channel_id=1, source_target_pairs={{0,64},{16,464},{64,128},{80,16},{128,192},{144,80},{192,256},{208... | collective-permute-start | bytes 1179656 | tf_op jit(solution)/shard_map/ppermute | solution.py:22
  37.5 9.4 %collective-permute-start.3 = (bf16[96,2048]{1,0:T(8,128)(2,1)S(1)}, bf16[96,2048]{1,0:T(8,128)(2,1)S(1)}, u32[]{:S(2)}, u32[]{:S(2)}) collective-permute-start(bf16[96,2048]{1,0:T(8,128)(2,1)S(1)} %pad_maximum_fusion.4), channel_id=1, source_target_pairs={{0,464},{16,64},{64,16},{80,128},{128,80},{144,192},{192,144},{208... | collective-permute-start | bytes 1179656 | tf_op jit(solution)/shard_map/ppermute | solution.py:22
  47.9 6.4 %copy-start.9 = (bf16[176,2048]{1,0:T(8,128)(2,1)S(1)}, bf16[176,2048]{1,0:T(8,128)(2,1)}, u32[]{:S(2)}) copy-start(bf16[176,2048]{1,0:T(8,128)(2,1)} %get-tuple-element.42) | copy-start | bytes 2162692
  47.9 13.6 %collective-permute-start.4 = (bf16[192,2048]{1,0:T(8,128)(2,1)S(1)}, bf16[192,2048]{1,0:T(8,128)(2,1)S(1)}, u32[]{:S(2)}, u32[]{:S(2)}) collective-permute-start(bf16[192,2048]{1,0:T(8,128)(2,1)S(1)} %maximum_add_fusion.1), channel_id=1, source_target_pairs={{0,64},{16,464},{64,128},{80,16},{128,192},{144,80},{192,256},{208... | collective-permute-start | bytes 2359304 | tf_op jit(solution)/shard_map/ppermute | solution.py:22
  56.0 1.1 copy-start.10
  63.7 22.0 %collective-permute-start.5 = (bf16[192,2048]{1,0:T(8,128)(2,1)S(1)}, bf16[192,2048]{1,0:T(8,128)(2,1)S(1)}, u32[]{:S(2)}, u32[]{:S(2)}) collective-permute-start(bf16[192,2048]{1,0:T(8,128)(2,1)S(1)} %collective-permute-done.4), channel_id=1, source_target_pairs={{0,64},{16,464},{64,128},{80,16},{128,192},{144,80},{192,256},{208... | collective-permute-start | bytes 2359304 | tf_op jit(solution)/shard_map/ppermute | solution.py:22
  69.2 14.2 %collective-permute-start.7 = (bf16[96,2048]{1,0:T(8,128)(2,1)S(1)}, bf16[96,2048]{1,0:T(8,128)(2,1)S(1)}, u32[]{:S(2)}, u32[]{:S(2)}) collective-permute-start(bf16[96,2048]{1,0:T(8,128)(2,1)S(1)} %fusion.2), channel_id=1, source_target_pairs={{0,448},{16,80},{64,0},{80,144},{128,64},{144,208},{192,128},{208,... | collective-permute-start | bytes 1179656 | tf_op jit(solution)/shard_map/ppermute | solution.py:22
  83.8 9.7 %collective-permute-start.8 = (bf16[96,2048]{1,0:T(8,128)(2,1)S(1)}, bf16[96,2048]{1,0:T(8,128)(2,1)S(1)}, u32[]{:S(2)}, u32[]{:S(2)}) collective-permute-start(bf16[96,2048]{1,0:T(8,128)(2,1)S(1)} %fusion.1), channel_id=1, source_target_pairs={{0,448},{16,80},{64,0},{80,144},{128,64},{144,208},{192,128},{208,... | collective-permute-start | bytes 1179656 | tf_op jit(solution)/shard_map/ppermute | solution.py:22
  88.0 9.4 %collective-permute-start.6 = (bf16[96,2048]{1,0:T(8,128)(2,1)S(1)}, bf16[96,2048]{1,0:T(8,128)(2,1)S(1)}, u32[]{:S(2)}, u32[]{:S(2)}) collective-permute-start(bf16[96,2048]{1,0:T(8,128)(2,1)S(1)} %pad_maximum_fusion.5), channel_id=1, source_target_pairs={{0,64},{16,464},{64,128},{80,16},{128,192},{144,80},{192,256},{208... | collective-permute-start | bytes 1179656 | tf_op jit(solution)/shard_map/ppermute | solution.py:22
  99.9 8.1 %collective-permute-start.9 = (bf16[48,2048]{1,0:T(8,128)(2,1)S(1)}, bf16[48,2048]{1,0:T(8,128)(2,1)S(1)}, u32[]{:S(2)}, u32[]{:S(2)}) collective-permute-start(bf16[48,2048]{1,0:T(8,128)(2,1)S(1)} %fusion.7), channel_id=1, source_target_pairs={{0,448},{16,80},{64,0},{80,144},{128,64},{144,208},{192,128},{208,... | collective-permute-start | bytes 589832 | tf_op jit(solution)/shard_map/ppermute | solution.py:22
  103.0 33.2 %copy-start.2 = (f32[352,2048]{1,0:T(8,128)}, f32[352,2048]{1,0:T(8,128)S(1)}, u32[]{:S(2)}) copy-start(f32[352,2048]{1,0:T(8,128)S(1)} %fusion.95) | copy-start | bytes 8650756
  103.9 32.2 %copy-start.3 = (f32[352,2048]{1,0:T(8,128)}, f32[352,2048]{1,0:T(8,128)S(1)}, u32[]{:S(2)}) copy-start(f32[352,2048]{1,0:T(8,128)S(1)} %fusion.94) | copy-start | bytes 8650756
  105.1 31.0 %copy-start.1 = (f32[352,2048]{1,0:T(8,128)}, f32[352,2048]{1,0:T(8,128)S(1)}, u32[]{:S(2)}) copy-start(f32[352,2048]{1,0:T(8,128)S(1)} %fusion.96) | copy-start | bytes 8650756
  108.0 7.2 %copy-start.5 = (bf16[176,2048]{1,0:T(8,128)(2,1)S(1)}, bf16[176,2048]{1,0:T(8,128)(2,1)}, u32[]{:S(2)}) copy-start(bf16[176,2048]{1,0:T(8,128)(2,1)} %copy-done.4) | copy-start | bytes 2162692
  109.7 41.6 %collective-permute-start.10 = (bf16[3,176,2048]{2,1,0:T(8,128)(2,1)}, bf16[3,176,2048]{2,1,0:T(8,128)(2,1)}, u32[]{:S(2)}, u32[]{:S(2)}) collective-permute-start(bf16[3,176,2048]{2,1,0:T(8,128)(2,1)} %maximum_add_fusion), channel_id=1, source_target_pairs={{0,16},{16,0},{1,17},{17,1},{2,18},{18,2},{3,19},{19,3},{4,20},{20... | collective-permute-start | bytes 6488072 | tf_op jit(solution)/shard_map/ppermute | solution.py:123
  115.6 10.6 %collective-permute-start.11 = (bf16[48,2048]{1,0:T(8,128)(2,1)S(1)}, bf16[48,2048]{1,0:T(8,128)(2,1)S(1)}, u32[]{:S(2)}, u32[]{:S(2)}) collective-permute-start(bf16[48,2048]{1,0:T(8,128)(2,1)S(1)} %slice.265), channel_id=1, source_target_pairs={{0,320},{16,208},{64,384},{80,272},{128,448},{144,336},{192,0},{20... | collective-permute-start | bytes 589832 | tf_op jit(solution)/shard_map/ppermute | solution.py:22
  126.2 9.9 %collective-permute-start.12 = (bf16[48,2048]{1,0:T(8,128)(2,1)S(1)}, bf16[48,2048]{1,0:T(8,128)(2,1)S(1)}, u32[]{:S(2)}, u32[]{:S(2)}) collective-permute-start(bf16[48,2048]{1,0:T(8,128)(2,1)S(1)} %add_convert_fusion), channel_id=1, source_target_pairs={{0,16},{16,0},{1,17},{17,1},{2,18},{18,2},{3,19},{19,3},{4,20},{20... | collective-permute-start | bytes 589832 | tf_op jit(solution)/shard_map/ppermute | solution.py:106
  130.5 9.7 %collective-permute-start.13 = (bf16[48,2048]{1,0:T(8,128)(2,1)S(1)}, bf16[48,2048]{1,0:T(8,128)(2,1)S(1)}, u32[]{:S(2)}, u32[]{:S(2)}) collective-permute-start(bf16[48,2048]{1,0:T(8,128)(2,1)S(1)} %fusion.20), channel_id=1, source_target_pairs={{0,320},{16,208},{64,384},{80,272},{128,448},{144,336},{192,0},{20... | collective-permute-start | bytes 589832 | tf_op jit(solution)/shard_map/ppermute | solution.py:22
  141.4 20.6 %all-to-all-start.1 = ((bf16[32,24,128]{2,1,0:T(8,128)(2,1)}), bf16[32,24,128]{2,1,0:T(8,128)(2,1)S(1)}, u32[]{:S(2)}, u32[]{:S(2)}) async-start(bf16[32,24,128]{2,1,0:T(8,128)(2,1)} %bitcast.26), calls=%async_computation.1 | async-start | bytes 393216 | tf_op jit(solution)/shard_map/all_to_all | solution.py:110
  151.2 2.0 %slice-start = ((f32[352,2048]{1,0:T(8,128)}), f32[176,2048]{1,0:T(8,128)S(1)}, s32[]{:S(2)}) async-start(f32[352,2048]{1,0:T(8,128)} %copy-done.1), calls=%async_computation.2 | async-start | bytes 2883584 | tf_op jit(solution)/shard_map/slice | solution.py:125
  153.0 1.6 slice-start.1
  154.3 2.6 %slice-start.2 = ((f32[352,2048]{1,0:T(8,128)}), f32[176,2048]{1,0:T(8,128)S(1)}, s32[]{:S(2)}) async-start(f32[352,2048]{1,0:T(8,128)} %copy-done.3), calls=%async_computation.4 | async-start | bytes 2883584 | tf_op jit(solution)/shard_map/slice | solution.py:125

commit v7 on v5

--- a/solution.py
+++ b/solution.py
@@ -42,8 +42,9 @@
     slot_rank = jnp.sum(before * one_hot, axis=1)
     kept = slot_rank < capacity
     slot = jnp.where(kept, expert_id * capacity + slot_rank, -1)
-    slots = jnp.arange(experts_all * capacity, dtype=jnp.int32)
-    select = (slot[None, :] == slots[:, None]).astype(BF)
+    all_slots = jnp.arange(XH * 2 * experts_all * capacity, dtype=jnp.int32)
+    all_slots = all_slots // (2 * capacity) % experts_all * capacity + all_slots % capacity
+    select = (slot[None, :] == all_slots[:, None]).astype(BF)
     own_slots = own_expert * capacity + jnp.arange(capacity, dtype=jnp.int32)
     select_own = (slot[None, :] == own_slots[:, None]).astype(BF)
 
@@ -57,9 +58,7 @@
     x_own = dot(select_own, tokens).astype(BF)
     x_across = lax.ppermute(x_own, "xh", SWAP)
     scaled = (gate_values[:, None] * out_grad.astype(F32)).astype(BF)
-    dy_slices = dot(select, scaled).astype(BF).reshape(1, experts_all, 1, capacity, -1)
-    dy_slices = jnp.broadcast_to(dy_slices, (XH, experts_all, 2) + dy_slices.shape[3:])
-    dy_slices = dy_slices.reshape((XH * XL * Y,) + dy_slices.shape[3:])
+    dy_slices = dot(select, scaled).astype(BF).reshape(XH * XL * Y, capacity, -1)
     dy_slices = lax.all_to_all(dy_slices, ("xh",) + EXPERT, 0, 0, tiled=True)
     dy_slices = dy_slices.reshape((XH, XL * Y) + dy_slices.shape[1:])
     dy_near = jnp.transpose(dy_slices, (0, 2, 1, 3)).reshape(2 * capacity, width)
@@ -96,24 +95,6 @@
         d_ups.append(d_up)
         terms.append(dot(d_gate, wg) + dot(d_up, wu))
 
-    home = jnp.concatenate([terms[4].astype(BF), terms[3][near:].astype(BF)], axis=0)
-    home = ring(home, -1)
-    home_a = (terms[3][:near] + home[:near].astype(F32)).astype(BF)
-    home_b = (terms[2][near:] + home[near:].astype(F32)).astype(BF)
-    home = ring(jnp.concatenate([home_a, home_b], axis=0), -1)
-    last_a = ring((terms[2][:near] + home[:near].astype(F32)).astype(BF), -1)
-    last_b = ring((terms[1][near:] + home[near:].astype(F32)).astype(BF), -1, cross=True)
-    last_a = ring((terms[1][:near] + last_a.astype(F32)).astype(BF), -1)
-    summed = terms[0] + last_a.astype(F32) + last_b.astype(F32)
-    summed = summed.reshape(XH, capacity, XL * Y, -1)
-    summed = jnp.transpose(summed, (0, 2, 1, 3)).astype(BF).reshape(XH * XL * Y, capacity, -1)
-    summed = lax.all_to_all(summed, ("xh",) + EXPERT, 0, 0, tiled=True)
-
-    from_slots = jnp.arange(XH * 2 * experts_all * capacity, dtype=jnp.int32)
-    from_slots = from_slots // (2 * capacity) % experts_all * capacity + from_slots % capacity
-    place = (slot[:, None] == from_slots[None, :]).astype(BF)
-    grad_tokens = dot(place, summed.reshape(from_slots.shape[0], -1)).astype(BF)
-
     x_all = jnp.concatenate([x for x, _ in chunks], axis=0)
     dy_all = jnp.concatenate([dy for _, dy in chunks], axis=0)
     rows = ((0,), (0,))
@@ -123,6 +104,26 @@
         dot(jnp.concatenate(hiddens, axis=0), dy_all, rows),
     ]
     received = lax.ppermute(jnp.stack([grad[PAD:].astype(BF) for grad in grads]), "core", SWAP)
+
+    home = jnp.concatenate([terms[4].astype(BF), terms[3][near:].astype(BF)], axis=0)
+    home = ring(home, -1)
+    home_a = (terms[3][:near] + home[:near].astype(F32)).astype(BF)
+    home_b = (terms[2][near:] + home[near:].astype(F32)).astype(BF)
+    home = ring(jnp.concatenate([home_a, home_b], axis=0), -1)
+    home_a = (terms[2][:near] + home[:near].astype(F32)).astype(BF)
+    home_b = (terms[1][near:] + home[near:].astype(F32)).astype(BF)
+    home = ring(jnp.concatenate([home_a, home_b], axis=0), -1)
+    last_a = ring((terms[1][:near] + home[:near].astype(F32)).astype(BF), -1)
+    last_b = lax.ppermute(home[near:], "core", SWAP)
+    summed = terms[0] + last_a.astype(F32) + last_b.astype(F32)
+    summed = summed + received[2, PAD - 1 :].astype(F32)
+    summed = summed.reshape(XH, capacity, XL * Y, -1)
+    summed = jnp.transpose(summed, (0, 2, 1, 3)).astype(BF).reshape(XH * XL * Y, capacity, -1)
+    summed = lax.all_to_all(summed, ("xh",) + EXPERT, 0, 0, tiled=True)
+
+    place = (slot[:, None] == all_slots[None, :]).astype(BF)
+    grad_tokens = dot(place, summed.reshape(all_slots.shape[0], -1)).astype(BF)
+
     outs = [
         (grad[:PAD] + extra.astype(F32))[:hidden_own].astype(BF)[None]
         for grad, extra in zip(grads, received)

time: 160 us -> 159 us (level)
  the two profiles are of different devices: /device:TPU:8 before, /device:TPU:1 now
where the time goes in v7:
time: 159 us; the launch traced here: 157 us
  starting transfers between devices  72.4 us (46%)
  waiting for transfers between devices  47.9 us (30%)
  matrix products  18.4 us (12%)
  local copies, waits for them, and re-layouts  10.1 us (6%)
  other arithmetic  6.76 us (4%)
    ppermute x9, waiting for transfers between devices, ring(): return lax.ppermute(a, ('z', 'core'), pairs)  41.6 us
    ppermute x9, starting transfers between devices, ring(): return lax.ppermute(a, ('z', 'core'), pairs)  39.2 us
    dot_general x31, matrix products, dot(): return lax.dot_general(a, b, (dims, ((), ())), preferred_element_type=F32)  18.4 us
    all_to_all x1, starting transfers between devices, local(): dy_slices = lax.all_to_all(dy_slices, ('xh',) + EXPERT, 0, 0, tiled=True)  7.79 us
    ppermute x1, starting transfers between devices, local(): lax.ppermute(jnp.stack([grad[PAD:].astype(BF) for grad in grads]), 'core'...  7.17 us
    all_to_all x1, starting transfers between devices, local(): summed = lax.all_to_all(summed, ('xh',) + EXPERT, 0, 0, tiled=True)  7.02 us
    ppermute x1, starting transfers between devices, local(): x_across = lax.ppermute(x_own, 'xh', SWAP)  5.61 us
    all_to_all x1, waiting for transfers between devices, local(): summed = lax.all_to_all(summed, ('xh',) + EXPERT, 0, 0, tiled=True)  3.86 us
  transfers between devices with their start and end apart: 15, of which 10 were waited for; matrix products, arithmetic and copies ran while one was open for 13% of the time, Pallas kernels for 0%

profile of v7, /device:TPU:1, one launch (start us, length us, event | category | flops | bytes accessed | tf_op | source)
XLA Modules:
  0.0 157.0 jit_solution(12608975235130016448)
XLA Ops:
  0.7 0.8 multiply_add_fusion
  2.2 5.6 %collective-permute-start.1 = (bf16[24,2048]{1,0:T(8,128)(2,1)S(1)}, bf16[24,2048]{1,0:T(8,128)(2,1)S(1)}, u32[]{:S(2)}, u32[]{:S(2)}) collective-permute-start(bf16[24,2048]{1,0:T(8,128)(2,1)S(1)} %convolution_convert_fusion), channel_id=1, source_target_pairs={{0,32},{32,0},{1,33},{33,1},{2,34},{34,2},{3,35},{35,3},{4,36},{36... | collective-permute-start | bytes 294920 | tf_op jit(solution)/shard_map/ppermute | solution.py:59
  7.8 1.8 %convolution_convert_fusion.1 = bf16[768,128]{1,0:T(8,128)(2,1)} fusion(s32[128]{0:T(128)S(1)} %compare_select_fusion, s32[768]{0:T(1024)S(1)} %fusion.71, bf16[128,128]{1,0:T(8,128)(2,1)} %param.9, f32[128]{0:T(128)} %param.12), kind=kOutput, calls=%fused_computation.25 | convolution fusion | flops 25411584 | bytes 233472 | tf_op jit(solution)/shard_map/dot_general | solution.py:26
  9.6 7.8 %all-to-all-start = ((bf16[32,24,128]{2,1,0:T(8,128)(2,1)}), bf16[32,24,128]{2,1,0:T(8,128)(2,1)S(1)}, u32[]{:S(2)}, u32[]{:S(2)}) async-start(bf16[32,24,128]{2,1,0:T(8,128)(2,1)} %bitcast), calls=%async_computation | async-start | bytes 393216 | tf_op jit(solution)/shard_map/all_to_all | solution.py:62
  17.4 1.0 fusion.86
  18.4 1.1 fusion.85
  19.5 1.6 %pad_maximum_fusion = bf16[3,176,2048]{2,1,0:T(8,128)(2,1)} fusion(bf16[1,176,2048]{2,1,0:T(8,128)(2,1)S(1)} %get-tuple-element.45, bf16[1,176,2048]{2,1,0:T(8,128)(2,1)S(1)} %get-tuple-element.43, bf16[1,176,2048]{2,1,0:T(8,128)(2,1)S(1)} %get-tuple-element.73), kind=kLoop, calls=%fused_computation.11 | loop fusion | flops 2162688 | bytes 4325376 | tf_op jit(solution)/shard_map/stack | solution.py:52
  21.1 3.1 %collective-permute-start = (bf16[3,176,2048]{2,1,0:T(8,128)(2,1)}, bf16[3,176,2048]{2,1,0:T(8,128)(2,1)}, u32[]{:S(2)}, u32[]{:S(2)}) collective-permute-start(bf16[3,176,2048]{2,1,0:T(8,128)(2,1)} %pad_maximum_fusion), channel_id=1, source_target_pairs={{0,16},{16,0},{1,17},{17,1},{2,18},{18,2},{3,19},{19,3},{4,20},{20... | collective-permute-start | bytes 6488072 | tf_op jit(solution)/shard_map/ppermute | solution.py:53
  24.3 2.5 %all-to-all-done = bf16[32,24,128]{2,1,0:T(8,128)(2,1)S(1)} async-done(((bf16[32,24,128]{2,1,0:T(8,128)(2,1)}), bf16[32,24,128]{2,1,0:T(8,128)(2,1)S(1)}, u32[]{:S(2)}, u32[]{:S(2)}) %all-to-all-start) | async-done | bytes 196640 | tf_op jit(solution)/shard_map/all_to_all | solution.py:62
  26.9 6.7 %collective-permute-start.3 = (bf16[96,2048]{1,0:T(8,128)(2,1)S(1)}, bf16[96,2048]{1,0:T(8,128)(2,1)S(1)}, u32[]{:S(2)}, u32[]{:S(2)}) collective-permute-start(bf16[96,2048]{1,0:T(8,128)(2,1)S(1)} %pad_maximum_fusion.5), channel_id=1, source_target_pairs={{0,464},{16,64},{64,16},{80,128},{128,80},{144,192},{192,144},{208... | collective-permute-start | bytes 1179656 | tf_op jit(solution)/shard_map/ppermute | solution.py:22
  33.6 5.9 %collective-permute-start.2 = (bf16[96,2048]{1,0:T(8,128)(2,1)S(1)}, bf16[96,2048]{1,0:T(8,128)(2,1)S(1)}, u32[]{:S(2)}, u32[]{:S(2)}) collective-permute-start(bf16[96,2048]{1,0:T(8,128)(2,1)S(1)} %pad_maximum_fusion.5), channel_id=1, source_target_pairs={{0,64},{16,464},{64,128},{80,16},{128,192},{144,80},{192,256},{208... | collective-permute-start | bytes 1179656 | tf_op jit(solution)/shard_map/ppermute | solution.py:22
  39.8 7.2 %collective-permute-done.2 = bf16[96,2048]{1,0:T(8,128)(2,1)S(1)} collective-permute-done((bf16[96,2048]{1,0:T(8,128)(2,1)S(1)}, bf16[96,2048]{1,0:T(8,128)(2,1)S(1)}, u32[]{:S(2)}, u32[]{:S(2)}) %collective-permute-start.2) | collective-permute-done | bytes 393248 | tf_op jit(solution)/shard_map/ppermute | solution.py:22
  47.1 1.8 %slice_bitcast_fusion.4 = (bf16[176,2048]{1,0:T(8,128)(2,1)S(1)}, bf16[176,2048]{1,0:T(8,128)(2,1)S(1)}, bf16[176,2048]{1,0:T(8,128)(2,1)S(1)}) fusion(bf16[3,176,2048]{2,1,0:T(8,128)(2,1)} %collective-permute-done), kind=kLoop, calls=%fused_computation.39 | loop fusion | bytes 4325376 | tf_op jit(solution)/shard_map/squeeze | solution.py:55
  48.9 0.6 fusion.54
  49.5 0.8 slice_reduce_fusion
  50.4 0.6 fusion.38
  51.0 0.6 fusion.53
  51.6 0.6 fusion.36
  52.2 5.0 %collective-permute-start.4 = (bf16[192,2048]{1,0:T(8,128)(2,1)S(1)}, bf16[192,2048]{1,0:T(8,128)(2,1)S(1)}, u32[]{:S(2)}, u32[]{:S(2)}) collective-permute-start(bf16[192,2048]{1,0:T(8,128)(2,1)S(1)} %maximum_add_fusion), channel_id=1, source_target_pairs={{0,64},{16,464},{64,128},{80,16},{128,192},{144,80},{192,256},{208... | collective-permute-start | bytes 2359304 | tf_op jit(solution)/shard_map/ppermute | solution.py:22
  57.2 0.6 constant_dynamic-update-slice_fusion.11
  57.8 0.6 constant_dynamic-update-slice_fusion.10
  58.4 7.7 %collective-permute-done.4 = bf16[192,2048]{1,0:T(8,128)(2,1)S(1)} collective-permute-done((bf16[192,2048]{1,0:T(8,128)(2,1)S(1)}, bf16[192,2048]{1,0:T(8,128)(2,1)S(1)}, u32[]{:S(2)}, u32[]{:S(2)}) %collective-permute-start.4) | collective-permute-done | bytes 786464 | tf_op jit(solution)/shard_map/ppermute | solution.py:22
  66.1 0.6 fusion.32
  66.7 0.6 fusion.34
  67.3 5.0 %collective-permute-start.5 = (bf16[192,2048]{1,0:T(8,128)(2,1)S(1)}, bf16[192,2048]{1,0:T(8,128)(2,1)S(1)}, u32[]{:S(2)}, u32[]{:S(2)}) collective-permute-start(bf16[192,2048]{1,0:T(8,128)(2,1)S(1)} %collective-permute-done.4), channel_id=1, source_target_pairs={{0,64},{16,464},{64,128},{80,16},{128,192},{144,80},{192,256},{208... | collective-permute-start | bytes 2359304 | tf_op jit(solution)/shard_map/ppermute | solution.py:22
  72.3 0.6 constant_dynamic-update-slice_fusion.9
  72.9 0.4 fusion.81
  73.3 0.4 convolution_add_fusion.1
  73.8 7.4 %collective-permute-done.5 = bf16[192,2048]{1,0:T(8,128)(2,1)S(1)} collective-permute-done((bf16[192,2048]{1,0:T(8,128)(2,1)S(1)}, bf16[192,2048]{1,0:T(8,128)(2,1)S(1)}, u32[]{:S(2)}, u32[]{:S(2)}) %collective-permute-start.5) | collective-permute-done | bytes 786464 | tf_op jit(solution)/shard_map/ppermute | solution.py:22
  81.3 5.0 %collective-permute-start.6 = (bf16[96,2048]{1,0:T(8,128)(2,1)S(1)}, bf16[96,2048]{1,0:T(8,128)(2,1)S(1)}, u32[]{:S(2)}, u32[]{:S(2)}) collective-permute-start(bf16[96,2048]{1,0:T(8,128)(2,1)S(1)} %pad_maximum_fusion.6), channel_id=1, source_target_pairs={{0,64},{16,464},{64,128},{80,16},{128,192},{144,80},{192,256},{208... | collective-permute-start | bytes 1179656 | tf_op jit(solution)/shard_map/ppermute | solution.py:22
  86.3 0.6 fusion.28
  86.9 0.6 fusion.30
  87.5 0.6 constant_dynamic-update-slice_fusion.8
  88.1 0.4 fusion.80
  88.5 0.4 convolution_add_fusion
  89.0 2.0 %collective-permute-done.6 = bf16[96,2048]{1,0:T(8,128)(2,1)S(1)} collective-permute-done((bf16[96,2048]{1,0:T(8,128)(2,1)S(1)}, bf16[96,2048]{1,0:T(8,128)(2,1)S(1)}, u32[]{:S(2)}, u32[]{:S(2)}) %collective-permute-start.6) | collective-permute-done | bytes 393248 | tf_op jit(solution)/shard_map/ppermute | solution.py:22
  91.0 0.6 fusion.46
  91.6 0.6 fusion.48
  92.1 0.6 constant_dynamic-update-slice_fusion.7
  93.1 0.4 fusion.4
  93.5 2.1 %collective-permute-start.8 = (bf16[96,2048]{1,0:T(8,128)(2,1)S(1)}, bf16[96,2048]{1,0:T(8,128)(2,1)S(1)}, u32[]{:S(2)}, u32[]{:S(2)}) collective-permute-start(bf16[96,2048]{1,0:T(8,128)(2,1)S(1)} %pad_maximum_fusion.7), channel_id=1, source_target_pairs={{0,448},{16,80},{64,0},{80,144},{128,64},{144,208},{192,128},{208,... | collective-permute-start | bytes 1179656 | tf_op jit(solution)/shard_map/ppermute | solution.py:22
  95.7 1.2 copy-done.6
  96.8 0.9 fusion.92
  98.2 0.9 fusion.91
  99.3 0.9 fusion.90
  100.6 7.2 %collective-permute-start.7 = (bf16[3,176,2048]{2,1,0:T(8,128)(2,1)S(1)}, bf16[3,176,2048]{2,1,0:T(8,128)(2,1)S(1)}, u32[]{:S(2)}, u32[]{:S(2)}) collective-permute-start(bf16[3,176,2048]{2,1,0:T(8,128)(2,1)S(1)} %pad_maximum_fusion.1), channel_id=1, source_target_pairs={{0,16},{16,0},{1,17},{17,1},{2,18},{18,2},{3,19},{19,3},{4,20},{20... | collective-permute-start | bytes 6488072 | tf_op jit(solution)/shard_map/ppermute | solution.py:106
  107.9 3.8 %collective-permute-start.9 = (bf16[96,2048]{1,0:T(8,128)(2,1)S(1)}, bf16[96,2048]{1,0:T(8,128)(2,1)S(1)}, u32[]{:S(2)}, u32[]{:S(2)}) collective-permute-start(bf16[96,2048]{1,0:T(8,128)(2,1)S(1)} %pad_maximum_fusion.8), channel_id=1, source_target_pairs={{0,448},{16,80},{64,0},{80,144},{128,64},{144,208},{192,128},{208,... | collective-permute-start | bytes 1179656 | tf_op jit(solution)/shard_map/ppermute | solution.py:22
  111.7 0.4 fusion.82
  112.1 0.4 convolution_add_fusion.2
  112.6 5.2 %collective-permute-done.9 = bf16[96,2048]{1,0:T(8,128)(2,1)S(1)} collective-permute-done((bf16[96,2048]{1,0:T(8,128)(2,1)S(1)}, bf16[96,2048]{1,0:T(8,128)(2,1)S(1)}, u32[]{:S(2)}, u32[]{:S(2)}) %collective-permute-start.9) | collective-permute-done | bytes 393248 | tf_op jit(solution)/shard_map/ppermute | solution.py:22
  117.9 2.7 %collective-permute-start.10 = (bf16[96,2048]{1,0:T(8,128)(2,1)S(1)}, bf16[96,2048]{1,0:T(8,128)(2,1)S(1)}, u32[]{:S(2)}, u32[]{:S(2)}) collective-permute-start(bf16[96,2048]{1,0:T(8,128)(2,1)S(1)} %pad_maximum_fusion.9), channel_id=1, source_target_pairs={{0,448},{16,80},{64,0},{80,144},{128,64},{144,208},{192,128},{208,... | collective-permute-start | bytes 1179656 | tf_op jit(solution)/shard_map/ppermute | solution.py:22
  121.0 6.6 %collective-permute-done.10 = bf16[96,2048]{1,0:T(8,128)(2,1)S(1)} collective-permute-done((bf16[96,2048]{1,0:T(8,128)(2,1)S(1)}, bf16[96,2048]{1,0:T(8,128)(2,1)S(1)}, u32[]{:S(2)}, u32[]{:S(2)}) %collective-permute-start.10) | collective-permute-done | bytes 393248 | tf_op jit(solution)/shard_map/ppermute | solution.py:22
  127.6 2.5 %collective-permute-start.12 = (bf16[48,2048]{1,0:T(8,128)(2,1)S(1)}, bf16[48,2048]{1,0:T(8,128)(2,1)S(1)}, u32[]{:S(2)}, u32[]{:S(2)}) collective-permute-start(bf16[48,2048]{1,0:T(8,128)(2,1)S(1)} %slice.208), channel_id=1, source_target_pairs={{0,16},{16,0},{1,17},{17,1},{2,18},{18,2},{3,19},{19,3},{4,20},{20... | collective-permute-start | bytes 589832 | tf_op jit(solution)/shard_map/ppermute | solution.py:117
  130.2 3.0 %collective-permute-start.11 = (bf16[48,2048]{1,0:T(8,128)(2,1)S(1)}, bf16[48,2048]{1,0:T(8,128)(2,1)S(1)}, u32[]{:S(2)}, u32[]{:S(2)}) collective-permute-start(bf16[48,2048]{1,0:T(8,128)(2,1)S(1)} %fusion.19), channel_id=1, source_target_pairs={{0,448},{16,80},{64,0},{80,144},{128,64},{144,208},{192,128},{208,... | collective-permute-start | bytes 589832 | tf_op jit(solution)/shard_map/ppermute | solution.py:22
  133.2 5.3 %collective-permute-done.11 = bf16[48,2048]{1,0:T(8,128)(2,1)S(1)} collective-permute-done((bf16[48,2048]{1,0:T(8,128)(2,1)S(1)}, bf16[48,2048]{1,0:T(8,128)(2,1)S(1)}, u32[]{:S(2)}, u32[]{:S(2)}) %collective-permute-start.11) | collective-permute-done | bytes 196640 | tf_op jit(solution)/shard_map/ppermute | solution.py:22
  138.5 0.4 fusion.8
  139.0 0.7 copy.14
  139.7 7.0 %all-to-all-start.1 = ((bf16[32,24,128]{2,1,0:T(8,128)(2,1)}), bf16[32,24,128]{2,1,0:T(8,128)(2,1)S(1)}, u32[]{:S(2)}, u32[]{:S(2)}) async-start(bf16[32,24,128]{2,1,0:T(8,128)(2,1)} %bitcast.23), calls=%async_computation.1 | async-start | bytes 393216 | tf_op jit(solution)/shard_map/all_to_all | solution.py:122
  146.7 1.8 %slice_bitcast_fusion = (bf16[176,2048]{1,0:T(8,128)(2,1)S(1)}, bf16[176,2048]{1,0:T(8,128)(2,1)S(1)}, bf16[176,2048]{1,0:T(8,128)(2,1)S(1)}) fusion(bf16[3,176,2048]{2,1,0:T(8,128)(2,1)} %copy-done.8), kind=kLoop, calls=%fused_computation.35 | loop fusion | bytes 4325376
  148.7 1.0 fusion.12
  150.1 1.1 fusion.14
  151.2 1.1 fusion.13
  152.2 3.9 %all-to-all-done.1 = bf16[32,24,128]{2,1,0:T(8,128)(2,1)S(1)} async-done(((bf16[32,24,128]{2,1,0:T(8,128)(2,1)}), bf16[32,24,128]{2,1,0:T(8,128)(2,1)S(1)}, u32[]{:S(2)}, u32[]{:S(2)}) %all-to-all-start.1) | async-done | bytes 196640 | tf_op jit(solution)/shard_map/all_to_all | solution.py:122
  156.1 0.9 convolution_convert_fusion.2
  (77 shorter events, 4.2 us)
Async XLA Ops:
  0.6 1.3 copy-start
  0.6 16.7 %copy-start.9 = (bf16[1,172,2048]{2,1,0:T(8,128)(2,1)S(1)}, bf16[1,172,2048]{2,1,0:T(8,128)(2,1)}, u32[]{:S(2)}) copy-start(bf16[1,172,2048]{2,1,0:T(8,128)(2,1)} %param.15) | copy-start | bytes 2113540
  1.9 16.4 %copy-start.11 = (bf16[1,172,2048]{2,1,0:T(8,128)(2,1)S(1)}, bf16[1,172,2048]{2,1,0:T(8,128)(2,1)}, u32[]{:S(2)}) copy-start(bf16[1,172,2048]{2,1,0:T(8,128)(2,1)} %param.14) | copy-start | bytes 2113540
  1.9 16.4 %copy-start.12 = (bf16[1,172,2048]{2,1,0:T(8,128)(2,1)S(1)}, bf16[1,172,2048]{2,1,0:T(8,128)(2,1)}, u32[]{:S(2)}) copy-start(bf16[1,172,2048]{2,1,0:T(8,128)(2,1)} %param.13) | copy-start | bytes 2113540
  2.2 22.1 %collective-permute-start.1 = (bf16[24,2048]{1,0:T(8,128)(2,1)S(1)}, bf16[24,2048]{1,0:T(8,128)(2,1)S(1)}, u32[]{:S(2)}, u32[]{:S(2)}) collective-permute-start(bf16[24,2048]{1,0:T(8,128)(2,1)S(1)} %convolution_convert_fusion), channel_id=1, source_target_pairs={{0,32},{32,0},{1,33},{33,1},{2,34},{34,2},{3,35},{35,3},{4,36},{36... | collective-permute-start | bytes 294920 | tf_op jit(solution)/shard_map/ppermute | solution.py:59
  9.6 17.2 %all-to-all-start = ((bf16[32,24,128]{2,1,0:T(8,128)(2,1)}), bf16[32,24,128]{2,1,0:T(8,128)(2,1)S(1)}, u32[]{:S(2)}, u32[]{:S(2)}) async-start(bf16[32,24,128]{2,1,0:T(8,128)(2,1)} %bitcast), calls=%async_computation | async-start | bytes 393216 | tf_op jit(solution)/shard_map/all_to_all | solution.py:62
  19.5 73.6 %copy-start.4 = (bf16[176,2048]{1,0:T(8,128)(2,1)}, bf16[176,2048]{1,0:T(8,128)(2,1)S(1)}, u32[]{:S(2)}) copy-start(bf16[176,2048]{1,0:T(8,128)(2,1)S(1)} %get-tuple-element.74) | copy-start | bytes 2162692
  21.1 26.0 %collective-permute-start = (bf16[3,176,2048]{2,1,0:T(8,128)(2,1)}, bf16[3,176,2048]{2,1,0:T(8,128)(2,1)}, u32[]{:S(2)}, u32[]{:S(2)}) collective-permute-start(bf16[3,176,2048]{2,1,0:T(8,128)(2,1)} %pad_maximum_fusion), channel_id=1, source_target_pairs={{0,16},{16,0},{1,17},{17,1},{2,18},{18,2},{3,19},{19,3},{4,20},{20... | collective-permute-start | bytes 6488072 | tf_op jit(solution)/shard_map/ppermute | solution.py:53
  26.9 12.9 %collective-permute-start.3 = (bf16[96,2048]{1,0:T(8,128)(2,1)S(1)}, bf16[96,2048]{1,0:T(8,128)(2,1)S(1)}, u32[]{:S(2)}, u32[]{:S(2)}) collective-permute-start(bf16[96,2048]{1,0:T(8,128)(2,1)S(1)} %pad_maximum_fusion.5), channel_id=1, source_target_pairs={{0,464},{16,64},{64,16},{80,128},{128,80},{144,192},{192,144},{208... | collective-permute-start | bytes 1179656 | tf_op jit(solution)/shard_map/ppermute | solution.py:22
  33.6 13.4 %collective-permute-start.2 = (bf16[96,2048]{1,0:T(8,128)(2,1)S(1)}, bf16[96,2048]{1,0:T(8,128)(2,1)S(1)}, u32[]{:S(2)}, u32[]{:S(2)}) collective-permute-start(bf16[96,2048]{1,0:T(8,128)(2,1)S(1)} %pad_maximum_fusion.5), channel_id=1, source_target_pairs={{0,64},{16,464},{64,128},{80,16},{128,192},{144,80},{192,256},{208... | collective-permute-start | bytes 1179656 | tf_op jit(solution)/shard_map/ppermute | solution.py:22
  47.1 1.8 %copy-start.13 = (bf16[176,2048]{1,0:T(8,128)(2,1)S(1)}, bf16[176,2048]{1,0:T(8,128)(2,1)}, u32[]{:S(2)}) copy-start(bf16[176,2048]{1,0:T(8,128)(2,1)} %get-tuple-element.42) | copy-start | bytes 2162692
  51.6 5.6 %copy-start.10 = (bf16[176,2048]{1,0:T(8,128)(2,1)S(1)}, bf16[176,2048]{1,0:T(8,128)(2,1)}, u32[]{:S(2)}) copy-start(bf16[176,2048]{1,0:T(8,128)(2,1)} %get-tuple-element.44) | copy-start | bytes 2162692
  52.2 13.9 %collective-permute-start.4 = (bf16[192,2048]{1,0:T(8,128)(2,1)S(1)}, bf16[192,2048]{1,0:T(8,128)(2,1)S(1)}, u32[]{:S(2)}, u32[]{:S(2)}) collective-permute-start(bf16[192,2048]{1,0:T(8,128)(2,1)S(1)} %maximum_add_fusion), channel_id=1, source_target_pairs={{0,64},{16,464},{64,128},{80,16},{128,192},{144,80},{192,256},{208... | collective-permute-start | bytes 2359304 | tf_op jit(solution)/shard_map/ppermute | solution.py:22
  67.3 13.9 %collective-permute-start.5 = (bf16[192,2048]{1,0:T(8,128)(2,1)S(1)}, bf16[192,2048]{1,0:T(8,128)(2,1)S(1)}, u32[]{:S(2)}, u32[]{:S(2)}) collective-permute-start(bf16[192,2048]{1,0:T(8,128)(2,1)S(1)} %collective-permute-done.4), channel_id=1, source_target_pairs={{0,64},{16,464},{64,128},{80,16},{128,192},{144,80},{192,256},{208... | collective-permute-start | bytes 2359304 | tf_op jit(solution)/shard_map/ppermute | solution.py:22
  81.3 9.7 %collective-permute-start.6 = (bf16[96,2048]{1,0:T(8,128)(2,1)S(1)}, bf16[96,2048]{1,0:T(8,128)(2,1)S(1)}, u32[]{:S(2)}, u32[]{:S(2)}) collective-permute-start(bf16[96,2048]{1,0:T(8,128)(2,1)S(1)} %pad_maximum_fusion.6), channel_id=1, source_target_pairs={{0,64},{16,464},{64,128},{80,16},{128,192},{144,80},{192,256},{208... | collective-permute-start | bytes 1179656 | tf_op jit(solution)/shard_map/ppermute | solution.py:22
  93.5 14.2 %collective-permute-start.8 = (bf16[96,2048]{1,0:T(8,128)(2,1)S(1)}, bf16[96,2048]{1,0:T(8,128)(2,1)S(1)}, u32[]{:S(2)}, u32[]{:S(2)}) collective-permute-start(bf16[96,2048]{1,0:T(8,128)(2,1)S(1)} %pad_maximum_fusion.7), channel_id=1, source_target_pairs={{0,448},{16,80},{64,0},{80,144},{128,64},{144,208},{192,128},{208,... | collective-permute-start | bytes 1179656 | tf_op jit(solution)/shard_map/ppermute | solution.py:22
  95.7 1.2 copy-start.6
  96.8 1.4 copy-start.7
  97.8 23.2 %copy-start.1 = (f32[352,2048]{1,0:T(8,128)}, f32[352,2048]{1,0:T(8,128)S(1)}, u32[]{:S(2)}) copy-start(f32[352,2048]{1,0:T(8,128)S(1)} %fusion.92) | copy-start | bytes 8650756
  99.2 21.8 %copy-start.2 = (f32[352,2048]{1,0:T(8,128)}, f32[352,2048]{1,0:T(8,128)S(1)}, u32[]{:S(2)}) copy-start(f32[352,2048]{1,0:T(8,128)S(1)} %fusion.91) | copy-start | bytes 8650756
  100.2 20.8 %copy-start.3 = (f32[352,2048]{1,0:T(8,128)}, f32[352,2048]{1,0:T(8,128)S(1)}, u32[]{:S(2)}) copy-start(f32[352,2048]{1,0:T(8,128)S(1)} %fusion.90) | copy-start | bytes 8650756
  100.6 32.6 %collective-permute-start.7 = (bf16[3,176,2048]{2,1,0:T(8,128)(2,1)S(1)}, bf16[3,176,2048]{2,1,0:T(8,128)(2,1)S(1)}, u32[]{:S(2)}, u32[]{:S(2)}) collective-permute-start(bf16[3,176,2048]{2,1,0:T(8,128)(2,1)S(1)} %pad_maximum_fusion.1), channel_id=1, source_target_pairs={{0,16},{16,0},{1,17},{17,1},{2,18},{18,2},{3,19},{19,3},{4,20},{20... | collective-permute-start | bytes 6488072 | tf_op jit(solution)/shard_map/ppermute | solution.py:106
  107.9 4.3 %copy-start.5 = (bf16[176,2048]{1,0:T(8,128)(2,1)S(1)}, bf16[176,2048]{1,0:T(8,128)(2,1)}, u32[]{:S(2)}) copy-start(bf16[176,2048]{1,0:T(8,128)(2,1)} %copy-done.4) | copy-start | bytes 2162692
  107.9 9.9 %collective-permute-start.9 = (bf16[96,2048]{1,0:T(8,128)(2,1)S(1)}, bf16[96,2048]{1,0:T(8,128)(2,1)S(1)}, u32[]{:S(2)}, u32[]{:S(2)}) collective-permute-start(bf16[96,2048]{1,0:T(8,128)(2,1)S(1)} %pad_maximum_fusion.8), channel_id=1, source_target_pairs={{0,448},{16,80},{64,0},{80,144},{128,64},{144,208},{192,128},{208,... | collective-permute-start | bytes 1179656 | tf_op jit(solution)/shard_map/ppermute | solution.py:22
  117.9 9.7 %collective-permute-start.10 = (bf16[96,2048]{1,0:T(8,128)(2,1)S(1)}, bf16[96,2048]{1,0:T(8,128)(2,1)S(1)}, u32[]{:S(2)}, u32[]{:S(2)}) collective-permute-start(bf16[96,2048]{1,0:T(8,128)(2,1)S(1)} %pad_maximum_fusion.9), channel_id=1, source_target_pairs={{0,448},{16,80},{64,0},{80,144},{128,64},{144,208},{192,128},{208,... | collective-permute-start | bytes 1179656 | tf_op jit(solution)/shard_map/ppermute | solution.py:22
  127.6 5.5 %collective-permute-start.12 = (bf16[48,2048]{1,0:T(8,128)(2,1)S(1)}, bf16[48,2048]{1,0:T(8,128)(2,1)S(1)}, u32[]{:S(2)}, u32[]{:S(2)}) collective-permute-start(bf16[48,2048]{1,0:T(8,128)(2,1)S(1)} %slice.208), channel_id=1, source_target_pairs={{0,16},{16,0},{1,17},{17,1},{2,18},{18,2},{3,19},{19,3},{4,20},{20... | collective-permute-start | bytes 589832 | tf_op jit(solution)/shard_map/ppermute | solution.py:117
  130.2 8.3 %collective-permute-start.11 = (bf16[48,2048]{1,0:T(8,128)(2,1)S(1)}, bf16[48,2048]{1,0:T(8,128)(2,1)S(1)}, u32[]{:S(2)}, u32[]{:S(2)}) collective-permute-start(bf16[48,2048]{1,0:T(8,128)(2,1)S(1)} %fusion.19), channel_id=1, source_target_pairs={{0,448},{16,80},{64,0},{80,144},{128,64},{144,208},{192,128},{208,... | collective-permute-start | bytes 589832 | tf_op jit(solution)/shard_map/ppermute | solution.py:22
  133.2 5.8 %copy-start.8 = (bf16[3,176,2048]{2,1,0:T(8,128)(2,1)}, bf16[3,176,2048]{2,1,0:T(8,128)(2,1)S(1)}, u32[]{:S(2)}) copy-start(bf16[3,176,2048]{2,1,0:T(8,128)(2,1)S(1)} %collective-permute-done.7) | copy-start | bytes 6488068
  139.7 16.4 %all-to-all-start.1 = ((bf16[32,24,128]{2,1,0:T(8,128)(2,1)}), bf16[32,24,128]{2,1,0:T(8,128)(2,1)S(1)}, u32[]{:S(2)}, u32[]{:S(2)}) async-start(bf16[32,24,128]{2,1,0:T(8,128)(2,1)} %bitcast.23), calls=%async_computation.1 | async-start | bytes 393216 | tf_op jit(solution)/shard_map/all_to_all | solution.py:122
  146.7 2.0 %slice-start.2 = ((f32[352,2048]{1,0:T(8,128)}), f32[176,2048]{1,0:T(8,128)S(1)}, s32[]{:S(2)}) async-start(f32[352,2048]{1,0:T(8,128)} %copy-done.3), calls=%async_computation.4 | async-start | bytes 2883584 | tf_op jit(solution)/shard_map/slice | solution.py:128
  148.5 1.5 slice-start
  149.8 1.4 slice-start.1

commit v8 on v7

--- a/solution.py
+++ b/solution.py
@@ -79,6 +79,7 @@
     for rows in (packet, one, two, three, four):
         half = rows.shape[0] // 2
         chunks.append((rows[:half], rows[half:]))
+    chunks = [tuple(jnp.concatenate(both, axis=0) for both in zip(*chunks[:2])), *chunks[2:]]
 
     cols = ((1,), (1,))
     terms, hiddens, d_gates, d_ups = [], [], [], []
@@ -104,6 +105,8 @@
         dot(jnp.concatenate(hiddens, axis=0), dy_all, rows),
     ]
     received = lax.ppermute(jnp.stack([grad[PAD:].astype(BF) for grad in grads]), "core", SWAP)
+
+    terms = [terms[0][:near], terms[0][near:], *terms[1:]]
 
     home = jnp.concatenate([terms[4].astype(BF), terms[3][near:].astype(BF)], axis=0)
     home = ring(home, -1)

time: 159 us -> 159 us (level)
  waiting for transfers between devices: 47.9 us -> 37.7 us
  starting transfers between devices: 72.4 us -> 78.8 us
  other arithmetic: 6.76 us -> 10.9 us
  matrix products: 18.4 us -> 16.2 us
    ppermute x9, waiting for transfers between devices: 41.6 us -> 32.8 us  [ring(): return lax.ppermute(a, ('z', 'core'), pairs)]
    ppermute x1, starting transfers between devices: 2.46 us -> 7.62 us  [local(): last_b = lax.ppermute(home[near:], 'core', SWAP)]
    unnamed x2 -> x3, other arithmetic: 0.06 us -> 3.21 us
    all_to_all x1, waiting for transfers between devices: 2.45 us -> 0.01 us  [local(): dy_slices = lax.all_to_all(dy_slices, ('xh',) + EXPERT, 0, 0, tiled=True)]
    all_to_all x1, starting transfers between devices: 7.02 us -> 9.44 us  [local(): summed = lax.all_to_all(summed, ('xh',) + EXPERT, 0, 0, tiled=True)]
    dot_general x31 -> x26, matrix products: 18.4 us -> 16.2 us  [dot(): return lax.dot_general(a, b, (dims, ((), ())), preferred_element_type=F32)]
    unnamed x35 -> x27, local copies, waits for them, and re-layouts: 3.67 us -> 3.66 us
  transfers between devices with their start and end apart: 15 -> 15, of which waited for: 10 -> 8; matrix products, arithmetic and copies ran while one was open for 13% -> 18% of each run, Pallas kernels for 0% -> 0%
where the time goes in v8:
time: 159 us; the launch traced here: 156 us
  starting transfers between devices  78.8 us (50%)
  waiting for transfers between devices  37.7 us (24%)
  matrix products  16.2 us (10%)
  local copies, waits for them, and re-layouts  11.5 us (7%)
  other arithmetic  10.9 us (7%)
    ppermute x9, starting transfers between devices, ring(): return lax.ppermute(a, ('z', 'core'), pairs)  38 us
    ppermute x9, waiting for transfers between devices, ring(): return lax.ppermute(a, ('z', 'core'), pairs)  32.8 us
    dot_general x26, matrix products, dot(): return lax.dot_general(a, b, (dims, ((), ())), preferred_element_type=F32)  16.2 us
    all_to_all x1, starting transfers between devices, local(): summed = lax.all_to_all(summed, ('xh',) + EXPERT, 0, 0, tiled=True)  9.44 us
    all_to_all x1, starting transfers between devices, local(): dy_slices = lax.all_to_all(dy_slices, ('xh',) + EXPERT, 0, 0, tiled=True)  7.9 us
    ppermute x1, starting transfers between devices, local(): last_b = lax.ppermute(home[near:], 'core', SWAP)  7.62 us
    ppermute x1, starting transfers between devices, local(): lax.ppermute(jnp.stack([grad[PAD:].astype(BF) for grad in grads]), 'core'...  7.15 us
    ppermute x1, starting transfers between devices, local(): x_across = lax.ppermute(x_own, 'xh', SWAP)  5.48 us
  transfers between devices with their start and end apart: 15, of which 8 were waited for; matrix products, arithmetic and copies ran while one was open for 18% of the time, Pallas kernels for 0%

profile of v8, /device:TPU:1, one launch (start us, length us, event | category | flops | bytes accessed | tf_op | source)
XLA Modules:
  0.0 156.3 jit_solution(1135705619478542030)
XLA Ops:
  0.7 0.8 multiply_add_fusion
  2.2 5.5 %collective-permute-start = (bf16[24,2048]{1,0:T(8,128)(2,1)S(1)}, bf16[24,2048]{1,0:T(8,128)(2,1)}, u32[]{:S(2)}, u32[]{:S(2)}) collective-permute-start(bf16[24,2048]{1,0:T(8,128)(2,1)S(1)} %convolution_convert_fusion), channel_id=1, source_target_pairs={{0,32},{32,0},{1,33},{33,1},{2,34},{34,2},{3,35},{35,3},{4,36},{36... | collective-permute-start | bytes 294920 | tf_op jit(solution)/shard_map/ppermute | solution.py:59
  7.7 1.7 %convolution_convert_fusion.1 = bf16[768,128]{1,0:T(8,128)(2,1)} fusion(s32[128]{0:T(128)S(1)} %compare_select_fusion, s32[768]{0:T(1024)S(1)} %fusion.88, bf16[128,128]{1,0:T(8,128)(2,1)} %param.9, f32[128]{0:T(128)} %param.12), kind=kOutput, calls=%fused_computation.20 | convolution fusion | flops 25411584 | bytes 233472 | tf_op jit(solution)/shard_map/dot_general | solution.py:26
  9.4 7.9 %all-to-all-start = ((bf16[32,24,128]{2,1,0:T(8,128)(2,1)}), bf16[32,24,128]{2,1,0:T(8,128)(2,1)}, u32[]{:S(2)}, u32[]{:S(2)}) async-start(bf16[32,24,128]{2,1,0:T(8,128)(2,1)} %bitcast), calls=%async_computation | async-start | bytes 393216 | tf_op jit(solution)/shard_map/all_to_all | solution.py:62
  17.4 2.6 %fusion.104 = (bf16[176,2048]{1,0:T(8,128)(2,1)S(1)}, bf16[1,176,2048]{2,1,0:T(8,128)(2,1)S(1)}, bf16[1,176,2048]{2,1,0:T(8,128)(2,1)S(1)}, bf16[176,2048]{1,0:T(8,128)(2,1)}) fusion(bf16[172,2048]{1,0:T(8,128)(2,1)} %bitcast.75, bf16[172,2048]{1,0:T(8,128)(2,1)} %bitcast.76), kind=kLoop, calls=%fused_computation.191 | loop fusion | bytes 4292608 | tf_op jit(solution)/shard_map/jit(_pad)/pad | solution.py:52
  20.0 1.6 %pad_maximum_fusion = bf16[3,176,2048]{2,1,0:T(8,128)(2,1)} fusion(bf16[1,176,2048]{2,1,0:T(8,128)(2,1)S(1)} %get-tuple-element.52, bf16[1,176,2048]{2,1,0:T(8,128)(2,1)S(1)} %get-tuple-element.25, bf16[1,176,2048]{2,1,0:T(8,128)(2,1)S(1)} %get-tuple-element.29), kind=kLoop, calls=%fused_computation.6 | loop fusion | flops 2162688 | bytes 4325376 | tf_op jit(solution)/shard_map/stack | solution.py:52
  21.6 3.1 %collective-permute-start.3 = (bf16[3,176,2048]{2,1,0:T(8,128)(2,1)}, bf16[3,176,2048]{2,1,0:T(8,128)(2,1)}, u32[]{:S(2)}, u32[]{:S(2)}) collective-permute-start(bf16[3,176,2048]{2,1,0:T(8,128)(2,1)} %pad_maximum_fusion), channel_id=1, source_target_pairs={{0,16},{16,0},{1,17},{17,1},{2,18},{18,2},{3,19},{19,3},{4,20},{20... | collective-permute-start | bytes 6488072 | tf_op jit(solution)/shard_map/ppermute | solution.py:53
  24.8 1.6 constant_dynamic-update-slice_fusion.2
  26.3 1.6 constant_dynamic-update-slice_fusion.1
  27.9 1.0 copy.13
  28.9 1.0 pad_maximum_fusion.6
  29.9 5.6 %collective-permute-start.2 = (bf16[96,2048]{1,0:T(8,128)(2,1)S(1)}, bf16[96,2048]{1,0:T(8,128)(2,1)S(1)}, u32[]{:S(2)}, u32[]{:S(2)}) collective-permute-start(bf16[96,2048]{1,0:T(8,128)(2,1)S(1)} %pad_maximum_fusion.6), channel_id=1, source_target_pairs={{0,464},{16,64},{64,16},{80,128},{128,80},{144,192},{192,144},{208... | collective-permute-start | bytes 1179656 | tf_op jit(solution)/shard_map/ppermute | solution.py:22
  35.4 7.0 %collective-permute-start.1 = (bf16[96,2048]{1,0:T(8,128)(2,1)S(1)}, bf16[96,2048]{1,0:T(8,128)(2,1)S(1)}, u32[]{:S(2)}, u32[]{:S(2)}) collective-permute-start(bf16[96,2048]{1,0:T(8,128)(2,1)S(1)} %pad_maximum_fusion.6), channel_id=1, source_target_pairs={{0,64},{16,464},{64,128},{80,16},{128,192},{144,80},{192,256},{208... | collective-permute-start | bytes 1179656 | tf_op jit(solution)/shard_map/ppermute | solution.py:22
  42.6 7.5 %collective-permute-done.1 = bf16[96,2048]{1,0:T(8,128)(2,1)S(1)} collective-permute-done((bf16[96,2048]{1,0:T(8,128)(2,1)S(1)}, bf16[96,2048]{1,0:T(8,128)(2,1)S(1)}, u32[]{:S(2)}, u32[]{:S(2)}) %collective-permute-start.1) | collective-permute-done | bytes 393248 | tf_op jit(solution)/shard_map/ppermute | solution.py:22
  50.1 0.8 slice_reduce_fusion
  51.0 5.0 %collective-permute-start.4 = (bf16[192,2048]{1,0:T(8,128)(2,1)S(1)}, bf16[192,2048]{1,0:T(8,128)(2,1)S(1)}, u32[]{:S(2)}, u32[]{:S(2)}) collective-permute-start(bf16[192,2048]{1,0:T(8,128)(2,1)S(1)} %maximum_add_fusion), channel_id=1, source_target_pairs={{0,64},{16,464},{64,128},{80,16},{128,192},{144,80},{192,256},{208... | collective-permute-start | bytes 2359304 | tf_op jit(solution)/shard_map/ppermute | solution.py:22
  56.1 1.7 %slice_bitcast_fusion.4 = (bf16[176,2048]{1,0:T(8,128)(2,1)S(1)}, bf16[176,2048]{1,0:T(8,128)(2,1)S(1)}, bf16[176,2048]{1,0:T(8,128)(2,1)S(1)}) fusion(bf16[3,176,2048]{2,1,0:T(8,128)(2,1)} %collective-permute-done.3), kind=kLoop, calls=%fused_computation.33 | loop fusion | bytes 4325376 | tf_op jit(solution)/shard_map/squeeze | solution.py:55
  57.9 0.8 copy-done.8
  58.7 0.6 fusion.60
  59.3 0.6 fusion.61
  60.0 0.5 copy-done.7
  60.4 0.6 multiply_convert_fusion.1
  61.1 3.9 %collective-permute-done.4 = bf16[192,2048]{1,0:T(8,128)(2,1)S(1)} collective-permute-done((bf16[192,2048]{1,0:T(8,128)(2,1)S(1)}, bf16[192,2048]{1,0:T(8,128)(2,1)S(1)}, u32[]{:S(2)}, u32[]{:S(2)}) %collective-permute-start.4) | collective-permute-done | bytes 786464 | tf_op jit(solution)/shard_map/ppermute | solution.py:22
  65.0 0.6 fusion.32
  65.6 0.6 fusion.34
  66.1 5.0 %collective-permute-start.5 = (bf16[192,2048]{1,0:T(8,128)(2,1)S(1)}, bf16[192,2048]{1,0:T(8,128)(2,1)S(1)}, u32[]{:S(2)}, u32[]{:S(2)}) collective-permute-start(bf16[192,2048]{1,0:T(8,128)(2,1)S(1)} %collective-permute-done.4), channel_id=1, source_target_pairs={{0,64},{16,464},{64,128},{80,16},{128,192},{144,80},{192,256},{208... | collective-permute-start | bytes 2359304 | tf_op jit(solution)/shard_map/ppermute | solution.py:22
  71.2 0.6 multiply_convert_fusion.6
  71.8 0.4 fusion.101
  72.2 0.4 convolution_add_fusion.2
  72.7 7.4 %collective-permute-done.5 = bf16[192,2048]{1,0:T(8,128)(2,1)S(1)} collective-permute-done((bf16[192,2048]{1,0:T(8,128)(2,1)S(1)}, bf16[192,2048]{1,0:T(8,128)(2,1)S(1)}, u32[]{:S(2)}, u32[]{:S(2)}) %collective-permute-start.5) | collective-permute-done | bytes 786464 | tf_op jit(solution)/shard_map/ppermute | solution.py:22
  80.1 5.0 %collective-permute-start.6 = (bf16[96,2048]{1,0:T(8,128)(2,1)S(1)}, bf16[96,2048]{1,0:T(8,128)(2,1)S(1)}, u32[]{:S(2)}, u32[]{:S(2)}) collective-permute-start(bf16[96,2048]{1,0:T(8,128)(2,1)S(1)} %pad_maximum_fusion.7), channel_id=1, source_target_pairs={{0,64},{16,464},{64,128},{80,16},{128,192},{144,80},{192,256},{208... | collective-permute-start | bytes 1179656 | tf_op jit(solution)/shard_map/ppermute | solution.py:22
  85.2 0.6 fusion.28
  85.8 0.6 fusion.30
  86.3 0.6 multiply_convert_fusion.5
  86.9 0.4 fusion.100
  87.4 0.4 convolution_add_fusion.1
  87.9 2.0 %collective-permute-done.6 = bf16[96,2048]{1,0:T(8,128)(2,1)S(1)} collective-permute-done((bf16[96,2048]{1,0:T(8,128)(2,1)S(1)}, bf16[96,2048]{1,0:T(8,128)(2,1)S(1)}, u32[]{:S(2)}, u32[]{:S(2)}) %collective-permute-start.6) | collective-permute-done | bytes 393248 | tf_op jit(solution)/shard_map/ppermute | solution.py:22
  89.9 0.6 fusion.70
  90.4 0.6 fusion.72
  91.0 0.6 multiply_convert_fusion.10
  91.6 0.4 fusion.99
  92.0 0.4 fusion
  92.4 2.1 %collective-permute-start.8 = (bf16[96,2048]{1,0:T(8,128)(2,1)S(1)}, bf16[96,2048]{1,0:T(8,128)(2,1)S(1)}, u32[]{:S(2)}, u32[]{:S(2)}) collective-permute-start(bf16[96,2048]{1,0:T(8,128)(2,1)S(1)} %pad_maximum_fusion.8), channel_id=1, source_target_pairs={{0,448},{16,80},{64,0},{80,144},{128,64},{144,208},{192,128},{208,... | collective-permute-start | bytes 1179656 | tf_op jit(solution)/shard_map/ppermute | solution.py:22
  94.5 0.9 fusion.52
  95.6 0.9 fusion.36
  96.6 0.9 fusion.44
  97.9 7.1 %collective-permute-start.7 = (bf16[3,176,2048]{2,1,0:T(8,128)(2,1)S(1)}, bf16[3,176,2048]{2,1,0:T(8,128)(2,1)S(1)}, u32[]{:S(2)}, u32[]{:S(2)}) collective-permute-start(bf16[3,176,2048]{2,1,0:T(8,128)(2,1)S(1)} %pad_maximum_fusion.1), channel_id=1, source_target_pairs={{0,16},{16,0},{1,17},{17,1},{2,18},{18,2},{3,19},{19,3},{4,20},{20... | collective-permute-start | bytes 6488072 | tf_op jit(solution)/shard_map/ppermute | solution.py:107
  105.2 3.6 %collective-permute-start.9 = (bf16[96,2048]{1,0:T(8,128)(2,1)S(1)}, bf16[96,2048]{1,0:T(8,128)(2,1)S(1)}, u32[]{:S(2)}, u32[]{:S(2)}) collective-permute-start(bf16[96,2048]{1,0:T(8,128)(2,1)S(1)} %pad_maximum_fusion.9), channel_id=1, source_target_pairs={{0,448},{16,80},{64,0},{80,144},{128,64},{144,208},{192,128},{208,... | collective-permute-start | bytes 1179656 | tf_op jit(solution)/shard_map/ppermute | solution.py:22
  108.9 0.5 fusion.102
  109.4 0.5 convolution_add_fusion
  109.9 5.1 %collective-permute-done.9 = bf16[96,2048]{1,0:T(8,128)(2,1)S(1)} collective-permute-done((bf16[96,2048]{1,0:T(8,128)(2,1)S(1)}, bf16[96,2048]{1,0:T(8,128)(2,1)S(1)}, u32[]{:S(2)}, u32[]{:S(2)}) %collective-permute-start.9) | collective-permute-done | bytes 393248 | tf_op jit(solution)/shard_map/ppermute | solution.py:22
  115.1 2.7 %collective-permute-start.10 = (bf16[96,2048]{1,0:T(8,128)(2,1)S(1)}, bf16[96,2048]{1,0:T(8,128)(2,1)S(1)}, u32[]{:S(2)}, u32[]{:S(2)}) collective-permute-start(bf16[96,2048]{1,0:T(8,128)(2,1)S(1)} %pad_maximum_fusion.10), channel_id=1, source_target_pairs={{0,448},{16,80},{64,0},{80,144},{128,64},{144,208},{192,128},{208,... | collective-permute-start | bytes 1179656 | tf_op jit(solution)/shard_map/ppermute | solution.py:22
  117.9 7.0 %collective-permute-done.10 = bf16[96,2048]{1,0:T(8,128)(2,1)S(1)} collective-permute-done((bf16[96,2048]{1,0:T(8,128)(2,1)S(1)}, bf16[96,2048]{1,0:T(8,128)(2,1)S(1)}, u32[]{:S(2)}, u32[]{:S(2)}) %collective-permute-start.10) | collective-permute-done | bytes 393248 | tf_op jit(solution)/shard_map/ppermute | solution.py:22
  124.9 1.9 %collective-permute-start.11 = (bf16[48,2048]{1,0:T(8,128)(2,1)S(1)}, bf16[48,2048]{1,0:T(8,128)(2,1)S(1)}, u32[]{:S(2)}, u32[]{:S(2)}) collective-permute-start(bf16[48,2048]{1,0:T(8,128)(2,1)S(1)} %fusion.18), channel_id=1, source_target_pairs={{0,448},{16,80},{64,0},{80,144},{128,64},{144,208},{192,128},{208,... | collective-permute-start | bytes 589832 | tf_op jit(solution)/shard_map/ppermute | solution.py:22
  126.8 7.6 %collective-permute-start.12 = (bf16[48,2048]{1,0:T(8,128)(2,1)S(1)}, bf16[48,2048]{1,0:T(8,128)(2,1)S(1)}, u32[]{:S(2)}, u32[]{:S(2)}) collective-permute-start(bf16[48,2048]{1,0:T(8,128)(2,1)S(1)} %slice.216), channel_id=1, source_target_pairs={{0,16},{16,0},{1,17},{17,1},{2,18},{18,2},{3,19},{19,3},{4,20},{20... | collective-permute-start | bytes 589832 | tf_op jit(solution)/shard_map/ppermute | solution.py:120
  134.5 1.0 collective-permute-done.12
  135.8 0.7 copy.14
  136.6 9.4 %all-to-all-start.1 = ((bf16[32,24,128]{2,1,0:T(8,128)(2,1)}), bf16[32,24,128]{2,1,0:T(8,128)(2,1)S(1)}, u32[]{:S(2)}, u32[]{:S(2)}) async-start(bf16[32,24,128]{2,1,0:T(8,128)(2,1)} %bitcast.23), calls=%async_computation.1 | async-start | bytes 393216 | tf_op jit(solution)/shard_map/all_to_all | solution.py:125
  146.0 1.8 %slice_bitcast_fusion = (bf16[176,2048]{1,0:T(8,128)(2,1)S(1)}, bf16[176,2048]{1,0:T(8,128)(2,1)S(1)}, bf16[176,2048]{1,0:T(8,128)(2,1)S(1)}) fusion(bf16[3,176,2048]{2,1,0:T(8,128)(2,1)} %copy-done.4), kind=kLoop, calls=%fused_computation.29 | loop fusion | bytes 4325376
  148.0 1.0 fusion.7
  149.4 1.1 fusion.9
  150.5 1.1 fusion.8
  151.5 3.9 %all-to-all-done.1 = bf16[32,24,128]{2,1,0:T(8,128)(2,1)S(1)} async-done(((bf16[32,24,128]{2,1,0:T(8,128)(2,1)}), bf16[32,24,128]{2,1,0:T(8,128)(2,1)S(1)}, u32[]{:S(2)}, u32[]{:S(2)}) %all-to-all-start.1) | async-done | bytes 196640 | tf_op jit(solution)/shard_map/all_to_all | solution.py:125
  155.4 0.9 convolution_convert_fusion.2
  (65 shorter events, 3.3 us)
Async XLA Ops:
  0.6 1.3 copy-start
  0.6 16.7 %copy-start.6 = (bf16[1,172,2048]{2,1,0:T(8,128)(2,1)S(1)}, bf16[1,172,2048]{2,1,0:T(8,128)(2,1)}, u32[]{:S(2)}) copy-start(bf16[1,172,2048]{2,1,0:T(8,128)(2,1)} %param.13) | copy-start | bytes 2113540
  2.1 17.9 %copy-start.5 = (bf16[24,2048]{1,0:T(8,128)(2,1)}, bf16[24,2048]{1,0:T(8,128)(2,1)S(1)}, u32[]{:S(2)}) copy-start(bf16[24,2048]{1,0:T(8,128)(2,1)S(1)} %convolution_convert_fusion) | copy-start | bytes 294916
  2.2 22.6 %collective-permute-start = (bf16[24,2048]{1,0:T(8,128)(2,1)S(1)}, bf16[24,2048]{1,0:T(8,128)(2,1)}, u32[]{:S(2)}, u32[]{:S(2)}) collective-permute-start(bf16[24,2048]{1,0:T(8,128)(2,1)S(1)} %convolution_convert_fusion), channel_id=1, source_target_pairs={{0,32},{32,0},{1,33},{33,1},{2,34},{34,2},{3,35},{35,3},{4,36},{36... | collective-permute-start | bytes 294920 | tf_op jit(solution)/shard_map/ppermute | solution.py:59
  9.4 18.5 %all-to-all-start = ((bf16[32,24,128]{2,1,0:T(8,128)(2,1)}), bf16[32,24,128]{2,1,0:T(8,128)(2,1)}, u32[]{:S(2)}, u32[]{:S(2)}) async-start(bf16[32,24,128]{2,1,0:T(8,128)(2,1)} %bitcast), calls=%async_computation | async-start | bytes 393216 | tf_op jit(solution)/shard_map/all_to_all | solution.py:62
  21.6 28.5 %collective-permute-start.3 = (bf16[3,176,2048]{2,1,0:T(8,128)(2,1)}, bf16[3,176,2048]{2,1,0:T(8,128)(2,1)}, u32[]{:S(2)}, u32[]{:S(2)}) collective-permute-start(bf16[3,176,2048]{2,1,0:T(8,128)(2,1)} %pad_maximum_fusion), channel_id=1, source_target_pairs={{0,16},{16,0},{1,17},{17,1},{2,18},{18,2},{3,19},{19,3},{4,20},{20... | collective-permute-start | bytes 6488072 | tf_op jit(solution)/shard_map/ppermute | solution.py:53
  29.9 12.7 %collective-permute-start.2 = (bf16[96,2048]{1,0:T(8,128)(2,1)S(1)}, bf16[96,2048]{1,0:T(8,128)(2,1)S(1)}, u32[]{:S(2)}, u32[]{:S(2)}) collective-permute-start(bf16[96,2048]{1,0:T(8,128)(2,1)S(1)} %pad_maximum_fusion.6), channel_id=1, source_target_pairs={{0,464},{16,64},{64,16},{80,128},{128,80},{144,192},{192,144},{208... | collective-permute-start | bytes 1179656 | tf_op jit(solution)/shard_map/ppermute | solution.py:22
  35.4 14.6 %collective-permute-start.1 = (bf16[96,2048]{1,0:T(8,128)(2,1)S(1)}, bf16[96,2048]{1,0:T(8,128)(2,1)S(1)}, u32[]{:S(2)}, u32[]{:S(2)}) collective-permute-start(bf16[96,2048]{1,0:T(8,128)(2,1)S(1)} %pad_maximum_fusion.6), channel_id=1, source_target_pairs={{0,64},{16,464},{64,128},{80,16},{128,192},{144,80},{192,256},{208... | collective-permute-start | bytes 1179656 | tf_op jit(solution)/shard_map/ppermute | solution.py:22
  51.0 13.9 %collective-permute-start.4 = (bf16[192,2048]{1,0:T(8,128)(2,1)S(1)}, bf16[192,2048]{1,0:T(8,128)(2,1)S(1)}, u32[]{:S(2)}, u32[]{:S(2)}) collective-permute-start(bf16[192,2048]{1,0:T(8,128)(2,1)S(1)} %maximum_add_fusion), channel_id=1, source_target_pairs={{0,64},{16,464},{64,128},{80,16},{128,192},{144,80},{192,256},{208... | collective-permute-start | bytes 2359304 | tf_op jit(solution)/shard_map/ppermute | solution.py:22
  57.7 0.9 copy-start.8
  57.8 0.9 copy-start.9
  59.3 1.1 copy-start.7
  66.1 13.9 %collective-permute-start.5 = (bf16[192,2048]{1,0:T(8,128)(2,1)S(1)}, bf16[192,2048]{1,0:T(8,128)(2,1)S(1)}, u32[]{:S(2)}, u32[]{:S(2)}) collective-permute-start(bf16[192,2048]{1,0:T(8,128)(2,1)S(1)} %collective-permute-done.4), channel_id=1, source_target_pairs={{0,64},{16,464},{64,128},{80,16},{128,192},{144,80},{192,256},{208... | collective-permute-start | bytes 2359304 | tf_op jit(solution)/shard_map/ppermute | solution.py:22
  80.1 9.7 %collective-permute-start.6 = (bf16[96,2048]{1,0:T(8,128)(2,1)S(1)}, bf16[96,2048]{1,0:T(8,128)(2,1)S(1)}, u32[]{:S(2)}, u32[]{:S(2)}) collective-permute-start(bf16[96,2048]{1,0:T(8,128)(2,1)S(1)} %pad_maximum_fusion.7), channel_id=1, source_target_pairs={{0,64},{16,464},{64,128},{80,16},{128,192},{144,80},{192,256},{208... | collective-permute-start | bytes 1179656 | tf_op jit(solution)/shard_map/ppermute | solution.py:22
  92.4 12.7 %collective-permute-start.8 = (bf16[96,2048]{1,0:T(8,128)(2,1)S(1)}, bf16[96,2048]{1,0:T(8,128)(2,1)S(1)}, u32[]{:S(2)}, u32[]{:S(2)}) collective-permute-start(bf16[96,2048]{1,0:T(8,128)(2,1)S(1)} %pad_maximum_fusion.8), channel_id=1, source_target_pairs={{0,448},{16,80},{64,0},{80,144},{128,64},{144,208},{192,128},{208,... | collective-permute-start | bytes 1179656 | tf_op jit(solution)/shard_map/ppermute | solution.py:22
  95.5 22.4 %copy-start.1 = (f32[352,2048]{1,0:T(8,128)}, f32[352,2048]{1,0:T(8,128)S(1)}, u32[]{:S(2)}) copy-start(f32[352,2048]{1,0:T(8,128)S(1)} %fusion.52) | copy-start | bytes 8650756
  96.5 21.3 %copy-start.2 = (f32[352,2048]{1,0:T(8,128)}, f32[352,2048]{1,0:T(8,128)S(1)}, u32[]{:S(2)}) copy-start(f32[352,2048]{1,0:T(8,128)S(1)} %fusion.36) | copy-start | bytes 8650756
  97.6 20.3 %copy-start.3 = (f32[352,2048]{1,0:T(8,128)}, f32[352,2048]{1,0:T(8,128)S(1)}, u32[]{:S(2)}) copy-start(f32[352,2048]{1,0:T(8,128)S(1)} %fusion.44) | copy-start | bytes 8650756
  97.9 36.5 %collective-permute-start.7 = (bf16[3,176,2048]{2,1,0:T(8,128)(2,1)S(1)}, bf16[3,176,2048]{2,1,0:T(8,128)(2,1)S(1)}, u32[]{:S(2)}, u32[]{:S(2)}) collective-permute-start(bf16[3,176,2048]{2,1,0:T(8,128)(2,1)S(1)} %pad_maximum_fusion.1), channel_id=1, source_target_pairs={{0,16},{16,0},{1,17},{17,1},{2,18},{18,2},{3,19},{19,3},{4,20},{20... | collective-permute-start | bytes 6488072 | tf_op jit(solution)/shard_map/ppermute | solution.py:107
  105.2 9.7 %collective-permute-start.9 = (bf16[96,2048]{1,0:T(8,128)(2,1)S(1)}, bf16[96,2048]{1,0:T(8,128)(2,1)S(1)}, u32[]{:S(2)}, u32[]{:S(2)}) collective-permute-start(bf16[96,2048]{1,0:T(8,128)(2,1)S(1)} %pad_maximum_fusion.9), channel_id=1, source_target_pairs={{0,448},{16,80},{64,0},{80,144},{128,64},{144,208},{192,128},{208,... | collective-permute-start | bytes 1179656 | tf_op jit(solution)/shard_map/ppermute | solution.py:22
  115.1 9.7 %collective-permute-start.10 = (bf16[96,2048]{1,0:T(8,128)(2,1)S(1)}, bf16[96,2048]{1,0:T(8,128)(2,1)S(1)}, u32[]{:S(2)}, u32[]{:S(2)}) collective-permute-start(bf16[96,2048]{1,0:T(8,128)(2,1)S(1)} %pad_maximum_fusion.10), channel_id=1, source_target_pairs={{0,448},{16,80},{64,0},{80,144},{128,64},{144,208},{192,128},{208,... | collective-permute-start | bytes 1179656 | tf_op jit(solution)/shard_map/ppermute | solution.py:22
  124.9 9.6 %collective-permute-start.11 = (bf16[48,2048]{1,0:T(8,128)(2,1)S(1)}, bf16[48,2048]{1,0:T(8,128)(2,1)S(1)}, u32[]{:S(2)}, u32[]{:S(2)}) collective-permute-start(bf16[48,2048]{1,0:T(8,128)(2,1)S(1)} %fusion.18), channel_id=1, source_target_pairs={{0,448},{16,80},{64,0},{80,144},{128,64},{144,208},{192,128},{208,... | collective-permute-start | bytes 589832 | tf_op jit(solution)/shard_map/ppermute | solution.py:22
  126.8 8.7 %collective-permute-start.12 = (bf16[48,2048]{1,0:T(8,128)(2,1)S(1)}, bf16[48,2048]{1,0:T(8,128)(2,1)S(1)}, u32[]{:S(2)}, u32[]{:S(2)}) collective-permute-start(bf16[48,2048]{1,0:T(8,128)(2,1)S(1)} %slice.216), channel_id=1, source_target_pairs={{0,16},{16,0},{1,17},{17,1},{2,18},{18,2},{3,19},{19,3},{4,20},{20... | collective-permute-start | bytes 589832 | tf_op jit(solution)/shard_map/ppermute | solution.py:120
  134.5 1.3 copy-start.4
  136.6 18.8 %all-to-all-start.1 = ((bf16[32,24,128]{2,1,0:T(8,128)(2,1)}), bf16[32,24,128]{2,1,0:T(8,128)(2,1)S(1)}, u32[]{:S(2)}, u32[]{:S(2)}) async-start(bf16[32,24,128]{2,1,0:T(8,128)(2,1)} %bitcast.23), calls=%async_computation.1 | async-start | bytes 393216 | tf_op jit(solution)/shard_map/all_to_all | solution.py:125
  146.0 2.0 %slice-start.1 = ((f32[352,2048]{1,0:T(8,128)}), f32[176,2048]{1,0:T(8,128)S(1)}, s32[]{:S(2)}) async-start(f32[352,2048]{1,0:T(8,128)} %copy-done.2), calls=%async_computation.3 | async-start | bytes 2883584 | tf_op jit(solution)/shard_map/slice | solution.py:131
  147.8 1.5 slice-start
  149.0 1.4 slice-start.2

commit v9 on v7

--- a/solution.py
+++ b/solution.py
@@ -17,7 +17,7 @@
     pairs = []
     for z in range(Z):
         for c in range(CORE):
-            up = step * (1 - 2 * c) * (-1 if cross and step == 1 else 1)
+            up = step * (1 - 2 * c) * (-1 if cross and step > 0 else 1)
             pairs.append((z * CORE + c, (z + up) % Z * CORE + (c ^ cross)))
     return lax.ppermute(a, ("z", "core"), pairs)
 
@@ -73,16 +73,10 @@
     one = one + other_w[2, PAD - 1 :]
     two = ring(one, 1)
     three = ring(two, 1)
-    four = jnp.concatenate([three[:near], three[2 * near : 3 * near]], axis=0)
-    four = ring(four, 1)
-    chunks = []
-    for rows in (packet, one, two, three, four):
-        half = rows.shape[0] // 2
-        chunks.append((rows[:half], rows[half:]))
+    cols = ((1,), (1,))
+    hiddens, d_gates, d_ups, x_parts, dy_parts = [], [], [], [], []
 
-    cols = ((1,), (1,))
-    terms, hiddens, d_gates, d_ups = [], [], [], []
-    for x_rows, dy_rows in chunks:
+    def work(x_rows, dy_rows):
         gate_pre = dot(x_rows, wg, cols)
         up_pre = dot(x_rows, wu, cols)
         sig_gate = jax.nn.sigmoid(gate_pre)
@@ -93,10 +87,24 @@
         d_up = (d_hidden * silu_gate).astype(BF)
         d_gates.append(d_gate)
         d_ups.append(d_up)
-        terms.append(dot(d_gate, wg) + dot(d_up, wu))
+        x_parts.append(x_rows)
+        dy_parts.append(dy_rows)
+        return dot(d_gate, wg) + dot(d_up, wu)
 
-    x_all = jnp.concatenate([x for x, _ in chunks], axis=0)
-    dy_all = jnp.concatenate([dy for _, dy in chunks], axis=0)
+    terms_one = work(one[: 2 * near], one[2 * near :])
+    terms_two = work(
+        jnp.concatenate([two[: 2 * near], packet[:near]], axis=0),
+        jnp.concatenate([two[2 * near :], packet[near:]], axis=0),
+    )
+    terms_two, terms_own = terms_two[: 2 * near], terms_two[2 * near :]
+    one_home = ring(terms_one.astype(BF), -1)
+    four = jnp.concatenate([three[:near], three[2 * near : 3 * near]], axis=0)
+    four = ring(four + one_home[:1] * 0, 1)
+    terms_three = work(three[: 2 * near], three[2 * near :])
+    terms_four = work(four[:near], four[near:])
+
+    x_all = jnp.concatenate(x_parts, axis=0)
+    dy_all = jnp.concatenate(dy_parts, axis=0)
     rows = ((0,), (0,))
     grads = [
         dot(jnp.concatenate(d_gates, axis=0), x_all, rows),
@@ -105,23 +113,21 @@
     ]
     received = lax.ppermute(jnp.stack([grad[PAD:].astype(BF) for grad in grads]), "core", SWAP)
 
-    home = jnp.concatenate([terms[4].astype(BF), terms[3][near:].astype(BF)], axis=0)
-    home = ring(home, -1)
-    home_a = (terms[3][:near] + home[:near].astype(F32)).astype(BF)
-    home_b = (terms[2][near:] + home[near:].astype(F32)).astype(BF)
-    home = ring(jnp.concatenate([home_a, home_b], axis=0), -1)
-    home_a = (terms[2][:near] + home[:near].astype(F32)).astype(BF)
-    home_b = (terms[1][near:] + home[near:].astype(F32)).astype(BF)
-    home = ring(jnp.concatenate([home_a, home_b], axis=0), -1)
-    last_a = ring((terms[1][:near] + home[:near].astype(F32)).astype(BF), -1)
-    last_b = lax.ppermute(home[near:], "core", SWAP)
-    summed = terms[0] + last_a.astype(F32) + last_b.astype(F32)
-    summed = summed + received[2, PAD - 1 :].astype(F32)
+    three_near = ring(terms_three.astype(BF), -1)
+    four_near = ring(terms_four.astype(BF), -2)
+    home_b = terms_two[near:] + three_near[near:].astype(F32)
+    home_b = ring(home_b.astype(BF), -2)
+    home_a = terms_two[:near] + three_near[:near].astype(F32) + four_near.astype(F32)
+    home_a = ring(home_a.astype(BF), -2)
+    crossing = one_home[near:].astype(F32) + home_b.astype(F32)
+    crossing = lax.ppermute(crossing.astype(BF), "core", SWAP)
+    summed = terms_own + one_home[:near].astype(F32) + crossing.astype(F32) + home_a.astype(F32)
     summed = summed.reshape(XH, capacity, XL * Y, -1)
     summed = jnp.transpose(summed, (0, 2, 1, 3)).astype(BF).reshape(XH * XL * Y, capacity, -1)
     summed = lax.all_to_all(summed, ("xh",) + EXPERT, 0, 0, tiled=True)
 
     place = (slot[:, None] == all_slots[None, :]).astype(BF)
+    place = place + received[2, PAD - 1, 0]
     grad_tokens = dot(place, summed.reshape(all_slots.shape[0], -1)).astype(BF)
 
     outs = [

time: 159 us -> 158 us (level)
  the two profiles are of different devices: /device:TPU:1 before, /device:TPU:64 now
where the time goes in v9:
time: 158 us; the launch traced here: 157 us
  starting transfers between devices  67.8 us (43%)
  waiting for transfers between devices  51.6 us (33%)
  matrix products  17 us (11%)
  local copies, waits for them, and re-layouts  11.1 us (7%)
  other arithmetic  8.19 us (5%)
    ppermute x10, starting transfers between devices, ring(): return lax.ppermute(a, ('z', 'core'), pairs)  41.1 us
    ppermute x10, waiting for transfers between devices, ring(): return lax.ppermute(a, ('z', 'core'), pairs)  28.9 us
    dot_general x26, matrix products, dot(): return lax.dot_general(a, b, (dims, ((), ())), preferred_element_type=F32)  17 us
    all_to_all x1, waiting for transfers between devices, local(): dy_slices = lax.all_to_all(dy_slices, ('xh',) + EXPERT, 0, 0, tiled=True)  12 us
    all_to_all x1, waiting for transfers between devices, local(): summed = lax.all_to_all(summed, ('xh',) + EXPERT, 0, 0, tiled=True)  10.7 us
    all_to_all x1, starting transfers between devices, local(): dy_slices = lax.all_to_all(dy_slices, ('xh',) + EXPERT, 0, 0, tiled=True)  8.07 us
    all_to_all x1, starting transfers between devices, local(): summed = lax.all_to_all(summed, ('xh',) + EXPERT, 0, 0, tiled=True)  8 us
    ppermute x1, starting transfers between devices, local(): x_across = lax.ppermute(x_own, 'xh', SWAP)  4.93 us
  transfers between devices with their start and end apart: 16, of which 9 were waited for; matrix products, arithmetic and copies ran while one was open for 14% of the time, Pallas kernels for 0%

profile of v9, /device:TPU:64, one launch (start us, length us, event | category | flops | bytes accessed | tf_op | source)
XLA Modules:
  0.0 157.1 jit_solution(6864834039857622891)
XLA Ops:
  0.7 0.7 multiply_add_fusion
  2.1 4.9 %collective-permute-start = (bf16[24,2048]{1,0:T(8,128)(2,1)S(1)}, bf16[24,2048]{1,0:T(8,128)(2,1)S(1)}, u32[]{:S(2)}, u32[]{:S(2)}) collective-permute-start(bf16[24,2048]{1,0:T(8,128)(2,1)S(1)} %convolution_convert_fusion), channel_id=1, source_target_pairs={{0,32},{32,0},{1,33},{33,1},{2,34},{34,2},{3,35},{35,3},{4,36},{36... | collective-permute-start | bytes 294920 | tf_op jit(solution)/shard_map/ppermute | solution.py:59
  7.1 1.2 fusion.109
  8.5 1.6 %pad_maximum_fusion = bf16[3,176,2048]{2,1,0:T(8,128)(2,1)} fusion(bf16[1,176,2048]{2,1,0:T(8,128)(2,1)S(1)} %get-tuple-element.27, bf16[1,176,2048]{2,1,0:T(8,128)(2,1)S(1)} %get-tuple-element.23, bf16[1,176,2048]{2,1,0:T(8,128)(2,1)S(1)} %get-tuple-element.48), kind=kLoop, calls=%fused_computation.8 | loop fusion | flops 2162688 | bytes 4325376 | tf_op jit(solution)/shard_map/stack | solution.py:52
  10.1 1.9 %collective-permute-start.3 = (bf16[3,176,2048]{2,1,0:T(8,128)(2,1)}, bf16[3,176,2048]{2,1,0:T(8,128)(2,1)}, u32[]{:S(2)}, u32[]{:S(2)}) collective-permute-start(bf16[3,176,2048]{2,1,0:T(8,128)(2,1)} %pad_maximum_fusion), channel_id=1, source_target_pairs={{0,16},{16,0},{1,17},{17,1},{2,18},{18,2},{3,19},{19,3},{4,20},{20... | collective-permute-start | bytes 6488072 | tf_op jit(solution)/shard_map/ppermute | solution.py:53
  12.1 1.0 convolution_convert_fusion.1
  13.1 8.1 %all-to-all-start = ((bf16[32,24,128]{2,1,0:T(8,128)(2,1)}), bf16[32,24,128]{2,1,0:T(8,128)(2,1)S(1)}, u32[]{:S(2)}, u32[]{:S(2)}) async-start(bf16[32,24,128]{2,1,0:T(8,128)(2,1)} %bitcast), calls=%async_computation | async-start | bytes 393216 | tf_op jit(solution)/shard_map/all_to_all | solution.py:62
  21.2 12.0 %all-to-all-done = bf16[32,24,128]{2,1,0:T(8,128)(2,1)S(1)} async-done(((bf16[32,24,128]{2,1,0:T(8,128)(2,1)}), bf16[32,24,128]{2,1,0:T(8,128)(2,1)S(1)}, u32[]{:S(2)}, u32[]{:S(2)}) %all-to-all-start) | async-done | bytes 196640 | tf_op jit(solution)/shard_map/all_to_all | solution.py:62
  33.3 1.9 %collective-permute-start.2 = (bf16[96,2048]{1,0:T(8,128)(2,1)S(1)}, bf16[96,2048]{1,0:T(8,128)(2,1)S(1)}, u32[]{:S(2)}, u32[]{:S(2)}) collective-permute-start(bf16[96,2048]{1,0:T(8,128)(2,1)S(1)} %pad_maximum_fusion.6), channel_id=1, source_target_pairs={{0,464},{16,64},{64,16},{80,128},{128,80},{144,192},{192,144},{208... | collective-permute-start | bytes 1179656 | tf_op jit(solution)/shard_map/ppermute | solution.py:22
  35.2 4.3 %collective-permute-start.1 = (bf16[96,2048]{1,0:T(8,128)(2,1)S(1)}, bf16[96,2048]{1,0:T(8,128)(2,1)S(1)}, u32[]{:S(2)}, u32[]{:S(2)}) collective-permute-start(bf16[96,2048]{1,0:T(8,128)(2,1)S(1)} %pad_maximum_fusion.6), channel_id=1, source_target_pairs={{0,64},{16,464},{64,128},{80,16},{128,192},{144,80},{192,256},{208... | collective-permute-start | bytes 1179656 | tf_op jit(solution)/shard_map/ppermute | solution.py:22
  39.5 2.9 %collective-permute-done.2 = bf16[96,2048]{1,0:T(8,128)(2,1)S(1)} collective-permute-done((bf16[96,2048]{1,0:T(8,128)(2,1)S(1)}, bf16[96,2048]{1,0:T(8,128)(2,1)S(1)}, u32[]{:S(2)}, u32[]{:S(2)}) %collective-permute-start.2) | collective-permute-done | bytes 393248 | tf_op jit(solution)/shard_map/ppermute | solution.py:22
  42.4 6.7 %collective-permute-done.1 = bf16[96,2048]{1,0:T(8,128)(2,1)S(1)} collective-permute-done((bf16[96,2048]{1,0:T(8,128)(2,1)S(1)}, bf16[96,2048]{1,0:T(8,128)(2,1)S(1)}, u32[]{:S(2)}, u32[]{:S(2)}) %collective-permute-start.1) | collective-permute-done | bytes 393248 | tf_op jit(solution)/shard_map/ppermute | solution.py:22
  49.2 0.8 slice_reduce_fusion
  50.1 1.9 %collective-permute-start.4 = (bf16[192,2048]{1,0:T(8,128)(2,1)S(1)}, bf16[192,2048]{1,0:T(8,128)(2,1)S(1)}, u32[]{:S(2)}, u32[]{:S(2)}) collective-permute-start(bf16[192,2048]{1,0:T(8,128)(2,1)S(1)} %maximum_add_fusion), channel_id=1, source_target_pairs={{0,64},{16,464},{64,128},{80,16},{128,192},{144,80},{192,256},{208... | collective-permute-start | bytes 2359304 | tf_op jit(solution)/shard_map/ppermute | solution.py:22
  52.0 1.7 %slice_bitcast_fusion.4 = (bf16[176,2048]{1,0:T(8,128)(2,1)S(1)}, bf16[176,2048]{1,0:T(8,128)(2,1)S(1)}, bf16[176,2048]{1,0:T(8,128)(2,1)S(1)}) fusion(bf16[3,176,2048]{2,1,0:T(8,128)(2,1)} %collective-permute-done.3), kind=kLoop, calls=%fused_computation.35 | loop fusion | bytes 4325376 | tf_op jit(solution)/shard_map/squeeze | solution.py:55
  53.7 0.6 fusion.25
  54.3 0.6 fusion.31
  54.9 0.6 multiply_convert_fusion.4
  55.5 0.4 fusion.105
  55.9 0.4 fusion
  56.4 5.1 %collective-permute-start.6 = (bf16[96,2048]{1,0:T(8,128)(2,1)S(1)}, bf16[96,2048]{1,0:T(8,128)(2,1)S(1)}, u32[]{:S(2)}, u32[]{:S(2)}) collective-permute-start(bf16[96,2048]{1,0:T(8,128)(2,1)S(1)} %fusion), channel_id=1, source_target_pairs={{0,448},{16,80},{64,0},{80,144},{128,64},{144,208},{192,128},{208,... | collective-permute-start | bytes 1179656 | tf_op jit(solution)/shard_map/ppermute | solution.py:22
  61.6 5.8 %collective-permute-done.6 = bf16[96,2048]{1,0:T(8,128)(2,1)S(1)} collective-permute-done((bf16[96,2048]{1,0:T(8,128)(2,1)S(1)}, bf16[96,2048]{1,0:T(8,128)(2,1)S(1)}, u32[]{:S(2)}, u32[]{:S(2)}) %collective-permute-start.6) | collective-permute-done | bytes 393248 | tf_op jit(solution)/shard_map/ppermute | solution.py:22
  67.5 0.6 fusion.59
  68.1 0.6 fusion.60
  68.8 0.6 multiply_convert_fusion.1
  69.4 5.6 %collective-permute-start.5 = (bf16[192,2048]{1,0:T(8,128)(2,1)S(1)}, bf16[192,2048]{1,0:T(8,128)(2,1)S(1)}, u32[]{:S(2)}, u32[]{:S(2)}) collective-permute-start(bf16[192,2048]{1,0:T(8,128)(2,1)S(1)} %collective-permute-done.4), channel_id=1, source_target_pairs={{0,64},{16,464},{64,128},{80,16},{128,192},{144,80},{192,256},{208... | collective-permute-start | bytes 2359304 | tf_op jit(solution)/shard_map/ppermute | solution.py:22
  75.1 0.5 fusion.104
  75.6 8.9 %collective-permute-done.5 = bf16[192,2048]{1,0:T(8,128)(2,1)S(1)} collective-permute-done((bf16[192,2048]{1,0:T(8,128)(2,1)S(1)}, bf16[192,2048]{1,0:T(8,128)(2,1)S(1)}, u32[]{:S(2)}, u32[]{:S(2)}) %collective-permute-start.5) | collective-permute-done | bytes 786464 | tf_op jit(solution)/shard_map/ppermute | solution.py:22
  84.6 5.1 %collective-permute-start.7 = (bf16[96,2048]{1,0:T(8,128)(2,1)S(1)}, bf16[96,2048]{1,0:T(8,128)(2,1)S(1)}, u32[]{:S(2)}, u32[]{:S(2)}) collective-permute-start(bf16[96,2048]{1,0:T(8,128)(2,1)S(1)} %maximum_add_fusion.1), channel_id=1, source_target_pairs={{0,64},{16,464},{64,128},{80,16},{128,192},{144,80},{192,256},{208... | collective-permute-start | bytes 1179656 | tf_op jit(solution)/shard_map/ppermute | solution.py:22
  89.8 0.6 fusion.27
  90.4 0.6 fusion.29
  91.0 0.6 multiply_convert_fusion.5
  91.5 0.4 fusion.103
  92.0 0.4 fusion.1
  92.4 1.9 %collective-permute-start.9 = (bf16[96,2048]{1,0:T(8,128)(2,1)S(1)}, bf16[96,2048]{1,0:T(8,128)(2,1)S(1)}, u32[]{:S(2)}, u32[]{:S(2)}) collective-permute-start(bf16[96,2048]{1,0:T(8,128)(2,1)S(1)} %fusion.1), channel_id=1, source_target_pairs={{0,448},{16,80},{64,0},{80,144},{128,64},{144,208},{192,128},{208,... | collective-permute-start | bytes 1179656 | tf_op jit(solution)/shard_map/ppermute | solution.py:22
  94.4 1.3 collective-permute-done.7
  95.8 0.6 fusion.71
  96.3 0.6 fusion.73
  96.9 0.6 multiply_convert_fusion.10
  97.5 0.4 fusion.102
  97.8 0.4 fusion.2
  98.2 5.4 %collective-permute-start.12 = (bf16[48,2048]{1,0:T(8,128)(2,1)S(1)}, bf16[48,2048]{1,0:T(8,128)(2,1)S(1)}, u32[]{:S(2)}, u32[]{:S(2)}) collective-permute-start(bf16[48,2048]{1,0:T(8,128)(2,1)S(1)} %fusion.2), channel_id=1, source_target_pairs={{0,384},{16,144},{64,448},{80,208},{128,0},{144,272},{192,64},{208... | collective-permute-start | bytes 589832 | tf_op jit(solution)/shard_map/ppermute | solution.py:22
  103.7 0.9 fusion.51
  104.7 0.9 fusion.43
  105.8 0.9 fusion.35
  106.7 0.5 copy-done.2
  107.2 1.6 %copy-done.3 = f32[352,2048]{1,0:T(8,128)} copy-done((f32[352,2048]{1,0:T(8,128)}, f32[352,2048]{1,0:T(8,128)S(1)}, u32[]{:S(2)}) %copy-start.3) | copy-done | bytes 2883608
  109.0 1.7 %pad_maximum_fusion.1 = bf16[3,176,2048]{2,1,0:T(8,128)(2,1)} fusion(bf16[1,176,2048]{2,1,0:T(8,128)(2,1)S(1)} %fusion.8, bf16[1,176,2048]{2,1,0:T(8,128)(2,1)S(1)} %fusion.7, bf16[1,176,2048]{2,1,0:T(8,128)(2,1)S(1)} %fusion.6), kind=kLoop, calls=%fused_computation.9 | loop fusion | flops 2162688 | bytes 4325376 | tf_op jit(solution)/shard_map/stack | solution.py:114
  110.6 1.9 %collective-permute-start.8 = (bf16[3,176,2048]{2,1,0:T(8,128)(2,1)}, bf16[3,176,2048]{2,1,0:T(8,128)(2,1)}, u32[]{:S(2)}, u32[]{:S(2)}) collective-permute-start(bf16[3,176,2048]{2,1,0:T(8,128)(2,1)} %pad_maximum_fusion.1), channel_id=1, source_target_pairs={{0,16},{16,0},{1,17},{17,1},{2,18},{18,2},{3,19},{19,3},{4,20},{20... | collective-permute-start | bytes 6488072 | tf_op jit(solution)/shard_map/ppermute | solution.py:114
  112.6 0.5 convolution_add_fusion
  113.2 3.7 %collective-permute-start.10 = (bf16[48,2048]{1,0:T(8,128)(2,1)S(1)}, bf16[48,2048]{1,0:T(8,128)(2,1)S(1)}, u32[]{:S(2)}, u32[]{:S(2)}) collective-permute-start(bf16[48,2048]{1,0:T(8,128)(2,1)S(1)} %get-tuple-element.10), channel_id=1, source_target_pairs={{0,384},{16,144},{64,448},{80,208},{128,0},{144,272},{192,64},{208... | collective-permute-start | bytes 589832 | tf_op jit(solution)/shard_map/ppermute | solution.py:22
  116.9 6.0 %collective-permute-start.13 = (bf16[48,2048]{1,0:T(8,128)(2,1)S(1)}, bf16[48,2048]{1,0:T(8,128)(2,1)S(1)}, u32[]{:S(2)}, u32[]{:S(2)}) collective-permute-start(bf16[48,2048]{1,0:T(8,128)(2,1)S(1)} %get-tuple-element.11), channel_id=1, source_target_pairs={{0,384},{16,144},{64,448},{80,208},{128,0},{144,272},{192,64},{208... | collective-permute-start | bytes 589832 | tf_op jit(solution)/shard_map/ppermute | solution.py:22
  123.0 0.8 collective-permute-done.10
  123.9 1.9 %collective-permute-start.11 = (bf16[48,2048]{1,0:T(8,128)(2,1)S(1)}, bf16[48,2048]{1,0:T(8,128)(2,1)S(1)}, u32[]{:S(2)}, u32[]{:S(2)}) collective-permute-start(bf16[48,2048]{1,0:T(8,128)(2,1)S(1)} %add_convert_fusion), channel_id=1, source_target_pairs={{0,16},{16,0},{1,17},{17,1},{2,18},{18,2},{3,19},{19,3},{4,20},{20... | collective-permute-start | bytes 589832 | tf_op jit(solution)/shard_map/ppermute | solution.py:123
  125.8 2.5 %collective-permute-done.13 = bf16[48,2048]{1,0:T(8,128)(2,1)S(1)} collective-permute-done((bf16[48,2048]{1,0:T(8,128)(2,1)S(1)}, bf16[48,2048]{1,0:T(8,128)(2,1)S(1)}, u32[]{:S(2)}, u32[]{:S(2)}) %collective-permute-start.13) | collective-permute-done | bytes 196640 | tf_op jit(solution)/shard_map/ppermute | solution.py:22
  128.4 0.7 copy.14
  129.1 8.0 %all-to-all-start.1 = ((bf16[32,24,128]{2,1,0:T(8,128)(2,1)}), bf16[32,24,128]{2,1,0:T(8,128)(2,1)}, u32[]{:S(2)}, u32[]{:S(2)}) async-start(bf16[32,24,128]{2,1,0:T(8,128)(2,1)} %bitcast.72), calls=%async_computation.1 | async-start | bytes 393216 | tf_op jit(solution)/shard_map/all_to_all | solution.py:127
  137.2 1.2 slice.184
  138.4 10.7 %all-to-all-done.1 = bf16[32,24,128]{2,1,0:T(8,128)(2,1)} async-done(((bf16[32,24,128]{2,1,0:T(8,128)(2,1)}), bf16[32,24,128]{2,1,0:T(8,128)(2,1)}, u32[]{:S(2)}, u32[]{:S(2)}) %all-to-all-start.1) | async-done | bytes 196640 | tf_op jit(solution)/shard_map/all_to_all | solution.py:127
  149.1 2.4 %convolution_convert_fusion.2 = bf16[128,128]{1,0:T(8,128)(2,1)} fusion(bf16[768,128]{1,0:T(8,128)(2,1)} %bitcast.24, s32[768]{0:T(1024)S(1)} %fusion.91, s32[128]{0:T(128)S(1)} %compare_select_fusion, bf16[]{:T(256)} %bitcast.21), kind=kOutput, calls=%fused_computation.23 | convolution fusion | flops 25477120 | bytes 232962 | tf_op jit(solution)/shard_map/dot_general | solution.py:26
  151.6 1.8 %slice_bitcast_fusion = (bf16[176,2048]{1,0:T(8,128)(2,1)S(1)}, bf16[176,2048]{1,0:T(8,128)(2,1)S(1)}, bf16[176,2048]{1,0:T(8,128)(2,1)S(1)}) fusion(bf16[3,176,2048]{2,1,0:T(8,128)(2,1)} %collective-permute-done.8), kind=kLoop, calls=%fused_computation.31 | loop fusion | bytes 4325376
  153.6 1.0 fusion.9
  154.9 1.1 fusion.11
  156.0 1.1 fusion.10
  (63 shorter events, 2.9 us)
Async XLA Ops:
  0.6 1.2 copy-start
  1.7 6.6 %copy-start.6 = (bf16[1,172,2048]{2,1,0:T(8,128)(2,1)S(1)}, bf16[1,172,2048]{2,1,0:T(8,128)(2,1)}, u32[]{:S(2)}) copy-start(bf16[1,172,2048]{2,1,0:T(8,128)(2,1)} %param.14) | copy-start | bytes 2113540
  1.7 6.6 %copy-start.7 = (bf16[1,172,2048]{2,1,0:T(8,128)(2,1)S(1)}, bf16[1,172,2048]{2,1,0:T(8,128)(2,1)}, u32[]{:S(2)}) copy-start(bf16[1,172,2048]{2,1,0:T(8,128)(2,1)} %param.13) | copy-start | bytes 2113540
  2.1 19.0 %collective-permute-start = (bf16[24,2048]{1,0:T(8,128)(2,1)S(1)}, bf16[24,2048]{1,0:T(8,128)(2,1)S(1)}, u32[]{:S(2)}, u32[]{:S(2)}) collective-permute-start(bf16[24,2048]{1,0:T(8,128)(2,1)S(1)} %convolution_convert_fusion), channel_id=1, source_target_pairs={{0,32},{32,0},{1,33},{33,1},{2,34},{34,2},{3,35},{35,3},{4,36},{36... | collective-permute-start | bytes 294920 | tf_op jit(solution)/shard_map/ppermute | solution.py:59
  8.5 89.4 %copy-start.4 = (bf16[176,2048]{1,0:T(8,128)(2,1)}, bf16[176,2048]{1,0:T(8,128)(2,1)S(1)}, u32[]{:S(2)}) copy-start(bf16[176,2048]{1,0:T(8,128)(2,1)S(1)} %get-tuple-element.49) | copy-start | bytes 2162692
  8.5 3.6 %copy-start.8 = (bf16[128,128]{1,0:T(8,128)(2,1)S(1)}, bf16[128,128]{1,0:T(8,128)(2,1)}, u32[]{:S(2)}) copy-start(bf16[128,128]{1,0:T(8,128)(2,1)} %param.9) | copy-start | bytes 98308
  8.5 3.6 %copy-start.9 = (f32[128]{0:T(128)S(1)}, f32[128]{0:T(128)}, u32[]{:S(2)}) copy-start(f32[128]{0:T(128)} %param.12) | copy-start | bytes 1540
  10.1 39.0 %collective-permute-start.3 = (bf16[3,176,2048]{2,1,0:T(8,128)(2,1)}, bf16[3,176,2048]{2,1,0:T(8,128)(2,1)}, u32[]{:S(2)}, u32[]{:S(2)}) collective-permute-start(bf16[3,176,2048]{2,1,0:T(8,128)(2,1)} %pad_maximum_fusion), channel_id=1, source_target_pairs={{0,16},{16,0},{1,17},{17,1},{2,18},{18,2},{3,19},{19,3},{4,20},{20... | collective-permute-start | bytes 6488072 | tf_op jit(solution)/shard_map/ppermute | solution.py:53
  13.1 20.1 %all-to-all-start = ((bf16[32,24,128]{2,1,0:T(8,128)(2,1)}), bf16[32,24,128]{2,1,0:T(8,128)(2,1)S(1)}, u32[]{:S(2)}, u32[]{:S(2)}) async-start(bf16[32,24,128]{2,1,0:T(8,128)(2,1)} %bitcast), calls=%async_computation | async-start | bytes 393216 | tf_op jit(solution)/shard_map/all_to_all | solution.py:62
  33.3 9.1 %collective-permute-start.2 = (bf16[96,2048]{1,0:T(8,128)(2,1)S(1)}, bf16[96,2048]{1,0:T(8,128)(2,1)S(1)}, u32[]{:S(2)}, u32[]{:S(2)}) collective-permute-start(bf16[96,2048]{1,0:T(8,128)(2,1)S(1)} %pad_maximum_fusion.6), channel_id=1, source_target_pairs={{0,464},{16,64},{64,16},{80,128},{128,80},{144,192},{192,144},{208... | collective-permute-start | bytes 1179656 | tf_op jit(solution)/shard_map/ppermute | solution.py:22
  35.2 13.9 %collective-permute-start.1 = (bf16[96,2048]{1,0:T(8,128)(2,1)S(1)}, bf16[96,2048]{1,0:T(8,128)(2,1)S(1)}, u32[]{:S(2)}, u32[]{:S(2)}) collective-permute-start(bf16[96,2048]{1,0:T(8,128)(2,1)S(1)} %pad_maximum_fusion.6), channel_id=1, source_target_pairs={{0,64},{16,464},{64,128},{80,16},{128,192},{144,80},{192,256},{208... | collective-permute-start | bytes 1179656 | tf_op jit(solution)/shard_map/ppermute | solution.py:22
  50.1 17.3 %collective-permute-start.4 = (bf16[192,2048]{1,0:T(8,128)(2,1)S(1)}, bf16[192,2048]{1,0:T(8,128)(2,1)S(1)}, u32[]{:S(2)}, u32[]{:S(2)}) collective-permute-start(bf16[192,2048]{1,0:T(8,128)(2,1)S(1)} %maximum_add_fusion), channel_id=1, source_target_pairs={{0,64},{16,464},{64,128},{80,16},{128,192},{144,80},{192,256},{208... | collective-permute-start | bytes 2359304 | tf_op jit(solution)/shard_map/ppermute | solution.py:22
  56.4 11.0 %collective-permute-start.6 = (bf16[96,2048]{1,0:T(8,128)(2,1)S(1)}, bf16[96,2048]{1,0:T(8,128)(2,1)S(1)}, u32[]{:S(2)}, u32[]{:S(2)}) collective-permute-start(bf16[96,2048]{1,0:T(8,128)(2,1)S(1)} %fusion), channel_id=1, source_target_pairs={{0,448},{16,80},{64,0},{80,144},{128,64},{144,208},{192,128},{208,... | collective-permute-start | bytes 1179656 | tf_op jit(solution)/shard_map/ppermute | solution.py:22
  69.4 15.1 %collective-permute-start.5 = (bf16[192,2048]{1,0:T(8,128)(2,1)S(1)}, bf16[192,2048]{1,0:T(8,128)(2,1)S(1)}, u32[]{:S(2)}, u32[]{:S(2)}) collective-permute-start(bf16[192,2048]{1,0:T(8,128)(2,1)S(1)} %collective-permute-done.4), channel_id=1, source_target_pairs={{0,64},{16,464},{64,128},{80,16},{128,192},{144,80},{192,256},{208... | collective-permute-start | bytes 2359304 | tf_op jit(solution)/shard_map/ppermute | solution.py:22
  84.6 11.1 %collective-permute-start.7 = (bf16[96,2048]{1,0:T(8,128)(2,1)S(1)}, bf16[96,2048]{1,0:T(8,128)(2,1)S(1)}, u32[]{:S(2)}, u32[]{:S(2)}) collective-permute-start(bf16[96,2048]{1,0:T(8,128)(2,1)S(1)} %maximum_add_fusion.1), channel_id=1, source_target_pairs={{0,64},{16,464},{64,128},{80,16},{128,192},{144,80},{192,256},{208... | collective-permute-start | bytes 1179656 | tf_op jit(solution)/shard_map/ppermute | solution.py:22
  92.4 20.6 %collective-permute-start.9 = (bf16[96,2048]{1,0:T(8,128)(2,1)S(1)}, bf16[96,2048]{1,0:T(8,128)(2,1)S(1)}, u32[]{:S(2)}, u32[]{:S(2)}) collective-permute-start(bf16[96,2048]{1,0:T(8,128)(2,1)S(1)} %fusion.1), channel_id=1, source_target_pairs={{0,448},{16,80},{64,0},{80,144},{128,64},{144,208},{192,128},{208,... | collective-permute-start | bytes 1179656 | tf_op jit(solution)/shard_map/ppermute | solution.py:22
  98.2 14.8 %collective-permute-start.12 = (bf16[48,2048]{1,0:T(8,128)(2,1)S(1)}, bf16[48,2048]{1,0:T(8,128)(2,1)S(1)}, u32[]{:S(2)}, u32[]{:S(2)}) collective-permute-start(bf16[48,2048]{1,0:T(8,128)(2,1)S(1)} %fusion.2), channel_id=1, source_target_pairs={{0,384},{16,144},{64,448},{80,208},{128,0},{144,272},{192,64},{208... | collective-permute-start | bytes 589832 | tf_op jit(solution)/shard_map/ppermute | solution.py:22
  104.6 32.5 %copy-start.1 = (f32[352,2048]{1,0:T(8,128)}, f32[352,2048]{1,0:T(8,128)S(1)}, u32[]{:S(2)}) copy-start(f32[352,2048]{1,0:T(8,128)S(1)} %fusion.51) | copy-start | bytes 8650756
  105.7 1.6 copy-start.2
  107.2 1.6 %copy-start.3 = (f32[352,2048]{1,0:T(8,128)}, f32[352,2048]{1,0:T(8,128)S(1)}, u32[]{:S(2)}) copy-start(f32[352,2048]{1,0:T(8,128)S(1)} %fusion.35) | copy-start | bytes 8650756
  108.9 3.6 %copy-start.5 = (bf16[176,2048]{1,0:T(8,128)(2,1)S(1)}, bf16[176,2048]{1,0:T(8,128)(2,1)}, u32[]{:S(2)}) copy-start(bf16[176,2048]{1,0:T(8,128)(2,1)} %copy-done.4) | copy-start | bytes 2162692
  110.6 26.5 %collective-permute-start.8 = (bf16[3,176,2048]{2,1,0:T(8,128)(2,1)}, bf16[3,176,2048]{2,1,0:T(8,128)(2,1)}, u32[]{:S(2)}, u32[]{:S(2)}) collective-permute-start(bf16[3,176,2048]{2,1,0:T(8,128)(2,1)} %pad_maximum_fusion.1), channel_id=1, source_target_pairs={{0,16},{16,0},{1,17},{17,1},{2,18},{18,2},{3,19},{19,3},{4,20},{20... | collective-permute-start | bytes 6488072 | tf_op jit(solution)/shard_map/ppermute | solution.py:114
  113.2 10.6 %collective-permute-start.10 = (bf16[48,2048]{1,0:T(8,128)(2,1)S(1)}, bf16[48,2048]{1,0:T(8,128)(2,1)S(1)}, u32[]{:S(2)}, u32[]{:S(2)}) collective-permute-start(bf16[48,2048]{1,0:T(8,128)(2,1)S(1)} %get-tuple-element.10), channel_id=1, source_target_pairs={{0,384},{16,144},{64,448},{80,208},{128,0},{144,272},{192,64},{208... | collective-permute-start | bytes 589832 | tf_op jit(solution)/shard_map/ppermute | solution.py:22
  116.9 11.3 %collective-permute-start.13 = (bf16[48,2048]{1,0:T(8,128)(2,1)S(1)}, bf16[48,2048]{1,0:T(8,128)(2,1)S(1)}, u32[]{:S(2)}, u32[]{:S(2)}) collective-permute-start(bf16[48,2048]{1,0:T(8,128)(2,1)S(1)} %get-tuple-element.11), channel_id=1, source_target_pairs={{0,384},{16,144},{64,448},{80,208},{128,0},{144,272},{192,64},{208... | collective-permute-start | bytes 589832 | tf_op jit(solution)/shard_map/ppermute | solution.py:22
  123.9 4.4 %collective-permute-start.11 = (bf16[48,2048]{1,0:T(8,128)(2,1)S(1)}, bf16[48,2048]{1,0:T(8,128)(2,1)S(1)}, u32[]{:S(2)}, u32[]{:S(2)}) collective-permute-start(bf16[48,2048]{1,0:T(8,128)(2,1)S(1)} %add_convert_fusion), channel_id=1, source_target_pairs={{0,16},{16,0},{1,17},{17,1},{2,18},{18,2},{3,19},{19,3},{4,20},{20... | collective-permute-start | bytes 589832 | tf_op jit(solution)/shard_map/ppermute | solution.py:123
  129.1 20.0 %all-to-all-start.1 = ((bf16[32,24,128]{2,1,0:T(8,128)(2,1)}), bf16[32,24,128]{2,1,0:T(8,128)(2,1)}, u32[]{:S(2)}, u32[]{:S(2)}) async-start(bf16[32,24,128]{2,1,0:T(8,128)(2,1)} %bitcast.72), calls=%async_computation.1 | async-start | bytes 393216 | tf_op jit(solution)/shard_map/all_to_all | solution.py:127
  151.6 2.0 %slice-start.2 = ((f32[352,2048]{1,0:T(8,128)}), f32[176,2048]{1,0:T(8,128)S(1)}, s32[]{:S(2)}) async-start(f32[352,2048]{1,0:T(8,128)} %copy-done.3), calls=%async_computation.4 | async-start | bytes 2883584 | tf_op jit(solution)/shard_map/slice | solution.py:134
  153.4 1.5 slice-start
  154.6 1.4 slice-start.1

commit v10 on v9

--- a/solution.py
+++ b/solution.py
@@ -49,11 +49,11 @@
     select_own = (slot[None, :] == own_slots[:, None]).astype(BF)
 
     pad = ((0, PAD - hidden_own), (0, 0))
-    own_w = jnp.stack([jnp.pad(w_gate[0], pad), jnp.pad(w_up[0], pad), jnp.pad(w_down[0], pad)])
-    other_w = lax.ppermute(own_w, "core", SWAP)
-    wg = jnp.concatenate([own_w[0], other_w[0]], axis=0)
-    wu = jnp.concatenate([own_w[1], other_w[1]], axis=0)
-    wd = jnp.concatenate([own_w[2], other_w[2]], axis=0)
+
+    def both_cores(w):
+        return jnp.concatenate([jnp.pad(w, pad), jnp.pad(lax.ppermute(w, "core", SWAP), pad)], axis=0)
+
+    wg, wu, wd = both_cores(w_gate[0]), both_cores(w_up[0]), both_cores(w_down[0])
 
     x_own = dot(select_own, tokens).astype(BF)
     x_across = lax.ppermute(x_own, "xh", SWAP)
@@ -70,7 +70,6 @@
     packet = jnp.concatenate([x_near, dy_near], axis=0)
     one = [ring(packet, 1), ring(packet, 1, cross=True)]
     one = jnp.concatenate([one[0][:near], one[1][:near], one[0][near:], one[1][near:]], axis=0)
-    one = one + other_w[2, PAD - 1 :]
     two = ring(one, 1)
     three = ring(two, 1)
     cols = ((1,), (1,))
@@ -126,14 +125,14 @@
     summed = jnp.transpose(summed, (0, 2, 1, 3)).astype(BF).reshape(XH * XL * Y, capacity, -1)
     summed = lax.all_to_all(summed, ("xh",) + EXPERT, 0, 0, tiled=True)
 
-    place = (slot[:, None] == all_slots[None, :]).astype(BF)
-    place = place + received[2, PAD - 1, 0]
-    grad_tokens = dot(place, summed.reshape(all_slots.shape[0], -1)).astype(BF)
-
     outs = [
         (grad[:PAD] + extra.astype(F32))[:hidden_own].astype(BF)[None]
         for grad, extra in zip(grads, received)
     ]
+
+    place = (slot[:, None] == all_slots[None, :]).astype(BF)
+    place = place + sum(out[0, 0, 0] * 0 for out in outs)
+    grad_tokens = dot(place, summed.reshape(all_slots.shape[0], -1)).astype(BF)
     return (*outs, grad_tokens)
 
 

time: 158 us -> 155 us (0.981)
  the two profiles are of different devices: /device:TPU:64 before, /device:TPU:1 now
where the time goes in v10:
time: 155 us; the launch traced here: 153 us
  starting transfers between devices  77.5 us (50%)
  waiting for transfers between devices  45.5 us (29%)
  matrix products  16.2 us (10%)
  local copies, waits for them, and re-layouts  6.62 us (4%)
  other arithmetic  4.28 us (3%)
  between operations  3.29 us (2%)
    ppermute x10, starting transfers between devices, ring(): return lax.ppermute(a, ('z', 'core'), pairs)  41.7 us
    ppermute x10, waiting for transfers between devices, ring(): return lax.ppermute(a, ('z', 'core'), pairs)  36.5 us
    dot_general x26, matrix products, dot(): return lax.dot_general(a, b, (dims, ((), ())), preferred_element_type=F32)  16.2 us
    all_to_all x1, starting transfers between devices, local(): dy_slices = lax.all_to_all(dy_slices, ('xh',) + EXPERT, 0, 0, tiled=True)  7.78 us
    ppermute x3, starting transfers between devices, both_cores(): lax.ppermute(w, 'core', SWAP)  7.47 us
    all_to_all x1, waiting for transfers between devices, local(): dy_slices = lax.all_to_all(dy_slices, ('xh',) + EXPERT, 0, 0, tiled=True)  6.19 us
    ppermute x1, starting transfers between devices, local(): lax.ppermute(jnp.stack([grad[PAD:].astype(BF) for grad in grads]), 'core'...  5.83 us
    ppermute x1, starting transfers between devices, local(): x_across = lax.ppermute(x_own, 'xh', SWAP)  5.61 us
  transfers between devices with their start and end apart: 18, of which 8 were waited for; matrix products, arithmetic and copies ran while one was open for 13% of the time, Pallas kernels for 0%

profile of v10, /device:TPU:1, one launch (start us, length us, event | category | flops | bytes accessed | tf_op | source)
XLA Modules:
  0.0 153.3 jit_solution(860206512477880175)
XLA Ops:
  0.7 0.8 multiply_add_fusion
  1.5 0.2 reduce_window_sum.11
  1.9 0.2 convolution_convert_fusion
  2.2 5.6 %collective-permute-start = (bf16[24,2048]{1,0:T(8,128)(2,1)S(1)}, bf16[24,2048]{1,0:T(8,128)(2,1)S(1)}, u32[]{:S(2)}, u32[]{:S(2)}) collective-permute-start(bf16[24,2048]{1,0:T(8,128)(2,1)S(1)} %convolution_convert_fusion), channel_id=1, source_target_pairs={{0,32},{32,0},{1,33},{33,1},{2,34},{34,2},{3,35},{35,3},{4,36},{36... | collective-permute-start | bytes 294920 | tf_op jit(solution)/shard_map/ppermute | solution.py:59
  7.8 1.7 %convolution_convert_fusion.1 = bf16[768,128]{1,0:T(8,128)(2,1)} fusion(s32[128]{0:T(128)S(1)} %compare_select_fusion, s32[768]{0:T(1024)S(1)} %fusion.100, bf16[128,128]{1,0:T(8,128)(2,1)} %param.9, f32[128]{0:T(128)} %param.12), kind=kOutput, calls=%fused_computation.29 | convolution fusion | flops 25411584 | bytes 233472 | tf_op jit(solution)/shard_map/dot_general | solution.py:26
  9.5 7.8 %all-to-all-start = ((bf16[32,24,128]{2,1,0:T(8,128)(2,1)}), bf16[32,24,128]{2,1,0:T(8,128)(2,1)S(1)}, u32[]{:S(2)}, u32[]{:S(2)}) async-start(bf16[32,24,128]{2,1,0:T(8,128)(2,1)} %bitcast), calls=%async_computation | async-start | bytes 393216 | tf_op jit(solution)/shard_map/all_to_all | solution.py:62
  17.3 3.1 %collective-permute-start.4 = (bf16[172,2048]{1,0:T(8,128)(2,1)S(1)}, bf16[172,2048]{1,0:T(8,128)(2,1)S(1)}, u32[]{:S(2)}, u32[]{:S(2)}) collective-permute-start(bf16[172,2048]{1,0:T(8,128)(2,1)S(1)} %bitcast.71), channel_id=1, source_target_pairs={{0,16},{16,0},{1,17},{17,1},{2,18},{18,2},{3,19},{19,3},{4,20},{20... | collective-permute-start | bytes 2113544 | tf_op jit(solution)/shard_map/ppermute | solution.py:54
  20.5 6.2 %all-to-all-done = bf16[32,24,128]{2,1,0:T(8,128)(2,1)S(1)} async-done(((bf16[32,24,128]{2,1,0:T(8,128)(2,1)}), bf16[32,24,128]{2,1,0:T(8,128)(2,1)S(1)}, u32[]{:S(2)}, u32[]{:S(2)}) %all-to-all-start) | async-done | bytes 196640 | tf_op jit(solution)/shard_map/all_to_all | solution.py:62
  26.9 10.8 %collective-permute-start.1 = (bf16[96,2048]{1,0:T(8,128)(2,1)S(1)}, bf16[96,2048]{1,0:T(8,128)(2,1)S(1)}, u32[]{:S(2)}, u32[]{:S(2)}) collective-permute-start(bf16[96,2048]{1,0:T(8,128)(2,1)S(1)} %pad_maximum_fusion.3), channel_id=1, source_target_pairs={{0,64},{16,464},{64,128},{80,16},{128,192},{144,80},{192,256},{208... | collective-permute-start | bytes 1179656 | tf_op jit(solution)/shard_map/ppermute | solution.py:22
  37.7 1.9 %collective-permute-start.5 = (bf16[172,2048]{1,0:T(8,128)(2,1)S(1)}, bf16[172,2048]{1,0:T(8,128)(2,1)S(1)}, u32[]{:S(2)}, u32[]{:S(2)}) collective-permute-start(bf16[172,2048]{1,0:T(8,128)(2,1)S(1)} %bitcast.79), channel_id=1, source_target_pairs={{0,16},{16,0},{1,17},{17,1},{2,18},{18,2},{3,19},{19,3},{4,20},{20... | collective-permute-start | bytes 2113544 | tf_op jit(solution)/shard_map/ppermute | solution.py:54
  39.6 2.4 %collective-permute-start.3 = (bf16[172,2048]{1,0:T(8,128)(2,1)S(1)}, bf16[172,2048]{1,0:T(8,128)(2,1)S(1)}, u32[]{:S(2)}, u32[]{:S(2)}) collective-permute-start(bf16[172,2048]{1,0:T(8,128)(2,1)S(1)} %bitcast.74), channel_id=1, source_target_pairs={{0,16},{16,0},{1,17},{17,1},{2,18},{18,2},{3,19},{19,3},{4,20},{20... | collective-permute-start | bytes 2113544 | tf_op jit(solution)/shard_map/ppermute | solution.py:54
  42.0 1.9 %collective-permute-start.2 = (bf16[96,2048]{1,0:T(8,128)(2,1)S(1)}, bf16[96,2048]{1,0:T(8,128)(2,1)S(1)}, u32[]{:S(2)}, u32[]{:S(2)}) collective-permute-start(bf16[96,2048]{1,0:T(8,128)(2,1)S(1)} %pad_maximum_fusion.3), channel_id=1, source_target_pairs={{0,464},{16,64},{64,16},{80,128},{128,80},{144,192},{192,144},{208... | collective-permute-start | bytes 1179656 | tf_op jit(solution)/shard_map/ppermute | solution.py:22
  44.2 7.2 %collective-permute-done.2 = bf16[96,2048]{1,0:T(8,128)(2,1)S(1)} collective-permute-done((bf16[96,2048]{1,0:T(8,128)(2,1)S(1)}, bf16[96,2048]{1,0:T(8,128)(2,1)S(1)}, u32[]{:S(2)}, u32[]{:S(2)}) %collective-permute-start.2) | collective-permute-done | bytes 393248 | tf_op jit(solution)/shard_map/ppermute | solution.py:22
  51.5 0.6 fusion.31
  52.2 0.6 fusion.66
  52.8 0.6 multiply_convert_fusion.4
  53.4 0.4 fusion.127
  53.8 5.2 %collective-permute-start.6 = (bf16[192,2048]{1,0:T(8,128)(2,1)S(1)}, bf16[192,2048]{1,0:T(8,128)(2,1)S(1)}, u32[]{:S(2)}, u32[]{:S(2)}) collective-permute-start(bf16[192,2048]{1,0:T(8,128)(2,1)S(1)} %pad_maximum_fusion.1), channel_id=1, source_target_pairs={{0,64},{16,464},{64,128},{80,16},{128,192},{144,80},{192,256},{208... | collective-permute-start | bytes 2359304 | tf_op jit(solution)/shard_map/ppermute | solution.py:22
  59.0 0.5 fusion.6
  59.5 1.9 %collective-permute-start.8 = (bf16[96,2048]{1,0:T(8,128)(2,1)S(1)}, bf16[96,2048]{1,0:T(8,128)(2,1)S(1)}, u32[]{:S(2)}, u32[]{:S(2)}) collective-permute-start(bf16[96,2048]{1,0:T(8,128)(2,1)S(1)} %fusion.6), channel_id=1, source_target_pairs={{0,448},{16,80},{64,0},{80,144},{128,64},{144,208},{192,128},{208,... | collective-permute-start | bytes 1179656 | tf_op jit(solution)/shard_map/ppermute | solution.py:22
  61.4 12.1 %collective-permute-done.8 = bf16[96,2048]{1,0:T(8,128)(2,1)S(1)} collective-permute-done((bf16[96,2048]{1,0:T(8,128)(2,1)S(1)}, bf16[96,2048]{1,0:T(8,128)(2,1)S(1)}, u32[]{:S(2)}, u32[]{:S(2)}) %collective-permute-start.8) | collective-permute-done | bytes 393248 | tf_op jit(solution)/shard_map/ppermute | solution.py:22
  73.7 0.6 fusion.69
  74.4 0.6 fusion.68
  75.0 3.6 %collective-permute-start.7 = (bf16[192,2048]{1,0:T(8,128)(2,1)S(1)}, bf16[192,2048]{1,0:T(8,128)(2,1)S(1)}, u32[]{:S(2)}, u32[]{:S(2)}) collective-permute-start(bf16[192,2048]{1,0:T(8,128)(2,1)S(1)} %collective-permute-done.6), channel_id=1, source_target_pairs={{0,64},{16,464},{64,128},{80,16},{128,192},{144,80},{192,256},{208... | collective-permute-start | bytes 2359304 | tf_op jit(solution)/shard_map/ppermute | solution.py:22
  78.6 0.6 multiply_convert_fusion.1
  79.3 0.5 fusion.128
  79.8 8.2 %collective-permute-done.7 = bf16[192,2048]{1,0:T(8,128)(2,1)S(1)} collective-permute-done((bf16[192,2048]{1,0:T(8,128)(2,1)S(1)}, bf16[192,2048]{1,0:T(8,128)(2,1)S(1)}, u32[]{:S(2)}, u32[]{:S(2)}) %collective-permute-start.7) | collective-permute-done | bytes 786464 | tf_op jit(solution)/shard_map/ppermute | solution.py:22
  88.2 4.5 %collective-permute-start.9 = (bf16[96,2048]{1,0:T(8,128)(2,1)S(1)}, bf16[96,2048]{1,0:T(8,128)(2,1)S(1)}, u32[]{:S(2)}, u32[]{:S(2)}) collective-permute-start(bf16[96,2048]{1,0:T(8,128)(2,1)S(1)} %maximum_add_fusion), channel_id=1, source_target_pairs={{0,64},{16,464},{64,128},{80,16},{128,192},{144,80},{192,256},{208... | collective-permute-start | bytes 1179656 | tf_op jit(solution)/shard_map/ppermute | solution.py:22
  92.7 0.6 fusion.38
  93.3 0.6 fusion.40
  93.8 0.6 multiply_convert_fusion.5
  94.4 0.4 fusion.129
  94.9 0.4 fusion.7
  95.3 2.1 %collective-permute-start.11 = (bf16[96,2048]{1,0:T(8,128)(2,1)S(1)}, bf16[96,2048]{1,0:T(8,128)(2,1)S(1)}, u32[]{:S(2)}, u32[]{:S(2)}) collective-permute-start(bf16[96,2048]{1,0:T(8,128)(2,1)S(1)} %fusion.7), channel_id=1, source_target_pairs={{0,448},{16,80},{64,0},{80,144},{128,64},{144,208},{192,128},{208,... | collective-permute-start | bytes 1179656 | tf_op jit(solution)/shard_map/ppermute | solution.py:22
  97.5 0.6 fusion.80
  98.1 0.6 fusion.82
  98.6 0.6 multiply_convert_fusion.10
  99.2 0.4 fusion.130
  99.6 0.9 fusion.58
  100.7 0.9 fusion.50
  101.6 0.9 fusion.42
  102.8 1.8 %pad_maximum_fusion = bf16[3,176,2048]{2,1,0:T(8,128)(2,1)} fusion(bf16[1,176,2048]{2,1,0:T(8,128)(2,1)S(1)} %fusion.17, bf16[1,176,2048]{2,1,0:T(8,128)(2,1)S(1)} %fusion.16, bf16[1,176,2048]{2,1,0:T(8,128)(2,1)S(1)} %fusion.15), kind=kLoop, calls=%fused_computation.16 | loop fusion | flops 2162688 | bytes 4325376 | tf_op jit(solution)/shard_map/stack | solution.py:113
  104.6 5.8 %collective-permute-start.10 = (bf16[3,176,2048]{2,1,0:T(8,128)(2,1)}, bf16[3,176,2048]{2,1,0:T(8,128)(2,1)}, u32[]{:S(2)}, u32[]{:S(2)}) collective-permute-start(bf16[3,176,2048]{2,1,0:T(8,128)(2,1)} %pad_maximum_fusion), channel_id=1, source_target_pairs={{0,16},{16,0},{1,17},{17,1},{2,18},{18,2},{3,19},{19,3},{4,20},{20... | collective-permute-start | bytes 6488072 | tf_op jit(solution)/shard_map/ppermute | solution.py:113
  110.4 0.4 fusion.8
  110.8 1.9 %collective-permute-start.14 = (bf16[48,2048]{1,0:T(8,128)(2,1)S(1)}, bf16[48,2048]{1,0:T(8,128)(2,1)S(1)}, u32[]{:S(2)}, u32[]{:S(2)}) collective-permute-start(bf16[48,2048]{1,0:T(8,128)(2,1)S(1)} %fusion.8), channel_id=1, source_target_pairs={{0,384},{16,144},{64,448},{80,208},{128,0},{144,272},{192,64},{208... | collective-permute-start | bytes 589832 | tf_op jit(solution)/shard_map/ppermute | solution.py:22
  112.7 0.5 convolution_add_fusion
  113.2 7.8 %collective-permute-done.14 = bf16[48,2048]{1,0:T(8,128)(2,1)S(1)} collective-permute-done((bf16[48,2048]{1,0:T(8,128)(2,1)S(1)}, bf16[48,2048]{1,0:T(8,128)(2,1)S(1)}, u32[]{:S(2)}, u32[]{:S(2)}) %collective-permute-start.14) | collective-permute-done | bytes 196640 | tf_op jit(solution)/shard_map/ppermute | solution.py:22
  121.2 3.8 %collective-permute-start.12 = (bf16[48,2048]{1,0:T(8,128)(2,1)S(1)}, bf16[48,2048]{1,0:T(8,128)(2,1)S(1)}, u32[]{:S(2)}, u32[]{:S(2)}) collective-permute-start(bf16[48,2048]{1,0:T(8,128)(2,1)S(1)} %get-tuple-element.7), channel_id=1, source_target_pairs={{0,384},{16,144},{64,448},{80,208},{128,0},{144,272},{192,64},{208... | collective-permute-start | bytes 589832 | tf_op jit(solution)/shard_map/ppermute | solution.py:22
  125.0 5.9 %collective-permute-start.15 = (bf16[48,2048]{1,0:T(8,128)(2,1)S(1)}, bf16[48,2048]{1,0:T(8,128)(2,1)S(1)}, u32[]{:S(2)}, u32[]{:S(2)}) collective-permute-start(bf16[48,2048]{1,0:T(8,128)(2,1)S(1)} %get-tuple-element.8), channel_id=1, source_target_pairs={{0,384},{16,144},{64,448},{80,208},{128,0},{144,272},{192,64},{208... | collective-permute-start | bytes 589832 | tf_op jit(solution)/shard_map/ppermute | solution.py:22
  131.0 1.1 collective-permute-done.12
  132.1 5.2 %collective-permute-start.13 = (bf16[48,2048]{1,0:T(8,128)(2,1)S(1)}, bf16[48,2048]{1,0:T(8,128)(2,1)S(1)}, u32[]{:S(2)}, u32[]{:S(2)}) collective-permute-start(bf16[48,2048]{1,0:T(8,128)(2,1)S(1)} %add_convert_fusion), channel_id=1, source_target_pairs={{0,16},{16,0},{1,17},{17,1},{2,18},{18,2},{3,19},{19,3},{4,20},{20... | collective-permute-start | bytes 589832 | tf_op jit(solution)/shard_map/ppermute | solution.py:122
  137.3 1.0 collective-permute-done.13
  138.5 0.7 copy.14
  139.2 3.9 %all-to-all-start.1 = ((bf16[32,24,128]{2,1,0:T(8,128)(2,1)}), bf16[32,24,128]{2,1,0:T(8,128)(2,1)S(1)}, u32[]{:S(2)}, u32[]{:S(2)}) async-start(bf16[32,24,128]{2,1,0:T(8,128)(2,1)} %bitcast.17), calls=%async_computation.1 | async-start | bytes 393216 | tf_op jit(solution)/shard_map/all_to_all | solution.py:126
  143.1 1.8 %slice_bitcast_fusion = (bf16[176,2048]{1,0:T(8,128)(2,1)S(1)}, bf16[176,2048]{1,0:T(8,128)(2,1)S(1)}, bf16[176,2048]{1,0:T(8,128)(2,1)S(1)}) fusion(bf16[3,176,2048]{2,1,0:T(8,128)(2,1)} %collective-permute-done.10), kind=kLoop, calls=%fused_computation.38 | loop fusion | bytes 4325376
  144.9 0.2 slice-done
  145.3 0.5 slice.168
  145.8 0.9 slice-done.1
  146.7 0.4 slice-done.2
  147.1 0.4 fusion.18
  147.6 0.6 slice.167
  148.2 0.5 slice.166
  150.7 1.8 %all-to-all-done.1 = bf16[32,24,128]{2,1,0:T(8,128)(2,1)S(1)} async-done(((bf16[32,24,128]{2,1,0:T(8,128)(2,1)}), bf16[32,24,128]{2,1,0:T(8,128)(2,1)S(1)}, u32[]{:S(2)}, u32[]{:S(2)}) %all-to-all-start.1) | async-done | bytes 196640 | tf_op jit(solution)/shard_map/all_to_all | solution.py:126
  152.5 0.9 convolution_convert_fusion.2
  (63 shorter events, 2.0 us)
Async XLA Ops:
  0.6 1.3 copy-start
  0.6 16.7 %copy-start.4 = (bf16[1,172,2048]{2,1,0:T(8,128)(2,1)S(1)}, bf16[1,172,2048]{2,1,0:T(8,128)(2,1)}, u32[]{:S(2)}) copy-start(bf16[1,172,2048]{2,1,0:T(8,128)(2,1)} %param.14) | copy-start | bytes 2113540
  2.1 37.5 %copy-start.8 = (bf16[1,172,2048]{2,1,0:T(8,128)(2,1)S(1)}, bf16[1,172,2048]{2,1,0:T(8,128)(2,1)}, u32[]{:S(2)}) copy-start(bf16[1,172,2048]{2,1,0:T(8,128)(2,1)} %param.15) | copy-start | bytes 2113540
  2.2 18.4 %collective-permute-start = (bf16[24,2048]{1,0:T(8,128)(2,1)S(1)}, bf16[24,2048]{1,0:T(8,128)(2,1)S(1)}, u32[]{:S(2)}, u32[]{:S(2)}) collective-permute-start(bf16[24,2048]{1,0:T(8,128)(2,1)S(1)} %convolution_convert_fusion), channel_id=1, source_target_pairs={{0,32},{32,0},{1,33},{33,1},{2,34},{34,2},{3,35},{35,3},{4,36},{36... | collective-permute-start | bytes 294920 | tf_op jit(solution)/shard_map/ppermute | solution.py:59
  9.5 17.2 %all-to-all-start = ((bf16[32,24,128]{2,1,0:T(8,128)(2,1)}), bf16[32,24,128]{2,1,0:T(8,128)(2,1)S(1)}, u32[]{:S(2)}, u32[]{:S(2)}) async-start(bf16[32,24,128]{2,1,0:T(8,128)(2,1)} %bitcast), calls=%async_computation | async-start | bytes 393216 | tf_op jit(solution)/shard_map/all_to_all | solution.py:62
  17.3 26.6 %collective-permute-start.4 = (bf16[172,2048]{1,0:T(8,128)(2,1)S(1)}, bf16[172,2048]{1,0:T(8,128)(2,1)S(1)}, u32[]{:S(2)}, u32[]{:S(2)}) collective-permute-start(bf16[172,2048]{1,0:T(8,128)(2,1)S(1)} %bitcast.71), channel_id=1, source_target_pairs={{0,16},{16,0},{1,17},{17,1},{2,18},{18,2},{3,19},{19,3},{4,20},{20... | collective-permute-start | bytes 2113544 | tf_op jit(solution)/shard_map/ppermute | solution.py:54
  26.7 10.9 %copy-start.9 = (bf16[1,172,2048]{2,1,0:T(8,128)(2,1)S(1)}, bf16[1,172,2048]{2,1,0:T(8,128)(2,1)}, u32[]{:S(2)}) copy-start(bf16[1,172,2048]{2,1,0:T(8,128)(2,1)} %param.13) | copy-start | bytes 2113540
  26.9 17.2 %collective-permute-start.1 = (bf16[96,2048]{1,0:T(8,128)(2,1)S(1)}, bf16[96,2048]{1,0:T(8,128)(2,1)S(1)}, u32[]{:S(2)}, u32[]{:S(2)}) collective-permute-start(bf16[96,2048]{1,0:T(8,128)(2,1)S(1)} %pad_maximum_fusion.3), channel_id=1, source_target_pairs={{0,64},{16,464},{64,128},{80,16},{128,192},{144,80},{192,256},{208... | collective-permute-start | bytes 1179656 | tf_op jit(solution)/shard_map/ppermute | solution.py:22
  37.7 14.5 %collective-permute-start.5 = (bf16[172,2048]{1,0:T(8,128)(2,1)S(1)}, bf16[172,2048]{1,0:T(8,128)(2,1)S(1)}, u32[]{:S(2)}, u32[]{:S(2)}) collective-permute-start(bf16[172,2048]{1,0:T(8,128)(2,1)S(1)} %bitcast.79), channel_id=1, source_target_pairs={{0,16},{16,0},{1,17},{17,1},{2,18},{18,2},{3,19},{19,3},{4,20},{20... | collective-permute-start | bytes 2113544 | tf_op jit(solution)/shard_map/ppermute | solution.py:54
  39.6 11.9 %collective-permute-start.3 = (bf16[172,2048]{1,0:T(8,128)(2,1)S(1)}, bf16[172,2048]{1,0:T(8,128)(2,1)S(1)}, u32[]{:S(2)}, u32[]{:S(2)}) collective-permute-start(bf16[172,2048]{1,0:T(8,128)(2,1)S(1)} %bitcast.74), channel_id=1, source_target_pairs={{0,16},{16,0},{1,17},{17,1},{2,18},{18,2},{3,19},{19,3},{4,20},{20... | collective-permute-start | bytes 2113544 | tf_op jit(solution)/shard_map/ppermute | solution.py:54
  42.0 9.4 %collective-permute-start.2 = (bf16[96,2048]{1,0:T(8,128)(2,1)S(1)}, bf16[96,2048]{1,0:T(8,128)(2,1)S(1)}, u32[]{:S(2)}, u32[]{:S(2)}) collective-permute-start(bf16[96,2048]{1,0:T(8,128)(2,1)S(1)} %pad_maximum_fusion.3), channel_id=1, source_target_pairs={{0,464},{16,64},{64,16},{80,128},{128,80},{144,192},{192,144},{208... | collective-permute-start | bytes 1179656 | tf_op jit(solution)/shard_map/ppermute | solution.py:22
  53.8 19.8 %collective-permute-start.6 = (bf16[192,2048]{1,0:T(8,128)(2,1)S(1)}, bf16[192,2048]{1,0:T(8,128)(2,1)S(1)}, u32[]{:S(2)}, u32[]{:S(2)}) collective-permute-start(bf16[192,2048]{1,0:T(8,128)(2,1)S(1)} %pad_maximum_fusion.1), channel_id=1, source_target_pairs={{0,64},{16,464},{64,128},{80,16},{128,192},{144,80},{192,256},{208... | collective-permute-start | bytes 2359304 | tf_op jit(solution)/shard_map/ppermute | solution.py:22
  59.5 14.1 %collective-permute-start.8 = (bf16[96,2048]{1,0:T(8,128)(2,1)S(1)}, bf16[96,2048]{1,0:T(8,128)(2,1)S(1)}, u32[]{:S(2)}, u32[]{:S(2)}) collective-permute-start(bf16[96,2048]{1,0:T(8,128)(2,1)S(1)} %fusion.6), channel_id=1, source_target_pairs={{0,448},{16,80},{64,0},{80,144},{128,64},{144,208},{192,128},{208,... | collective-permute-start | bytes 1179656 | tf_op jit(solution)/shard_map/ppermute | solution.py:22
  75.0 13.0 %collective-permute-start.7 = (bf16[192,2048]{1,0:T(8,128)(2,1)S(1)}, bf16[192,2048]{1,0:T(8,128)(2,1)S(1)}, u32[]{:S(2)}, u32[]{:S(2)}) collective-permute-start(bf16[192,2048]{1,0:T(8,128)(2,1)S(1)} %collective-permute-done.6), channel_id=1, source_target_pairs={{0,64},{16,464},{64,128},{80,16},{128,192},{144,80},{192,256},{208... | collective-permute-start | bytes 2359304 | tf_op jit(solution)/shard_map/ppermute | solution.py:22
  88.2 9.4 %collective-permute-start.9 = (bf16[96,2048]{1,0:T(8,128)(2,1)S(1)}, bf16[96,2048]{1,0:T(8,128)(2,1)S(1)}, u32[]{:S(2)}, u32[]{:S(2)}) collective-permute-start(bf16[96,2048]{1,0:T(8,128)(2,1)S(1)} %maximum_add_fusion), channel_id=1, source_target_pairs={{0,64},{16,464},{64,128},{80,16},{128,192},{144,80},{192,256},{208... | collective-permute-start | bytes 1179656 | tf_op jit(solution)/shard_map/ppermute | solution.py:22
  95.3 17.9 %collective-permute-start.11 = (bf16[96,2048]{1,0:T(8,128)(2,1)S(1)}, bf16[96,2048]{1,0:T(8,128)(2,1)S(1)}, u32[]{:S(2)}, u32[]{:S(2)}) collective-permute-start(bf16[96,2048]{1,0:T(8,128)(2,1)S(1)} %fusion.7), channel_id=1, source_target_pairs={{0,448},{16,80},{64,0},{80,144},{128,64},{144,208},{192,128},{208,... | collective-permute-start | bytes 1179656 | tf_op jit(solution)/shard_map/ppermute | solution.py:22
  100.6 36.7 %copy-start.1 = (f32[352,2048]{1,0:T(8,128)}, f32[352,2048]{1,0:T(8,128)S(1)}, u32[]{:S(2)}) copy-start(f32[352,2048]{1,0:T(8,128)S(1)} %fusion.58) | copy-start | bytes 8650756
  101.6 35.7 %copy-start.2 = (f32[352,2048]{1,0:T(8,128)}, f32[352,2048]{1,0:T(8,128)S(1)}, u32[]{:S(2)}) copy-start(f32[352,2048]{1,0:T(8,128)S(1)} %fusion.50) | copy-start | bytes 8650756
  102.6 34.7 %copy-start.3 = (f32[352,2048]{1,0:T(8,128)}, f32[352,2048]{1,0:T(8,128)S(1)}, u32[]{:S(2)}) copy-start(f32[352,2048]{1,0:T(8,128)S(1)} %fusion.42) | copy-start | bytes 8650756
  104.6 38.5 %collective-permute-start.10 = (bf16[3,176,2048]{2,1,0:T(8,128)(2,1)}, bf16[3,176,2048]{2,1,0:T(8,128)(2,1)}, u32[]{:S(2)}, u32[]{:S(2)}) collective-permute-start(bf16[3,176,2048]{2,1,0:T(8,128)(2,1)} %pad_maximum_fusion), channel_id=1, source_target_pairs={{0,16},{16,0},{1,17},{17,1},{2,18},{18,2},{3,19},{19,3},{4,20},{20... | collective-permute-start | bytes 6488072 | tf_op jit(solution)/shard_map/ppermute | solution.py:113
  110.8 10.3 %collective-permute-start.14 = (bf16[48,2048]{1,0:T(8,128)(2,1)S(1)}, bf16[48,2048]{1,0:T(8,128)(2,1)S(1)}, u32[]{:S(2)}, u32[]{:S(2)}) collective-permute-start(bf16[48,2048]{1,0:T(8,128)(2,1)S(1)} %fusion.8), channel_id=1, source_target_pairs={{0,384},{16,144},{64,448},{80,208},{128,0},{144,272},{192,64},{208... | collective-permute-start | bytes 589832 | tf_op jit(solution)/shard_map/ppermute | solution.py:22
  121.2 10.8 %collective-permute-start.12 = (bf16[48,2048]{1,0:T(8,128)(2,1)S(1)}, bf16[48,2048]{1,0:T(8,128)(2,1)S(1)}, u32[]{:S(2)}, u32[]{:S(2)}) collective-permute-start(bf16[48,2048]{1,0:T(8,128)(2,1)S(1)} %get-tuple-element.7), channel_id=1, source_target_pairs={{0,384},{16,144},{64,448},{80,208},{128,0},{144,272},{192,64},{208... | collective-permute-start | bytes 589832 | tf_op jit(solution)/shard_map/ppermute | solution.py:22
  125.0 12.3 %collective-permute-start.15 = (bf16[48,2048]{1,0:T(8,128)(2,1)S(1)}, bf16[48,2048]{1,0:T(8,128)(2,1)S(1)}, u32[]{:S(2)}, u32[]{:S(2)}) collective-permute-start(bf16[48,2048]{1,0:T(8,128)(2,1)S(1)} %get-tuple-element.8), channel_id=1, source_target_pairs={{0,384},{16,144},{64,448},{80,208},{128,0},{144,272},{192,64},{208... | collective-permute-start | bytes 589832 | tf_op jit(solution)/shard_map/ppermute | solution.py:22
  132.1 6.3 %collective-permute-start.13 = (bf16[48,2048]{1,0:T(8,128)(2,1)S(1)}, bf16[48,2048]{1,0:T(8,128)(2,1)S(1)}, u32[]{:S(2)}, u32[]{:S(2)}) collective-permute-start(bf16[48,2048]{1,0:T(8,128)(2,1)S(1)} %add_convert_fusion), channel_id=1, source_target_pairs={{0,16},{16,0},{1,17},{17,1},{2,18},{18,2},{3,19},{19,3},{4,20},{20... | collective-permute-start | bytes 589832 | tf_op jit(solution)/shard_map/ppermute | solution.py:122
  139.2 13.3 %all-to-all-start.1 = ((bf16[32,24,128]{2,1,0:T(8,128)(2,1)}), bf16[32,24,128]{2,1,0:T(8,128)(2,1)S(1)}, u32[]{:S(2)}, u32[]{:S(2)}) async-start(bf16[32,24,128]{2,1,0:T(8,128)(2,1)} %bitcast.17), calls=%async_computation.1 | async-start | bytes 393216 | tf_op jit(solution)/shard_map/all_to_all | solution.py:126
  143.1 2.0 %slice-start = ((f32[352,2048]{1,0:T(8,128)}), f32[176,2048]{1,0:T(8,128)S(1)}, s32[]{:S(2)}) async-start(f32[352,2048]{1,0:T(8,128)} %copy-done.1), calls=%async_computation.2 | async-start | bytes 2883584 | tf_op jit(solution)/shard_map/slice | solution.py:129
  145.1 1.6 %slice-start.1 = ((f32[352,2048]{1,0:T(8,128)}), f32[176,2048]{1,0:T(8,128)S(1)}, s32[]{:S(2)}) async-start(f32[352,2048]{1,0:T(8,128)} %copy-done.2), calls=%async_computation.3 | async-start | bytes 2883584 | tf_op jit(solution)/shard_map/slice | solution.py:129
  145.1 2.1 %slice-start.2 = ((f32[352,2048]{1,0:T(8,128)}), f32[176,2048]{1,0:T(8,128)S(1)}, s32[]{:S(2)}) async-start(f32[352,2048]{1,0:T(8,128)} %copy-done.3), calls=%async_computation.4 | async-start | bytes 2883584 | tf_op jit(solution)/shard_map/slice | solution.py:129
  145.3 2.3 %copy-start.5 = (bf16[1,172,2048]{2,1,0:T(8,128)(2,1)}, bf16[1,172,2048]{2,1,0:T(8,128)(2,1)S(1)}, u32[]{:S(2)}) copy-start(bf16[1,172,2048]{2,1,0:T(8,128)(2,1)S(1)} %fusion.20) | copy-start | bytes 2113540
  147.6 5.7 %copy-start.6 = (bf16[1,172,2048]{2,1,0:T(8,128)(2,1)}, bf16[1,172,2048]{2,1,0:T(8,128)(2,1)S(1)}, u32[]{:S(2)}) copy-start(bf16[1,172,2048]{2,1,0:T(8,128)(2,1)S(1)} %get-tuple-element.41) | copy-start | bytes 2113540
  147.6 5.7 %copy-start.7 = (bf16[1,172,2048]{2,1,0:T(8,128)(2,1)}, bf16[1,172,2048]{2,1,0:T(8,128)(2,1)S(1)}, u32[]{:S(2)}) copy-start(bf16[1,172,2048]{2,1,0:T(8,128)(2,1)S(1)} %get-tuple-element.42) | copy-start | bytes 2113540

commit v11 on v10

--- a/solution.py
+++ b/solution.py
@@ -110,7 +110,7 @@
         dot(jnp.concatenate(d_ups, axis=0), x_all, rows),
         dot(jnp.concatenate(hiddens, axis=0), dy_all, rows),
     ]
-    received = lax.ppermute(jnp.stack([grad[PAD:].astype(BF) for grad in grads]), "core", SWAP)
+    received = [lax.ppermute(grad[PAD:].astype(BF), "core", SWAP) for grad in grads]
 
     three_near = ring(terms_three.astype(BF), -1)
     four_near = ring(terms_four.astype(BF), -2)

time: 155 us -> 154 us (level)
  waiting for transfers between devices: 45.5 us -> 39.1 us
  starting transfers between devices: 77.5 us -> 79.7 us
  local copies, waits for them, and re-layouts: 6.62 us -> 8.56 us
    ppermute x10, waiting for transfers between devices: 36.5 us -> 29.7 us  [ring(): return lax.ppermute(a, ('z', 'core'), pairs)]
    ppermute x1 -> x3, starting transfers between devices: 5.83 us -> 11 us  [local(): lax.ppermute(grad[PAD:].astype(BF), 'core', SWAP)]
    slice x0 -> x3, local copies, waits for them, and re-layouts: none -> 3.14 us  [local(): grad[PAD:].astype(BF)]
    broadcast_in_dim x2 -> x3, other arithmetic: 0.61 us -> 2.96 us  [local(): (grad[:PAD] + extra.astype(F32))[:hidden_own].astype(BF)[None]]
    ppermute x10, starting transfers between devices: 41.7 us -> 39.4 us  [ring(): return lax.ppermute(a, ('z', 'core'), pairs)]
    another operation x1 -> x0, other arithmetic: 1.84 us -> none  [local(): jnp.stack([grad[PAD:].astype(BF) for grad in grads])]
  transfers between devices with their start and end apart: 18 -> 20, of which waited for: 8 -> 7; matrix products, arithmetic and copies ran while one was open for 13% -> 14% of each run, Pallas kernels for 0% -> 0%
where the time goes in v11:
time: 154 us; the launch traced here: 153 us
  starting transfers between devices  79.7 us (52%)
  waiting for transfers between devices  39.1 us (25%)
  matrix products  17.1 us (11%)
  local copies, waits for them, and re-layouts  8.56 us (6%)
  other arithmetic  4.78 us (3%)
  between operations  3.27 us (2%)
    ppermute x10, starting transfers between devices, ring(): return lax.ppermute(a, ('z', 'core'), pairs)  39.4 us
    ppermute x10, waiting for transfers between devices, ring(): return lax.ppermute(a, ('z', 'core'), pairs)  29.7 us
    dot_general x26, matrix products, dot(): return lax.dot_general(a, b, (dims, ((), ())), preferred_element_type=F32)  17.1 us
    ppermute x3, starting transfers between devices, local(): lax.ppermute(grad[PAD:].astype(BF), 'core', SWAP)  11 us
    all_to_all x1, starting transfers between devices, local(): dy_slices = lax.all_to_all(dy_slices, ('xh',) + EXPERT, 0, 0, tiled=True)  7.79 us
    ppermute x3, starting transfers between devices, both_cores(): lax.ppermute(w, 'core', SWAP)  7.47 us
    all_to_all x1, waiting for transfers between devices, local(): dy_slices = lax.all_to_all(dy_slices, ('xh',) + EXPERT, 0, 0, tiled=True)  6.19 us
    ppermute x1, starting transfers between devices, local(): x_across = lax.ppermute(x_own, 'xh', SWAP)  5.61 us
  transfers between devices with their start and end apart: 20, of which 7 were waited for; matrix products, arithmetic and copies ran while one was open for 14% of the time, Pallas kernels for 0%

profile of v11, /device:TPU:1, one launch (start us, length us, event | category | flops | bytes accessed | tf_op | source)
XLA Modules:
  0.0 152.5 jit_solution(13403866063008326307)
XLA Ops:
  0.7 0.8 multiply_add_fusion
  2.2 5.6 %collective-permute-start = (bf16[24,2048]{1,0:T(8,128)(2,1)S(1)}, bf16[24,2048]{1,0:T(8,128)(2,1)S(1)}, u32[]{:S(2)}, u32[]{:S(2)}) collective-permute-start(bf16[24,2048]{1,0:T(8,128)(2,1)S(1)} %convolution_convert_fusion), channel_id=1, source_target_pairs={{0,32},{32,0},{1,33},{33,1},{2,34},{34,2},{3,35},{35,3},{4,36},{36... | collective-permute-start | bytes 294920 | tf_op jit(solution)/shard_map/ppermute | solution.py:59
  7.8 1.7 %convolution_convert_fusion.1 = bf16[768,128]{1,0:T(8,128)(2,1)} fusion(s32[128]{0:T(128)S(1)} %compare_select_fusion, s32[768]{0:T(1024)S(1)} %fusion.97, bf16[128,128]{1,0:T(8,128)(2,1)} %param.9, f32[128]{0:T(128)} %param.12), kind=kOutput, calls=%fused_computation.28 | convolution fusion | flops 25411584 | bytes 233472 | tf_op jit(solution)/shard_map/dot_general | solution.py:26
  9.5 7.8 %all-to-all-start = ((bf16[32,24,128]{2,1,0:T(8,128)(2,1)}), bf16[32,24,128]{2,1,0:T(8,128)(2,1)S(1)}, u32[]{:S(2)}, u32[]{:S(2)}) async-start(bf16[32,24,128]{2,1,0:T(8,128)(2,1)} %bitcast), calls=%async_computation | async-start | bytes 393216 | tf_op jit(solution)/shard_map/all_to_all | solution.py:62
  17.4 3.1 %collective-permute-start.4 = (bf16[172,2048]{1,0:T(8,128)(2,1)S(1)}, bf16[172,2048]{1,0:T(8,128)(2,1)S(1)}, u32[]{:S(2)}, u32[]{:S(2)}) collective-permute-start(bf16[172,2048]{1,0:T(8,128)(2,1)S(1)} %bitcast.56), channel_id=1, source_target_pairs={{0,16},{16,0},{1,17},{17,1},{2,18},{18,2},{3,19},{19,3},{4,20},{20... | collective-permute-start | bytes 2113544 | tf_op jit(solution)/shard_map/ppermute | solution.py:54
  20.5 6.2 %all-to-all-done = bf16[32,24,128]{2,1,0:T(8,128)(2,1)S(1)} async-done(((bf16[32,24,128]{2,1,0:T(8,128)(2,1)}), bf16[32,24,128]{2,1,0:T(8,128)(2,1)S(1)}, u32[]{:S(2)}, u32[]{:S(2)}) %all-to-all-start) | async-done | bytes 196640 | tf_op jit(solution)/shard_map/all_to_all | solution.py:62
  26.9 10.8 %collective-permute-start.1 = (bf16[96,2048]{1,0:T(8,128)(2,1)S(1)}, bf16[96,2048]{1,0:T(8,128)(2,1)S(1)}, u32[]{:S(2)}, u32[]{:S(2)}) collective-permute-start(bf16[96,2048]{1,0:T(8,128)(2,1)S(1)} %pad_maximum_fusion.2), channel_id=1, source_target_pairs={{0,64},{16,464},{64,128},{80,16},{128,192},{144,80},{192,256},{208... | collective-permute-start | bytes 1179656 | tf_op jit(solution)/shard_map/ppermute | solution.py:22
  37.7 1.9 %collective-permute-start.5 = (bf16[172,2048]{1,0:T(8,128)(2,1)S(1)}, bf16[172,2048]{1,0:T(8,128)(2,1)S(1)}, u32[]{:S(2)}, u32[]{:S(2)}) collective-permute-start(bf16[172,2048]{1,0:T(8,128)(2,1)S(1)} %bitcast.63), channel_id=1, source_target_pairs={{0,16},{16,0},{1,17},{17,1},{2,18},{18,2},{3,19},{19,3},{4,20},{20... | collective-permute-start | bytes 2113544 | tf_op jit(solution)/shard_map/ppermute | solution.py:54
  39.6 2.4 %collective-permute-start.3 = (bf16[172,2048]{1,0:T(8,128)(2,1)S(1)}, bf16[172,2048]{1,0:T(8,128)(2,1)S(1)}, u32[]{:S(2)}, u32[]{:S(2)}) collective-permute-start(bf16[172,2048]{1,0:T(8,128)(2,1)S(1)} %bitcast.58), channel_id=1, source_target_pairs={{0,16},{16,0},{1,17},{17,1},{2,18},{18,2},{3,19},{19,3},{4,20},{20... | collective-permute-start | bytes 2113544 | tf_op jit(solution)/shard_map/ppermute | solution.py:54
  42.0 1.9 %collective-permute-start.2 = (bf16[96,2048]{1,0:T(8,128)(2,1)S(1)}, bf16[96,2048]{1,0:T(8,128)(2,1)S(1)}, u32[]{:S(2)}, u32[]{:S(2)}) collective-permute-start(bf16[96,2048]{1,0:T(8,128)(2,1)S(1)} %pad_maximum_fusion.2), channel_id=1, source_target_pairs={{0,464},{16,64},{64,16},{80,128},{128,80},{144,192},{192,144},{208... | collective-permute-start | bytes 1179656 | tf_op jit(solution)/shard_map/ppermute | solution.py:22
  44.2 7.3 %collective-permute-done.2 = bf16[96,2048]{1,0:T(8,128)(2,1)S(1)} collective-permute-done((bf16[96,2048]{1,0:T(8,128)(2,1)S(1)}, bf16[96,2048]{1,0:T(8,128)(2,1)S(1)}, u32[]{:S(2)}, u32[]{:S(2)}) %collective-permute-start.2) | collective-permute-done | bytes 393248 | tf_op jit(solution)/shard_map/ppermute | solution.py:22
  51.6 5.2 %collective-permute-start.6 = (bf16[192,2048]{1,0:T(8,128)(2,1)S(1)}, bf16[192,2048]{1,0:T(8,128)(2,1)S(1)}, u32[]{:S(2)}, u32[]{:S(2)}) collective-permute-start(bf16[192,2048]{1,0:T(8,128)(2,1)S(1)} %pad_maximum_fusion), channel_id=1, source_target_pairs={{0,64},{16,464},{64,128},{80,16},{128,192},{144,80},{192,256},{208... | collective-permute-start | bytes 2359304 | tf_op jit(solution)/shard_map/ppermute | solution.py:22
  56.8 0.6 fusion.28
  57.4 0.6 fusion.63
  58.0 0.6 multiply_convert_fusion.4
  58.6 0.4 fusion.124
  59.0 0.5 fusion.6
  59.4 1.9 %collective-permute-start.8 = (bf16[96,2048]{1,0:T(8,128)(2,1)S(1)}, bf16[96,2048]{1,0:T(8,128)(2,1)S(1)}, u32[]{:S(2)}, u32[]{:S(2)}) collective-permute-start(bf16[96,2048]{1,0:T(8,128)(2,1)S(1)} %fusion.6), channel_id=1, source_target_pairs={{0,448},{16,80},{64,0},{80,144},{128,64},{144,208},{192,128},{208,... | collective-permute-start | bytes 1179656 | tf_op jit(solution)/shard_map/ppermute | solution.py:22
  61.4 9.7 %collective-permute-done.8 = bf16[96,2048]{1,0:T(8,128)(2,1)S(1)} collective-permute-done((bf16[96,2048]{1,0:T(8,128)(2,1)S(1)}, bf16[96,2048]{1,0:T(8,128)(2,1)S(1)}, u32[]{:S(2)}, u32[]{:S(2)}) %collective-permute-start.8) | collective-permute-done | bytes 393248 | tf_op jit(solution)/shard_map/ppermute | solution.py:22
  71.3 0.6 fusion.65
  72.0 0.6 fusion.18
  72.6 0.6 multiply_convert_fusion
  73.3 0.5 fusion.125
  73.7 2.6 %collective-permute-start.7 = (bf16[192,2048]{1,0:T(8,128)(2,1)S(1)}, bf16[192,2048]{1,0:T(8,128)(2,1)S(1)}, u32[]{:S(2)}, u32[]{:S(2)}) collective-permute-start(bf16[192,2048]{1,0:T(8,128)(2,1)S(1)} %collective-permute-done.6), channel_id=1, source_target_pairs={{0,64},{16,464},{64,128},{80,16},{128,192},{144,80},{192,256},{208... | collective-permute-start | bytes 2359304 | tf_op jit(solution)/shard_map/ppermute | solution.py:22
  76.4 0.5 convolution_add_fusion
  76.9 9.8 %collective-permute-done.7 = bf16[192,2048]{1,0:T(8,128)(2,1)S(1)} collective-permute-done((bf16[192,2048]{1,0:T(8,128)(2,1)S(1)}, bf16[192,2048]{1,0:T(8,128)(2,1)S(1)}, u32[]{:S(2)}, u32[]{:S(2)}) %collective-permute-start.7) | collective-permute-done | bytes 786464 | tf_op jit(solution)/shard_map/ppermute | solution.py:22
  86.9 3.6 %collective-permute-start.9 = (bf16[96,2048]{1,0:T(8,128)(2,1)S(1)}, bf16[96,2048]{1,0:T(8,128)(2,1)S(1)}, u32[]{:S(2)}, u32[]{:S(2)}) collective-permute-start(bf16[96,2048]{1,0:T(8,128)(2,1)S(1)} %maximum_add_fusion), channel_id=1, source_target_pairs={{0,64},{16,464},{64,128},{80,16},{128,192},{144,80},{192,256},{208... | collective-permute-start | bytes 1179656 | tf_op jit(solution)/shard_map/ppermute | solution.py:22
  90.4 0.6 fusion.33
  91.0 0.6 fusion.35
  91.6 0.6 multiply_convert_fusion.3
  92.2 0.4 fusion.126
  92.6 0.5 fusion.7
  93.1 1.9 %collective-permute-start.13 = (bf16[96,2048]{1,0:T(8,128)(2,1)S(1)}, bf16[96,2048]{1,0:T(8,128)(2,1)S(1)}, u32[]{:S(2)}, u32[]{:S(2)}) collective-permute-start(bf16[96,2048]{1,0:T(8,128)(2,1)S(1)} %fusion.7), channel_id=1, source_target_pairs={{0,448},{16,80},{64,0},{80,144},{128,64},{144,208},{192,128},{208,... | collective-permute-start | bytes 1179656 | tf_op jit(solution)/shard_map/ppermute | solution.py:22
  95.1 0.6 collective-permute-done.9
  95.7 0.6 fusion.75
  96.2 0.6 fusion.77
  96.8 0.6 multiply_convert_fusion.9
  97.7 0.4 fusion.8
  98.1 3.6 %collective-permute-start.16 = (bf16[48,2048]{1,0:T(8,128)(2,1)S(1)}, bf16[48,2048]{1,0:T(8,128)(2,1)S(1)}, u32[]{:S(2)}, u32[]{:S(2)}) collective-permute-start(bf16[48,2048]{1,0:T(8,128)(2,1)S(1)} %fusion.8), channel_id=1, source_target_pairs={{0,384},{16,144},{64,448},{80,208},{128,0},{144,272},{192,64},{208... | collective-permute-start | bytes 589832 | tf_op jit(solution)/shard_map/ppermute | solution.py:22
  101.7 0.9 fusion.47
  102.7 1.1 slice.244
  103.7 0.8 copy-done.3
  104.5 2.3 %collective-permute-done.16 = bf16[48,2048]{1,0:T(8,128)(2,1)S(1)} collective-permute-done((bf16[48,2048]{1,0:T(8,128)(2,1)S(1)}, bf16[48,2048]{1,0:T(8,128)(2,1)S(1)}, u32[]{:S(2)}, u32[]{:S(2)}) %collective-permute-start.16) | collective-permute-done | bytes 196640 | tf_op jit(solution)/shard_map/ppermute | solution.py:22
  106.9 4.6 %collective-permute-start.14 = (bf16[48,2048]{1,0:T(8,128)(2,1)S(1)}, bf16[48,2048]{1,0:T(8,128)(2,1)S(1)}, u32[]{:S(2)}, u32[]{:S(2)}) collective-permute-start(bf16[48,2048]{1,0:T(8,128)(2,1)S(1)} %get-tuple-element.4), channel_id=1, source_target_pairs={{0,384},{16,144},{64,448},{80,208},{128,0},{144,272},{192,64},{208... | collective-permute-start | bytes 589832 | tf_op jit(solution)/shard_map/ppermute | solution.py:22
  111.5 0.9 fusion.39
  112.5 1.1 slice.245
  113.5 0.8 copy-done.1
  114.3 6.5 %collective-permute-start.11 = (bf16[176,2048]{1,0:T(8,128)(2,1)}, bf16[176,2048]{1,0:T(8,128)(2,1)}, u32[]{:S(2)}, u32[]{:S(2)}) collective-permute-start(bf16[176,2048]{1,0:T(8,128)(2,1)} %slice.244), channel_id=1, source_target_pairs={{0,16},{16,0},{1,17},{17,1},{2,18},{18,2},{3,19},{19,3},{4,20},{20... | collective-permute-start | bytes 2162696 | tf_op jit(solution)/shard_map/ppermute | solution.py:113
  120.8 3.3 %collective-permute-start.17 = (bf16[48,2048]{1,0:T(8,128)(2,1)S(1)}, bf16[48,2048]{1,0:T(8,128)(2,1)S(1)}, u32[]{:S(2)}, u32[]{:S(2)}) collective-permute-start(bf16[48,2048]{1,0:T(8,128)(2,1)S(1)} %get-tuple-element.5), channel_id=1, source_target_pairs={{0,384},{16,144},{64,448},{80,208},{128,0},{144,272},{192,64},{208... | collective-permute-start | bytes 589832 | tf_op jit(solution)/shard_map/ppermute | solution.py:22
  124.2 3.9 %collective-permute-start.15 = (bf16[48,2048]{1,0:T(8,128)(2,1)S(1)}, bf16[48,2048]{1,0:T(8,128)(2,1)S(1)}, u32[]{:S(2)}, u32[]{:S(2)}) collective-permute-start(bf16[48,2048]{1,0:T(8,128)(2,1)S(1)} %add_convert_fusion), channel_id=1, source_target_pairs={{0,16},{16,0},{1,17},{17,1},{2,18},{18,2},{3,19},{19,3},{4,20},{20... | collective-permute-start | bytes 589832 | tf_op jit(solution)/shard_map/ppermute | solution.py:122
  128.1 0.9 fusion.55
  129.1 1.0 slice.243
  130.1 0.7 copy-done.2
  130.8 1.9 %collective-permute-start.10 = (bf16[176,2048]{1,0:T(8,128)(2,1)}, bf16[176,2048]{1,0:T(8,128)(2,1)}, u32[]{:S(2)}, u32[]{:S(2)}) collective-permute-start(bf16[176,2048]{1,0:T(8,128)(2,1)} %slice.245), channel_id=1, source_target_pairs={{0,16},{16,0},{1,17},{17,1},{2,18},{18,2},{3,19},{19,3},{4,20},{20... | collective-permute-start | bytes 2162696 | tf_op jit(solution)/shard_map/ppermute | solution.py:113
  132.8 2.5 %collective-permute-start.12 = (bf16[176,2048]{1,0:T(8,128)(2,1)}, bf16[176,2048]{1,0:T(8,128)(2,1)S(1)}, u32[]{:S(2)}, u32[]{:S(2)}) collective-permute-start(bf16[176,2048]{1,0:T(8,128)(2,1)} %slice.243), channel_id=1, source_target_pairs={{0,16},{16,0},{1,17},{17,1},{2,18},{18,2},{3,19},{19,3},{4,20},{20... | collective-permute-start | bytes 2162696 | tf_op jit(solution)/shard_map/ppermute | solution.py:113
  135.5 0.7 copy.14
  136.2 4.6 %all-to-all-start.1 = ((bf16[32,24,128]{2,1,0:T(8,128)(2,1)}), bf16[32,24,128]{2,1,0:T(8,128)(2,1)}, u32[]{:S(2)}, u32[]{:S(2)}) async-start(bf16[32,24,128]{2,1,0:T(8,128)(2,1)} %bitcast.11), calls=%async_computation.1 | async-start | bytes 393216 | tf_op jit(solution)/shard_map/all_to_all | solution.py:126
  140.8 1.4 fusion.16
  142.2 0.6 slice.167
  142.8 1.4 fusion.15
  144.2 0.6 slice.166
  145.1 0.6 slice.168
  147.6 3.1 %all-to-all-done.1 = bf16[32,24,128]{2,1,0:T(8,128)(2,1)} async-done(((bf16[32,24,128]{2,1,0:T(8,128)(2,1)}), bf16[32,24,128]{2,1,0:T(8,128)(2,1)}, u32[]{:S(2)}, u32[]{:S(2)}) %all-to-all-start.1) | async-done | bytes 196640 | tf_op jit(solution)/shard_map/all_to_all | solution.py:126
  150.7 1.8 %convolution_convert_fusion.2 = bf16[128,128]{1,0:T(8,128)(2,1)} fusion(bf16[768,128]{1,0:T(8,128)(2,1)} %bitcast.12, s32[768]{0:T(1024)S(1)} %fusion.97, s32[128]{0:T(128)S(1)} %compare_select_fusion, bf16[]{:T(256)} %bitcast.9), kind=kOutput, calls=%fused_computation.29 | convolution fusion | flops 25477120 | bytes 232962 | tf_op jit(solution)/shard_map/dot_general | solution.py:26
  (66 shorter events, 2.6 us)
Async XLA Ops:
  0.6 1.3 copy-start
  0.6 16.7 %copy-start.4 = (bf16[1,172,2048]{2,1,0:T(8,128)(2,1)S(1)}, bf16[1,172,2048]{2,1,0:T(8,128)(2,1)}, u32[]{:S(2)}) copy-start(bf16[1,172,2048]{2,1,0:T(8,128)(2,1)} %param.14) | copy-start | bytes 2113540
  2.1 37.5 %copy-start.8 = (bf16[1,172,2048]{2,1,0:T(8,128)(2,1)S(1)}, bf16[1,172,2048]{2,1,0:T(8,128)(2,1)}, u32[]{:S(2)}) copy-start(bf16[1,172,2048]{2,1,0:T(8,128)(2,1)} %param.15) | copy-start | bytes 2113540
  2.2 18.4 %collective-permute-start = (bf16[24,2048]{1,0:T(8,128)(2,1)S(1)}, bf16[24,2048]{1,0:T(8,128)(2,1)S(1)}, u32[]{:S(2)}, u32[]{:S(2)}) collective-permute-start(bf16[24,2048]{1,0:T(8,128)(2,1)S(1)} %convolution_convert_fusion), channel_id=1, source_target_pairs={{0,32},{32,0},{1,33},{33,1},{2,34},{34,2},{3,35},{35,3},{4,36},{36... | collective-permute-start | bytes 294920 | tf_op jit(solution)/shard_map/ppermute | solution.py:59
  9.5 17.2 %all-to-all-start = ((bf16[32,24,128]{2,1,0:T(8,128)(2,1)}), bf16[32,24,128]{2,1,0:T(8,128)(2,1)S(1)}, u32[]{:S(2)}, u32[]{:S(2)}) async-start(bf16[32,24,128]{2,1,0:T(8,128)(2,1)} %bitcast), calls=%async_computation | async-start | bytes 393216 | tf_op jit(solution)/shard_map/all_to_all | solution.py:62
  17.4 26.6 %collective-permute-start.4 = (bf16[172,2048]{1,0:T(8,128)(2,1)S(1)}, bf16[172,2048]{1,0:T(8,128)(2,1)S(1)}, u32[]{:S(2)}, u32[]{:S(2)}) collective-permute-start(bf16[172,2048]{1,0:T(8,128)(2,1)S(1)} %bitcast.56), channel_id=1, source_target_pairs={{0,16},{16,0},{1,17},{17,1},{2,18},{18,2},{3,19},{19,3},{4,20},{20... | collective-permute-start | bytes 2113544 | tf_op jit(solution)/shard_map/ppermute | solution.py:54
  26.7 10.9 %copy-start.9 = (bf16[1,172,2048]{2,1,0:T(8,128)(2,1)S(1)}, bf16[1,172,2048]{2,1,0:T(8,128)(2,1)}, u32[]{:S(2)}) copy-start(bf16[1,172,2048]{2,1,0:T(8,128)(2,1)} %param.13) | copy-start | bytes 2113540
  26.9 17.2 %collective-permute-start.1 = (bf16[96,2048]{1,0:T(8,128)(2,1)S(1)}, bf16[96,2048]{1,0:T(8,128)(2,1)S(1)}, u32[]{:S(2)}, u32[]{:S(2)}) collective-permute-start(bf16[96,2048]{1,0:T(8,128)(2,1)S(1)} %pad_maximum_fusion.2), channel_id=1, source_target_pairs={{0,64},{16,464},{64,128},{80,16},{128,192},{144,80},{192,256},{208... | collective-permute-start | bytes 1179656 | tf_op jit(solution)/shard_map/ppermute | solution.py:22
  37.7 19.7 %collective-permute-start.5 = (bf16[172,2048]{1,0:T(8,128)(2,1)S(1)}, bf16[172,2048]{1,0:T(8,128)(2,1)S(1)}, u32[]{:S(2)}, u32[]{:S(2)}) collective-permute-start(bf16[172,2048]{1,0:T(8,128)(2,1)S(1)} %bitcast.63), channel_id=1, source_target_pairs={{0,16},{16,0},{1,17},{17,1},{2,18},{18,2},{3,19},{19,3},{4,20},{20... | collective-permute-start | bytes 2113544 | tf_op jit(solution)/shard_map/ppermute | solution.py:54
  39.6 17.2 %collective-permute-start.3 = (bf16[172,2048]{1,0:T(8,128)(2,1)S(1)}, bf16[172,2048]{1,0:T(8,128)(2,1)S(1)}, u32[]{:S(2)}, u32[]{:S(2)}) collective-permute-start(bf16[172,2048]{1,0:T(8,128)(2,1)S(1)} %bitcast.58), channel_id=1, source_target_pairs={{0,16},{16,0},{1,17},{17,1},{2,18},{18,2},{3,19},{19,3},{4,20},{20... | collective-permute-start | bytes 2113544 | tf_op jit(solution)/shard_map/ppermute | solution.py:54
  42.0 9.4 %collective-permute-start.2 = (bf16[96,2048]{1,0:T(8,128)(2,1)S(1)}, bf16[96,2048]{1,0:T(8,128)(2,1)S(1)}, u32[]{:S(2)}, u32[]{:S(2)}) collective-permute-start(bf16[96,2048]{1,0:T(8,128)(2,1)S(1)} %pad_maximum_fusion.2), channel_id=1, source_target_pairs={{0,464},{16,64},{64,16},{80,128},{128,80},{144,192},{192,144},{208... | collective-permute-start | bytes 1179656 | tf_op jit(solution)/shard_map/ppermute | solution.py:22
  51.6 19.6 %collective-permute-start.6 = (bf16[192,2048]{1,0:T(8,128)(2,1)S(1)}, bf16[192,2048]{1,0:T(8,128)(2,1)S(1)}, u32[]{:S(2)}, u32[]{:S(2)}) collective-permute-start(bf16[192,2048]{1,0:T(8,128)(2,1)S(1)} %pad_maximum_fusion), channel_id=1, source_target_pairs={{0,64},{16,464},{64,128},{80,16},{128,192},{144,80},{192,256},{208... | collective-permute-start | bytes 2359304 | tf_op jit(solution)/shard_map/ppermute | solution.py:22
  59.4 11.7 %collective-permute-start.8 = (bf16[96,2048]{1,0:T(8,128)(2,1)S(1)}, bf16[96,2048]{1,0:T(8,128)(2,1)S(1)}, u32[]{:S(2)}, u32[]{:S(2)}) collective-permute-start(bf16[96,2048]{1,0:T(8,128)(2,1)S(1)} %fusion.6), channel_id=1, source_target_pairs={{0,448},{16,80},{64,0},{80,144},{128,64},{144,208},{192,128},{208,... | collective-permute-start | bytes 1179656 | tf_op jit(solution)/shard_map/ppermute | solution.py:22
  73.7 13.0 %collective-permute-start.7 = (bf16[192,2048]{1,0:T(8,128)(2,1)S(1)}, bf16[192,2048]{1,0:T(8,128)(2,1)S(1)}, u32[]{:S(2)}, u32[]{:S(2)}) collective-permute-start(bf16[192,2048]{1,0:T(8,128)(2,1)S(1)} %collective-permute-done.6), channel_id=1, source_target_pairs={{0,64},{16,464},{64,128},{80,16},{128,192},{144,80},{192,256},{208... | collective-permute-start | bytes 2359304 | tf_op jit(solution)/shard_map/ppermute | solution.py:22
  86.9 8.8 %collective-permute-start.9 = (bf16[96,2048]{1,0:T(8,128)(2,1)S(1)}, bf16[96,2048]{1,0:T(8,128)(2,1)S(1)}, u32[]{:S(2)}, u32[]{:S(2)}) collective-permute-start(bf16[96,2048]{1,0:T(8,128)(2,1)S(1)} %maximum_add_fusion), channel_id=1, source_target_pairs={{0,64},{16,464},{64,128},{80,16},{128,192},{144,80},{192,256},{208... | collective-permute-start | bytes 1179656 | tf_op jit(solution)/shard_map/ppermute | solution.py:22
  93.1 11.4 %collective-permute-start.13 = (bf16[96,2048]{1,0:T(8,128)(2,1)S(1)}, bf16[96,2048]{1,0:T(8,128)(2,1)S(1)}, u32[]{:S(2)}, u32[]{:S(2)}) collective-permute-start(bf16[96,2048]{1,0:T(8,128)(2,1)S(1)} %fusion.7), channel_id=1, source_target_pairs={{0,448},{16,80},{64,0},{80,144},{128,64},{144,208},{192,128},{208,... | collective-permute-start | bytes 1179656 | tf_op jit(solution)/shard_map/ppermute | solution.py:22
  98.1 8.7 %collective-permute-start.16 = (bf16[48,2048]{1,0:T(8,128)(2,1)S(1)}, bf16[48,2048]{1,0:T(8,128)(2,1)S(1)}, u32[]{:S(2)}, u32[]{:S(2)}) collective-permute-start(bf16[48,2048]{1,0:T(8,128)(2,1)S(1)} %fusion.8), channel_id=1, source_target_pairs={{0,384},{16,144},{64,448},{80,208},{128,0},{144,272},{192,64},{208... | collective-permute-start | bytes 589832 | tf_op jit(solution)/shard_map/ppermute | solution.py:22
  102.7 1.8 %copy-start.3 = (f32[352,2048]{1,0:T(8,128)}, f32[352,2048]{1,0:T(8,128)S(1)}, u32[]{:S(2)}) copy-start(f32[352,2048]{1,0:T(8,128)S(1)} %fusion.47) | copy-start | bytes 8650756
  106.9 17.2 %collective-permute-start.14 = (bf16[48,2048]{1,0:T(8,128)(2,1)S(1)}, bf16[48,2048]{1,0:T(8,128)(2,1)S(1)}, u32[]{:S(2)}, u32[]{:S(2)}) collective-permute-start(bf16[48,2048]{1,0:T(8,128)(2,1)S(1)} %get-tuple-element.4), channel_id=1, source_target_pairs={{0,384},{16,144},{64,448},{80,208},{128,0},{144,272},{192,64},{208... | collective-permute-start | bytes 589832 | tf_op jit(solution)/shard_map/ppermute | solution.py:22
  112.5 1.8 %copy-start.1 = (f32[352,2048]{1,0:T(8,128)}, f32[352,2048]{1,0:T(8,128)S(1)}, u32[]{:S(2)}) copy-start(f32[352,2048]{1,0:T(8,128)S(1)} %fusion.39) | copy-start | bytes 8650756
  114.3 26.5 %collective-permute-start.11 = (bf16[176,2048]{1,0:T(8,128)(2,1)}, bf16[176,2048]{1,0:T(8,128)(2,1)}, u32[]{:S(2)}, u32[]{:S(2)}) collective-permute-start(bf16[176,2048]{1,0:T(8,128)(2,1)} %slice.244), channel_id=1, source_target_pairs={{0,16},{16,0},{1,17},{17,1},{2,18},{18,2},{3,19},{19,3},{4,20},{20... | collective-permute-start | bytes 2162696 | tf_op jit(solution)/shard_map/ppermute | solution.py:113
  120.8 14.5 %collective-permute-start.17 = (bf16[48,2048]{1,0:T(8,128)(2,1)S(1)}, bf16[48,2048]{1,0:T(8,128)(2,1)S(1)}, u32[]{:S(2)}, u32[]{:S(2)}) collective-permute-start(bf16[48,2048]{1,0:T(8,128)(2,1)S(1)} %get-tuple-element.5), channel_id=1, source_target_pairs={{0,384},{16,144},{64,448},{80,208},{128,0},{144,272},{192,64},{208... | collective-permute-start | bytes 589832 | tf_op jit(solution)/shard_map/ppermute | solution.py:22
  124.2 11.1 %collective-permute-start.15 = (bf16[48,2048]{1,0:T(8,128)(2,1)S(1)}, bf16[48,2048]{1,0:T(8,128)(2,1)S(1)}, u32[]{:S(2)}, u32[]{:S(2)}) collective-permute-start(bf16[48,2048]{1,0:T(8,128)(2,1)S(1)} %add_convert_fusion), channel_id=1, source_target_pairs={{0,16},{16,0},{1,17},{17,1},{2,18},{18,2},{3,19},{19,3},{4,20},{20... | collective-permute-start | bytes 589832 | tf_op jit(solution)/shard_map/ppermute | solution.py:122
  129.1 1.8 %copy-start.2 = (f32[352,2048]{1,0:T(8,128)}, f32[352,2048]{1,0:T(8,128)S(1)}, u32[]{:S(2)}) copy-start(f32[352,2048]{1,0:T(8,128)S(1)} %fusion.55) | copy-start | bytes 8650756
  130.8 11.9 %collective-permute-start.10 = (bf16[176,2048]{1,0:T(8,128)(2,1)}, bf16[176,2048]{1,0:T(8,128)(2,1)}, u32[]{:S(2)}, u32[]{:S(2)}) collective-permute-start(bf16[176,2048]{1,0:T(8,128)(2,1)} %slice.245), channel_id=1, source_target_pairs={{0,16},{16,0},{1,17},{17,1},{2,18},{18,2},{3,19},{19,3},{4,20},{20... | collective-permute-start | bytes 2162696 | tf_op jit(solution)/shard_map/ppermute | solution.py:113
  132.8 8.0 %slice-start.2 = ((f32[352,2048]{1,0:T(8,128)}), f32[176,2048]{1,0:T(8,128)S(1)}, s32[]{:S(2)}) async-start(f32[352,2048]{1,0:T(8,128)} %copy-done.3), calls=%async_computation.4 | async-start | bytes 2883584 | tf_op jit(solution)/shard_map/slice | solution.py:129
  132.8 12.0 %collective-permute-start.12 = (bf16[176,2048]{1,0:T(8,128)(2,1)}, bf16[176,2048]{1,0:T(8,128)(2,1)S(1)}, u32[]{:S(2)}, u32[]{:S(2)}) collective-permute-start(bf16[176,2048]{1,0:T(8,128)(2,1)} %slice.243), channel_id=1, source_target_pairs={{0,16},{16,0},{1,17},{17,1},{2,18},{18,2},{3,19},{19,3},{4,20},{20... | collective-permute-start | bytes 2162696 | tf_op jit(solution)/shard_map/ppermute | solution.py:113
  136.2 14.5 %all-to-all-start.1 = ((bf16[32,24,128]{2,1,0:T(8,128)(2,1)}), bf16[32,24,128]{2,1,0:T(8,128)(2,1)}, u32[]{:S(2)}, u32[]{:S(2)}) async-start(bf16[32,24,128]{2,1,0:T(8,128)(2,1)} %bitcast.11), calls=%async_computation.1 | async-start | bytes 393216 | tf_op jit(solution)/shard_map/all_to_all | solution.py:126
  140.8 2.0 %slice-start = ((f32[352,2048]{1,0:T(8,128)}), f32[176,2048]{1,0:T(8,128)S(1)}, s32[]{:S(2)}) async-start(f32[352,2048]{1,0:T(8,128)} %copy-done.1), calls=%async_computation.2 | async-start | bytes 2883584 | tf_op jit(solution)/shard_map/slice | solution.py:129
  142.2 2.0 %copy-start.5 = (bf16[1,172,2048]{2,1,0:T(8,128)(2,1)}, bf16[1,172,2048]{2,1,0:T(8,128)(2,1)S(1)}, u32[]{:S(2)}) copy-start(bf16[1,172,2048]{2,1,0:T(8,128)(2,1)S(1)} %fusion.16) | copy-start | bytes 2113540
  142.8 2.0 %slice-start.1 = ((f32[352,2048]{1,0:T(8,128)}), f32[176,2048]{1,0:T(8,128)S(1)}, s32[]{:S(2)}) async-start(f32[352,2048]{1,0:T(8,128)} %copy-done.2), calls=%async_computation.3 | async-start | bytes 2883584 | tf_op jit(solution)/shard_map/slice | solution.py:129
  144.2 0.9 copy-start.6
  145.1 7.4 %copy-start.7 = (bf16[1,172,2048]{2,1,0:T(8,128)(2,1)}, bf16[1,172,2048]{2,1,0:T(8,128)(2,1)S(1)}, u32[]{:S(2)}) copy-start(bf16[1,172,2048]{2,1,0:T(8,128)(2,1)S(1)} %fusion.17) | copy-start | bytes 2113540

commit v12 on v11

--- a/solution.py
+++ b/solution.py
@@ -102,8 +102,9 @@
     terms_three = work(three[: 2 * near], three[2 * near :])
     terms_four = work(four[:near], four[near:])
 
-    x_all = jnp.concatenate(x_parts, axis=0)
-    dy_all = jnp.concatenate(dy_parts, axis=0)
+    first = terms_four[:1].astype(BF) * 0
+    x_all = jnp.concatenate([*x_parts[:-1], x_parts[-1] + first], axis=0)
+    dy_all = jnp.concatenate([*dy_parts[:-1], dy_parts[-1] + first], axis=0)
     rows = ((0,), (0,))
     grads = [
         dot(jnp.concatenate(d_gates, axis=0), x_all, rows),
@@ -112,15 +113,16 @@
     ]
     received = [lax.ppermute(grad[PAD:].astype(BF), "core", SWAP) for grad in grads]
 
+    one_across = lax.ppermute(one_home[near:], "core", SWAP)
     three_near = ring(terms_three.astype(BF), -1)
     four_near = ring(terms_four.astype(BF), -2)
     home_b = terms_two[near:] + three_near[near:].astype(F32)
-    home_b = ring(home_b.astype(BF), -2)
+    home_b = ring(home_b.astype(BF), -2, cross=True)
     home_a = terms_two[:near] + three_near[:near].astype(F32) + four_near.astype(F32)
     home_a = ring(home_a.astype(BF), -2)
-    crossing = one_home[near:].astype(F32) + home_b.astype(F32)
-    crossing = lax.ppermute(crossing.astype(BF), "core", SWAP)
-    summed = terms_own + one_home[:near].astype(F32) + crossing.astype(F32) + home_a.astype(F32)
+    summed = terms_own
+    for came in (one_home[:near], one_across, home_b, home_a):
+        summed = summed + came.astype(F32)
     summed = summed.reshape(XH, capacity, XL * Y, -1)
     summed = jnp.transpose(summed, (0, 2, 1, 3)).astype(BF).reshape(XH * XL * Y, capacity, -1)
     summed = lax.all_to_all(summed, ("xh",) + EXPERT, 0, 0, tiled=True)

time: 154 us -> 152 us (0.987)
  waiting for transfers between devices: 39.1 us -> 34.8 us
  starting transfers between devices: 79.7 us -> 81.8 us
    ppermute x10, starting transfers between devices: 39.4 us -> 46.3 us  [ring(): return lax.ppermute(a, ('z', 'core'), pairs)]
    ppermute x10, waiting for transfers between devices: 29.7 us -> 25.5 us  [ring(): return lax.ppermute(a, ('z', 'core'), pairs)]
    ppermute x3, starting transfers between devices: 11 us -> 8.15 us  [local(): lax.ppermute(grad[PAD:].astype(BF), 'core', SWAP)]
    ppermute x1, starting transfers between devices: 3.93 us -> 1.92 us  [local(): one_across = lax.ppermute(one_home[near:], 'core', SWAP)]
  transfers between devices with their start and end apart: 20 -> 20, of which waited for: 7 -> 6; matrix products, arithmetic and copies ran while one was open for 14% -> 17% of each run, Pallas kernels for 0% -> 0%
where the time goes in v12:
time: 152 us; the launch traced here: 150 us
  starting transfers between devices  81.8 us (54%)
  waiting for transfers between devices  34.8 us (23%)
  matrix products  17.1 us (11%)
  local copies, waits for them, and re-layouts  8.55 us (6%)
  other arithmetic  4.86 us (3%)
  between operations  3.28 us (2%)
    ppermute x10, starting transfers between devices, ring(): return lax.ppermute(a, ('z', 'core'), pairs)  46.3 us
    ppermute x10, waiting for transfers between devices, ring(): return lax.ppermute(a, ('z', 'core'), pairs)  25.5 us
    dot_general x26, matrix products, dot(): return lax.dot_general(a, b, (dims, ((), ())), preferred_element_type=F32)  17.1 us
    ppermute x3, starting transfers between devices, local(): lax.ppermute(grad[PAD:].astype(BF), 'core', SWAP)  8.15 us
    all_to_all x1, starting transfers between devices, local(): dy_slices = lax.all_to_all(dy_slices, ('xh',) + EXPERT, 0, 0, tiled=True)  7.79 us
    ppermute x3, starting transfers between devices, both_cores(): lax.ppermute(w, 'core', SWAP)  7.47 us
    all_to_all x1, waiting for transfers between devices, local(): dy_slices = lax.all_to_all(dy_slices, ('xh',) + EXPERT, 0, 0, tiled=True)  6.19 us
    ppermute x1, starting transfers between devices, local(): x_across = lax.ppermute(x_own, 'xh', SWAP)  5.61 us
  transfers between devices with their start and end apart: 20, of which 6 were waited for; matrix products, arithmetic and copies ran while one was open for 17% of the time, Pallas kernels for 0%

profile of v12, /device:TPU:1, one launch (start us, length us, event | category | flops | bytes accessed | tf_op | source)
XLA Modules:
  0.0 150.4 jit_solution(14313022670248709043)
XLA Ops:
  0.7 0.8 multiply_add_fusion
  1.9 0.2 convolution_convert_fusion
  2.2 5.6 %collective-permute-start = (bf16[24,2048]{1,0:T(8,128)(2,1)S(1)}, bf16[24,2048]{1,0:T(8,128)(2,1)S(1)}, u32[]{:S(2)}, u32[]{:S(2)}) collective-permute-start(bf16[24,2048]{1,0:T(8,128)(2,1)S(1)} %convolution_convert_fusion), channel_id=1, source_target_pairs={{0,32},{32,0},{1,33},{33,1},{2,34},{34,2},{3,35},{35,3},{4,36},{36... | collective-permute-start | bytes 294920 | tf_op jit(solution)/shard_map/ppermute | solution.py:59
  7.8 1.7 %convolution_convert_fusion.1 = bf16[768,128]{1,0:T(8,128)(2,1)} fusion(s32[128]{0:T(128)S(1)} %compare_select_fusion, s32[768]{0:T(1024)S(1)} %fusion.99, bf16[128,128]{1,0:T(8,128)(2,1)} %param.9, f32[128]{0:T(128)} %param.12), kind=kOutput, calls=%fused_computation.28 | convolution fusion | flops 25411584 | bytes 233472 | tf_op jit(solution)/shard_map/dot_general | solution.py:26
  9.5 7.8 %all-to-all-start = ((bf16[32,24,128]{2,1,0:T(8,128)(2,1)}), bf16[32,24,128]{2,1,0:T(8,128)(2,1)S(1)}, u32[]{:S(2)}, u32[]{:S(2)}) async-start(bf16[32,24,128]{2,1,0:T(8,128)(2,1)} %bitcast), calls=%async_computation | async-start | bytes 393216 | tf_op jit(solution)/shard_map/all_to_all | solution.py:62
  17.4 3.1 %collective-permute-start.4 = (bf16[172,2048]{1,0:T(8,128)(2,1)S(1)}, bf16[172,2048]{1,0:T(8,128)(2,1)S(1)}, u32[]{:S(2)}, u32[]{:S(2)}) collective-permute-start(bf16[172,2048]{1,0:T(8,128)(2,1)S(1)} %bitcast.56), channel_id=1, source_target_pairs={{0,16},{16,0},{1,17},{17,1},{2,18},{18,2},{3,19},{19,3},{4,20},{20... | collective-permute-start | bytes 2113544 | tf_op jit(solution)/shard_map/ppermute | solution.py:54
  20.5 6.2 %all-to-all-done = bf16[32,24,128]{2,1,0:T(8,128)(2,1)S(1)} async-done(((bf16[32,24,128]{2,1,0:T(8,128)(2,1)}), bf16[32,24,128]{2,1,0:T(8,128)(2,1)S(1)}, u32[]{:S(2)}, u32[]{:S(2)}) %all-to-all-start) | async-done | bytes 196640 | tf_op jit(solution)/shard_map/all_to_all | solution.py:62
  26.9 10.8 %collective-permute-start.1 = (bf16[96,2048]{1,0:T(8,128)(2,1)S(1)}, bf16[96,2048]{1,0:T(8,128)(2,1)S(1)}, u32[]{:S(2)}, u32[]{:S(2)}) collective-permute-start(bf16[96,2048]{1,0:T(8,128)(2,1)S(1)} %pad_maximum_fusion.2), channel_id=1, source_target_pairs={{0,64},{16,464},{64,128},{80,16},{128,192},{144,80},{192,256},{208... | collective-permute-start | bytes 1179656 | tf_op jit(solution)/shard_map/ppermute | solution.py:22
  37.7 1.9 %collective-permute-start.5 = (bf16[172,2048]{1,0:T(8,128)(2,1)S(1)}, bf16[172,2048]{1,0:T(8,128)(2,1)S(1)}, u32[]{:S(2)}, u32[]{:S(2)}) collective-permute-start(bf16[172,2048]{1,0:T(8,128)(2,1)S(1)} %bitcast.63), channel_id=1, source_target_pairs={{0,16},{16,0},{1,17},{17,1},{2,18},{18,2},{3,19},{19,3},{4,20},{20... | collective-permute-start | bytes 2113544 | tf_op jit(solution)/shard_map/ppermute | solution.py:54
  39.6 2.4 %collective-permute-start.3 = (bf16[172,2048]{1,0:T(8,128)(2,1)S(1)}, bf16[172,2048]{1,0:T(8,128)(2,1)S(1)}, u32[]{:S(2)}, u32[]{:S(2)}) collective-permute-start(bf16[172,2048]{1,0:T(8,128)(2,1)S(1)} %bitcast.58), channel_id=1, source_target_pairs={{0,16},{16,0},{1,17},{17,1},{2,18},{18,2},{3,19},{19,3},{4,20},{20... | collective-permute-start | bytes 2113544 | tf_op jit(solution)/shard_map/ppermute | solution.py:54
  42.0 1.9 %collective-permute-start.2 = (bf16[96,2048]{1,0:T(8,128)(2,1)S(1)}, bf16[96,2048]{1,0:T(8,128)(2,1)S(1)}, u32[]{:S(2)}, u32[]{:S(2)}) collective-permute-start(bf16[96,2048]{1,0:T(8,128)(2,1)S(1)} %pad_maximum_fusion.2), channel_id=1, source_target_pairs={{0,464},{16,64},{64,16},{80,128},{128,80},{144,192},{192,144},{208... | collective-permute-start | bytes 1179656 | tf_op jit(solution)/shard_map/ppermute | solution.py:22
  44.2 7.3 %collective-permute-done.2 = bf16[96,2048]{1,0:T(8,128)(2,1)S(1)} collective-permute-done((bf16[96,2048]{1,0:T(8,128)(2,1)S(1)}, bf16[96,2048]{1,0:T(8,128)(2,1)S(1)}, u32[]{:S(2)}, u32[]{:S(2)}) %collective-permute-start.2) | collective-permute-done | bytes 393248 | tf_op jit(solution)/shard_map/ppermute | solution.py:22
  51.6 5.2 %collective-permute-start.6 = (bf16[192,2048]{1,0:T(8,128)(2,1)S(1)}, bf16[192,2048]{1,0:T(8,128)(2,1)S(1)}, u32[]{:S(2)}, u32[]{:S(2)}) collective-permute-start(bf16[192,2048]{1,0:T(8,128)(2,1)S(1)} %pad_maximum_fusion), channel_id=1, source_target_pairs={{0,64},{16,464},{64,128},{80,16},{128,192},{144,80},{192,256},{208... | collective-permute-start | bytes 2359304 | tf_op jit(solution)/shard_map/ppermute | solution.py:22
  56.8 0.6 fusion.29
  57.4 0.6 fusion.64
  58.0 0.6 multiply_convert_fusion.4
  58.5 0.4 fusion.126
  59.0 0.5 fusion.6
  59.4 1.9 %collective-permute-start.8 = (bf16[96,2048]{1,0:T(8,128)(2,1)S(1)}, bf16[96,2048]{1,0:T(8,128)(2,1)S(1)}, u32[]{:S(2)}, u32[]{:S(2)}) collective-permute-start(bf16[96,2048]{1,0:T(8,128)(2,1)S(1)} %fusion.6), channel_id=1, source_target_pairs={{0,448},{16,80},{64,0},{80,144},{128,64},{144,208},{192,128},{208,... | collective-permute-start | bytes 1179656 | tf_op jit(solution)/shard_map/ppermute | solution.py:22
  61.4 9.8 %collective-permute-done.8 = bf16[96,2048]{1,0:T(8,128)(2,1)S(1)} collective-permute-done((bf16[96,2048]{1,0:T(8,128)(2,1)S(1)}, bf16[96,2048]{1,0:T(8,128)(2,1)S(1)}, u32[]{:S(2)}, u32[]{:S(2)}) %collective-permute-start.8) | collective-permute-done | bytes 393248 | tf_op jit(solution)/shard_map/ppermute | solution.py:22
  71.1 1.9 %collective-permute-start.13 = (bf16[48,2048]{1,0:T(8,128)(2,1)S(1)}, bf16[48,2048]{1,0:T(8,128)(2,1)S(1)}, u32[]{:S(2)}, u32[]{:S(2)}) collective-permute-start(bf16[48,2048]{1,0:T(8,128)(2,1)S(1)} %slice.177), channel_id=1, source_target_pairs={{0,16},{16,0},{1,17},{17,1},{2,18},{18,2},{3,19},{19,3},{4,20},{20... | collective-permute-start | bytes 589832 | tf_op jit(solution)/shard_map/ppermute | solution.py:116
  73.3 0.6 fusion.66
  73.9 0.6 fusion.18
  74.6 0.6 multiply_convert_fusion
  75.2 0.5 fusion.128
  75.7 4.5 %collective-permute-start.7 = (bf16[192,2048]{1,0:T(8,128)(2,1)S(1)}, bf16[192,2048]{1,0:T(8,128)(2,1)S(1)}, u32[]{:S(2)}, u32[]{:S(2)}) collective-permute-start(bf16[192,2048]{1,0:T(8,128)(2,1)S(1)} %collective-permute-done.6), channel_id=1, source_target_pairs={{0,64},{16,464},{64,128},{80,16},{128,192},{144,80},{192,256},{208... | collective-permute-start | bytes 2359304 | tf_op jit(solution)/shard_map/ppermute | solution.py:22
  80.2 0.5 convolution_add_fusion
  80.7 8.4 %collective-permute-done.7 = bf16[192,2048]{1,0:T(8,128)(2,1)S(1)} collective-permute-done((bf16[192,2048]{1,0:T(8,128)(2,1)S(1)}, bf16[192,2048]{1,0:T(8,128)(2,1)S(1)}, u32[]{:S(2)}, u32[]{:S(2)}) %collective-permute-start.7) | collective-permute-done | bytes 786464 | tf_op jit(solution)/shard_map/ppermute | solution.py:22
  89.2 5.0 %collective-permute-start.9 = (bf16[96,2048]{1,0:T(8,128)(2,1)S(1)}, bf16[96,2048]{1,0:T(8,128)(2,1)S(1)}, u32[]{:S(2)}, u32[]{:S(2)}) collective-permute-start(bf16[96,2048]{1,0:T(8,128)(2,1)S(1)} %maximum_add_fusion), channel_id=1, source_target_pairs={{0,64},{16,464},{64,128},{80,16},{128,192},{144,80},{192,256},{208... | collective-permute-start | bytes 1179656 | tf_op jit(solution)/shard_map/ppermute | solution.py:22
  94.2 0.6 fusion.34
  94.8 0.6 fusion.36
  95.4 0.6 multiply_convert_fusion.3
  96.0 0.4 fusion.129
  96.4 0.4 fusion.7
  96.9 1.9 %collective-permute-start.14 = (bf16[96,2048]{1,0:T(8,128)(2,1)S(1)}, bf16[96,2048]{1,0:T(8,128)(2,1)S(1)}, u32[]{:S(2)}, u32[]{:S(2)}) collective-permute-start(bf16[96,2048]{1,0:T(8,128)(2,1)S(1)} %fusion.7), channel_id=1, source_target_pairs={{0,448},{16,80},{64,0},{80,144},{128,64},{144,208},{192,128},{208,... | collective-permute-start | bytes 1179656 | tf_op jit(solution)/shard_map/ppermute | solution.py:22
  98.9 0.6 fusion.76
  99.5 0.6 fusion.78
  100.1 0.6 multiply_convert_fusion.9
  100.6 0.4 fusion.127
  101.0 0.4 fusion.8
  101.5 0.9 fusion.48
  102.4 1.1 slice.254
  103.5 0.8 copy-done.3
  104.3 3.6 %collective-permute-start.16 = (bf16[48,2048]{1,0:T(8,128)(2,1)S(1)}, bf16[48,2048]{1,0:T(8,128)(2,1)S(1)}, u32[]{:S(2)}, u32[]{:S(2)}) collective-permute-start(bf16[48,2048]{1,0:T(8,128)(2,1)S(1)} %fusion.8), channel_id=1, source_target_pairs={{0,384},{16,144},{64,448},{80,208},{128,0},{144,272},{192,64},{208... | collective-permute-start | bytes 589832 | tf_op jit(solution)/shard_map/ppermute | solution.py:22
  107.9 0.9 fusion.40
  108.8 1.0 slice.255
  109.9 0.8 copy-done.1
  110.7 3.7 %collective-permute-start.11 = (bf16[176,2048]{1,0:T(8,128)(2,1)}, bf16[176,2048]{1,0:T(8,128)(2,1)}, u32[]{:S(2)}, u32[]{:S(2)}) collective-permute-start(bf16[176,2048]{1,0:T(8,128)(2,1)} %slice.254), channel_id=1, source_target_pairs={{0,16},{16,0},{1,17},{17,1},{2,18},{18,2},{3,19},{19,3},{4,20},{20... | collective-permute-start | bytes 2162696 | tf_op jit(solution)/shard_map/ppermute | solution.py:114
  114.5 8.0 %collective-permute-start.15 = (bf16[48,2048]{1,0:T(8,128)(2,1)S(1)}, bf16[48,2048]{1,0:T(8,128)(2,1)S(1)}, u32[]{:S(2)}, u32[]{:S(2)}) collective-permute-start(bf16[48,2048]{1,0:T(8,128)(2,1)S(1)} %get-tuple-element.4), channel_id=1, source_target_pairs={{0,400},{16,128},{64,464},{80,192},{128,16},{144,256},{192,80},{20... | collective-permute-start | bytes 589832 | tf_op jit(solution)/shard_map/ppermute | solution.py:22
  122.5 3.4 %collective-permute-start.17 = (bf16[48,2048]{1,0:T(8,128)(2,1)S(1)}, bf16[48,2048]{1,0:T(8,128)(2,1)S(1)}, u32[]{:S(2)}, u32[]{:S(2)}) collective-permute-start(bf16[48,2048]{1,0:T(8,128)(2,1)S(1)} %get-tuple-element.5), channel_id=1, source_target_pairs={{0,384},{16,144},{64,448},{80,208},{128,0},{144,272},{192,64},{208... | collective-permute-start | bytes 589832 | tf_op jit(solution)/shard_map/ppermute | solution.py:22
  125.9 0.9 fusion.56
  126.9 1.0 slice.253
  127.9 0.7 copy-done.2
  128.7 1.9 %collective-permute-start.10 = (bf16[176,2048]{1,0:T(8,128)(2,1)}, bf16[176,2048]{1,0:T(8,128)(2,1)}, u32[]{:S(2)}, u32[]{:S(2)}) collective-permute-start(bf16[176,2048]{1,0:T(8,128)(2,1)} %slice.255), channel_id=1, source_target_pairs={{0,16},{16,0},{1,17},{17,1},{2,18},{18,2},{3,19},{19,3},{4,20},{20... | collective-permute-start | bytes 2162696 | tf_op jit(solution)/shard_map/ppermute | solution.py:114
  130.6 2.5 %collective-permute-start.12 = (bf16[176,2048]{1,0:T(8,128)(2,1)}, bf16[176,2048]{1,0:T(8,128)(2,1)S(1)}, u32[]{:S(2)}, u32[]{:S(2)}) collective-permute-start(bf16[176,2048]{1,0:T(8,128)(2,1)} %slice.253), channel_id=1, source_target_pairs={{0,16},{16,0},{1,17},{17,1},{2,18},{18,2},{3,19},{19,3},{4,20},{20... | collective-permute-start | bytes 2162696 | tf_op jit(solution)/shard_map/ppermute | solution.py:114
  133.4 0.7 copy.14
  134.1 4.6 %all-to-all-start.1 = ((bf16[32,24,128]{2,1,0:T(8,128)(2,1)}), bf16[32,24,128]{2,1,0:T(8,128)(2,1)}, u32[]{:S(2)}, u32[]{:S(2)}) async-start(bf16[32,24,128]{2,1,0:T(8,128)(2,1)} %bitcast.11), calls=%async_computation.1 | async-start | bytes 393216 | tf_op jit(solution)/shard_map/all_to_all | solution.py:128
  138.7 1.4 fusion.16
  140.1 0.6 slice.173
  140.7 1.4 fusion.15
  142.1 0.6 slice.172
  143.0 0.6 slice.174
  145.5 3.1 %all-to-all-done.1 = bf16[32,24,128]{2,1,0:T(8,128)(2,1)} async-done(((bf16[32,24,128]{2,1,0:T(8,128)(2,1)}), bf16[32,24,128]{2,1,0:T(8,128)(2,1)}, u32[]{:S(2)}, u32[]{:S(2)}) %all-to-all-start.1) | async-done | bytes 196640 | tf_op jit(solution)/shard_map/all_to_all | solution.py:128
  148.6 1.8 %convolution_convert_fusion.2 = bf16[128,128]{1,0:T(8,128)(2,1)} fusion(bf16[768,128]{1,0:T(8,128)(2,1)} %bitcast.12, s32[768]{0:T(1024)S(1)} %fusion.99, s32[128]{0:T(128)S(1)} %compare_select_fusion, bf16[]{:T(256)} %bitcast.9), kind=kOutput, calls=%fused_computation.29 | convolution fusion | flops 25477120 | bytes 232962 | tf_op jit(solution)/shard_map/dot_general | solution.py:26
  (67 shorter events, 2.1 us)
Async XLA Ops:
  0.6 1.3 copy-start
  0.6 16.7 %copy-start.4 = (bf16[1,172,2048]{2,1,0:T(8,128)(2,1)S(1)}, bf16[1,172,2048]{2,1,0:T(8,128)(2,1)}, u32[]{:S(2)}) copy-start(bf16[1,172,2048]{2,1,0:T(8,128)(2,1)} %param.14) | copy-start | bytes 2113540
  2.1 37.5 %copy-start.8 = (bf16[1,172,2048]{2,1,0:T(8,128)(2,1)S(1)}, bf16[1,172,2048]{2,1,0:T(8,128)(2,1)}, u32[]{:S(2)}) copy-start(bf16[1,172,2048]{2,1,0:T(8,128)(2,1)} %param.15) | copy-start | bytes 2113540
  2.2 18.4 %collective-permute-start = (bf16[24,2048]{1,0:T(8,128)(2,1)S(1)}, bf16[24,2048]{1,0:T(8,128)(2,1)S(1)}, u32[]{:S(2)}, u32[]{:S(2)}) collective-permute-start(bf16[24,2048]{1,0:T(8,128)(2,1)S(1)} %convolution_convert_fusion), channel_id=1, source_target_pairs={{0,32},{32,0},{1,33},{33,1},{2,34},{34,2},{3,35},{35,3},{4,36},{36... | collective-permute-start | bytes 294920 | tf_op jit(solution)/shard_map/ppermute | solution.py:59
  9.5 17.2 %all-to-all-start = ((bf16[32,24,128]{2,1,0:T(8,128)(2,1)}), bf16[32,24,128]{2,1,0:T(8,128)(2,1)S(1)}, u32[]{:S(2)}, u32[]{:S(2)}) async-start(bf16[32,24,128]{2,1,0:T(8,128)(2,1)} %bitcast), calls=%async_computation | async-start | bytes 393216 | tf_op jit(solution)/shard_map/all_to_all | solution.py:62
  17.4 26.6 %collective-permute-start.4 = (bf16[172,2048]{1,0:T(8,128)(2,1)S(1)}, bf16[172,2048]{1,0:T(8,128)(2,1)S(1)}, u32[]{:S(2)}, u32[]{:S(2)}) collective-permute-start(bf16[172,2048]{1,0:T(8,128)(2,1)S(1)} %bitcast.56), channel_id=1, source_target_pairs={{0,16},{16,0},{1,17},{17,1},{2,18},{18,2},{3,19},{19,3},{4,20},{20... | collective-permute-start | bytes 2113544 | tf_op jit(solution)/shard_map/ppermute | solution.py:54
  26.7 10.9 %copy-start.9 = (bf16[1,172,2048]{2,1,0:T(8,128)(2,1)S(1)}, bf16[1,172,2048]{2,1,0:T(8,128)(2,1)}, u32[]{:S(2)}) copy-start(bf16[1,172,2048]{2,1,0:T(8,128)(2,1)} %param.13) | copy-start | bytes 2113540
  26.9 17.2 %collective-permute-start.1 = (bf16[96,2048]{1,0:T(8,128)(2,1)S(1)}, bf16[96,2048]{1,0:T(8,128)(2,1)S(1)}, u32[]{:S(2)}, u32[]{:S(2)}) collective-permute-start(bf16[96,2048]{1,0:T(8,128)(2,1)S(1)} %pad_maximum_fusion.2), channel_id=1, source_target_pairs={{0,64},{16,464},{64,128},{80,16},{128,192},{144,80},{192,256},{208... | collective-permute-start | bytes 1179656 | tf_op jit(solution)/shard_map/ppermute | solution.py:22
  37.7 19.7 %collective-permute-start.5 = (bf16[172,2048]{1,0:T(8,128)(2,1)S(1)}, bf16[172,2048]{1,0:T(8,128)(2,1)S(1)}, u32[]{:S(2)}, u32[]{:S(2)}) collective-permute-start(bf16[172,2048]{1,0:T(8,128)(2,1)S(1)} %bitcast.63), channel_id=1, source_target_pairs={{0,16},{16,0},{1,17},{17,1},{2,18},{18,2},{3,19},{19,3},{4,20},{20... | collective-permute-start | bytes 2113544 | tf_op jit(solution)/shard_map/ppermute | solution.py:54
  39.6 17.2 %collective-permute-start.3 = (bf16[172,2048]{1,0:T(8,128)(2,1)S(1)}, bf16[172,2048]{1,0:T(8,128)(2,1)S(1)}, u32[]{:S(2)}, u32[]{:S(2)}) collective-permute-start(bf16[172,2048]{1,0:T(8,128)(2,1)S(1)} %bitcast.58), channel_id=1, source_target_pairs={{0,16},{16,0},{1,17},{17,1},{2,18},{18,2},{3,19},{19,3},{4,20},{20... | collective-permute-start | bytes 2113544 | tf_op jit(solution)/shard_map/ppermute | solution.py:54
  42.0 9.4 %collective-permute-start.2 = (bf16[96,2048]{1,0:T(8,128)(2,1)S(1)}, bf16[96,2048]{1,0:T(8,128)(2,1)S(1)}, u32[]{:S(2)}, u32[]{:S(2)}) collective-permute-start(bf16[96,2048]{1,0:T(8,128)(2,1)S(1)} %pad_maximum_fusion.2), channel_id=1, source_target_pairs={{0,464},{16,64},{64,16},{80,128},{128,80},{144,192},{192,144},{208... | collective-permute-start | bytes 1179656 | tf_op jit(solution)/shard_map/ppermute | solution.py:22
  51.6 21.5 %collective-permute-start.6 = (bf16[192,2048]{1,0:T(8,128)(2,1)S(1)}, bf16[192,2048]{1,0:T(8,128)(2,1)S(1)}, u32[]{:S(2)}, u32[]{:S(2)}) collective-permute-start(bf16[192,2048]{1,0:T(8,128)(2,1)S(1)} %pad_maximum_fusion), channel_id=1, source_target_pairs={{0,64},{16,464},{64,128},{80,16},{128,192},{144,80},{192,256},{208... | collective-permute-start | bytes 2359304 | tf_op jit(solution)/shard_map/ppermute | solution.py:22
  59.4 11.7 %collective-permute-start.8 = (bf16[96,2048]{1,0:T(8,128)(2,1)S(1)}, bf16[96,2048]{1,0:T(8,128)(2,1)S(1)}, u32[]{:S(2)}, u32[]{:S(2)}) collective-permute-start(bf16[96,2048]{1,0:T(8,128)(2,1)S(1)} %fusion.6), channel_id=1, source_target_pairs={{0,448},{16,80},{64,0},{80,144},{128,64},{144,208},{192,128},{208,... | collective-permute-start | bytes 1179656 | tf_op jit(solution)/shard_map/ppermute | solution.py:22
  71.1 59.5 %collective-permute-start.13 = (bf16[48,2048]{1,0:T(8,128)(2,1)S(1)}, bf16[48,2048]{1,0:T(8,128)(2,1)S(1)}, u32[]{:S(2)}, u32[]{:S(2)}) collective-permute-start(bf16[48,2048]{1,0:T(8,128)(2,1)S(1)} %slice.177), channel_id=1, source_target_pairs={{0,16},{16,0},{1,17},{17,1},{2,18},{18,2},{3,19},{19,3},{4,20},{20... | collective-permute-start | bytes 589832 | tf_op jit(solution)/shard_map/ppermute | solution.py:116
  75.7 13.4 %collective-permute-start.7 = (bf16[192,2048]{1,0:T(8,128)(2,1)S(1)}, bf16[192,2048]{1,0:T(8,128)(2,1)S(1)}, u32[]{:S(2)}, u32[]{:S(2)}) collective-permute-start(bf16[192,2048]{1,0:T(8,128)(2,1)S(1)} %collective-permute-done.6), channel_id=1, source_target_pairs={{0,64},{16,464},{64,128},{80,16},{128,192},{144,80},{192,256},{208... | collective-permute-start | bytes 2359304 | tf_op jit(solution)/shard_map/ppermute | solution.py:22
  89.2 9.7 %collective-permute-start.9 = (bf16[96,2048]{1,0:T(8,128)(2,1)S(1)}, bf16[96,2048]{1,0:T(8,128)(2,1)S(1)}, u32[]{:S(2)}, u32[]{:S(2)}) collective-permute-start(bf16[96,2048]{1,0:T(8,128)(2,1)S(1)} %maximum_add_fusion), channel_id=1, source_target_pairs={{0,64},{16,464},{64,128},{80,16},{128,192},{144,80},{192,256},{208... | collective-permute-start | bytes 1179656 | tf_op jit(solution)/shard_map/ppermute | solution.py:22
  96.9 17.5 %collective-permute-start.14 = (bf16[96,2048]{1,0:T(8,128)(2,1)S(1)}, bf16[96,2048]{1,0:T(8,128)(2,1)S(1)}, u32[]{:S(2)}, u32[]{:S(2)}) collective-permute-start(bf16[96,2048]{1,0:T(8,128)(2,1)S(1)} %fusion.7), channel_id=1, source_target_pairs={{0,448},{16,80},{64,0},{80,144},{128,64},{144,208},{192,128},{208,... | collective-permute-start | bytes 1179656 | tf_op jit(solution)/shard_map/ppermute | solution.py:22
  102.4 1.8 %copy-start.3 = (f32[352,2048]{1,0:T(8,128)}, f32[352,2048]{1,0:T(8,128)S(1)}, u32[]{:S(2)}) copy-start(f32[352,2048]{1,0:T(8,128)S(1)} %fusion.48) | copy-start | bytes 8650756
  104.3 10.1 %collective-permute-start.16 = (bf16[48,2048]{1,0:T(8,128)(2,1)S(1)}, bf16[48,2048]{1,0:T(8,128)(2,1)S(1)}, u32[]{:S(2)}, u32[]{:S(2)}) collective-permute-start(bf16[48,2048]{1,0:T(8,128)(2,1)S(1)} %fusion.8), channel_id=1, source_target_pairs={{0,384},{16,144},{64,448},{80,208},{128,0},{144,272},{192,64},{208... | collective-permute-start | bytes 589832 | tf_op jit(solution)/shard_map/ppermute | solution.py:22
  108.8 1.8 %copy-start.1 = (f32[352,2048]{1,0:T(8,128)}, f32[352,2048]{1,0:T(8,128)S(1)}, u32[]{:S(2)}) copy-start(f32[352,2048]{1,0:T(8,128)S(1)} %fusion.40) | copy-start | bytes 8650756
  110.7 28.0 %collective-permute-start.11 = (bf16[176,2048]{1,0:T(8,128)(2,1)}, bf16[176,2048]{1,0:T(8,128)(2,1)}, u32[]{:S(2)}, u32[]{:S(2)}) collective-permute-start(bf16[176,2048]{1,0:T(8,128)(2,1)} %slice.254), channel_id=1, source_target_pairs={{0,16},{16,0},{1,17},{17,1},{2,18},{18,2},{3,19},{19,3},{4,20},{20... | collective-permute-start | bytes 2162696 | tf_op jit(solution)/shard_map/ppermute | solution.py:114
  114.5 18.7 %collective-permute-start.15 = (bf16[48,2048]{1,0:T(8,128)(2,1)S(1)}, bf16[48,2048]{1,0:T(8,128)(2,1)S(1)}, u32[]{:S(2)}, u32[]{:S(2)}) collective-permute-start(bf16[48,2048]{1,0:T(8,128)(2,1)S(1)} %get-tuple-element.4), channel_id=1, source_target_pairs={{0,400},{16,128},{64,464},{80,192},{128,16},{144,256},{192,80},{20... | collective-permute-start | bytes 589832 | tf_op jit(solution)/shard_map/ppermute | solution.py:22
  122.5 10.7 %collective-permute-start.17 = (bf16[48,2048]{1,0:T(8,128)(2,1)S(1)}, bf16[48,2048]{1,0:T(8,128)(2,1)S(1)}, u32[]{:S(2)}, u32[]{:S(2)}) collective-permute-start(bf16[48,2048]{1,0:T(8,128)(2,1)S(1)} %get-tuple-element.5), channel_id=1, source_target_pairs={{0,384},{16,144},{64,448},{80,208},{128,0},{144,272},{192,64},{208... | collective-permute-start | bytes 589832 | tf_op jit(solution)/shard_map/ppermute | solution.py:22
  126.9 1.8 %copy-start.2 = (f32[352,2048]{1,0:T(8,128)}, f32[352,2048]{1,0:T(8,128)S(1)}, u32[]{:S(2)}) copy-start(f32[352,2048]{1,0:T(8,128)S(1)} %fusion.56) | copy-start | bytes 8650756
  128.7 12.0 %collective-permute-start.10 = (bf16[176,2048]{1,0:T(8,128)(2,1)}, bf16[176,2048]{1,0:T(8,128)(2,1)}, u32[]{:S(2)}, u32[]{:S(2)}) collective-permute-start(bf16[176,2048]{1,0:T(8,128)(2,1)} %slice.255), channel_id=1, source_target_pairs={{0,16},{16,0},{1,17},{17,1},{2,18},{18,2},{3,19},{19,3},{4,20},{20... | collective-permute-start | bytes 2162696 | tf_op jit(solution)/shard_map/ppermute | solution.py:114
  130.6 8.1 %slice-start.2 = ((f32[352,2048]{1,0:T(8,128)}), f32[176,2048]{1,0:T(8,128)S(1)}, s32[]{:S(2)}) async-start(f32[352,2048]{1,0:T(8,128)} %copy-done.3), calls=%async_computation.4 | async-start | bytes 2883584 | tf_op jit(solution)/shard_map/slice | solution.py:131
  130.6 12.0 %collective-permute-start.12 = (bf16[176,2048]{1,0:T(8,128)(2,1)}, bf16[176,2048]{1,0:T(8,128)(2,1)S(1)}, u32[]{:S(2)}, u32[]{:S(2)}) collective-permute-start(bf16[176,2048]{1,0:T(8,128)(2,1)} %slice.253), channel_id=1, source_target_pairs={{0,16},{16,0},{1,17},{17,1},{2,18},{18,2},{3,19},{19,3},{4,20},{20... | collective-permute-start | bytes 2162696 | tf_op jit(solution)/shard_map/ppermute | solution.py:114
  134.1 14.5 %all-to-all-start.1 = ((bf16[32,24,128]{2,1,0:T(8,128)(2,1)}), bf16[32,24,128]{2,1,0:T(8,128)(2,1)}, u32[]{:S(2)}, u32[]{:S(2)}) async-start(bf16[32,24,128]{2,1,0:T(8,128)(2,1)} %bitcast.11), calls=%async_computation.1 | async-start | bytes 393216 | tf_op jit(solution)/shard_map/all_to_all | solution.py:128
  138.7 2.0 %slice-start = ((f32[352,2048]{1,0:T(8,128)}), f32[176,2048]{1,0:T(8,128)S(1)}, s32[]{:S(2)}) async-start(f32[352,2048]{1,0:T(8,128)} %copy-done.1), calls=%async_computation.2 | async-start | bytes 2883584 | tf_op jit(solution)/shard_map/slice | solution.py:131
  140.1 2.0 %copy-start.5 = (bf16[1,172,2048]{2,1,0:T(8,128)(2,1)}, bf16[1,172,2048]{2,1,0:T(8,128)(2,1)S(1)}, u32[]{:S(2)}) copy-start(bf16[1,172,2048]{2,1,0:T(8,128)(2,1)S(1)} %fusion.16) | copy-start | bytes 2113540
  140.7 2.0 %slice-start.1 = ((f32[352,2048]{1,0:T(8,128)}), f32[176,2048]{1,0:T(8,128)S(1)}, s32[]{:S(2)}) async-start(f32[352,2048]{1,0:T(8,128)} %copy-done.2), calls=%async_computation.3 | async-start | bytes 2883584 | tf_op jit(solution)/shard_map/slice | solution.py:131
  142.1 0.9 copy-start.6
  142.9 7.4 %copy-start.7 = (bf16[1,172,2048]{2,1,0:T(8,128)(2,1)}, bf16[1,172,2048]{2,1,0:T(8,128)(2,1)S(1)}, u32[]{:S(2)}) copy-start(bf16[1,172,2048]{2,1,0:T(8,128)(2,1)S(1)} %fusion.17) | copy-start | bytes 2113540

commit v13 on v12

--- a/solution.py
+++ b/solution.py
@@ -113,13 +113,13 @@
     ]
     received = [lax.ppermute(grad[PAD:].astype(BF), "core", SWAP) for grad in grads]
 
-    one_across = lax.ppermute(one_home[near:], "core", SWAP)
     three_near = ring(terms_three.astype(BF), -1)
     four_near = ring(terms_four.astype(BF), -2)
     home_b = terms_two[near:] + three_near[near:].astype(F32)
     home_b = ring(home_b.astype(BF), -2, cross=True)
     home_a = terms_two[:near] + three_near[:near].astype(F32) + four_near.astype(F32)
     home_a = ring(home_a.astype(BF), -2)
+    one_across = lax.ppermute(one_home[near:] + three_near[:1] * 0, "core", SWAP)
     summed = terms_own
     for came in (one_home[:near], one_across, home_b, home_a):
         summed = summed + came.astype(F32)

time: 152 us -> 152 us (level)
  waiting for transfers between devices: 34.8 us -> 36.8 us
  starting transfers between devices: 81.8 us -> 80.2 us
    ppermute x10, starting transfers between devices: 46.3 us -> 43.4 us  [ring(): return lax.ppermute(a, ('z', 'core'), pairs)]
    ppermute x10, waiting for transfers between devices: 25.5 us -> 27.3 us  [ring(): return lax.ppermute(a, ('z', 'core'), pairs)]
  transfers between devices with their start and end apart: 20 -> 20, of which waited for: 6 -> 6; matrix products, arithmetic and copies ran while one was open for 17% -> 15% of each run, Pallas kernels for 0% -> 0%
where the time goes in v13:
time: 152 us; the launch traced here: 151 us
  starting transfers between devices  80.2 us (53%)
  waiting for transfers between devices  36.8 us (24%)
  matrix products  17.1 us (11%)
  local copies, waits for them, and re-layouts  8.45 us (6%)
  other arithmetic  4.92 us (3%)
  between operations  3.2 us (2%)
    ppermute x10, starting transfers between devices, ring(): return lax.ppermute(a, ('z', 'core'), pairs)  43.4 us
    ppermute x10, waiting for transfers between devices, ring(): return lax.ppermute(a, ('z', 'core'), pairs)  27.3 us
    dot_general x26, matrix products, dot(): return lax.dot_general(a, b, (dims, ((), ())), preferred_element_type=F32)  17.1 us
    ppermute x3, starting transfers between devices, local(): lax.ppermute(grad[PAD:].astype(BF), 'core', SWAP)  9.44 us
    all_to_all x1, starting transfers between devices, local(): dy_slices = lax.all_to_all(dy_slices, ('xh',) + EXPERT, 0, 0, tiled=True)  7.79 us
    ppermute x3, starting transfers between devices, both_cores(): lax.ppermute(w, 'core', SWAP)  7.47 us
    all_to_all x1, waiting for transfers between devices, local(): dy_slices = lax.all_to_all(dy_slices, ('xh',) + EXPERT, 0, 0, tiled=True)  6.19 us
    ppermute x1, starting transfers between devices, local(): x_across = lax.ppermute(x_own, 'xh', SWAP)  5.61 us
  transfers between devices with their start and end apart: 20, of which 6 were waited for; matrix products, arithmetic and copies ran while one was open for 15% of the time, Pallas kernels for 0%

profile of v13, /device:TPU:1, one launch (start us, length us, event | category | flops | bytes accessed | tf_op | source)
XLA Modules:
  0.0 150.7 jit_solution(8419373151568852710)
XLA Ops:
  0.7 0.8 multiply_add_fusion
  2.2 5.6 %collective-permute-start = (bf16[24,2048]{1,0:T(8,128)(2,1)S(1)}, bf16[24,2048]{1,0:T(8,128)(2,1)S(1)}, u32[]{:S(2)}, u32[]{:S(2)}) collective-permute-start(bf16[24,2048]{1,0:T(8,128)(2,1)S(1)} %convolution_convert_fusion), channel_id=1, source_target_pairs={{0,32},{32,0},{1,33},{33,1},{2,34},{34,2},{3,35},{35,3},{4,36},{36... | collective-permute-start | bytes 294920 | tf_op jit(solution)/shard_map/ppermute | solution.py:59
  7.8 1.7 %convolution_convert_fusion.1 = bf16[768,128]{1,0:T(8,128)(2,1)} fusion(s32[128]{0:T(128)S(1)} %compare_select_fusion, s32[768]{0:T(1024)S(1)} %fusion.100, bf16[128,128]{1,0:T(8,128)(2,1)} %param.9, f32[128]{0:T(128)} %param.12), kind=kOutput, calls=%fused_computation.28 | convolution fusion | flops 25411584 | bytes 233472 | tf_op jit(solution)/shard_map/dot_general | solution.py:26
  9.5 7.8 %all-to-all-start = ((bf16[32,24,128]{2,1,0:T(8,128)(2,1)}), bf16[32,24,128]{2,1,0:T(8,128)(2,1)S(1)}, u32[]{:S(2)}, u32[]{:S(2)}) async-start(bf16[32,24,128]{2,1,0:T(8,128)(2,1)} %bitcast), calls=%async_computation | async-start | bytes 393216 | tf_op jit(solution)/shard_map/all_to_all | solution.py:62
  17.4 3.1 %collective-permute-start.4 = (bf16[172,2048]{1,0:T(8,128)(2,1)S(1)}, bf16[172,2048]{1,0:T(8,128)(2,1)S(1)}, u32[]{:S(2)}, u32[]{:S(2)}) collective-permute-start(bf16[172,2048]{1,0:T(8,128)(2,1)S(1)} %bitcast.56), channel_id=1, source_target_pairs={{0,16},{16,0},{1,17},{17,1},{2,18},{18,2},{3,19},{19,3},{4,20},{20... | collective-permute-start | bytes 2113544 | tf_op jit(solution)/shard_map/ppermute | solution.py:54
  20.5 6.2 %all-to-all-done = bf16[32,24,128]{2,1,0:T(8,128)(2,1)S(1)} async-done(((bf16[32,24,128]{2,1,0:T(8,128)(2,1)}), bf16[32,24,128]{2,1,0:T(8,128)(2,1)S(1)}, u32[]{:S(2)}, u32[]{:S(2)}) %all-to-all-start) | async-done | bytes 196640 | tf_op jit(solution)/shard_map/all_to_all | solution.py:62
  26.9 10.8 %collective-permute-start.1 = (bf16[96,2048]{1,0:T(8,128)(2,1)S(1)}, bf16[96,2048]{1,0:T(8,128)(2,1)S(1)}, u32[]{:S(2)}, u32[]{:S(2)}) collective-permute-start(bf16[96,2048]{1,0:T(8,128)(2,1)S(1)} %pad_maximum_fusion.2), channel_id=1, source_target_pairs={{0,64},{16,464},{64,128},{80,16},{128,192},{144,80},{192,256},{208... | collective-permute-start | bytes 1179656 | tf_op jit(solution)/shard_map/ppermute | solution.py:22
  37.7 1.9 %collective-permute-start.5 = (bf16[172,2048]{1,0:T(8,128)(2,1)S(1)}, bf16[172,2048]{1,0:T(8,128)(2,1)S(1)}, u32[]{:S(2)}, u32[]{:S(2)}) collective-permute-start(bf16[172,2048]{1,0:T(8,128)(2,1)S(1)} %bitcast.63), channel_id=1, source_target_pairs={{0,16},{16,0},{1,17},{17,1},{2,18},{18,2},{3,19},{19,3},{4,20},{20... | collective-permute-start | bytes 2113544 | tf_op jit(solution)/shard_map/ppermute | solution.py:54
  39.6 2.4 %collective-permute-start.3 = (bf16[172,2048]{1,0:T(8,128)(2,1)S(1)}, bf16[172,2048]{1,0:T(8,128)(2,1)S(1)}, u32[]{:S(2)}, u32[]{:S(2)}) collective-permute-start(bf16[172,2048]{1,0:T(8,128)(2,1)S(1)} %bitcast.58), channel_id=1, source_target_pairs={{0,16},{16,0},{1,17},{17,1},{2,18},{18,2},{3,19},{19,3},{4,20},{20... | collective-permute-start | bytes 2113544 | tf_op jit(solution)/shard_map/ppermute | solution.py:54
  42.0 1.9 %collective-permute-start.2 = (bf16[96,2048]{1,0:T(8,128)(2,1)S(1)}, bf16[96,2048]{1,0:T(8,128)(2,1)S(1)}, u32[]{:S(2)}, u32[]{:S(2)}) collective-permute-start(bf16[96,2048]{1,0:T(8,128)(2,1)S(1)} %pad_maximum_fusion.2), channel_id=1, source_target_pairs={{0,464},{16,64},{64,16},{80,128},{128,80},{144,192},{192,144},{208... | collective-permute-start | bytes 1179656 | tf_op jit(solution)/shard_map/ppermute | solution.py:22
  44.2 7.3 %collective-permute-done.2 = bf16[96,2048]{1,0:T(8,128)(2,1)S(1)} collective-permute-done((bf16[96,2048]{1,0:T(8,128)(2,1)S(1)}, bf16[96,2048]{1,0:T(8,128)(2,1)S(1)}, u32[]{:S(2)}, u32[]{:S(2)}) %collective-permute-start.2) | collective-permute-done | bytes 393248 | tf_op jit(solution)/shard_map/ppermute | solution.py:22
  51.6 5.2 %collective-permute-start.6 = (bf16[192,2048]{1,0:T(8,128)(2,1)S(1)}, bf16[192,2048]{1,0:T(8,128)(2,1)S(1)}, u32[]{:S(2)}, u32[]{:S(2)}) collective-permute-start(bf16[192,2048]{1,0:T(8,128)(2,1)S(1)} %pad_maximum_fusion), channel_id=1, source_target_pairs={{0,64},{16,464},{64,128},{80,16},{128,192},{144,80},{192,256},{208... | collective-permute-start | bytes 2359304 | tf_op jit(solution)/shard_map/ppermute | solution.py:22
  56.8 0.6 fusion.29
  57.4 0.6 fusion.64
  58.0 0.6 multiply_convert_fusion.4
  58.5 0.4 fusion.127
  59.0 0.5 fusion.6
  59.4 1.9 %collective-permute-start.8 = (bf16[96,2048]{1,0:T(8,128)(2,1)S(1)}, bf16[96,2048]{1,0:T(8,128)(2,1)S(1)}, u32[]{:S(2)}, u32[]{:S(2)}) collective-permute-start(bf16[96,2048]{1,0:T(8,128)(2,1)S(1)} %fusion.6), channel_id=1, source_target_pairs={{0,448},{16,80},{64,0},{80,144},{128,64},{144,208},{192,128},{208,... | collective-permute-start | bytes 1179656 | tf_op jit(solution)/shard_map/ppermute | solution.py:22
  61.4 9.8 %collective-permute-done.8 = bf16[96,2048]{1,0:T(8,128)(2,1)S(1)} collective-permute-done((bf16[96,2048]{1,0:T(8,128)(2,1)S(1)}, bf16[96,2048]{1,0:T(8,128)(2,1)S(1)}, u32[]{:S(2)}, u32[]{:S(2)}) %collective-permute-start.8) | collective-permute-done | bytes 393248 | tf_op jit(solution)/shard_map/ppermute | solution.py:22
  71.3 0.6 fusion.66
  72.0 0.6 fusion.18
  72.6 0.6 multiply_convert_fusion
  73.3 0.5 fusion.129
  73.7 2.6 %collective-permute-start.7 = (bf16[192,2048]{1,0:T(8,128)(2,1)S(1)}, bf16[192,2048]{1,0:T(8,128)(2,1)S(1)}, u32[]{:S(2)}, u32[]{:S(2)}) collective-permute-start(bf16[192,2048]{1,0:T(8,128)(2,1)S(1)} %collective-permute-done.6), channel_id=1, source_target_pairs={{0,64},{16,464},{64,128},{80,16},{128,192},{144,80},{192,256},{208... | collective-permute-start | bytes 2359304 | tf_op jit(solution)/shard_map/ppermute | solution.py:22
  76.4 0.5 convolution_add_fusion
  76.9 9.8 %collective-permute-done.7 = bf16[192,2048]{1,0:T(8,128)(2,1)S(1)} collective-permute-done((bf16[192,2048]{1,0:T(8,128)(2,1)S(1)}, bf16[192,2048]{1,0:T(8,128)(2,1)S(1)}, u32[]{:S(2)}, u32[]{:S(2)}) %collective-permute-start.7) | collective-permute-done | bytes 786464 | tf_op jit(solution)/shard_map/ppermute | solution.py:22
  86.9 3.6 %collective-permute-start.9 = (bf16[96,2048]{1,0:T(8,128)(2,1)S(1)}, bf16[96,2048]{1,0:T(8,128)(2,1)S(1)}, u32[]{:S(2)}, u32[]{:S(2)}) collective-permute-start(bf16[96,2048]{1,0:T(8,128)(2,1)S(1)} %maximum_add_fusion), channel_id=1, source_target_pairs={{0,64},{16,464},{64,128},{80,16},{128,192},{144,80},{192,256},{208... | collective-permute-start | bytes 1179656 | tf_op jit(solution)/shard_map/ppermute | solution.py:22
  90.4 0.6 fusion.34
  91.0 0.6 fusion.36
  91.6 0.6 multiply_convert_fusion.3
  92.2 0.4 fusion.130
  92.6 0.4 fusion.7
  93.1 2.1 %collective-permute-start.13 = (bf16[96,2048]{1,0:T(8,128)(2,1)S(1)}, bf16[96,2048]{1,0:T(8,128)(2,1)S(1)}, u32[]{:S(2)}, u32[]{:S(2)}) collective-permute-start(bf16[96,2048]{1,0:T(8,128)(2,1)S(1)} %fusion.7), channel_id=1, source_target_pairs={{0,448},{16,80},{64,0},{80,144},{128,64},{144,208},{192,128},{208,... | collective-permute-start | bytes 1179656 | tf_op jit(solution)/shard_map/ppermute | solution.py:22
  95.2 0.4 collective-permute-done.9
  95.7 0.6 fusion.76
  96.3 0.6 fusion.78
  96.8 0.6 multiply_convert_fusion.9
  97.4 0.4 fusion.128
  97.7 0.4 fusion.8
  98.2 0.9 fusion.48
  99.2 1.0 slice.263
  100.2 0.8 copy-done.3
  101.0 0.9 fusion.40
  102.0 1.0 slice.264
  103.0 0.8 copy-done.1
  103.8 3.6 %collective-permute-start.16 = (bf16[48,2048]{1,0:T(8,128)(2,1)S(1)}, bf16[48,2048]{1,0:T(8,128)(2,1)S(1)}, u32[]{:S(2)}, u32[]{:S(2)}) collective-permute-start(bf16[48,2048]{1,0:T(8,128)(2,1)S(1)} %fusion.8), channel_id=1, source_target_pairs={{0,384},{16,144},{64,448},{80,208},{128,0},{144,272},{192,64},{208... | collective-permute-start | bytes 589832 | tf_op jit(solution)/shard_map/ppermute | solution.py:22
  107.3 5.0 %collective-permute-start.11 = (bf16[176,2048]{1,0:T(8,128)(2,1)}, bf16[176,2048]{1,0:T(8,128)(2,1)}, u32[]{:S(2)}, u32[]{:S(2)}) collective-permute-start(bf16[176,2048]{1,0:T(8,128)(2,1)} %slice.263), channel_id=1, source_target_pairs={{0,16},{16,0},{1,17},{17,1},{2,18},{18,2},{3,19},{19,3},{4,20},{20... | collective-permute-start | bytes 2162696 | tf_op jit(solution)/shard_map/ppermute | solution.py:114
  112.4 1.9 %collective-permute-start.14 = (bf16[48,2048]{1,0:T(8,128)(2,1)S(1)}, bf16[48,2048]{1,0:T(8,128)(2,1)S(1)}, u32[]{:S(2)}, u32[]{:S(2)}) collective-permute-start(bf16[48,2048]{1,0:T(8,128)(2,1)S(1)} %slice_add_fusion.6), channel_id=1, source_target_pairs={{0,16},{16,0},{1,17},{17,1},{2,18},{18,2},{3,19},{19,3},{4,20},{20... | collective-permute-start | bytes 589832 | tf_op jit(solution)/shard_map/ppermute | solution.py:122
  114.5 8.4 %collective-permute-start.15 = (bf16[48,2048]{1,0:T(8,128)(2,1)S(1)}, bf16[48,2048]{1,0:T(8,128)(2,1)S(1)}, u32[]{:S(2)}, u32[]{:S(2)}) collective-permute-start(bf16[48,2048]{1,0:T(8,128)(2,1)S(1)} %get-tuple-element.4), channel_id=1, source_target_pairs={{0,400},{16,128},{64,464},{80,192},{128,16},{144,256},{192,80},{20... | collective-permute-start | bytes 589832 | tf_op jit(solution)/shard_map/ppermute | solution.py:22
  122.9 3.4 %collective-permute-start.17 = (bf16[48,2048]{1,0:T(8,128)(2,1)S(1)}, bf16[48,2048]{1,0:T(8,128)(2,1)S(1)}, u32[]{:S(2)}, u32[]{:S(2)}) collective-permute-start(bf16[48,2048]{1,0:T(8,128)(2,1)S(1)} %get-tuple-element.5), channel_id=1, source_target_pairs={{0,384},{16,144},{64,448},{80,208},{128,0},{144,272},{192,64},{208... | collective-permute-start | bytes 589832 | tf_op jit(solution)/shard_map/ppermute | solution.py:22
  126.2 0.9 fusion.56
  127.2 1.0 slice.262
  128.2 0.7 copy-done.2
  129.0 1.9 %collective-permute-start.10 = (bf16[176,2048]{1,0:T(8,128)(2,1)}, bf16[176,2048]{1,0:T(8,128)(2,1)}, u32[]{:S(2)}, u32[]{:S(2)}) collective-permute-start(bf16[176,2048]{1,0:T(8,128)(2,1)} %slice.264), channel_id=1, source_target_pairs={{0,16},{16,0},{1,17},{17,1},{2,18},{18,2},{3,19},{19,3},{4,20},{20... | collective-permute-start | bytes 2162696 | tf_op jit(solution)/shard_map/ppermute | solution.py:114
  130.9 2.5 %collective-permute-start.12 = (bf16[176,2048]{1,0:T(8,128)(2,1)}, bf16[176,2048]{1,0:T(8,128)(2,1)S(1)}, u32[]{:S(2)}, u32[]{:S(2)}) collective-permute-start(bf16[176,2048]{1,0:T(8,128)(2,1)} %slice.262), channel_id=1, source_target_pairs={{0,16},{16,0},{1,17},{17,1},{2,18},{18,2},{3,19},{19,3},{4,20},{20... | collective-permute-start | bytes 2162696 | tf_op jit(solution)/shard_map/ppermute | solution.py:114
  133.6 0.7 copy.14
  134.4 4.6 %all-to-all-start.1 = ((bf16[32,24,128]{2,1,0:T(8,128)(2,1)}), bf16[32,24,128]{2,1,0:T(8,128)(2,1)}, u32[]{:S(2)}, u32[]{:S(2)}) async-start(bf16[32,24,128]{2,1,0:T(8,128)(2,1)} %bitcast.11), calls=%async_computation.1 | async-start | bytes 393216 | tf_op jit(solution)/shard_map/all_to_all | solution.py:128
  139.0 1.4 fusion.16
  140.4 0.5 slice.177
  140.9 1.4 fusion.15
  142.3 0.6 slice.176
  143.2 0.6 slice.178
  145.6 3.3 %all-to-all-done.1 = bf16[32,24,128]{2,1,0:T(8,128)(2,1)} async-done(((bf16[32,24,128]{2,1,0:T(8,128)(2,1)}), bf16[32,24,128]{2,1,0:T(8,128)(2,1)}, u32[]{:S(2)}, u32[]{:S(2)}) %all-to-all-start.1) | async-done | bytes 196640 | tf_op jit(solution)/shard_map/all_to_all | solution.py:128
  148.9 1.8 %convolution_convert_fusion.2 = bf16[128,128]{1,0:T(8,128)(2,1)} fusion(bf16[768,128]{1,0:T(8,128)(2,1)} %bitcast.12, s32[768]{0:T(1024)S(1)} %fusion.100, s32[128]{0:T(128)S(1)} %compare_select_fusion, bf16[]{:T(256)} %bitcast.9), kind=kOutput, calls=%fused_computation.29 | convolution fusion | flops 25477120 | bytes 232962 | tf_op jit(solution)/shard_map/dot_general | solution.py:26
  (68 shorter events, 2.3 us)
Async XLA Ops:
  0.6 1.3 copy-start
  0.6 16.7 %copy-start.4 = (bf16[1,172,2048]{2,1,0:T(8,128)(2,1)S(1)}, bf16[1,172,2048]{2,1,0:T(8,128)(2,1)}, u32[]{:S(2)}) copy-start(bf16[1,172,2048]{2,1,0:T(8,128)(2,1)} %param.14) | copy-start | bytes 2113540
  2.1 37.5 %copy-start.8 = (bf16[1,172,2048]{2,1,0:T(8,128)(2,1)S(1)}, bf16[1,172,2048]{2,1,0:T(8,128)(2,1)}, u32[]{:S(2)}) copy-start(bf16[1,172,2048]{2,1,0:T(8,128)(2,1)} %param.15) | copy-start | bytes 2113540
  2.2 18.4 %collective-permute-start = (bf16[24,2048]{1,0:T(8,128)(2,1)S(1)}, bf16[24,2048]{1,0:T(8,128)(2,1)S(1)}, u32[]{:S(2)}, u32[]{:S(2)}) collective-permute-start(bf16[24,2048]{1,0:T(8,128)(2,1)S(1)} %convolution_convert_fusion), channel_id=1, source_target_pairs={{0,32},{32,0},{1,33},{33,1},{2,34},{34,2},{3,35},{35,3},{4,36},{36... | collective-permute-start | bytes 294920 | tf_op jit(solution)/shard_map/ppermute | solution.py:59
  9.5 17.2 %all-to-all-start = ((bf16[32,24,128]{2,1,0:T(8,128)(2,1)}), bf16[32,24,128]{2,1,0:T(8,128)(2,1)S(1)}, u32[]{:S(2)}, u32[]{:S(2)}) async-start(bf16[32,24,128]{2,1,0:T(8,128)(2,1)} %bitcast), calls=%async_computation | async-start | bytes 393216 | tf_op jit(solution)/shard_map/all_to_all | solution.py:62
  17.4 26.6 %collective-permute-start.4 = (bf16[172,2048]{1,0:T(8,128)(2,1)S(1)}, bf16[172,2048]{1,0:T(8,128)(2,1)S(1)}, u32[]{:S(2)}, u32[]{:S(2)}) collective-permute-start(bf16[172,2048]{1,0:T(8,128)(2,1)S(1)} %bitcast.56), channel_id=1, source_target_pairs={{0,16},{16,0},{1,17},{17,1},{2,18},{18,2},{3,19},{19,3},{4,20},{20... | collective-permute-start | bytes 2113544 | tf_op jit(solution)/shard_map/ppermute | solution.py:54
  26.7 10.9 %copy-start.9 = (bf16[1,172,2048]{2,1,0:T(8,128)(2,1)S(1)}, bf16[1,172,2048]{2,1,0:T(8,128)(2,1)}, u32[]{:S(2)}) copy-start(bf16[1,172,2048]{2,1,0:T(8,128)(2,1)} %param.13) | copy-start | bytes 2113540
  26.9 17.2 %collective-permute-start.1 = (bf16[96,2048]{1,0:T(8,128)(2,1)S(1)}, bf16[96,2048]{1,0:T(8,128)(2,1)S(1)}, u32[]{:S(2)}, u32[]{:S(2)}) collective-permute-start(bf16[96,2048]{1,0:T(8,128)(2,1)S(1)} %pad_maximum_fusion.2), channel_id=1, source_target_pairs={{0,64},{16,464},{64,128},{80,16},{128,192},{144,80},{192,256},{208... | collective-permute-start | bytes 1179656 | tf_op jit(solution)/shard_map/ppermute | solution.py:22
  37.7 19.7 %collective-permute-start.5 = (bf16[172,2048]{1,0:T(8,128)(2,1)S(1)}, bf16[172,2048]{1,0:T(8,128)(2,1)S(1)}, u32[]{:S(2)}, u32[]{:S(2)}) collective-permute-start(bf16[172,2048]{1,0:T(8,128)(2,1)S(1)} %bitcast.63), channel_id=1, source_target_pairs={{0,16},{16,0},{1,17},{17,1},{2,18},{18,2},{3,19},{19,3},{4,20},{20... | collective-permute-start | bytes 2113544 | tf_op jit(solution)/shard_map/ppermute | solution.py:54
  39.6 17.2 %collective-permute-start.3 = (bf16[172,2048]{1,0:T(8,128)(2,1)S(1)}, bf16[172,2048]{1,0:T(8,128)(2,1)S(1)}, u32[]{:S(2)}, u32[]{:S(2)}) collective-permute-start(bf16[172,2048]{1,0:T(8,128)(2,1)S(1)} %bitcast.58), channel_id=1, source_target_pairs={{0,16},{16,0},{1,17},{17,1},{2,18},{18,2},{3,19},{19,3},{4,20},{20... | collective-permute-start | bytes 2113544 | tf_op jit(solution)/shard_map/ppermute | solution.py:54
  42.0 9.4 %collective-permute-start.2 = (bf16[96,2048]{1,0:T(8,128)(2,1)S(1)}, bf16[96,2048]{1,0:T(8,128)(2,1)S(1)}, u32[]{:S(2)}, u32[]{:S(2)}) collective-permute-start(bf16[96,2048]{1,0:T(8,128)(2,1)S(1)} %pad_maximum_fusion.2), channel_id=1, source_target_pairs={{0,464},{16,64},{64,16},{80,128},{128,80},{144,192},{192,144},{208... | collective-permute-start | bytes 1179656 | tf_op jit(solution)/shard_map/ppermute | solution.py:22
  51.6 19.6 %collective-permute-start.6 = (bf16[192,2048]{1,0:T(8,128)(2,1)S(1)}, bf16[192,2048]{1,0:T(8,128)(2,1)S(1)}, u32[]{:S(2)}, u32[]{:S(2)}) collective-permute-start(bf16[192,2048]{1,0:T(8,128)(2,1)S(1)} %pad_maximum_fusion), channel_id=1, source_target_pairs={{0,64},{16,464},{64,128},{80,16},{128,192},{144,80},{192,256},{208... | collective-permute-start | bytes 2359304 | tf_op jit(solution)/shard_map/ppermute | solution.py:22
  59.4 11.7 %collective-permute-start.8 = (bf16[96,2048]{1,0:T(8,128)(2,1)S(1)}, bf16[96,2048]{1,0:T(8,128)(2,1)S(1)}, u32[]{:S(2)}, u32[]{:S(2)}) collective-permute-start(bf16[96,2048]{1,0:T(8,128)(2,1)S(1)} %fusion.6), channel_id=1, source_target_pairs={{0,448},{16,80},{64,0},{80,144},{128,64},{144,208},{192,128},{208,... | collective-permute-start | bytes 1179656 | tf_op jit(solution)/shard_map/ppermute | solution.py:22
  73.7 13.0 %collective-permute-start.7 = (bf16[192,2048]{1,0:T(8,128)(2,1)S(1)}, bf16[192,2048]{1,0:T(8,128)(2,1)S(1)}, u32[]{:S(2)}, u32[]{:S(2)}) collective-permute-start(bf16[192,2048]{1,0:T(8,128)(2,1)S(1)} %collective-permute-done.6), channel_id=1, source_target_pairs={{0,64},{16,464},{64,128},{80,16},{128,192},{144,80},{192,256},{208... | collective-permute-start | bytes 2359304 | tf_op jit(solution)/shard_map/ppermute | solution.py:22
  86.9 8.8 %collective-permute-start.9 = (bf16[96,2048]{1,0:T(8,128)(2,1)S(1)}, bf16[96,2048]{1,0:T(8,128)(2,1)S(1)}, u32[]{:S(2)}, u32[]{:S(2)}) collective-permute-start(bf16[96,2048]{1,0:T(8,128)(2,1)S(1)} %maximum_add_fusion), channel_id=1, source_target_pairs={{0,64},{16,464},{64,128},{80,16},{128,192},{144,80},{192,256},{208... | collective-permute-start | bytes 1179656 | tf_op jit(solution)/shard_map/ppermute | solution.py:22
  93.1 19.3 %collective-permute-start.13 = (bf16[96,2048]{1,0:T(8,128)(2,1)S(1)}, bf16[96,2048]{1,0:T(8,128)(2,1)S(1)}, u32[]{:S(2)}, u32[]{:S(2)}) collective-permute-start(bf16[96,2048]{1,0:T(8,128)(2,1)S(1)} %fusion.7), channel_id=1, source_target_pairs={{0,448},{16,80},{64,0},{80,144},{128,64},{144,208},{192,128},{208,... | collective-permute-start | bytes 1179656 | tf_op jit(solution)/shard_map/ppermute | solution.py:22
  99.2 1.8 %copy-start.3 = (f32[352,2048]{1,0:T(8,128)}, f32[352,2048]{1,0:T(8,128)S(1)}, u32[]{:S(2)}) copy-start(f32[352,2048]{1,0:T(8,128)S(1)} %fusion.48) | copy-start | bytes 8650756
  102.0 1.8 %copy-start.1 = (f32[352,2048]{1,0:T(8,128)}, f32[352,2048]{1,0:T(8,128)S(1)}, u32[]{:S(2)}) copy-start(f32[352,2048]{1,0:T(8,128)S(1)} %fusion.40) | copy-start | bytes 8650756
  103.8 10.6 %collective-permute-start.16 = (bf16[48,2048]{1,0:T(8,128)(2,1)S(1)}, bf16[48,2048]{1,0:T(8,128)(2,1)S(1)}, u32[]{:S(2)}, u32[]{:S(2)}) collective-permute-start(bf16[48,2048]{1,0:T(8,128)(2,1)S(1)} %fusion.8), channel_id=1, source_target_pairs={{0,384},{16,144},{64,448},{80,208},{128,0},{144,272},{192,64},{208... | collective-permute-start | bytes 589832 | tf_op jit(solution)/shard_map/ppermute | solution.py:22
  107.3 31.6 %collective-permute-start.11 = (bf16[176,2048]{1,0:T(8,128)(2,1)}, bf16[176,2048]{1,0:T(8,128)(2,1)}, u32[]{:S(2)}, u32[]{:S(2)}) collective-permute-start(bf16[176,2048]{1,0:T(8,128)(2,1)} %slice.263), channel_id=1, source_target_pairs={{0,16},{16,0},{1,17},{17,1},{2,18},{18,2},{3,19},{19,3},{4,20},{20... | collective-permute-start | bytes 2162696 | tf_op jit(solution)/shard_map/ppermute | solution.py:114
  112.4 18.5 %collective-permute-start.14 = (bf16[48,2048]{1,0:T(8,128)(2,1)S(1)}, bf16[48,2048]{1,0:T(8,128)(2,1)S(1)}, u32[]{:S(2)}, u32[]{:S(2)}) collective-permute-start(bf16[48,2048]{1,0:T(8,128)(2,1)S(1)} %slice_add_fusion.6), channel_id=1, source_target_pairs={{0,16},{16,0},{1,17},{17,1},{2,18},{18,2},{3,19},{19,3},{4,20},{20... | collective-permute-start | bytes 589832 | tf_op jit(solution)/shard_map/ppermute | solution.py:122
  114.5 19.0 %collective-permute-start.15 = (bf16[48,2048]{1,0:T(8,128)(2,1)S(1)}, bf16[48,2048]{1,0:T(8,128)(2,1)S(1)}, u32[]{:S(2)}, u32[]{:S(2)}) collective-permute-start(bf16[48,2048]{1,0:T(8,128)(2,1)S(1)} %get-tuple-element.4), channel_id=1, source_target_pairs={{0,400},{16,128},{64,464},{80,192},{128,16},{144,256},{192,80},{20... | collective-permute-start | bytes 589832 | tf_op jit(solution)/shard_map/ppermute | solution.py:22
  122.9 10.6 %collective-permute-start.17 = (bf16[48,2048]{1,0:T(8,128)(2,1)S(1)}, bf16[48,2048]{1,0:T(8,128)(2,1)S(1)}, u32[]{:S(2)}, u32[]{:S(2)}) collective-permute-start(bf16[48,2048]{1,0:T(8,128)(2,1)S(1)} %get-tuple-element.5), channel_id=1, source_target_pairs={{0,384},{16,144},{64,448},{80,208},{128,0},{144,272},{192,64},{208... | collective-permute-start | bytes 589832 | tf_op jit(solution)/shard_map/ppermute | solution.py:22
  127.2 1.8 %copy-start.2 = (f32[352,2048]{1,0:T(8,128)}, f32[352,2048]{1,0:T(8,128)S(1)}, u32[]{:S(2)}) copy-start(f32[352,2048]{1,0:T(8,128)S(1)} %fusion.56) | copy-start | bytes 8650756
  129.0 11.9 %collective-permute-start.10 = (bf16[176,2048]{1,0:T(8,128)(2,1)}, bf16[176,2048]{1,0:T(8,128)(2,1)}, u32[]{:S(2)}, u32[]{:S(2)}) collective-permute-start(bf16[176,2048]{1,0:T(8,128)(2,1)} %slice.264), channel_id=1, source_target_pairs={{0,16},{16,0},{1,17},{17,1},{2,18},{18,2},{3,19},{19,3},{4,20},{20... | collective-permute-start | bytes 2162696 | tf_op jit(solution)/shard_map/ppermute | solution.py:114
  130.9 8.1 %slice-start.2 = ((f32[352,2048]{1,0:T(8,128)}), f32[176,2048]{1,0:T(8,128)S(1)}, s32[]{:S(2)}) async-start(f32[352,2048]{1,0:T(8,128)} %copy-done.3), calls=%async_computation.4 | async-start | bytes 2883584 | tf_op jit(solution)/shard_map/slice | solution.py:131
  130.9 12.0 %collective-permute-start.12 = (bf16[176,2048]{1,0:T(8,128)(2,1)}, bf16[176,2048]{1,0:T(8,128)(2,1)S(1)}, u32[]{:S(2)}, u32[]{:S(2)}) collective-permute-start(bf16[176,2048]{1,0:T(8,128)(2,1)} %slice.262), channel_id=1, source_target_pairs={{0,16},{16,0},{1,17},{17,1},{2,18},{18,2},{3,19},{19,3},{4,20},{20... | collective-permute-start | bytes 2162696 | tf_op jit(solution)/shard_map/ppermute | solution.py:114
  134.4 14.5 %all-to-all-start.1 = ((bf16[32,24,128]{2,1,0:T(8,128)(2,1)}), bf16[32,24,128]{2,1,0:T(8,128)(2,1)}, u32[]{:S(2)}, u32[]{:S(2)}) async-start(bf16[32,24,128]{2,1,0:T(8,128)(2,1)} %bitcast.11), calls=%async_computation.1 | async-start | bytes 393216 | tf_op jit(solution)/shard_map/all_to_all | solution.py:128
  138.9 1.9 %slice-start = ((f32[352,2048]{1,0:T(8,128)}), f32[176,2048]{1,0:T(8,128)S(1)}, s32[]{:S(2)}) async-start(f32[352,2048]{1,0:T(8,128)} %copy-done.1), calls=%async_computation.2 | async-start | bytes 2883584 | tf_op jit(solution)/shard_map/slice | solution.py:131
  140.3 1.9 %copy-start.5 = (bf16[1,172,2048]{2,1,0:T(8,128)(2,1)}, bf16[1,172,2048]{2,1,0:T(8,128)(2,1)S(1)}, u32[]{:S(2)}) copy-start(bf16[1,172,2048]{2,1,0:T(8,128)(2,1)S(1)} %fusion.16) | copy-start | bytes 2113540
  140.9 2.0 %slice-start.1 = ((f32[352,2048]{1,0:T(8,128)}), f32[176,2048]{1,0:T(8,128)S(1)}, s32[]{:S(2)}) async-start(f32[352,2048]{1,0:T(8,128)} %copy-done.2), calls=%async_computation.3 | async-start | bytes 2883584 | tf_op jit(solution)/shard_map/slice | solution.py:131
  142.3 0.9 copy-start.6
  143.2 7.5 %copy-start.7 = (bf16[1,172,2048]{2,1,0:T(8,128)(2,1)}, bf16[1,172,2048]{2,1,0:T(8,128)(2,1)S(1)}, u32[]{:S(2)}) copy-start(bf16[1,172,2048]{2,1,0:T(8,128)(2,1)S(1)} %fusion.17) | copy-start | bytes 2113540

commit v14 on v12

--- a/solution.py
+++ b/solution.py
@@ -50,10 +50,12 @@
 
     pad = ((0, PAD - hidden_own), (0, 0))
 
-    def both_cores(w):
-        return jnp.concatenate([jnp.pad(w, pad), jnp.pad(lax.ppermute(w, "core", SWAP), pad)], axis=0)
-
-    wg, wu, wd = both_cores(w_gate[0]), both_cores(w_up[0]), both_cores(w_down[0])
+    own_w = (w_gate[0], w_up[0], w_down[0])
+    other_w = [lax.ppermute(w, "core", SWAP) for w in own_w]
+    wg, wu, wd = (
+        jnp.concatenate([jnp.pad(own, pad), jnp.pad(other, pad)], axis=0)
+        for own, other in zip(own_w, other_w)
+    )
 
     x_own = dot(select_own, tokens).astype(BF)
     x_across = lax.ppermute(x_own, "xh", SWAP)
@@ -67,6 +69,7 @@
         [jnp.where(side == 0, x_own, x_across), jnp.where(side == 0, x_across, x_own)], axis=0
     )
     near = 2 * capacity
+    x_near = x_near + (other_w[0][:1] + other_w[1][:1] + other_w[2][:1]) * 0
     packet = jnp.concatenate([x_near, dy_near], axis=0)
     one = [ring(packet, 1), ring(packet, 1, cross=True)]
     one = jnp.concatenate([one[0][:near], one[1][:near], one[0][near:], one[1][near:]], axis=0)

time: 152 us -> 160 us (1.053)
  waiting for transfers between devices: 34.8 us -> 41.1 us
  matrix products: 17.1 us -> 21.5 us
  starting transfers between devices: 81.8 us -> 77.6 us
    ppermute x10, starting transfers between devices: 46.3 us -> 41.5 us  [ring(): return lax.ppermute(a, ('z', 'core'), pairs)]
    dot_general x26, matrix products: 17.1 us -> 21.5 us  [dot(): return lax.dot_general(a, b, (dims, ((), ())), preferred_element_type=F32)]
    all_to_all x1, waiting for transfers between devices: 6.19 us -> 9.7 us  [local(): dy_slices = lax.all_to_all(dy_slices, ('xh',) + EXPERT, 0, 0, tiled=True)]
    ppermute x10, waiting for transfers between devices: 25.5 us -> 28.2 us  [ring(): return lax.ppermute(a, ('z', 'core'), pairs)]
    all_to_all x1, starting transfers between devices: 7.79 us -> 5.56 us  [local(): dy_slices = lax.all_to_all(dy_slices, ('xh',) + EXPERT, 0, 0, tiled=True)]
    ppermute x3, starting transfers between devices: 7.47 us -> 9.56 us  [local(): other_w = [lax.ppermute(w, 'core', SWAP) for w in own_w]]
  transfers between devices with their start and end apart: 20 -> 20, of which waited for: 6 -> 7; matrix products, arithmetic and copies ran while one was open for 17% -> 18% of each run, Pallas kernels for 0% -> 0%
where the time goes in v14:
time: 160 us; the launch traced here: 158 us
  starting transfers between devices  77.6 us (48%)
  waiting for transfers between devices  41.1 us (26%)
  matrix products  21.5 us (13%)
  local copies, waits for them, and re-layouts  8.52 us (5%)
  other arithmetic  5.66 us (4%)
  between operations  3.2 us (2%)
    ppermute x10, starting transfers between devices, ring(): return lax.ppermute(a, ('z', 'core'), pairs)  41.5 us
    ppermute x10, waiting for transfers between devices, ring(): return lax.ppermute(a, ('z', 'core'), pairs)  28.2 us
    dot_general x26, matrix products, dot(): return lax.dot_general(a, b, (dims, ((), ())), preferred_element_type=F32)  21.5 us
    all_to_all x1, waiting for transfers between devices, local(): dy_slices = lax.all_to_all(dy_slices, ('xh',) + EXPERT, 0, 0, tiled=True)  9.7 us
    ppermute x3, starting transfers between devices, local(): other_w = [lax.ppermute(w, 'core', SWAP) for w in own_w]  9.56 us
    ppermute x3, starting transfers between devices, local(): lax.ppermute(grad[PAD:].astype(BF), 'core', SWAP)  9.05 us
    all_to_all x1, starting transfers between devices, local(): dy_slices = lax.all_to_all(dy_slices, ('xh',) + EXPERT, 0, 0, tiled=True)  5.56 us
    ppermute x1, starting transfers between devices, local(): x_across = lax.ppermute(x_own, 'xh', SWAP)  5.48 us
  transfers between devices with their start and end apart: 20, of which 7 were waited for; matrix products, arithmetic and copies ran while one was open for 18% of the time, Pallas kernels for 0%

profile of v14, /device:TPU:1, one launch (start us, length us, event | category | flops | bytes accessed | tf_op | source)
XLA Modules:
  0.0 157.6 jit_solution(7617311079288077410)
XLA Ops:
  0.7 0.7 multiply_add_fusion
  2.1 5.5 %collective-permute-start = (bf16[24,2048]{1,0:T(8,128)(2,1)S(1)}, bf16[24,2048]{1,0:T(8,128)(2,1)S(1)}, u32[]{:S(2)}, u32[]{:S(2)}) collective-permute-start(bf16[24,2048]{1,0:T(8,128)(2,1)S(1)} %convolution_convert_fusion), channel_id=1, source_target_pairs={{0,32},{32,0},{1,33},{33,1},{2,34},{34,2},{3,35},{35,3},{4,36},{36... | collective-permute-start | bytes 294920 | tf_op jit(solution)/shard_map/ppermute | solution.py:61
  7.6 5.2 %collective-permute-start.1 = (bf16[172,2048]{1,0:T(8,128)(2,1)}, bf16[172,2048]{1,0:T(8,128)(2,1)S(1)}, u32[]{:S(2)}, u32[]{:S(2)}) collective-permute-start(bf16[172,2048]{1,0:T(8,128)(2,1)} %bitcast.63), channel_id=1, source_target_pairs={{0,16},{16,0},{1,17},{17,1},{2,18},{18,2},{3,19},{19,3},{4,20},{20... | collective-permute-start | bytes 2113544 | tf_op jit(solution)/shard_map/ppermute | solution.py:54
  12.8 1.9 %collective-permute-start.3 = (bf16[172,2048]{1,0:T(8,128)(2,1)}, bf16[172,2048]{1,0:T(8,128)(2,1)}, u32[]{:S(2)}, u32[]{:S(2)}) collective-permute-start(bf16[172,2048]{1,0:T(8,128)(2,1)} %bitcast.58), channel_id=1, source_target_pairs={{0,16},{16,0},{1,17},{17,1},{2,18},{18,2},{3,19},{19,3},{4,20},{20... | collective-permute-start | bytes 2113544 | tf_op jit(solution)/shard_map/ppermute | solution.py:54
  14.8 2.4 %collective-permute-start.2 = (bf16[172,2048]{1,0:T(8,128)(2,1)}, bf16[172,2048]{1,0:T(8,128)(2,1)S(1)}, u32[]{:S(2)}, u32[]{:S(2)}) collective-permute-start(bf16[172,2048]{1,0:T(8,128)(2,1)} %bitcast.56), channel_id=1, source_target_pairs={{0,16},{16,0},{1,17},{17,1},{2,18},{18,2},{3,19},{19,3},{4,20},{20... | collective-permute-start | bytes 2113544 | tf_op jit(solution)/shard_map/ppermute | solution.py:54
  17.2 1.7 %convolution_convert_fusion.1 = bf16[768,128]{1,0:T(8,128)(2,1)} fusion(s32[128]{0:T(128)S(1)} %compare_select_fusion, s32[768]{0:T(1024)S(1)} %fusion.101, bf16[128,128]{1,0:T(8,128)(2,1)} %param.9, f32[128]{0:T(128)} %param.12), kind=kOutput, calls=%fused_computation.28 | convolution fusion | flops 25411584 | bytes 233472 | tf_op jit(solution)/shard_map/dot_general | solution.py:26
  18.9 5.6 %all-to-all-start = ((bf16[32,24,128]{2,1,0:T(8,128)(2,1)}), bf16[32,24,128]{2,1,0:T(8,128)(2,1)S(1)}, u32[]{:S(2)}, u32[]{:S(2)}) async-start(bf16[32,24,128]{2,1,0:T(8,128)(2,1)} %bitcast.3), calls=%async_computation | async-start | bytes 393216 | tf_op jit(solution)/shard_map/all_to_all | solution.py:64
  24.5 9.7 %all-to-all-done = bf16[32,24,128]{2,1,0:T(8,128)(2,1)S(1)} async-done(((bf16[32,24,128]{2,1,0:T(8,128)(2,1)}), bf16[32,24,128]{2,1,0:T(8,128)(2,1)S(1)}, u32[]{:S(2)}, u32[]{:S(2)}) %all-to-all-start) | async-done | bytes 196640 | tf_op jit(solution)/shard_map/all_to_all | solution.py:64
  34.4 0.8 fusion.96
  35.3 10.7 %collective-permute-start.4 = (bf16[96,2048]{1,0:T(8,128)(2,1)S(1)}, bf16[96,2048]{1,0:T(8,128)(2,1)S(1)}, u32[]{:S(2)}, u32[]{:S(2)}) collective-permute-start(bf16[96,2048]{1,0:T(8,128)(2,1)S(1)} %pad_maximum_fusion.2), channel_id=1, source_target_pairs={{0,64},{16,464},{64,128},{80,16},{128,192},{144,80},{192,256},{208... | collective-permute-start | bytes 1179656 | tf_op jit(solution)/shard_map/ppermute | solution.py:22
  45.9 1.9 %collective-permute-start.5 = (bf16[96,2048]{1,0:T(8,128)(2,1)S(1)}, bf16[96,2048]{1,0:T(8,128)(2,1)S(1)}, u32[]{:S(2)}, u32[]{:S(2)}) collective-permute-start(bf16[96,2048]{1,0:T(8,128)(2,1)S(1)} %pad_maximum_fusion.2), channel_id=1, source_target_pairs={{0,464},{16,64},{64,16},{80,128},{128,80},{144,192},{192,144},{208... | collective-permute-start | bytes 1179656 | tf_op jit(solution)/shard_map/ppermute | solution.py:22
  48.0 4.0 %collective-permute-done.4 = bf16[96,2048]{1,0:T(8,128)(2,1)S(1)} collective-permute-done((bf16[96,2048]{1,0:T(8,128)(2,1)S(1)}, bf16[96,2048]{1,0:T(8,128)(2,1)S(1)}, u32[]{:S(2)}, u32[]{:S(2)}) %collective-permute-start.4) | collective-permute-done | bytes 393248 | tf_op jit(solution)/shard_map/ppermute | solution.py:22
  52.1 3.2 %collective-permute-done.5 = bf16[96,2048]{1,0:T(8,128)(2,1)S(1)} collective-permute-done((bf16[96,2048]{1,0:T(8,128)(2,1)S(1)}, bf16[96,2048]{1,0:T(8,128)(2,1)S(1)}, u32[]{:S(2)}, u32[]{:S(2)}) %collective-permute-start.5) | collective-permute-done | bytes 393248 | tf_op jit(solution)/shard_map/ppermute | solution.py:22
  55.5 4.7 %collective-permute-start.6 = (bf16[192,2048]{1,0:T(8,128)(2,1)S(1)}, bf16[192,2048]{1,0:T(8,128)(2,1)S(1)}, u32[]{:S(2)}, u32[]{:S(2)}) collective-permute-start(bf16[192,2048]{1,0:T(8,128)(2,1)S(1)} %pad_maximum_fusion), channel_id=1, source_target_pairs={{0,64},{16,464},{64,128},{80,16},{128,192},{144,80},{192,256},{208... | collective-permute-start | bytes 2359304 | tf_op jit(solution)/shard_map/ppermute | solution.py:22
  60.2 1.7 %fusion.29 = f32[96,352]{1,0:T(8,128)S(1)} fusion(bf16[48,2048]{1,0:T(8,128)(2,1)S(1)} %get-tuple-element.22, bf16[48,2048]{1,0:T(8,128)(2,1)S(1)} %get-tuple-element.26, bf16[172,2048]{1,0:T(8,128)(2,1)} %collective-permute-done.3, bf16[172,2048]{1,0:T(8,128)(2,1)S(1)} %bitcast.59), kind=kOutput, calls=%fused_computation.50 | convolution fusion | flops 144965632 | bytes 1937408 | tf_op jit(solution)/shard_map/dot_general | solution.py:26
  61.9 0.6 fusion.66
  62.5 0.6 multiply_convert_fusion.4
  63.1 0.4 fusion.128
  63.5 0.5 fusion.6
  63.9 1.9 %collective-permute-start.8 = (bf16[96,2048]{1,0:T(8,128)(2,1)S(1)}, bf16[96,2048]{1,0:T(8,128)(2,1)S(1)}, u32[]{:S(2)}, u32[]{:S(2)}) collective-permute-start(bf16[96,2048]{1,0:T(8,128)(2,1)S(1)} %fusion.6), channel_id=1, source_target_pairs={{0,448},{16,80},{64,0},{80,144},{128,64},{144,208},{192,128},{208,... | collective-permute-start | bytes 1179656 | tf_op jit(solution)/shard_map/ppermute | solution.py:22
  65.9 11.3 %collective-permute-done.8 = bf16[96,2048]{1,0:T(8,128)(2,1)S(1)} collective-permute-done((bf16[96,2048]{1,0:T(8,128)(2,1)S(1)}, bf16[96,2048]{1,0:T(8,128)(2,1)S(1)}, u32[]{:S(2)}, u32[]{:S(2)}) %collective-permute-start.8) | collective-permute-done | bytes 393248 | tf_op jit(solution)/shard_map/ppermute | solution.py:22
  77.2 1.9 %collective-permute-start.13 = (bf16[48,2048]{1,0:T(8,128)(2,1)S(1)}, bf16[48,2048]{1,0:T(8,128)(2,1)S(1)}, u32[]{:S(2)}, u32[]{:S(2)}) collective-permute-start(bf16[48,2048]{1,0:T(8,128)(2,1)S(1)} %slice.192), channel_id=1, source_target_pairs={{0,16},{16,0},{1,17},{17,1},{2,18},{18,2},{3,19},{19,3},{4,20},{20... | collective-permute-start | bytes 589832 | tf_op jit(solution)/shard_map/ppermute | solution.py:119
  79.3 0.6 fusion.34
  79.9 1.7 %fusion.18 = f32[144,352]{1,0:T(8,128)S(1)} fusion(bf16[48,2048]{1,0:T(8,128)(2,1)S(1)} %bitcast.55, bf16[96,2048]{1,0:T(8,128)(2,1)S(1)} %get-tuple-element.11, bf16[172,2048]{1,0:T(8,128)(2,1)} %collective-permute-done.3, bf16[172,2048]{1,0:T(8,128)(2,1)S(1)} %bitcast.60), kind=kOutput, calls=%fused_computation.34 | convolution fusion | flops 214564864 | bytes 2201600 | tf_op jit(solution)/shard_map/dot_general | solution.py:26
  81.7 0.6 multiply_convert_fusion
  82.3 0.5 fusion.130
  82.8 3.1 %collective-permute-start.7 = (bf16[192,2048]{1,0:T(8,128)(2,1)S(1)}, bf16[192,2048]{1,0:T(8,128)(2,1)S(1)}, u32[]{:S(2)}, u32[]{:S(2)}) collective-permute-start(bf16[192,2048]{1,0:T(8,128)(2,1)S(1)} %collective-permute-done.6), channel_id=1, source_target_pairs={{0,64},{16,464},{64,128},{80,16},{128,192},{144,80},{192,256},{208... | collective-permute-start | bytes 2359304 | tf_op jit(solution)/shard_map/ppermute | solution.py:22
  85.9 0.5 convolution_add_fusion
  86.5 9.3 %collective-permute-done.7 = bf16[192,2048]{1,0:T(8,128)(2,1)S(1)} collective-permute-done((bf16[192,2048]{1,0:T(8,128)(2,1)S(1)}, bf16[192,2048]{1,0:T(8,128)(2,1)S(1)}, u32[]{:S(2)}, u32[]{:S(2)}) %collective-permute-start.7) | collective-permute-done | bytes 786464 | tf_op jit(solution)/shard_map/ppermute | solution.py:22
  95.9 4.1 %collective-permute-start.9 = (bf16[96,2048]{1,0:T(8,128)(2,1)S(1)}, bf16[96,2048]{1,0:T(8,128)(2,1)S(1)}, u32[]{:S(2)}, u32[]{:S(2)}) collective-permute-start(bf16[96,2048]{1,0:T(8,128)(2,1)S(1)} %maximum_add_fusion), channel_id=1, source_target_pairs={{0,64},{16,464},{64,128},{80,16},{128,192},{144,80},{192,256},{208... | collective-permute-start | bytes 1179656 | tf_op jit(solution)/shard_map/ppermute | solution.py:22
  100.0 1.7 %fusion.36 = f32[96,352]{1,0:T(8,128)S(1)} fusion(bf16[192,2048]{1,0:T(8,128)(2,1)S(1)} %collective-permute-done.7, bf16[172,2048]{1,0:T(8,128)(2,1)} %collective-permute-done.3, bf16[172,2048]{1,0:T(8,128)(2,1)S(1)} %bitcast.61), kind=kOutput, calls=%fused_computation.61 | convolution fusion | flops 144179200 | bytes 1953792 | tf_op jit(solution)/shard_map/dot_general | solution.py:26
  101.7 0.6 fusion.38
  102.3 0.6 multiply_convert_fusion.3
  102.9 0.4 fusion.131
  103.3 0.4 fusion.7
  103.7 1.9 %collective-permute-start.14 = (bf16[96,2048]{1,0:T(8,128)(2,1)S(1)}, bf16[96,2048]{1,0:T(8,128)(2,1)S(1)}, u32[]{:S(2)}, u32[]{:S(2)}) collective-permute-start(bf16[96,2048]{1,0:T(8,128)(2,1)S(1)} %fusion.7), channel_id=1, source_target_pairs={{0,448},{16,80},{64,0},{80,144},{128,64},{144,208},{192,128},{208,... | collective-permute-start | bytes 1179656 | tf_op jit(solution)/shard_map/ppermute | solution.py:22
  105.8 1.7 %fusion.76 = f32[48,352]{1,0:T(8,128)S(1)} fusion(bf16[96,2048]{1,0:T(8,128)(2,1)S(1)} %collective-permute-done.9, bf16[172,2048]{1,0:T(8,128)(2,1)} %collective-permute-done.3, bf16[172,2048]{1,0:T(8,128)(2,1)S(1)} %bitcast.62), kind=kOutput, calls=%fused_computation.109 | convolution fusion | flops 74973184 | bytes 1689600 | tf_op jit(solution)/shard_map/dot_general | solution.py:26
  107.4 0.6 fusion.78
  108.0 0.6 multiply_convert_fusion.9
  108.9 0.4 fusion.8
  109.4 0.9 fusion.50
  110.4 1.0 slice.282
  111.4 0.8 copy-done.3
  112.2 3.0 %collective-permute-start.16 = (bf16[48,2048]{1,0:T(8,128)(2,1)S(1)}, bf16[48,2048]{1,0:T(8,128)(2,1)S(1)}, u32[]{:S(2)}, u32[]{:S(2)}) collective-permute-start(bf16[48,2048]{1,0:T(8,128)(2,1)S(1)} %fusion.8), channel_id=1, source_target_pairs={{0,384},{16,144},{64,448},{80,208},{128,0},{144,272},{192,64},{208... | collective-permute-start | bytes 589832 | tf_op jit(solution)/shard_map/ppermute | solution.py:22
  115.2 0.9 fusion.42
  116.2 1.1 slice.283
  117.2 0.7 copy-done.1
  118.0 4.6 %collective-permute-start.11 = (bf16[176,2048]{1,0:T(8,128)(2,1)}, bf16[176,2048]{1,0:T(8,128)(2,1)}, u32[]{:S(2)}, u32[]{:S(2)}) collective-permute-start(bf16[176,2048]{1,0:T(8,128)(2,1)} %slice.282), channel_id=1, source_target_pairs={{0,16},{16,0},{1,17},{17,1},{2,18},{18,2},{3,19},{19,3},{4,20},{20... | collective-permute-start | bytes 2162696 | tf_op jit(solution)/shard_map/ppermute | solution.py:117
  123.0 6.6 %collective-permute-start.15 = (bf16[48,2048]{1,0:T(8,128)(2,1)S(1)}, bf16[48,2048]{1,0:T(8,128)(2,1)S(1)}, u32[]{:S(2)}, u32[]{:S(2)}) collective-permute-start(bf16[48,2048]{1,0:T(8,128)(2,1)S(1)} %get-tuple-element.4), channel_id=1, source_target_pairs={{0,400},{16,128},{64,464},{80,192},{128,16},{144,256},{192,80},{20... | collective-permute-start | bytes 589832 | tf_op jit(solution)/shard_map/ppermute | solution.py:22
  129.6 3.6 %collective-permute-start.17 = (bf16[48,2048]{1,0:T(8,128)(2,1)S(1)}, bf16[48,2048]{1,0:T(8,128)(2,1)S(1)}, u32[]{:S(2)}, u32[]{:S(2)}) collective-permute-start(bf16[48,2048]{1,0:T(8,128)(2,1)S(1)} %get-tuple-element.5), channel_id=1, source_target_pairs={{0,384},{16,144},{64,448},{80,208},{128,0},{144,272},{192,64},{208... | collective-permute-start | bytes 589832 | tf_op jit(solution)/shard_map/ppermute | solution.py:22
  133.2 0.9 fusion.58
  134.1 1.1 slice.281
  135.2 0.7 copy-done.2
  135.9 1.9 %collective-permute-start.10 = (bf16[176,2048]{1,0:T(8,128)(2,1)}, bf16[176,2048]{1,0:T(8,128)(2,1)}, u32[]{:S(2)}, u32[]{:S(2)}) collective-permute-start(bf16[176,2048]{1,0:T(8,128)(2,1)} %slice.283), channel_id=1, source_target_pairs={{0,16},{16,0},{1,17},{17,1},{2,18},{18,2},{3,19},{19,3},{4,20},{20... | collective-permute-start | bytes 2162696 | tf_op jit(solution)/shard_map/ppermute | solution.py:117
  137.9 2.5 %collective-permute-start.12 = (bf16[176,2048]{1,0:T(8,128)(2,1)}, bf16[176,2048]{1,0:T(8,128)(2,1)S(1)}, u32[]{:S(2)}, u32[]{:S(2)}) collective-permute-start(bf16[176,2048]{1,0:T(8,128)(2,1)} %slice.281), channel_id=1, source_target_pairs={{0,16},{16,0},{1,17},{17,1},{2,18},{18,2},{3,19},{19,3},{4,20},{20... | collective-permute-start | bytes 2162696 | tf_op jit(solution)/shard_map/ppermute | solution.py:117
  140.6 0.7 copy.13
  141.3 4.6 %all-to-all-start.1 = ((bf16[32,24,128]{2,1,0:T(8,128)(2,1)}), bf16[32,24,128]{2,1,0:T(8,128)(2,1)}, u32[]{:S(2)}, u32[]{:S(2)}) async-start(bf16[32,24,128]{2,1,0:T(8,128)(2,1)} %bitcast.11), calls=%async_computation.1 | async-start | bytes 393216 | tf_op jit(solution)/shard_map/all_to_all | solution.py:131
  145.9 1.4 fusion.16
  147.3 0.6 slice.188
  147.9 1.4 fusion.15
  149.3 0.6 slice.187
  150.2 0.5 slice.189
  152.6 3.2 %all-to-all-done.1 = bf16[32,24,128]{2,1,0:T(8,128)(2,1)} async-done(((bf16[32,24,128]{2,1,0:T(8,128)(2,1)}), bf16[32,24,128]{2,1,0:T(8,128)(2,1)}, u32[]{:S(2)}, u32[]{:S(2)}) %all-to-all-start.1) | async-done | bytes 196640 | tf_op jit(solution)/shard_map/all_to_all | solution.py:131
  155.8 1.8 %convolution_convert_fusion.2 = bf16[128,128]{1,0:T(8,128)(2,1)} fusion(bf16[768,128]{1,0:T(8,128)(2,1)} %bitcast.12, s32[768]{0:T(1024)S(1)} %fusion.101, s32[128]{0:T(128)S(1)} %compare_select_fusion, bf16[]{:T(256)} %bitcast.9), kind=kOutput, calls=%fused_computation.29 | convolution fusion | flops 25477120 | bytes 232962 | tf_op jit(solution)/shard_map/dot_general | solution.py:26
  (67 shorter events, 2.9 us)
Async XLA Ops:
  0.6 1.2 copy-start
  2.1 22.4 %collective-permute-start = (bf16[24,2048]{1,0:T(8,128)(2,1)S(1)}, bf16[24,2048]{1,0:T(8,128)(2,1)S(1)}, u32[]{:S(2)}, u32[]{:S(2)}) collective-permute-start(bf16[24,2048]{1,0:T(8,128)(2,1)S(1)} %convolution_convert_fusion), channel_id=1, source_target_pairs={{0,32},{32,0},{1,33},{33,1},{2,34},{34,2},{3,35},{35,3},{4,36},{36... | collective-permute-start | bytes 294920 | tf_op jit(solution)/shard_map/ppermute | solution.py:61
  7.6 26.8 %collective-permute-start.1 = (bf16[172,2048]{1,0:T(8,128)(2,1)}, bf16[172,2048]{1,0:T(8,128)(2,1)S(1)}, u32[]{:S(2)}, u32[]{:S(2)}) collective-permute-start(bf16[172,2048]{1,0:T(8,128)(2,1)} %bitcast.63), channel_id=1, source_target_pairs={{0,16},{16,0},{1,17},{17,1},{2,18},{18,2},{3,19},{19,3},{4,20},{20... | collective-permute-start | bytes 2113544 | tf_op jit(solution)/shard_map/ppermute | solution.py:54
  12.8 21.5 %collective-permute-start.3 = (bf16[172,2048]{1,0:T(8,128)(2,1)}, bf16[172,2048]{1,0:T(8,128)(2,1)}, u32[]{:S(2)}, u32[]{:S(2)}) collective-permute-start(bf16[172,2048]{1,0:T(8,128)(2,1)} %bitcast.58), channel_id=1, source_target_pairs={{0,16},{16,0},{1,17},{17,1},{2,18},{18,2},{3,19},{19,3},{4,20},{20... | collective-permute-start | bytes 2113544 | tf_op jit(solution)/shard_map/ppermute | solution.py:54
  14.8 19.6 %collective-permute-start.2 = (bf16[172,2048]{1,0:T(8,128)(2,1)}, bf16[172,2048]{1,0:T(8,128)(2,1)S(1)}, u32[]{:S(2)}, u32[]{:S(2)}) collective-permute-start(bf16[172,2048]{1,0:T(8,128)(2,1)} %bitcast.56), channel_id=1, source_target_pairs={{0,16},{16,0},{1,17},{17,1},{2,18},{18,2},{3,19},{19,3},{4,20},{20... | collective-permute-start | bytes 2113544 | tf_op jit(solution)/shard_map/ppermute | solution.py:54
  18.9 28.9 %copy-start.4 = (bf16[1,172,2048]{2,1,0:T(8,128)(2,1)S(1)}, bf16[1,172,2048]{2,1,0:T(8,128)(2,1)}, u32[]{:S(2)}) copy-start(bf16[1,172,2048]{2,1,0:T(8,128)(2,1)} %param.14) | copy-start | bytes 2113540
  18.9 15.3 %all-to-all-start = ((bf16[32,24,128]{2,1,0:T(8,128)(2,1)}), bf16[32,24,128]{2,1,0:T(8,128)(2,1)S(1)}, u32[]{:S(2)}, u32[]{:S(2)}) async-start(bf16[32,24,128]{2,1,0:T(8,128)(2,1)} %bitcast.3), calls=%async_computation | async-start | bytes 393216 | tf_op jit(solution)/shard_map/all_to_all | solution.py:64
  35.3 16.8 %collective-permute-start.4 = (bf16[96,2048]{1,0:T(8,128)(2,1)S(1)}, bf16[96,2048]{1,0:T(8,128)(2,1)S(1)}, u32[]{:S(2)}, u32[]{:S(2)}) collective-permute-start(bf16[96,2048]{1,0:T(8,128)(2,1)S(1)} %pad_maximum_fusion.2), channel_id=1, source_target_pairs={{0,64},{16,464},{64,128},{80,16},{128,192},{144,80},{192,256},{208... | collective-permute-start | bytes 1179656 | tf_op jit(solution)/shard_map/ppermute | solution.py:22
  45.9 9.4 %collective-permute-start.5 = (bf16[96,2048]{1,0:T(8,128)(2,1)S(1)}, bf16[96,2048]{1,0:T(8,128)(2,1)S(1)}, u32[]{:S(2)}, u32[]{:S(2)}) collective-permute-start(bf16[96,2048]{1,0:T(8,128)(2,1)S(1)} %pad_maximum_fusion.2), channel_id=1, source_target_pairs={{0,464},{16,64},{64,16},{80,128},{128,80},{144,192},{192,144},{208... | collective-permute-start | bytes 1179656 | tf_op jit(solution)/shard_map/ppermute | solution.py:22
  52.1 8.1 %copy-start.8 = (bf16[1,172,2048]{2,1,0:T(8,128)(2,1)S(1)}, bf16[1,172,2048]{2,1,0:T(8,128)(2,1)}, u32[]{:S(2)}) copy-start(bf16[1,172,2048]{2,1,0:T(8,128)(2,1)} %param.15) | copy-start | bytes 2113540
  55.5 6.4 %copy-start.9 = (bf16[1,172,2048]{2,1,0:T(8,128)(2,1)S(1)}, bf16[1,172,2048]{2,1,0:T(8,128)(2,1)}, u32[]{:S(2)}) copy-start(bf16[1,172,2048]{2,1,0:T(8,128)(2,1)} %param.13) | copy-start | bytes 2113540
  55.5 23.7 %collective-permute-start.6 = (bf16[192,2048]{1,0:T(8,128)(2,1)S(1)}, bf16[192,2048]{1,0:T(8,128)(2,1)S(1)}, u32[]{:S(2)}, u32[]{:S(2)}) collective-permute-start(bf16[192,2048]{1,0:T(8,128)(2,1)S(1)} %pad_maximum_fusion), channel_id=1, source_target_pairs={{0,64},{16,464},{64,128},{80,16},{128,192},{144,80},{192,256},{208... | collective-permute-start | bytes 2359304 | tf_op jit(solution)/shard_map/ppermute | solution.py:22
  63.9 13.2 %collective-permute-start.8 = (bf16[96,2048]{1,0:T(8,128)(2,1)S(1)}, bf16[96,2048]{1,0:T(8,128)(2,1)S(1)}, u32[]{:S(2)}, u32[]{:S(2)}) collective-permute-start(bf16[96,2048]{1,0:T(8,128)(2,1)S(1)} %fusion.6), channel_id=1, source_target_pairs={{0,448},{16,80},{64,0},{80,144},{128,64},{144,208},{192,128},{208,... | collective-permute-start | bytes 1179656 | tf_op jit(solution)/shard_map/ppermute | solution.py:22
  77.2 60.7 %collective-permute-start.13 = (bf16[48,2048]{1,0:T(8,128)(2,1)S(1)}, bf16[48,2048]{1,0:T(8,128)(2,1)S(1)}, u32[]{:S(2)}, u32[]{:S(2)}) collective-permute-start(bf16[48,2048]{1,0:T(8,128)(2,1)S(1)} %slice.192), channel_id=1, source_target_pairs={{0,16},{16,0},{1,17},{17,1},{2,18},{18,2},{3,19},{19,3},{4,20},{20... | collective-permute-start | bytes 589832 | tf_op jit(solution)/shard_map/ppermute | solution.py:119
  82.8 13.0 %collective-permute-start.7 = (bf16[192,2048]{1,0:T(8,128)(2,1)S(1)}, bf16[192,2048]{1,0:T(8,128)(2,1)S(1)}, u32[]{:S(2)}, u32[]{:S(2)}) collective-permute-start(bf16[192,2048]{1,0:T(8,128)(2,1)S(1)} %collective-permute-done.6), channel_id=1, source_target_pairs={{0,64},{16,464},{64,128},{80,16},{128,192},{144,80},{192,256},{208... | collective-permute-start | bytes 2359304 | tf_op jit(solution)/shard_map/ppermute | solution.py:22
  95.9 9.8 %collective-permute-start.9 = (bf16[96,2048]{1,0:T(8,128)(2,1)S(1)}, bf16[96,2048]{1,0:T(8,128)(2,1)S(1)}, u32[]{:S(2)}, u32[]{:S(2)}) collective-permute-start(bf16[96,2048]{1,0:T(8,128)(2,1)S(1)} %maximum_add_fusion), channel_id=1, source_target_pairs={{0,64},{16,464},{64,128},{80,16},{128,192},{144,80},{192,256},{208... | collective-permute-start | bytes 1179656 | tf_op jit(solution)/shard_map/ppermute | solution.py:22
  103.7 18.9 %collective-permute-start.14 = (bf16[96,2048]{1,0:T(8,128)(2,1)S(1)}, bf16[96,2048]{1,0:T(8,128)(2,1)S(1)}, u32[]{:S(2)}, u32[]{:S(2)}) collective-permute-start(bf16[96,2048]{1,0:T(8,128)(2,1)S(1)} %fusion.7), channel_id=1, source_target_pairs={{0,448},{16,80},{64,0},{80,144},{128,64},{144,208},{192,128},{208,... | collective-permute-start | bytes 1179656 | tf_op jit(solution)/shard_map/ppermute | solution.py:22
  110.4 1.9 %copy-start.3 = (f32[352,2048]{1,0:T(8,128)}, f32[352,2048]{1,0:T(8,128)S(1)}, u32[]{:S(2)}) copy-start(f32[352,2048]{1,0:T(8,128)S(1)} %fusion.50) | copy-start | bytes 8650756
  112.2 10.7 %collective-permute-start.16 = (bf16[48,2048]{1,0:T(8,128)(2,1)S(1)}, bf16[48,2048]{1,0:T(8,128)(2,1)S(1)}, u32[]{:S(2)}, u32[]{:S(2)}) collective-permute-start(bf16[48,2048]{1,0:T(8,128)(2,1)S(1)} %fusion.8), channel_id=1, source_target_pairs={{0,384},{16,144},{64,448},{80,208},{128,0},{144,272},{192,64},{208... | collective-permute-start | bytes 589832 | tf_op jit(solution)/shard_map/ppermute | solution.py:22
  116.2 1.8 %copy-start.1 = (f32[352,2048]{1,0:T(8,128)}, f32[352,2048]{1,0:T(8,128)S(1)}, u32[]{:S(2)}) copy-start(f32[352,2048]{1,0:T(8,128)S(1)} %fusion.42) | copy-start | bytes 8650756
  118.0 27.9 %collective-permute-start.11 = (bf16[176,2048]{1,0:T(8,128)(2,1)}, bf16[176,2048]{1,0:T(8,128)(2,1)}, u32[]{:S(2)}, u32[]{:S(2)}) collective-permute-start(bf16[176,2048]{1,0:T(8,128)(2,1)} %slice.282), channel_id=1, source_target_pairs={{0,16},{16,0},{1,17},{17,1},{2,18},{18,2},{3,19},{19,3},{4,20},{20... | collective-permute-start | bytes 2162696 | tf_op jit(solution)/shard_map/ppermute | solution.py:117
  123.0 17.4 %collective-permute-start.15 = (bf16[48,2048]{1,0:T(8,128)(2,1)S(1)}, bf16[48,2048]{1,0:T(8,128)(2,1)S(1)}, u32[]{:S(2)}, u32[]{:S(2)}) collective-permute-start(bf16[48,2048]{1,0:T(8,128)(2,1)S(1)} %get-tuple-element.4), channel_id=1, source_target_pairs={{0,400},{16,128},{64,464},{80,192},{128,16},{144,256},{192,80},{20... | collective-permute-start | bytes 589832 | tf_op jit(solution)/shard_map/ppermute | solution.py:22
  129.6 10.8 %collective-permute-start.17 = (bf16[48,2048]{1,0:T(8,128)(2,1)S(1)}, bf16[48,2048]{1,0:T(8,128)(2,1)S(1)}, u32[]{:S(2)}, u32[]{:S(2)}) collective-permute-start(bf16[48,2048]{1,0:T(8,128)(2,1)S(1)} %get-tuple-element.5), channel_id=1, source_target_pairs={{0,384},{16,144},{64,448},{80,208},{128,0},{144,272},{192,64},{208... | collective-permute-start | bytes 589832 | tf_op jit(solution)/shard_map/ppermute | solution.py:22
  134.1 1.8 %copy-start.2 = (f32[352,2048]{1,0:T(8,128)}, f32[352,2048]{1,0:T(8,128)S(1)}, u32[]{:S(2)}) copy-start(f32[352,2048]{1,0:T(8,128)S(1)} %fusion.58) | copy-start | bytes 8650756
  135.9 12.0 %collective-permute-start.10 = (bf16[176,2048]{1,0:T(8,128)(2,1)}, bf16[176,2048]{1,0:T(8,128)(2,1)}, u32[]{:S(2)}, u32[]{:S(2)}) collective-permute-start(bf16[176,2048]{1,0:T(8,128)(2,1)} %slice.283), channel_id=1, source_target_pairs={{0,16},{16,0},{1,17},{17,1},{2,18},{18,2},{3,19},{19,3},{4,20},{20... | collective-permute-start | bytes 2162696 | tf_op jit(solution)/shard_map/ppermute | solution.py:117
  137.8 8.1 %slice-start.2 = ((f32[352,2048]{1,0:T(8,128)}), f32[176,2048]{1,0:T(8,128)S(1)}, s32[]{:S(2)}) async-start(f32[352,2048]{1,0:T(8,128)} %copy-done.3), calls=%async_computation.4 | async-start | bytes 2883584 | tf_op jit(solution)/shard_map/slice | solution.py:134
  137.9 12.1 %collective-permute-start.12 = (bf16[176,2048]{1,0:T(8,128)(2,1)}, bf16[176,2048]{1,0:T(8,128)(2,1)S(1)}, u32[]{:S(2)}, u32[]{:S(2)}) collective-permute-start(bf16[176,2048]{1,0:T(8,128)(2,1)} %slice.281), channel_id=1, source_target_pairs={{0,16},{16,0},{1,17},{17,1},{2,18},{18,2},{3,19},{19,3},{4,20},{20... | collective-permute-start | bytes 2162696 | tf_op jit(solution)/shard_map/ppermute | solution.py:117
  141.3 14.5 %all-to-all-start.1 = ((bf16[32,24,128]{2,1,0:T(8,128)(2,1)}), bf16[32,24,128]{2,1,0:T(8,128)(2,1)}, u32[]{:S(2)}, u32[]{:S(2)}) async-start(bf16[32,24,128]{2,1,0:T(8,128)(2,1)} %bitcast.11), calls=%async_computation.1 | async-start | bytes 393216 | tf_op jit(solution)/shard_map/all_to_all | solution.py:131
  145.9 2.0 %slice-start = ((f32[352,2048]{1,0:T(8,128)}), f32[176,2048]{1,0:T(8,128)S(1)}, s32[]{:S(2)}) async-start(f32[352,2048]{1,0:T(8,128)} %copy-done.1), calls=%async_computation.2 | async-start | bytes 2883584 | tf_op jit(solution)/shard_map/slice | solution.py:134
  147.3 2.0 %copy-start.5 = (bf16[1,172,2048]{2,1,0:T(8,128)(2,1)}, bf16[1,172,2048]{2,1,0:T(8,128)(2,1)S(1)}, u32[]{:S(2)}) copy-start(bf16[1,172,2048]{2,1,0:T(8,128)(2,1)S(1)} %fusion.16) | copy-start | bytes 2113540
  147.9 2.0 %slice-start.1 = ((f32[352,2048]{1,0:T(8,128)}), f32[176,2048]{1,0:T(8,128)S(1)}, s32[]{:S(2)}) async-start(f32[352,2048]{1,0:T(8,128)} %copy-done.2), calls=%async_computation.3 | async-start | bytes 2883584 | tf_op jit(solution)/shard_map/slice | solution.py:134
  149.3 0.9 copy-start.6
  150.2 7.4 %copy-start.7 = (bf16[1,172,2048]{2,1,0:T(8,128)(2,1)}, bf16[1,172,2048]{2,1,0:T(8,128)(2,1)S(1)}, u32[]{:S(2)}) copy-start(bf16[1,172,2048]{2,1,0:T(8,128)(2,1)S(1)} %fusion.17) | copy-start | bytes 2113540
